TPU v7x, 32 devices: a whole 2x2x4 slice. The times are simulated.
32 devices in a mesh: seq: 2 (over y), shard: 4 (over x, core), replica: 4 (over z).
Axes of the slice: x: 2, y: 2, z: 4, core: 2. Of those that a mesh axis runs over, the one named last changes fastest.
Arguments:
- tokens: bfloat16 [16, 256, 2048], P(('shard', 'replica'), 'seq'), may hold values from -6 to 6
- segments: int32 [16, 256], P(('shard', 'replica'), 'seq'), may hold values from 0 to 5, never falling along the last dimension, each value on 1 to 96 neighbouring positions
- cotangent: bfloat16 [16, 256, 2048], P(('shard', 'replica'), 'seq'), may hold values from -6 to 6
- norm_gain: float32 [2048], P(('seq', 'shard')), may hold values from 0.5 to 1.5
- branch_weight: float32 [2048, 2560], P(('seq', 'shard')), may hold values from -0.125 to 0.125
- input_weight: float32 [2048, 2560], P(('seq', 'shard')), may hold values from -0.125 to 0.125
- conv_weight: float32 [4, 2560], P(None, ('seq', 'shard')), may hold values from -3 to 3
- conv_bias: float32 [2560], P(('seq', 'shard')), may hold values from -3 to 3
- recur_gate_weight: float32 [16, 160, 160], P(('seq', 'shard')), may hold values from -0.5 to 0.5
- recur_gate_bias: float32 [2560], P(('seq', 'shard')), may hold values from -4 to 4
- input_gate_weight: float32 [16, 160, 160], P(('seq', 'shard')), may hold values from -0.5 to 0.5
- input_gate_bias: float32 [2560], P(('seq', 'shard')), may hold values from -4 to 4
- decay_param: float32 [2560], P(('seq', 'shard'))
- output_weight: float32 [2560, 2048], P(('seq', 'shard')), may hold values from -0.3125 to 0.3125
- mlp_norm_gain: float32 [2048], P(('seq', 'shard')), may hold values from 0.5 to 1.5
- gate_weight: float32 [2048, 6144], P(('seq', 'shard')), may hold values from -0.125 to 0.125
- up_weight: float32 [2048, 6144], P(('seq', 'shard')), may hold values from -0.125 to 0.125
- down_weight: float32 [6144, 2048], P(('seq', 'shard')), may hold values from -0.109375 to 0.109375
Outputs:
- block_out: bfloat16 [16, 256, 2048], P(('shard', 'replica'), 'seq')
- tokens_grad: bfloat16 [16, 256, 2048], P(('shard', 'replica'), 'seq')
- norm_gain_grad: float32 [2048], P(('seq', 'shard'))
- branch_weight_grad: float32 [2048, 2560], P(('seq', 'shard'))
- input_weight_grad: float32 [2048, 2560], P(('seq', 'shard'))
- conv_weight_grad: float32 [4, 2560], P(None, ('seq', 'shard'))
- conv_bias_grad: float32 [2560], P(('seq', 'shard'))
- recur_gate_weight_grad: float32 [16, 160, 160], P(('seq', 'shard'))
- recur_gate_bias_grad: float32 [2560], P(('seq', 'shard'))
- input_gate_weight_grad: float32 [16, 160, 160], P(('seq', 'shard'))
- input_gate_bias_grad: float32 [2560], P(('seq', 'shard'))
- decay_param_grad: float32 [2560], P(('seq', 'shard'))
- output_weight_grad: float32 [2560, 2048], P(('seq', 'shard'))
- mlp_norm_gain_grad: float32 [2048], P(('seq', 'shard'))
- gate_weight_grad: float32 [2048, 6144], P(('seq', 'shard'))
- up_weight_grad: float32 [2048, 6144], P(('seq', 'shard'))
- down_weight_grad: float32 [6144, 2048], P(('seq', 'shard'))
Inputs may be any that keep to these rules, and one draw needn't show every extreme that they name: `segments`: segment numbers never fall along a sequence; each document has 1 to 96 tokens and one has exactly 96.
All inputs are finite; a program needn't handle non-finite values.
Results may differ from a plain program's by a relative error of at most 0.02.
Values may be sent and summed in bfloat16 or wider, within the bound.
A program may use at most 576 MiB of HBM per device.

v0:
```python
import jax
import jax.numpy as jnp
from jax import lax
from jax.sharding import PartitionSpec as P

epsilon = 1e-06
decay_scale = 8.0


def from_behind(block, axis, distance):
    devices = range(lax.axis_size(axis))
    route = [(i - distance, i) for i in devices if i - distance in devices]
    return lax.ppermute(block, axis, route)


def carried_in(array, axis, combine, identity, reverse):
    length, mine = (lax.axis_size(axis), lax.axis_index(axis))
    everything = jax.tree.map(lambda part: lax.all_gather(part, axis), array)
    start = jax.tree.map(
        lambda part, zero: jnp.broadcast_to(jnp.asarray(zero, part.dtype), part.shape),
        array,
        identity,
    )

    def lap(k, before):
        at = length - 1 - k if reverse else k
        reached = at > mine if reverse else at < mine
        new = combine(before, jax.tree.map(lambda part: part[at], everything))
        return jax.tree.map(lambda a, b: jnp.where(reached, a, b), new, before)

    return lax.fori_loop(0, length, lap, start)


def link(earlier, later):
    return (earlier[0] * later[0], earlier[1] * later[0] + later[1])


def transposed(left, right):
    return lax.dot_general(
        left, right, (((1,), (1,)), ((), ())), preferred_element_type=jnp.float32
    )


def spread_rows(left, right):
    return lax.psum_scatter(
        lax.dot_general(
            left, right, (((0,), (0,)), ((), ())), preferred_element_type=jnp.float32
        ).astype(jnp.bfloat16),
        ("seq", "shard"),
        scatter_dimension=0,
        tiled=True,
    ).astype(jnp.float32)


def norm_backward(grad_unit, unit, inverse):
    return inverse * (grad_unit - unit * jnp.mean(grad_unit * unit, axis=-1, keepdims=True))


def body(
    tokens,
    segments,
    cotangent,
    norm_gain,
    branch_weight,
    input_weight,
    conv_weight,
    conv_bias,
    recur_gate_weight,
    recur_gate_bias,
    input_gate_weight,
    input_gate_bias,
    decay_param,
    output_weight,
    mlp_norm_gain,
    gate_weight,
    up_weight,
    down_weight,
):
    masters = (
        norm_gain,
        branch_weight,
        input_weight,
        conv_weight,
        conv_bias,
        recur_gate_weight,
        recur_gate_bias,
        input_gate_weight,
        input_gate_bias,
        decay_param,
        output_weight,
        mlp_norm_gain,
        gate_weight,
        up_weight,
        down_weight,
    )
    lowered = [item.astype(jnp.bfloat16) for item in masters]
    forward_set = (
        lax.all_gather(lowered[0], ("seq", "shard"), axis=0, tiled=True),
        lax.all_gather(lowered[1], ("seq", "shard"), axis=0, tiled=True),
        lax.all_gather(lowered[2], ("seq", "shard"), axis=0, tiled=True),
        lax.all_gather(lowered[3], ("seq", "shard"), axis=1, tiled=True),
        lax.all_gather(lowered[4], ("seq", "shard"), axis=0, tiled=True),
        lax.all_gather(lowered[5], ("seq", "shard"), axis=0, tiled=True),
        lax.all_gather(lowered[6], ("seq", "shard"), axis=0, tiled=True),
        lax.all_gather(lowered[7], ("seq", "shard"), axis=0, tiled=True),
        lax.all_gather(lowered[8], ("seq", "shard"), axis=0, tiled=True),
        lax.all_gather(lowered[9], ("seq", "shard"), axis=0, tiled=True),
        lax.all_gather(lowered[10], ("seq", "shard"), axis=0, tiled=True),
        lax.all_gather(lowered[11], ("seq", "shard"), axis=0, tiled=True),
        lax.all_gather(lowered[12], ("seq", "shard"), axis=0, tiled=True),
        lax.all_gather(lowered[13], ("seq", "shard"), axis=0, tiled=True),
        lax.all_gather(lowered[14], ("seq", "shard"), axis=0, tiled=True),
    )
    (
        gain_full,
        branch_full,
        input_full,
        conv_full,
        conv_bias_full,
        recur_full,
        recur_bias_full,
        inject_full,
        inject_bias_full,
        decay_full,
        output_full,
        mlp_gain_full,
        gate_full,
        up_full,
        down_full,
    ) = forward_set
    f32 = jnp.float32
    bf16 = jnp.bfloat16
    rows = tokens[0].astype(f32)
    count_rows = rows.shape[0]
    labels = segments[0] + 1
    conv_taps = conv_full.shape[0]
    lead = conv_taps - 1
    blocks_count = recur_full.shape[0]
    inverse = lax.rsqrt(jnp.mean(rows * rows, axis=-1, keepdims=True) + epsilon)
    unit = rows * inverse
    gain_f = gain_full.astype(f32)
    normed = (unit * gain_f).astype(bf16)
    branch_pre = jnp.dot(normed, branch_full, preferred_element_type=f32)
    branch_act, branch_pull = jax.vjp(jax.nn.gelu, branch_pre)
    conv_in = jnp.dot(normed, input_full, preferred_element_type=f32).astype(bf16)
    edge_rows, edge_labels = from_behind(
        (conv_in[count_rows - lead :], labels[count_rows - lead :]), "seq", 1
    )
    ext_in = jnp.concatenate([edge_rows, conv_in], 0).astype(f32)
    ext_labels = jnp.concatenate([edge_labels, labels], 0)
    conv_f = conv_full.astype(f32)
    masks = []
    conv_out = jnp.zeros((count_rows, conv_f.shape[1]), f32) + conv_bias_full.astype(f32)
    for offset in range(conv_taps):
        mask = (ext_labels[lead - offset : lead - offset + count_rows] == labels).astype(f32)[
            :, None
        ]
        masks.append(mask)
        conv_out = (
            conv_out + conv_f[offset] * ext_in[lead - offset : lead - offset + count_rows] * mask
        )
    values = conv_out.astype(bf16)
    values_f = values.astype(f32)
    blocks = values.reshape(count_rows, blocks_count, -1)
    recur_pre = jnp.einsum("thi,hij->thj", blocks, recur_full, preferred_element_type=f32).reshape(
        count_rows, -1
    )
    recur_gate = jax.nn.sigmoid(recur_pre + recur_bias_full.astype(f32))
    inject_pre = jnp.einsum(
        "thi,hij->thj", blocks, inject_full, preferred_element_type=f32
    ).reshape(count_rows, -1)
    inject_gate = jax.nn.sigmoid(inject_pre + inject_bias_full.astype(f32))
    starts = (labels != ext_labels[lead - 1 : lead - 1 + count_rows])[:, None]
    decay_f = decay_full.astype(f32)
    rate = jax.nn.softplus(-decay_f)
    log_decay = -decay_scale * rate * recur_gate
    decay = jnp.where(starts, 0.0, jnp.exp(log_decay))
    scale = jnp.where(starts, 1.0, jnp.sqrt(-jnp.expm1(2.0 * log_decay)))
    driven = scale * inject_gate * values_f
    cumul, local = lax.associative_scan(link, (decay, driven), axis=0)
    width = decay.shape[1]
    ones_row = jnp.ones((width,), f32)
    zero_row = jnp.zeros((width,), f32)
    carried = carried_in((cumul[-1], local[-1]), "seq", link, (ones_row, zero_row), False)
    incoming = carried[1]
    states = local + cumul * incoming
    product = (branch_act * states).astype(bf16)
    middle = rows + jnp.dot(product, output_full, preferred_element_type=f32)
    inverse_two = lax.rsqrt(jnp.mean(middle * middle, axis=-1, keepdims=True) + epsilon)
    unit_two = middle * inverse_two
    mlp_gain_f = mlp_gain_full.astype(f32)
    normed_two = (unit_two * mlp_gain_f).astype(bf16)
    gate_pre = jnp.dot(normed_two, gate_full, preferred_element_type=f32)
    up_pre = jnp.dot(normed_two, up_full, preferred_element_type=f32)
    gate_act, gate_pull = jax.vjp(jax.nn.gelu, gate_pre)
    hidden = (gate_act * up_pre).astype(bf16)
    block_out = (middle + jnp.dot(hidden, down_full, preferred_element_type=f32)).astype(bf16)
    branch_back = forward_set[1]
    input_back = forward_set[2]
    recur_back = forward_set[5]
    inject_back = forward_set[7]
    output_back = forward_set[10]
    gate_back = forward_set[12]
    up_back = forward_set[13]
    down_back = forward_set[14]
    out_low = cotangent[0]
    grad_out = out_low.astype(f32)
    hidden_grad = transposed(out_low, down_back)
    gate_low = gate_pull(hidden_grad * up_pre)[0].astype(bf16)
    up_low = (hidden_grad * gate_act).astype(bf16)
    two_grad = transposed(gate_low, gate_back) + transposed(up_low, up_back)
    mlp_gain_grad = jnp.sum(two_grad * unit_two, axis=0)
    middle_grad = grad_out + norm_backward(two_grad * mlp_gain_f, unit_two, inverse_two)
    mid_low = middle_grad.astype(bf16)
    product_grad = transposed(mid_low, output_back)
    branch_low = branch_pull(product_grad * states)[0].astype(bf16)
    states_grad = product_grad * branch_act
    following = jnp.concatenate([decay[1:], jnp.ones((1, width), f32)], 0)
    flip_cum, flip_local = lax.associative_scan(
        link, (jnp.flip(following, 0), jnp.flip(states_grad, 0)), axis=0
    )
    back_cum = jnp.flip(flip_cum, 0)
    back_local = jnp.flip(flip_local, 0)
    from_above = carried_in(
        (decay[0] * back_cum[0], decay[0] * back_local[0]), "seq", link, (ones_row, zero_row), True
    )
    adjoint = back_local + back_cum * from_above[1]
    previous = jnp.concatenate([incoming[None], states[:-1]], 0)
    scale_grad = adjoint * inject_gate * values_f
    log_grad = jnp.where(
        starts, 0.0, adjoint * previous * decay - scale_grad * decay * decay / scale
    )
    decay_param_grad = jnp.sum(log_grad * decay_scale * recur_gate, axis=0) * jax.nn.sigmoid(
        -decay_f
    )
    recur_low = (log_grad * (-decay_scale * rate) * recur_gate * (1.0 - recur_gate)).astype(bf16)
    inject_low = (adjoint * scale * values_f * inject_gate * (1.0 - inject_gate)).astype(bf16)
    recur_bias_grad = jnp.sum(recur_low.astype(f32), axis=0)
    inject_bias_grad = jnp.sum(inject_low.astype(f32), axis=0)
    recur_blocks = recur_low.reshape(count_rows, blocks_count, -1)
    inject_blocks = inject_low.reshape(count_rows, blocks_count, -1)
    recur_weight_grad = jnp.einsum("thi,thj->hij", blocks, recur_blocks, preferred_element_type=f32)
    inject_weight_grad = jnp.einsum(
        "thi,thj->hij", blocks, inject_blocks, preferred_element_type=f32
    )
    values_grad = adjoint * scale * inject_gate
    values_grad = values_grad + jnp.einsum(
        "thj,hij->thi", recur_blocks, recur_back, preferred_element_type=f32
    ).reshape(count_rows, -1)
    values_grad = values_grad + jnp.einsum(
        "thj,hij->thi", inject_blocks, inject_back, preferred_element_type=f32
    ).reshape(count_rows, -1)
    conv_bias_grad = jnp.sum(values_grad, axis=0)
    tap_grads = []
    ext_grad = jnp.zeros((count_rows + lead, width), f32)
    for offset in range(conv_taps):
        tap_grads.append(
            jnp.sum(
                values_grad * ext_in[lead - offset : lead - offset + count_rows] * masks[offset],
                axis=0,
            )
        )
        piece = values_grad * conv_f[offset] * masks[offset]
        ext_grad = ext_grad + jnp.pad(piece, ((lead - offset, offset), (0, 0)))
    conv_weight_grad = jnp.stack(tap_grads, 0)
    sent = from_behind(ext_grad[:lead], "seq", -1)
    conv_in_grad = ext_grad[lead:] + jnp.pad(sent, ((count_rows - lead, 0), (0, 0)))
    conv_low = conv_in_grad.astype(bf16)
    normed_grad = transposed(branch_low, branch_back) + transposed(conv_low, input_back)
    gain_grad = jnp.sum(normed_grad * unit, axis=0)
    tokens_grad = (middle_grad + norm_backward(normed_grad * gain_f, unit, inverse)).astype(bf16)
    branch_weight_grad = spread_rows(normed, branch_low)
    input_weight_grad = spread_rows(normed, conv_low)
    output_weight_grad = spread_rows(product, mid_low)
    gate_weight_grad = spread_rows(normed_two, gate_low)
    up_weight_grad = spread_rows(normed_two, up_low)
    down_weight_grad = spread_rows(hidden, out_low)
    small = (
        lax.psum_scatter(gain_grad, ("seq", "shard"), scatter_dimension=0, tiled=True),
        lax.psum_scatter(conv_weight_grad, ("seq", "shard"), scatter_dimension=1, tiled=True),
        lax.psum_scatter(conv_bias_grad, ("seq", "shard"), scatter_dimension=0, tiled=True),
        lax.psum_scatter(recur_weight_grad, ("seq", "shard"), scatter_dimension=0, tiled=True),
        lax.psum_scatter(recur_bias_grad, ("seq", "shard"), scatter_dimension=0, tiled=True),
        lax.psum_scatter(inject_weight_grad, ("seq", "shard"), scatter_dimension=0, tiled=True),
        lax.psum_scatter(inject_bias_grad, ("seq", "shard"), scatter_dimension=0, tiled=True),
        lax.psum_scatter(decay_param_grad, ("seq", "shard"), scatter_dimension=0, tiled=True),
        lax.psum_scatter(mlp_gain_grad, ("seq", "shard"), scatter_dimension=0, tiled=True),
    )
    summed = (
        lax.psum(small[0].astype(jnp.bfloat16), "replica").astype(jnp.float32),
        lax.psum(branch_weight_grad.astype(jnp.bfloat16), "replica").astype(jnp.float32),
        lax.psum(input_weight_grad.astype(jnp.bfloat16), "replica").astype(jnp.float32),
        lax.psum(small[1].astype(jnp.bfloat16), "replica").astype(jnp.float32),
        lax.psum(small[2].astype(jnp.bfloat16), "replica").astype(jnp.float32),
        lax.psum(small[3].astype(jnp.bfloat16), "replica").astype(jnp.float32),
        lax.psum(small[4].astype(jnp.bfloat16), "replica").astype(jnp.float32),
        lax.psum(small[5].astype(jnp.bfloat16), "replica").astype(jnp.float32),
        lax.psum(small[6].astype(jnp.bfloat16), "replica").astype(jnp.float32),
        lax.psum(small[7].astype(jnp.bfloat16), "replica").astype(jnp.float32),
        lax.psum(output_weight_grad.astype(jnp.bfloat16), "replica").astype(jnp.float32),
        lax.psum(small[8].astype(jnp.bfloat16), "replica").astype(jnp.float32),
        lax.psum(gate_weight_grad.astype(jnp.bfloat16), "replica").astype(jnp.float32),
        lax.psum(up_weight_grad.astype(jnp.bfloat16), "replica").astype(jnp.float32),
        lax.psum(down_weight_grad.astype(jnp.bfloat16), "replica").astype(jnp.float32),
    )
    return (
        block_out[None],
        tokens_grad[None],
        summed[0],
        summed[1],
        summed[2],
        summed[3],
        summed[4],
        summed[5],
        summed[6],
        summed[7],
        summed[8],
        summed[9],
        summed[10],
        summed[11],
        summed[12],
        summed[13],
        summed[14],
    )


def solution(mesh):
    in_specs = (
        P(("shard", "replica"), "seq", None),
        P(("shard", "replica"), "seq"),
        P(("shard", "replica"), "seq", None),
        P(("seq", "shard")),
        P(("seq", "shard"), None),
        P(("seq", "shard"), None),
        P(None, ("seq", "shard")),
        P(("seq", "shard")),
        P(("seq", "shard"), None, None),
        P(("seq", "shard")),
        P(("seq", "shard"), None, None),
        P(("seq", "shard")),
        P(("seq", "shard")),
        P(("seq", "shard"), None),
        P(("seq", "shard")),
        P(("seq", "shard"), None),
        P(("seq", "shard"), None),
        P(("seq", "shard"), None),
    )
    out_specs = (
        P(("shard", "replica"), "seq", None),
        P(("shard", "replica"), "seq", None),
        P(("seq", "shard")),
        P(("seq", "shard"), None),
        P(("seq", "shard"), None),
        P(None, ("seq", "shard")),
        P(("seq", "shard")),
        P(("seq", "shard"), None, None),
        P(("seq", "shard")),
        P(("seq", "shard"), None, None),
        P(("seq", "shard")),
        P(("seq", "shard")),
        P(("seq", "shard"), None),
        P(("seq", "shard")),
        P(("seq", "shard"), None),
        P(("seq", "shard"), None),
        P(("seq", "shard"), None),
    )
    return jax.shard_map(body, mesh=mesh, in_specs=in_specs, out_specs=out_specs, check_vma=False)
```

profile of v0, /device:TPU:0, one launch (start us, length us, event | category | flops | bytes accessed | tf_op | source)
XLA Modules:
  0.0 2261.2 jit_solution(12420942235608009827)
XLA Ops:
  19.8 5.6 convert_element_type.285
  36.0 8.9 all-gather
  47.1 24.4 %all-reduce.74 = (bf16[2560]{0:T(1024)(128)(2,1)S(1)}, bf16[2560]{0:T(1024)(128)(2,1)S(1)}, bf16[2560]{0:T(1024)(128)(2,1)S(1)}, bf16[2560]{0:T(1024)(128)(2,1)S(1)}) all-reduce(bf16[2560]{0:T(1024)(128)(2,1)S(1)} %dynamic-update-slice, ...), channel_id=1, replica_groups=mesh['seq'=2,'shard'=4,'replica'=4] {'seq','shard'}, use_global_device_ids=true, to_apply=%add.63 | all-reduce | flops 10240 | bytes 40960
  71.6 8.1 all-gather.1
  79.9 8.8 all-gather.4
  89.7 19.0 all_gather.65
  108.7 16.9 all_gather.67
  125.7 5.7 convolution_convert_fusion.6
  148.8 5.2 convert_multiply_fusion.2
  306.7 5.1 pad.206
  340.0 9.9 slice.582
  349.9 9.9 slice.588
  359.8 9.9 slice.632
  370.6 9.2 multiply_convert_fusion.3
  379.8 5.9 multiply_reduce_fusion.7
  387.6 13.9 fusion.98
  401.4 70.7 %all-gather.22.cloned.1.call-done = bf16[2048,6144]{1,0:T(8,128)(2,1)} async-done(((bf16[256,6144]{1,0:T(8,128)(2,1)}), bf16[2048,6144]{1,0:T(8,128)(2,1)}) %all-gather.22.cloned.1.call-update) | async-done | bytes 25165840 | tf_op jit(solution)/shard_map/all_gather | solution.py:111
  472.1 13.4 fusion.99
  485.5 114.2 %all-gather.24.cloned.1.call-done = bf16[6144,2048]{1,0:T(8,128)(2,1)} async-done(((bf16[768,2048]{1,0:T(8,128)(2,1)}), bf16[6144,2048]{1,0:T(8,128)(2,1)}) %all-gather.24.cloned.1.call-update) | async-done | bytes 25165840 | tf_op jit(solution)/shard_map/all_gather | solution.py:112
  599.8 17.6 multiply_convert_fusion
  617.4 14.3 fusion.100
  631.7 15.9 multiply_reduce_fusion.5
  650.1 9.5 fusion.38
  666.3 9.8 slice.579
  676.1 9.9 slice.584
  798.8 5.1 pad.249
  817.9 9.9 slice.634
  858.0 10.7 rev.10
  868.8 10.7 rev.9
  879.6 5.0 multiply_reduce_fusion
  899.3 8.3 convolution_convert_fusion.3
  908.3 6.7 convolution_convert_fusion.5
  937.8 5.7 convolution_convert_fusion.4
  944.5 13.7 convolution_convert_fusion.2
  958.3 13.3 convolution_convert_fusion.1
  972.7 13.6 convolution_convert_fusion
  991.3 79.3 %reduce-scatter.20.cloned.1.call-done = bf16[320,2048]{1,0:T(8,128)(2,1)} async-done(((bf16[2560,2048]{1,0:T(8,128)(2,1)}), bf16[320,2048]{1,0:T(8,128)(2,1)}) %reduce-scatter.20.cloned.1.call-update) | async-done | bytes 1310736 | tf_op jit(solution)/shard_map/reduce_scatter | solution.py:45
  1070.6 84.9 %reduce-scatter.12.cloned.1.call-done = bf16[256,2560]{1,0:T(8,128)(2,1)} async-done(((bf16[2048,2560]{1,0:T(8,128)(2,1)}), bf16[256,2560]{1,0:T(8,128)(2,1)}) %reduce-scatter.12.cloned.1.call-update) | async-done | bytes 1310736 | tf_op jit(solution)/shard_map/reduce_scatter | solution.py:45
  1155.5 85.1 %reduce-scatter.14.cloned.1.call-done = bf16[256,2560]{1,0:T(8,128)(2,1)} async-done(((bf16[2048,2560]{1,0:T(8,128)(2,1)}), bf16[256,2560]{1,0:T(8,128)(2,1)}) %reduce-scatter.14.cloned.1.call-update) | async-done | bytes 1310736 | tf_op jit(solution)/shard_map/reduce_scatter | solution.py:45
  1240.6 160.4 %reduce-scatter.22.cloned.1.call-done = bf16[256,6144]{1,0:T(8,128)(2,1)} async-done(((bf16[2048,6144]{1,0:T(8,128)(2,1)}), bf16[256,6144]{1,0:T(8,128)(2,1)}) %reduce-scatter.22.cloned.1.call-update) | async-done | bytes 3145744 | tf_op jit(solution)/shard_map/reduce_scatter | solution.py:45
  1401.0 160.5 %reduce-scatter.24.cloned.1.call-done = bf16[256,6144]{1,0:T(8,128)(2,1)} async-done(((bf16[2048,6144]{1,0:T(8,128)(2,1)}), bf16[256,6144]{1,0:T(8,128)(2,1)}) %reduce-scatter.24.cloned.1.call-update) | async-done | bytes 3145744 | tf_op jit(solution)/shard_map/reduce_scatter | solution.py:45
  1561.5 160.4 %reduce-scatter.26.cloned.1.call-done = bf16[768,2048]{1,0:T(8,128)(2,1)} async-done(((bf16[6144,2048]{1,0:T(8,128)(2,1)}), bf16[768,2048]{1,0:T(8,128)(2,1)}) %reduce-scatter.26.cloned.1.call-update) | async-done | bytes 3145744 | tf_op jit(solution)/shard_map/reduce_scatter | solution.py:45
  1723.4 7.5 fusion.101
  1731.0 11.7 fusion.8
  1747.2 23.9 %all-reduce.73 = (bf16[2048]{0:T(1024)(128)(2,1)S(1)}, bf16[2560]{0:T(1024)(128)(2,1)S(1)}, bf16[2560]{0:T(1024)(128)(2,1)S(1)}, bf16[2560]{0:T(1024)(128)(2,1)S...) all-reduce(f32[2048]{0:T(1024)S(1)} %get-tuple-element.287, ...), channel_id=2, replica_groups=mesh['seq'=2,'shard'=4,'replica'=4] {'seq','shard'}, use_global_device_ids=true, to_apply=%region_9.10.clone | all-reduce | flops 14336 | bytes 86016
  1775.0 14.0 all-reduce.75
  1793.1 441.7 %all-reduce.79.cloned.1.call-done = (bf16[256,2560]{1,0:T(8,128)(2,1)}, bf16[256,2560]{1,0:T(8,128)(2,1)}, bf16[2,160,160]{2,1,0:T(8,128)(2,1)}, bf16[2,160,160]...) async-done(((bf16[256,2560]{1,0:T(8,128)(2,1)}, ...) | async-done | bytes 13574160 | tf_op jit(solution)/shard_map/psum | solution.py:291
  2234.8 5.5 convert_element_type.325
  (609 shorter events, 464.1 us)
Async XLA Ops:
  7.2 118.5 %all-gather.16.cloned.1.call-start = ((), (), s32[]{:S(2)}) async-start(), calls=%async_computation.10 | async-start | bytes 11796480 | tf_op jit(solution)/shard_map/all_gather | solution.py:100
  10.3 360.2 %all-gather.14.cloned.1.call-start = ((), (), s32[]{:S(2)}) async-start(), calls=%async_computation.9 | async-start | bytes 11796480 | tf_op jit(solution)/shard_map/all_gather | solution.py:99
  11.6 368.1 %all-gather.18.cloned.1.call-start = ((), (), s32[]{:S(2)}) async-start(), calls=%async_computation.11 | async-start | bytes 11796480 | tf_op jit(solution)/shard_map/all_gather | solution.py:108
  14.8 372.8 %all-gather.20.cloned.1.call-start = ((), (), s32[]{:S(2)}) async-start(), calls=%async_computation.12 | async-start | bytes 28311552 | tf_op jit(solution)/shard_map/all_gather | solution.py:110
  19.7 452.4 %all-gather.22.cloned.1.call-start = ((), (), s32[]{:S(2)}) async-start(), calls=%async_computation.13 | async-start | bytes 28311552 | tf_op jit(solution)/shard_map/all_gather | solution.py:111
  25.4 574.4 %all-gather.24.cloned.1.call-start = ((), (), s32[]{:S(2)}) async-start(), calls=%async_computation.14 | async-start | bytes 28311552 | tf_op jit(solution)/shard_map/all_gather | solution.py:112
  30.3 14.5 copy-start.106
  30.3 14.5 copy-start.107
  30.4 14.5 copy-start.108
  30.4 14.5 copy-start.109
  30.4 14.6 copy-start.105
  30.4 41.1 %copy-start.104 = (f32[4,320]{1,0:T(4,128)S(1)}, f32[4,320]{1,0:T(4,128)}, u32[]{:S(2)}) copy-start(f32[4,320]{1,0:T(4,128)} %param.28) | copy-start | bytes 15364
  30.4 49.4 %copy-start.53 = (f32[2,160,160]{2,1,0:T(8,128)S(1)}, f32[2,160,160]{2,1,0:T(8,128)}, u32[]{:S(2)}) copy-start(f32[2,160,160]{2,1,0:T(8,128)} %param.30) | copy-start | bytes 614404
  30.4 49.4 %copy-start.54 = (f32[2,160,160]{2,1,0:T(8,128)S(1)}, f32[2,160,160]{2,1,0:T(8,128)}, u32[]{:S(2)}) copy-start(f32[2,160,160]{2,1,0:T(8,128)} %param.32) | copy-start | bytes 614404
  30.5 49.4 %copy-start.112 = (f32[256]{0:T(256)S(1)}, f32[256]{0:T(256)}, u32[]{:S(2)}) copy-start(f32[256]{0:T(256)} %param.36) | copy-start | bytes 3076
  30.5 59.0 %copy-start = (bf16[1,128,2048]{2,1,0:T(8,128)(2,1)S(1)}, bf16[1,128,2048]{2,1,0:T(8,128)(2,1)}, u32[]{:S(2)}) copy-start(bf16[1,128,2048]{2,1,0:T(8,128)(2,1)} %param.22) | copy-start | bytes 1572868
  30.5 957.5 %reduce-scatter.16.cloned.1.call-start = ((), (), s32[]{:S(2)}) async-start(), calls=%async_computation.17 | async-start | bytes 2949120 | tf_op jit(solution)/shard_map/reduce_scatter | solution.py:282
  31.1 94.5 %collective-permute-start = (s32[3]{0:T(128)S(1)}, s32[3]{0:T(128)S(1)}, u32[]{:S(2)}, u32[]{:S(2)}) collective-permute-start(s32[3]{0:T(128)S(1)} %slice_bitcast_fusion), channel_id=1, source_target_pairs={{0,16},{1,17},{2,18},{3,19},{4,20},{5,21},{6,22},{7,23},{8,24},{9,... | collective-permute-start | bytes 44 | tf_op jit(solution)/shard_map/ppermute | solution.py:13
  44.8 80.9 %copy-start.30 = (f32[8,1,256]{2,1,0:T(1,128)}, f32[8,1,256]{2,1,0:T(1,128)S(1)}, u32[]{:S(2)}) copy-start(f32[8,1,256]{2,1,0:T(1,128)S(1)} %convert_element_type.331) | copy-start | bytes 24580
  71.5 54.1 %copy-start.100 = (bf16[2560]{0:T(1024)(128)(2,1)}, bf16[2560]{0:T(1024)(128)(2,1)S(1)}, u32[]{:S(2)}) copy-start(bf16[2560]{0:T(1024)(128)(2,1)S(1)} %get-tuple-element.320) | copy-start | bytes 15364
  71.5 77.2 %copy-start.55 = (f32[2560]{0:T(1024)}, f32[2560]{0:T(1024)S(1)}, u32[]{:S(2)}) copy-start(f32[2560]{0:T(1024)S(1)} %convert_element_type.262) | copy-start | bytes 30724
  79.9 68.8 %copy-start.57 = (f32[2560]{0:T(1024)}, f32[2560]{0:T(1024)S(1)}, u32[]{:S(2)}) copy-start(f32[2560]{0:T(1024)S(1)} %convert_element_type.274) | copy-start | bytes 30724
  79.9 68.8 %copy-start.59 = (f32[2560]{0:T(1024)}, f32[2560]{0:T(1024)S(1)}, u32[]{:S(2)}) copy-start(f32[2560]{0:T(1024)S(1)} %convert_element_type.277) | copy-start | bytes 30724
  89.5 59.2 %copy-start.45 = (f32[2560]{0:T(1024)}, f32[2560]{0:T(1024)S(1)}, u32[]{:S(2)}) copy-start(f32[2560]{0:T(1024)S(1)} %get-tuple-element.290) | copy-start | bytes 30724
  89.5 59.2 %copy-start.47 = (f32[2560]{0:T(1024)}, f32[2560]{0:T(1024)S(1)}, u32[]{:S(2)}) copy-start(f32[2560]{0:T(1024)S(1)} %get-tuple-element.291) | copy-start | bytes 30724
  89.5 59.2 %copy-start.49 = (f32[2560]{0:T(1024)}, f32[2560]{0:T(1024)S(1)}, u32[]{:S(2)}) copy-start(f32[2560]{0:T(1024)S(1)} %get-tuple-element.292) | copy-start | bytes 30724
  89.5 59.2 %copy-start.51 = (f32[2560]{0:T(1024)}, f32[2560]{0:T(1024)S(1)}, u32[]{:S(2)}) copy-start(f32[2560]{0:T(1024)S(1)} %get-tuple-element.293) | copy-start | bytes 30724
  125.6 23.1 %copy-start.61 = (f32[2560]{0:T(1024)}, f32[2560]{0:T(1024)S(1)}, u32[]{:S(2)}) copy-start(f32[2560]{0:T(1024)S(1)} %fusion.65) | copy-start | bytes 30724
  131.5 4.7 collective-permute-start.1
  135.1 13.7 copy-start.94
  135.1 13.7 copy-start.96
  135.1 13.7 copy-start.98
  135.1 13.7 copy-start.102
  349.9 19.9 copy-start.43
  893.7 96.0 %reduce-scatter.18.cloned.1.call-start = ((), (), s32[]{:S(2)}) async-start(), calls=%async_computation.18 | async-start | bytes 2949120 | tf_op jit(solution)/shard_map/reduce_scatter | solution.py:284
  899.2 171.4 %reduce-scatter.20.cloned.1.call-start = ((), (), s32[]{:S(2)}) async-start(), calls=%async_computation.19 | async-start | bytes 11796480 | tf_op jit(solution)/shard_map/reduce_scatter | solution.py:45
  907.6 247.9 %reduce-scatter.12.cloned.1.call-start = ((), (), s32[]{:S(2)}) async-start(), calls=%async_computation.15 | async-start | bytes 11796480 | tf_op jit(solution)/shard_map/reduce_scatter | solution.py:45
  915.0 325.6 %reduce-scatter.14.cloned.1.call-start = ((), (), s32[]{:S(2)}) async-start(), calls=%async_computation.16 | async-start | bytes 11796480 | tf_op jit(solution)/shard_map/reduce_scatter | solution.py:45
  931.9 5.9 collective-permute-start.2
  943.5 457.5 %reduce-scatter.22.cloned.1.call-start = ((), (), s32[]{:S(2)}) async-start(), calls=%async_computation.20 | async-start | bytes 28311552 | tf_op jit(solution)/shard_map/reduce_scatter | solution.py:45
  958.2 603.3 %reduce-scatter.24.cloned.1.call-start = ((), (), s32[]{:S(2)}) async-start(), calls=%async_computation.21 | async-start | bytes 28311552 | tf_op jit(solution)/shard_map/reduce_scatter | solution.py:45
  971.6 750.3 %reduce-scatter.26.cloned.1.call-start = ((), (), s32[]{:S(2)}) async-start(), calls=%async_computation.22 | async-start | bytes 28311552 | tf_op jit(solution)/shard_map/reduce_scatter | solution.py:45
  986.3 787.7 %reduce-scatter.28.cloned.1.call-start = ((), (), s32[]{:S(2)}) async-start(), calls=%async_computation.23 | async-start | bytes 1474560
  988.0 1246.8 %all-reduce.79.cloned.1.call-start = ((), (), s32[]{:S(2)}) async-start(), calls=%async_computation.24 | async-start | bytes 27394048 | tf_op jit(solution)/shard_map/psum | solution.py:291
  1723.4 19.3 slice-start
  1730.9 11.8 slice-start.1
  1731.0 11.7 slice-start.2
  1742.7 28.9 %copy-start.9 = (f32[128,2048]{1,0:T(8,128)S(1)}, f32[128,2048]{1,0:T(8,128)}, u32[]{:S(2)}) copy-start(f32[128,2048]{1,0:T(8,128)} %copy-done.8) | copy-start | bytes 3145732
  (87 other events, 502.3 us)
Sparse Core Ops, SparseCore 0:
  10.5 66.2 all-gather.15
  78.7 71.8 all-gather.13
  152.5 63.8 all-gather.17
  218.6 125.7 all-gather.19
  346.8 125.3 all-gather.21
  474.4 125.3 all-gather.23
  893.8 44.0 reduce-scatter.15
  941.8 43.6 reduce-scatter.17
  989.0 81.5 reduce-scatter.19
  1074.0 81.5 reduce-scatter.11
  1159.0 81.5 reduce-scatter.13
  1244.1 156.8 reduce-scatter.21
  1404.6 156.8 reduce-scatter.23
  1565.0 156.8 reduce-scatter.25
  1725.6 37.5 reduce-scatter.27
  1767.6 467.1 all-reduce.78
where the time goes:
time: 2280 us; the launch traced here: 2260 us
  waiting for transfers between devices  1360 us (60%)
  local copies, waits for them, and re-layouts  353 us (15%)
  matrix products  210 us (9%)
  other arithmetic  164 us (7%)
  blocking collectives  142 us (6%)
    reduce_scatter x6, waiting for transfers between devices, spread_rows(): lax.psum_scatter(lax.dot_general(left, right, (((0,), (0,)), ((), ())), p...  731 us
    psum x1, waiting for transfers between devices, body(): lax.psum(branch_weight_grad.astype(jnp.bfloat16), 'replica')  442 us
    slice x49, local copies, waits for them, and re-layouts, body(): lax.associative_scan(link, (jnp.flip(following, 0), jnp.flip(states_grad,...  134 us
    all_gather x1, waiting for transfers between devices, body(): lax.all_gather(lowered[14], ('seq', 'shard'), axis=0, tiled=True)  114 us
    slice x44, local copies, waits for them, and re-layouts, body(): cumul, local = lax.associative_scan(link, (decay, driven), axis=0)  76.7 us
    all_gather x1, waiting for transfers between devices, body(): lax.all_gather(lowered[13], ('seq', 'shard'), axis=0, tiled=True)  70.7 us
    dot_general x6, matrix products, transposed(): lax.dot_general(left, right, (((1,), (1,)), ((), ())), preferred_element_...  69.4 us
    dot_general x6, matrix products, spread_rows(): lax.dot_general(left, right, (((0,), (0,)), ((), ())), preferred_element_...  61.3 us
  transfers between devices with their start and end apart: 19, of which 11 were waited for; matrix products, arithmetic and copies ran while one was open for 18% of the time, Pallas kernels for 0%

commit v1 on v0

v1 whole, which is shorter than its diff:
```python
import jax
import jax.numpy as jnp
from jax import lax
from jax.sharding import PartitionSpec as P

epsilon = 1e-06
decay_scale = 8.0
GROUP = ("seq", "shard")
ROWS = ("shard", "seq")
f32 = jnp.float32
bf16 = jnp.bfloat16


def link(earlier, later):
    return (earlier[0] * later[0], earlier[1] * later[0] + later[1])


def mm(left, right):
    return jnp.dot(left, right, preferred_element_type=f32)


def mm_nt(left, right):
    return lax.dot_general(left, right, (((1,), (1,)), ((), ())), preferred_element_type=f32)


def mm_tn(left, right):
    return lax.dot_general(left, right, (((0,), (0,)), ((), ())), preferred_element_type=f32)


def gather_rows(part):
    return lax.all_gather(part, ROWS, axis=0, tiled=True)


def scatter_rows(partial):
    return lax.psum_scatter(
        partial.astype(bf16), ROWS, scatter_dimension=0, tiled=True
    ).astype(f32)


def to_columns(weight):
    return lax.all_to_all(weight.astype(bf16), GROUP, split_axis=1, concat_axis=0, tiled=True)


def reduce_rows(grad):
    return lax.psum(grad.astype(bf16), "replica").astype(f32)


def reduce_columns(grad):
    owners = lax.axis_size(GROUP)
    copies = lax.axis_size("replica")
    depth, width = grad.shape
    piece = depth // (owners * copies)
    cut = grad.astype(bf16).reshape(owners, copies, piece, width)
    cut = jnp.swapaxes(cut, 0, 1).reshape(depth, width)
    cut = lax.psum_scatter(cut, "replica", scatter_dimension=0, tiled=True)
    cut = lax.all_to_all(cut, GROUP, split_axis=0, concat_axis=1, tiled=True)
    return lax.all_gather(cut, "replica", axis=0, tiled=True).astype(f32)


def norm_backward(grad_unit, unit, inverse):
    return inverse * (grad_unit - unit * jnp.mean(grad_unit * unit, axis=-1, keepdims=True))


def shift_down(array, distance):
    if distance == 0:
        return array
    return jnp.pad(array, ((0, 0), (distance, 0), (0, 0)))[:, : array.shape[1]]


def shift_up(array, distance):
    if distance == 0:
        return array
    return jnp.pad(array, ((0, 0), (0, distance), (0, 0)))[:, distance:]


def body(
    tokens,
    segments,
    cotangent,
    norm_gain,
    branch_weight,
    input_weight,
    conv_weight,
    conv_bias,
    recur_gate_weight,
    recur_gate_bias,
    input_gate_weight,
    input_gate_bias,
    decay_param,
    output_weight,
    mlp_norm_gain,
    gate_weight,
    up_weight,
    down_weight,
):
    def low(item):
        return item.astype(bf16).astype(f32)

    gains = lax.all_gather(
        jnp.stack([norm_gain, mlp_norm_gain]).astype(bf16), GROUP, axis=1, tiled=True
    ).astype(f32)
    gain_f, mlp_gain_f = gains[0], gains[1]
    rows = tokens[0].astype(f32)
    count_rows = rows.shape[0]
    halves = lax.axis_size("seq")
    inverse = lax.rsqrt(jnp.mean(rows * rows, axis=-1, keepdims=True) + epsilon)
    unit = rows * inverse
    normed = (unit * gain_f).astype(bf16)
    normed_all = gather_rows(normed)
    branch_w = to_columns(branch_weight)
    input_w = to_columns(input_weight)
    labels = gather_rows(segments).reshape(-1, halves * count_rows) + 1
    out_low = gather_rows(cotangent[0])
    gate_w = to_columns(gate_weight)
    up_w = to_columns(up_weight)
    recur_w = recur_gate_weight.astype(bf16)
    inject_w = input_gate_weight.astype(bf16)
    output_w = output_weight.astype(bf16)
    down_w = down_weight.astype(bf16)
    total = normed_all.shape[0]
    sequences, length = labels.shape
    width = branch_w.shape[1]
    blocks_count = recur_w.shape[0]

    branch_pre = mm(normed_all, branch_w)
    branch_act, branch_pull = jax.vjp(jax.nn.gelu, branch_pre)
    conv_in = mm(normed_all, input_w).astype(bf16)
    conv_f = low(conv_weight)
    taps = conv_f.shape[0]
    shaped_in = conv_in.astype(f32).reshape(sequences, length, width)
    masks = []
    conv_out = jnp.zeros_like(shaped_in) + low(conv_bias)
    for offset in range(taps):
        earlier = jnp.pad(labels, ((0, 0), (offset, 0)))[:, :length]
        mask = (earlier == labels).astype(f32)[..., None]
        masks.append(mask)
        conv_out = conv_out + conv_f[offset] * shift_down(shaped_in, offset) * mask
    values = conv_out.astype(bf16).reshape(total, width)
    values_f = values.astype(f32)
    blocks = values.reshape(total, blocks_count, -1)
    recur_pre = jnp.einsum("thi,hij->thj", blocks, recur_w, preferred_element_type=f32)
    recur_gate = jax.nn.sigmoid(recur_pre.reshape(total, width) + low(recur_gate_bias))
    inject_pre = jnp.einsum("thi,hij->thj", blocks, inject_w, preferred_element_type=f32)
    inject_gate = jax.nn.sigmoid(inject_pre.reshape(total, width) + low(input_gate_bias))
    starts = (labels != jnp.pad(labels, ((0, 0), (1, 0)))[:, :length]).reshape(total, 1)
    decay_f = low(decay_param)
    rate = jax.nn.softplus(-decay_f)
    log_decay = -decay_scale * rate * recur_gate
    decay = jnp.where(starts, 0.0, jnp.exp(log_decay))
    scale = jnp.where(starts, 1.0, jnp.sqrt(-jnp.expm1(2.0 * log_decay)))
    driven = scale * inject_gate * values_f
    decay3 = decay.reshape(sequences, length, width)
    _, states3 = lax.associative_scan(
        link, (decay3, driven.reshape(sequences, length, width)), axis=1
    )
    states = states3.reshape(total, width)
    product = (branch_act * states).astype(bf16)
    middle = rows + scatter_rows(mm(product, output_w))
    inverse_two = lax.rsqrt(jnp.mean(middle * middle, axis=-1, keepdims=True) + epsilon)
    unit_two = middle * inverse_two
    normed_two = gather_rows((unit_two * mlp_gain_f).astype(bf16))
    gate_pre = mm(normed_two, gate_w)
    up_pre = mm(normed_two, up_w)
    gate_act, gate_pull = jax.vjp(jax.nn.gelu, gate_pre)
    hidden = (gate_act * up_pre).astype(bf16)
    block_out = (middle + scatter_rows(mm(hidden, down_w))).astype(bf16)

    grad_out = cotangent[0].astype(f32)
    hidden_grad = mm_nt(out_low, down_w)
    gate_low = gate_pull(hidden_grad * up_pre)[0].astype(bf16)
    up_low = (hidden_grad * gate_act).astype(bf16)
    down_weight_grad = reduce_rows(mm_tn(hidden, out_low))
    gate_weight_grad = reduce_columns(mm_tn(normed_two, gate_low))
    up_weight_grad = reduce_columns(mm_tn(normed_two, up_low))
    two_grad = scatter_rows(mm_nt(gate_low, gate_w) + mm_nt(up_low, up_w))
    mlp_gain_grad = jnp.sum(two_grad * unit_two, axis=0)
    middle_grad = grad_out + norm_backward(two_grad * mlp_gain_f, unit_two, inverse_two)
    mid_low = gather_rows(middle_grad.astype(bf16))
    output_weight_grad = reduce_rows(mm_tn(product, mid_low))
    product_grad = mm_nt(mid_low, output_w)
    branch_low = branch_pull(product_grad * states)[0].astype(bf16)
    states_grad = (product_grad * branch_act).reshape(sequences, length, width)
    _, adjoint3 = lax.associative_scan(
        link, (shift_up(decay3, 1)[:, ::-1], states_grad[:, ::-1]), axis=1
    )
    adjoint = adjoint3[:, ::-1].reshape(total, width)
    previous = shift_down(states3, 1).reshape(total, width)
    scale_grad = adjoint * inject_gate * values_f
    log_grad = jnp.where(
        starts, 0.0, adjoint * previous * decay - scale_grad * decay * decay / scale
    )
    decay_param_grad = jnp.sum(log_grad * decay_scale * recur_gate, axis=0) * jax.nn.sigmoid(
        -decay_f
    )
    recur_low = (log_grad * (-decay_scale * rate) * recur_gate * (1.0 - recur_gate)).astype(bf16)
    inject_low = (adjoint * scale * values_f * inject_gate * (1.0 - inject_gate)).astype(bf16)
    recur_bias_grad = jnp.sum(recur_low.astype(f32), axis=0)
    inject_bias_grad = jnp.sum(inject_low.astype(f32), axis=0)
    recur_blocks = recur_low.reshape(total, blocks_count, -1)
    inject_blocks = inject_low.reshape(total, blocks_count, -1)
    recur_weight_grad = jnp.einsum("thi,thj->hij", blocks, recur_blocks, preferred_element_type=f32)
    inject_weight_grad = jnp.einsum(
        "thi,thj->hij", blocks, inject_blocks, preferred_element_type=f32
    )
    values_grad = adjoint * scale * inject_gate
    values_grad = values_grad + jnp.einsum(
        "thj,hij->thi", recur_blocks, recur_w, preferred_element_type=f32
    ).reshape(total, width)
    values_grad = values_grad + jnp.einsum(
        "thj,hij->thi", inject_blocks, inject_w, preferred_element_type=f32
    ).reshape(total, width)
    conv_bias_grad = jnp.sum(values_grad, axis=0)
    shaped_grad = values_grad.reshape(sequences, length, width)
    tap_grads = []
    conv_in_grad = jnp.zeros_like(shaped_grad)
    for offset in range(taps):
        masked = shaped_grad * masks[offset]
        tap_grads.append(jnp.sum(masked * shift_down(shaped_in, offset), axis=(0, 1)))
        conv_in_grad = conv_in_grad + shift_up(masked * conv_f[offset], offset)
    conv_weight_grad = jnp.stack(tap_grads, 0)
    conv_low = conv_in_grad.reshape(total, width).astype(bf16)
    normed_grad = scatter_rows(mm_nt(branch_low, branch_w) + mm_nt(conv_low, input_w))
    gain_grad = jnp.sum(normed_grad * unit, axis=0)
    tokens_grad = (middle_grad + norm_backward(normed_grad * gain_f, unit, inverse)).astype(bf16)
    branch_weight_grad = reduce_columns(mm_tn(normed_all, branch_low))
    input_weight_grad = reduce_columns(mm_tn(normed_all, conv_low))
    gain_pair = lax.psum_scatter(
        jnp.stack([gain_grad, mlp_gain_grad]), GROUP, scatter_dimension=1, tiled=True
    )
    small = (
        gain_pair,
        conv_weight_grad,
        conv_bias_grad,
        recur_weight_grad,
        recur_bias_grad,
        inject_weight_grad,
        inject_bias_grad,
        decay_param_grad,
    )
    small = lax.psum(tuple(item.astype(bf16) for item in small), "replica")
    small = [item.astype(f32) for item in small]
    return (
        block_out[None],
        tokens_grad[None],
        small[0][0],
        branch_weight_grad,
        input_weight_grad,
        small[1],
        small[2],
        small[3],
        small[4],
        small[5],
        small[6],
        small[7],
        output_weight_grad,
        small[0][1],
        gate_weight_grad,
        up_weight_grad,
        down_weight_grad,
    )


def solution(mesh):
    row3 = P(("shard", "replica"), "seq", None)
    vec = P(("seq", "shard"))
    mat = P(("seq", "shard"), None)
    cube = P(("seq", "shard"), None, None)
    taps = P(None, ("seq", "shard"))
    params = (vec, mat, mat, taps, vec, cube, vec, cube, vec, vec, mat, vec, mat, mat, mat)
    in_specs = (row3, P(("shard", "replica"), "seq"), row3) + params
    out_specs = (row3, row3) + params
    return jax.shard_map(body, mesh=mesh, in_specs=in_specs, out_specs=out_specs, check_vma=False)
```

time: 2280 us -> 1690 us (0.74)
  waiting for transfers between devices: 1360 us -> 664 us
  local copies, waits for them, and re-layouts: 353 us -> 597 us
  matrix products: 210 us -> 120 us
  blocking collectives: 142 us -> 108 us
    reduce_scatter x8, waiting for transfers between devices: 731 us -> 204 us  [the longest x4 204 us: scatter_rows(): lax.psum_scatter(partial.astype(bf16), ROWS, scatter_dimension=0, tiled=T...]
    pad x48 -> x28, local copies, waits for them, and re-layouts: 90.6 us -> 382 us  [the longest x14 216 us: body(): lax.associative_scan(link, (shift_up(decay3, 1)[:, ::-1], states_grad[:,...]
    psum x1, waiting for transfers between devices: 442 us -> 165 us  [body(): small = lax.psum(tuple((item.astype(bf16) for item in small)), 'replica')]
    slice x97 -> x24, local copies, waits for them, and re-layouts: 212 us -> 93.9 us  [the longest x11 86.8 us: body(): lax.associative_scan(link, (shift_up(decay3, 1)[:, ::-1], states_grad[:,...]
    all_to_all x0 -> x4, waiting for transfers between devices: none -> 110 us  [to_columns(): lax.all_to_all(weight.astype(bf16), GROUP, split_axis=1, concat_axis=0, t...]
    dot_general x22, matrix products: 203 us -> 118 us  [the longest x6 37.2 us: mm_nt(): lax.dot_general(left, right, (((1,), (1,)), ((), ())), preferred_element_...]
    all_to_all x0 -> x4, blocking collectives: none -> 55.7 us  [reduce_columns(): cut = lax.all_to_all(cut, GROUP, split_axis=0, concat_axis=1, tiled=True)]
    unnamed x2 -> x0, blocking collectives: 48.2 us -> none
  transfers between devices with their start and end apart: 19 -> 22, of which waited for: 11 -> 14; matrix products, arithmetic and copies ran while one was open for 18% -> 34% of each run, Pallas kernels for 0% -> 0%
where the time goes in v1:
time: 1690 us; the launch traced here: 1670 us
  waiting for transfers between devices  664 us (39%)
  local copies, waits for them, and re-layouts  597 us (35%)
  other arithmetic  144 us (9%)
  matrix products  120 us (7%)
  blocking collectives  108 us (6%)
  starting transfers between devices  17.9 us (1%)
    pad x14, local copies, waits for them, and re-layouts, body(): lax.associative_scan(link, (shift_up(decay3, 1)[:, ::-1], states_grad[:,...  216 us
    reduce_scatter x4, waiting for transfers between devices, scatter_rows(): lax.psum_scatter(partial.astype(bf16), ROWS, scatter_dimension=0, tiled=T...  204 us
    pad x14, local copies, waits for them, and re-layouts, body(): lax.associative_scan(link, (decay3, driven.reshape(sequences, length, wid...  167 us
    psum x1, waiting for transfers between devices, body(): small = lax.psum(tuple((item.astype(bf16) for item in small)), 'replica')  165 us
    all_gather x4, waiting for transfers between devices, reduce_columns(): return lax.all_gather(cut, 'replica', axis=0, tiled=True).astype(f32)  145 us
    all_to_all x4, waiting for transfers between devices, to_columns(): lax.all_to_all(weight.astype(bf16), GROUP, split_axis=1, concat_axis=0, t...  110 us
    slice x11, local copies, waits for them, and re-layouts, body(): lax.associative_scan(link, (shift_up(decay3, 1)[:, ::-1], states_grad[:,...  86.8 us
    all_to_all x4, blocking collectives, reduce_columns(): cut = lax.all_to_all(cut, GROUP, split_axis=0, concat_axis=1, tiled=True)  55.7 us
  transfers between devices with their start and end apart: 22, of which 14 were waited for; matrix products, arithmetic and copies ran while one was open for 34% of the time, Pallas kernels for 0%

profile of v1, /device:TPU:0, one launch (start us, length us, event | category | flops | bytes accessed | tf_op | source)
XLA Modules:
  0.0 1666.2 jit_solution(2006537491882646361)
XLA Ops:
  8.6 10.3 all_gather.30
  28.7 30.1 %all-gather.1 = s32[8,1,128]{2,1,0:T(1,128)S(1)} all-gather(s32[1,1,128]{2,1,0:T(1,128)S(1)} %bitcast.208), channel_id=1, replica_groups=mesh['seq'=2,'shard'=4,'replica'=4] {'shard','seq'}, dimensions={0}, use_global_device_ids=true | all-gather | bytes 4608 | tf_op jit(solution)/shard_map/all_gather | solution.py:31
  67.2 17.3 %all-to-all-done = bf16[256,8,320]{0,2,1:T(8,128)(2,1)} async-done(((bf16[256,8,320]{0,2,1:T(8,128)(2,1)}), bf16[256,8,320]{0,2,1:T(8,128)(2,1)}, u32[]{:S(2)}, u32[]{:S(2)}) %all-to-all-start) | async-done | bytes 1310752 | tf_op jit(solution)/shard_map/all_to_all | solution.py:41
  151.5 8.4 pad.159
  163.5 11.3 pad.161
  176.5 11.3 pad.160
  190.8 20.2 %pad.163 = f32[4,128,320]{2,0,1:T(4,128)} pad(f32[4,64,320]{2,0,1:T(4,128)S(1)} %copy-done.36, f32[]{:T(128)} %constant.15.clone.1), padding=0_0_0x1_0_1x0_0_0 | pad | bytes 983044 | tf_op jit(solution)/shard_map/pad | solution.py:153
  215.7 56.9 %pad.165 = f32[4,256,320]{2,0,1:T(4,128)} pad(f32[4,128,320]{2,0,1:T(4,128)} %add.476, f32[]{:T(128)} %constant.15.clone.1), padding=0_0_0x1_0_1x0_0_0 | pad | bytes 1966084 | tf_op jit(solution)/shard_map/pad | solution.py:153
  274.0 39.8 %pad.164 = f32[4,256,320]{2,0,1:T(4,128)} pad(f32[4,128,320]{2,0,1:T(4,128)S(1)} %pad_maximum_fusion, f32[]{:T(128)} %constant.15.clone.1), padding=0_0_0x0_1_1x0_0_0 | pad | bytes 1966084 | tf_op jit(solution)/shard_map/pad | solution.py:153
  331.7 50.6 %reduce-scatter.12.cloned.1.call-done = bf16[128,2048]{1,0:T(8,128)(2,1)} async-done(((bf16[1024,2048]{1,0:T(8,128)(2,1)}), bf16[128,2048]{1,0:T(8,128)(2,1)}) %reduce-scatter.12.cloned.1.call-update) | async-done | bytes 524304 | tf_op jit(solution)/shard_map/reduce_scatter | solution.py:35
  401.4 46.2 %all-to-all-done.2 = bf16[256,8,768]{0,2,1:T(8,128)(2,1)} async-done(((bf16[256,8,768]{0,2,1:T(8,128)(2,1)}), bf16[256,8,768]{0,2,1:T(8,128)(2,1)}, u32[]{:S(2)}, u32[]{:S(2)}) %all-to-all-start.2) | async-done | bytes 3145760 | tf_op jit(solution)/shard_map/all_to_all | solution.py:41
  456.8 46.1 %all-to-all-done.3 = bf16[256,8,768]{0,2,1:T(8,128)(2,1)} async-done(((bf16[256,8,768]{0,2,1:T(8,128)(2,1)}), bf16[256,8,768]{0,2,1:T(8,128)(2,1)}, u32[]{:S(2)}, u32[]{:S(2)}) %all-to-all-start.3) | async-done | bytes 3145760 | tf_op jit(solution)/shard_map/all_to_all | solution.py:41
  507.6 8.4 fusion.118
  521.0 12.6 multiply_convert_fusion
  542.4 50.7 %reduce-scatter.16.cloned.1.call-done = bf16[128,2048]{1,0:T(8,128)(2,1)} async-done(((bf16[1024,2048]{1,0:T(8,128)(2,1)}), bf16[128,2048]{1,0:T(8,128)(2,1)}) %reduce-scatter.16.cloned.1.call-update) | async-done | bytes 524304 | tf_op jit(solution)/shard_map/reduce_scatter | solution.py:35
  596.7 6.2 convolution_convert_fusion.3
  621.8 5.7 convolution_convert_fusion.2
  633.5 7.3 fusion.69
  644.1 25.3 %slice.522 = f32[4,128,320]{1,0,2:T(4,128)} slice(f32[4,256,320]{1,0,2:T(4,128)} %reshape.379), slice={[0:4:1], [1:256:2], [0:320:1]} | slice | bytes 1310720 | tf_op jit(solution)/shard_map/slice | solution.py:183
  669.4 25.0 %slice.527 = f32[4,128,320]{1,0,2:T(4,128)S(1)} slice(f32[4,256,320]{1,0,2:T(4,128)} %reshape.379), slice={[0:4:1], [0:255:2], [0:320:1]} | slice | bytes 1310720 | tf_op jit(solution)/shard_map/slice | solution.py:183
  741.2 25.3 %slice.585 = f32[4,127,320]{1,0,2:T(4,128)} slice(f32[4,256,320]{1,0,2:T(4,128)} %reshape.379), slice={[0:4:1], [1:254:2], [0:320:1]} | slice | bytes 1300480 | tf_op jit(solution)/shard_map/slice | solution.py:183
  770.4 8.4 pad.175
  778.8 8.4 pad.176
  789.0 15.2 pad.178
  806.9 15.1 pad.177
  826.2 22.6 %pad.179 = f32[4,128,320]{2,0,1:T(4,128)S(1)} pad(f32[4,64,320]{2,0,1:T(4,128)} %pad_maximum_fusion.3, f32[]{:T(128)} %constant.15.clone.1), padding=0_0_0x0_1_1x0_0_0 | pad | bytes 983044 | tf_op jit(solution)/shard_map/pad | solution.py:183
  848.8 29.4 %pad.180 = f32[4,128,320]{2,0,1:T(4,128)} pad(f32[4,64,320]{2,0,1:T(4,128)} %add.504, f32[]{:T(128)} %constant.15.clone.1), padding=0_0_0x1_0_1x0_0_0 | pad | bytes 983044 | tf_op jit(solution)/shard_map/pad | solution.py:183
  880.4 56.9 %pad.182 = f32[4,256,320]{2,0,1:T(4,128)} pad(f32[4,128,320]{2,0,1:T(4,128)} %add.506, f32[]{:T(128)} %constant.15.clone.1), padding=0_0_0x1_0_1x0_0_0 | pad | bytes 1966084 | tf_op jit(solution)/shard_map/pad | solution.py:183
  943.8 39.8 %pad.181 = f32[4,256,320]{2,0,1:T(4,128)} pad(f32[4,128,320]{2,0,1:T(4,128)S(1)} %pad_maximum_fusion.1, f32[]{:T(128)} %constant.15.clone.1), padding=0_0_0x0_1_1x0_0_0 | pad | bytes 1966084 | tf_op jit(solution)/shard_map/pad | solution.py:183
  1005.6 6.1 add_reduce_fusion
  1019.5 12.2 multiply_reduce_fusion
  1059.9 16.0 all_to_all.152
  1077.0 16.0 all_to_all.153
  1094.1 7.9 fusion.4
  1106.7 11.7 all_to_all.154
  1121.5 12.0 all_to_all.155
  1145.6 8.7 convolution_convert_fusion.1
  1154.3 31.3 %all-gather.21.cloned.1.call-done = bf16[256,6144]{1,0:T(8,128)(2,1)} async-done(((bf16[64,6144]{1,0:T(8,128)(2,1)}), bf16[256,6144]{1,0:T(8,128)(2,1)}) %all-gather.21.cloned.1.call-update) | async-done | bytes 3145744 | tf_op jit(solution)/shard_map/all_gather | solution.py:57
  1191.1 58.7 %all-gather.23.cloned.1.call-done = bf16[256,6144]{1,0:T(8,128)(2,1)} async-done(((bf16[64,6144]{1,0:T(8,128)(2,1)}), bf16[256,6144]{1,0:T(8,128)(2,1)}) %all-gather.23.cloned.1.call-update) | async-done | bytes 3145744 | tf_op jit(solution)/shard_map/all_gather | solution.py:57
  1255.4 7.8 fusion.63
  1263.3 164.6 %all-reduce.47.cloned.1.call-done = (bf16[2,160,160]{2,1,0:T(8,128)(2,1)}, bf16[2,160,160]{2,1,0:T(8,128)(2,1)}, bf16[320,2048]{1,0:T(8,128)(2,1)}, bf16[768,2048]{1,0:T(8,128)(2,1)}) async-done(((bf16[2,160,160]{2,1,0:T(8,128)(2,1)}, bf16[2,160,160]{2,1,0:T(8,128)(2,1)}, bf16[320,2048]{1,0:T(8,128)(2,1)}, bf16[768,2048]{1,0:T(8,128)(2,1)}), (bf16[2,160,160]{2,1,0:T(8,128)(2,1)}, ...) | async-done | bytes 4661264 | tf_op jit(solution)/shard_map/psum | solution.py:240
  1427.8 5.5 convert_element_type.350
  1436.7 24.3 %all-gather.19.cloned.1.call-done = bf16[256,2560]{1,0:T(8,128)(2,1)} async-done(((bf16[64,2560]{1,0:T(8,128)(2,1)}), bf16[256,2560]{1,0:T(8,128)(2,1)}) %all-gather.19.cloned.1.call-update) | async-done | bytes 1310736 | tf_op jit(solution)/shard_map/all_gather | solution.py:57
  1464.1 30.7 %all-gather.17.cloned.1.call-done = bf16[256,2560]{1,0:T(8,128)(2,1)} async-done(((bf16[64,2560]{1,0:T(8,128)(2,1)}), bf16[256,2560]{1,0:T(8,128)(2,1)}) %all-gather.17.cloned.1.call-update) | async-done | bytes 1310736 | tf_op jit(solution)/shard_map/all_gather | solution.py:57
  1497.9 50.8 %reduce-scatter.18.cloned.1.call-done = bf16[128,2048]{1,0:T(8,128)(2,1)} async-done(((bf16[1024,2048]{1,0:T(8,128)(2,1)}), bf16[128,2048]{1,0:T(8,128)(2,1)}) %reduce-scatter.18.cloned.1.call-update) | async-done | bytes 524304 | tf_op jit(solution)/shard_map/reduce_scatter | solution.py:35
  1551.7 51.6 %reduce-scatter.14.cloned.1.call-done = bf16[128,2048]{1,0:T(8,128)(2,1)} async-done(((bf16[1024,2048]{1,0:T(8,128)(2,1)}), bf16[128,2048]{1,0:T(8,128)(2,1)}) %reduce-scatter.14.cloned.1.call-update) | async-done | bytes 524304 | tf_op jit(solution)/shard_map/reduce_scatter | solution.py:35
  1606.1 36.6 %reduce-scatter.28.cloned.1.call-done = f32[256,2]{1,0:T(8,128)} async-done(((f32[2048,2]{1,0:T(8,128)}), f32[256,2]{1,0:T(8,128)}) %reduce-scatter.28.cloned.1.call-update) | async-done | bytes 2064
  1643.7 11.9 all-reduce.43
  (483 shorter events, 374.9 us)
Async XLA Ops:
  7.2 79.8 %all-gather.11.cloned.1.call-start = ((), (), s32[]{:S(2)}) async-start(), calls=%async_computation.17 | async-start | bytes 4718592 | tf_op jit(solution)/shard_map/all_gather | solution.py:31
  25.1 36.5 %all-to-all-start.1 = ((bf16[256,8,320]{0,2,1:T(8,128)(2,1)}), bf16[256,8,320]{0,2,1:T(8,128)(2,1)S(1)}, u32[]{:S(2)}, u32[]{:S(2)}) async-start(bf16[256,8,320]{0,2,1:T(8,128)(2,1)} %bitcast.6), calls=%async_computation.1 | async-start | bytes 2621440 | tf_op jit(solution)/shard_map/all_to_all | solution.py:41
  61.6 22.8 %all-to-all-start = ((bf16[256,8,320]{0,2,1:T(8,128)(2,1)}), bf16[256,8,320]{0,2,1:T(8,128)(2,1)}, u32[]{:S(2)}, u32[]{:S(2)}) async-start(bf16[256,8,320]{0,2,1:T(8,128)(2,1)} %bitcast.3), calls=%async_computation | async-start | bytes 2621440 | tf_op jit(solution)/shard_map/all_to_all | solution.py:41
  66.0 316.3 %reduce-scatter.12.cloned.1.call-start = ((), (), s32[]{:S(2)}) async-start(), calls=%async_computation.18 | async-start | bytes 4718592 | tf_op jit(solution)/shard_map/reduce_scatter | solution.py:35
  215.7 56.9 %slice-start = ((f32[4,256,320]{2,0,1:T(4,128)}), f32[4,1,320]{2,0,1:T(4,128)S(1)}, s32[]{:S(2)}) async-start(f32[4,256,320]{2,0,1:T(4,128)} %copy-done.8), calls=%async_computation.35 | async-start | bytes 12288 | tf_op jit(solution)/shard_map/slice | solution.py:153
  331.6 175.9 %all-gather.13.cloned.1.call-start = ((), (), s32[]{:S(2)}) async-start(), calls=%async_computation.19 | async-start | bytes 4718592 | tf_op jit(solution)/shard_map/all_gather | solution.py:31
  383.6 211.7 %copy-start.80 = (f32[128]{0:T(128)}, f32[128]{0:T(128)S(1)}, u32[]{:S(2)}) copy-start(f32[128]{0:T(128)S(1)} %add_rsqrt_fusion) | copy-start | bytes 1540
  385.7 135.3 %all-gather.25.cloned.1.call-start = ((), (), s32[]{:S(2)}) async-start(), calls=%async_computation.32 | async-start | bytes 4718592 | tf_op jit(solution)/shard_map/all_gather | solution.py:31
  391.6 56.0 %all-to-all-start.2 = ((bf16[256,8,768]{0,2,1:T(8,128)(2,1)}), bf16[256,8,768]{0,2,1:T(8,128)(2,1)}, u32[]{:S(2)}, u32[]{:S(2)}) async-start(bf16[256,8,768]{0,2,1:T(8,128)(2,1)} %bitcast.163), calls=%async_computation.3 | async-start | bytes 6291456 | tf_op jit(solution)/shard_map/all_to_all | solution.py:41
  447.7 55.3 %all-to-all-start.3 = ((bf16[256,8,768]{0,2,1:T(8,128)(2,1)}), bf16[256,8,768]{0,2,1:T(8,128)(2,1)}, u32[]{:S(2)}, u32[]{:S(2)}) async-start(bf16[256,8,768]{0,2,1:T(8,128)(2,1)} %bitcast.162), calls=%async_computation.4 | async-start | bytes 6291456 | tf_op jit(solution)/shard_map/all_to_all | solution.py:41
  452.1 141.0 %reduce-scatter.16.cloned.1.call-start = ((), (), s32[]{:S(2)}) async-start(), calls=%async_computation.21 | async-start | bytes 4718592 | tf_op jit(solution)/shard_map/reduce_scatter | solution.py:35
  542.3 50.8 %copy-start.5 = (bf16[128,2048]{1,0:T(8,128)(2,1)S(1)}, bf16[128,2048]{1,0:T(8,128)(2,1)}, u32[]{:S(2)}) copy-start(bf16[128,2048]{1,0:T(8,128)(2,1)} %reduce-scatter.12.cloned.1.call-done) | copy-start | bytes 1572868
  542.3 53.0 %copy-start.22 = (bf16[1,128,2048]{2,1,0:T(8,128)(2,1)S(1)}, bf16[1,128,2048]{2,1,0:T(8,128)(2,1)}, u32[]{:S(2)}) copy-start(bf16[1,128,2048]{2,1,0:T(8,128)(2,1)} %param.20) | copy-start | bytes 1572868
  542.3 91.1 %all-gather.15.cloned.1.call-start = ((), (), s32[]{:S(2)}) async-start(), calls=%async_computation.22 | async-start | bytes 4718592 | tf_op jit(solution)/shard_map/all_gather | solution.py:31
  596.6 463.3 %reduce-scatter.24.cloned.1.call-start = ((), (), s32[]{:S(2)}) async-start(), calls=%async_computation.28 | async-start | bytes 3932160 | tf_op jit(solution)/shard_map/reduce_scatter | solution.py:55
  604.9 472.1 %reduce-scatter.26.cloned.1.call-start = ((), (), s32[]{:S(2)}) async-start(), calls=%async_computation.30 | async-start | bytes 3932160 | tf_op jit(solution)/shard_map/reduce_scatter | solution.py:55
  629.6 477.2 %reduce-scatter.22.cloned.1.call-start = ((), (), s32[]{:S(2)}) async-start(), calls=%async_computation.26 | async-start | bytes 1966080 | tf_op jit(solution)/shard_map/reduce_scatter | solution.py:55
  1049.2 72.4 %reduce-scatter.20.cloned.1.call-start = ((), (), s32[]{:S(2)}) async-start(), calls=%async_computation.24 | async-start | bytes 1966080 | tf_op jit(solution)/shard_map/reduce_scatter | solution.py:55
  1059.8 125.8 %all-gather.21.cloned.1.call-start = ((), (), s32[]{:S(2)}) async-start(), calls=%async_computation.29 | async-start | bytes 3932160 | tf_op jit(solution)/shard_map/all_gather | solution.py:57
  1076.9 172.9 %all-gather.23.cloned.1.call-start = ((), (), s32[]{:S(2)}) async-start(), calls=%async_computation.31 | async-start | bytes 3932160 | tf_op jit(solution)/shard_map/all_gather | solution.py:57
  1094.0 333.9 %all-reduce.47.cloned.1.call-start = ((), (), s32[]{:S(2)}) async-start(), calls=%async_computation.34 | async-start | bytes 9568256 | tf_op jit(solution)/shard_map/psum | solution.py:240
  1106.7 354.3 %all-gather.19.cloned.1.call-start = ((), (), s32[]{:S(2)}) async-start(), calls=%async_computation.27 | async-start | bytes 1638400 | tf_op jit(solution)/shard_map/all_gather | solution.py:57
  1121.5 373.3 %all-gather.17.cloned.1.call-start = ((), (), s32[]{:S(2)}) async-start(), calls=%async_computation.25 | async-start | bytes 1638400 | tf_op jit(solution)/shard_map/all_gather | solution.py:57
  1136.6 412.2 %reduce-scatter.18.cloned.1.call-start = ((), (), s32[]{:S(2)}) async-start(), calls=%async_computation.23 | async-start | bytes 4718592 | tf_op jit(solution)/shard_map/reduce_scatter | solution.py:35
  1145.3 457.9 %reduce-scatter.14.cloned.1.call-start = ((), (), s32[]{:S(2)}) async-start(), calls=%async_computation.20 | async-start | bytes 4718592 | tf_op jit(solution)/shard_map/reduce_scatter | solution.py:35
  1154.3 488.4 %reduce-scatter.28.cloned.1.call-start = ((), (), s32[]{:S(2)}) async-start(), calls=%async_computation.33 | async-start | bytes 1179648
  1191.0 64.2 %copy-start.93 = (bf16[320]{0:T(512)(128)(2,1)S(1)}, bf16[320]{0:T(512)(128)(2,1)}, u32[]{:S(2)}) copy-start(bf16[320]{0:T(512)(128)(2,1)} %get-tuple-element.52) | copy-start | bytes 1924
  1191.0 64.2 %copy-start.92 = (bf16[320]{0:T(512)(128)(2,1)S(1)}, bf16[320]{0:T(512)(128)(2,1)}, u32[]{:S(2)}) copy-start(bf16[320]{0:T(512)(128)(2,1)} %get-tuple-element.51) | copy-start | bytes 1924
  1191.0 64.2 %copy-start.91 = (bf16[320]{0:T(512)(128)(2,1)S(1)}, bf16[320]{0:T(512)(128)(2,1)}, u32[]{:S(2)}) copy-start(bf16[320]{0:T(512)(128)(2,1)} %get-tuple-element.50) | copy-start | bytes 1924
  1191.0 64.2 %copy-start.90 = (bf16[320]{0:T(512)(128)(2,1)S(1)}, bf16[320]{0:T(512)(128)(2,1)}, u32[]{:S(2)}) copy-start(bf16[320]{0:T(512)(128)(2,1)} %get-tuple-element.49) | copy-start | bytes 1924
  1191.0 64.2 %copy-start.99 = (bf16[2,160]{1,0:T(2,128)(2,1)S(1)}, bf16[2,160]{1,0:T(2,128)(2,1)}, u32[]{:S(2)}) copy-start(bf16[2,160]{1,0:T(2,128)(2,1)} %get-tuple-element.113) | copy-start | bytes 1924
  1191.0 64.3 %copy-start.79 = (f32[320]{0:T(512)S(1)}, f32[320]{0:T(512)}, u32[]{:S(2)}) copy-start(f32[320]{0:T(512)} %param.30) | copy-start | bytes 3844
  1191.0 64.3 %copy-start.85 = (f32[320]{0:T(512)S(1)}, f32[320]{0:T(512)}, u32[]{:S(2)}) copy-start(f32[320]{0:T(512)} %get-tuple-element.41) | copy-start | bytes 3844
  1191.0 64.3 %copy-start.21 = (f32[4,256]{0,1:T(8,128)S(1)}, f32[4,256]{0,1:T(8,128)}, u32[]{:S(2)}) copy-start(f32[4,256]{0,1:T(8,128)} %copy-done.19) | copy-start | bytes 12292
  1191.0 64.3 %copy-start.45 = (pred[4,256]{0,1:T(8,128)(4,1)S(1)}, pred[4,256]{0,1:T(8,128)(4,1)}, u32[]{:S(2)}) copy-start(pred[4,256]{0,1:T(8,128)(4,1)} %copy-done.44) | copy-start | bytes 3076
  1191.0 64.3 %copy-start.59 = (f32[320]{0:T(512)S(1)}, f32[320]{0:T(512)}, u32[]{:S(2)}) copy-start(f32[320]{0:T(512)} %copy-done.57) | copy-start | bytes 3844
  1191.0 64.3 %copy-start.62 = (f32[320]{0:T(512)S(1)}, f32[320]{0:T(512)}, u32[]{:S(2)}) copy-start(f32[320]{0:T(512)} %copy-done.60) | copy-start | bytes 3844
  1191.0 64.3 %copy-start.65 = (f32[320]{0:T(512)S(1)}, f32[320]{0:T(512)}, u32[]{:S(2)}) copy-start(f32[320]{0:T(512)} %copy-done.63) | copy-start | bytes 3844
  1191.1 64.3 %copy-start.67 = (f32[320]{0:T(512)S(1)}, f32[320]{0:T(512)}, u32[]{:S(2)}) copy-start(f32[320]{0:T(512)} %copy-done.66) | copy-start | bytes 3844
  1191.1 64.3 %copy-start.70 = (f32[320]{0:T(512)S(1)}, f32[320]{0:T(512)}, u32[]{:S(2)}) copy-start(f32[320]{0:T(512)} %copy-done.68) | copy-start | bytes 3844
  1464.1 84.6 %copy-start.56 = (f32[1,2048]{1,0:T(1,128)S(1)}, f32[1,2048]{1,0:T(1,128)}, u32[]{:S(2)}) copy-start(f32[1,2048]{1,0:T(1,128)} %copy-done.55) | copy-start | bytes 24580
  1464.1 84.6 %copy-start.88 = (f32[128]{0:T(128)S(1)}, f32[128]{0:T(128)}, u32[]{:S(2)}) copy-start(f32[128]{0:T(128)} %copy-done.87) | copy-start | bytes 1540
  1464.1 86.2 %copy-start.71 = (f32[2048]{0:T(1024)S(1)}, f32[2048]{0:T(1024)}, u32[]{:S(2)}) copy-start(f32[2048]{0:T(1024)} %get-tuple-element.23) | copy-start | bytes 24580
  1497.9 105.4 %copy-start.23 = (bf16[1,128,2048]{2,1,0:T(8,128)(2,1)S(1)}, bf16[1,128,2048]{2,1,0:T(8,128)(2,1)}, u32[]{:S(2)}) copy-start(bf16[1,128,2048]{2,1,0:T(8,128)(2,1)} %param.20) | copy-start | bytes 1572868
  1497.9 105.4 %copy-start.25 = (bf16[128,2048]{1,0:T(8,128)(2,1)S(1)}, bf16[128,2048]{1,0:T(8,128)(2,1)}, u32[]{:S(2)}) copy-start(bf16[128,2048]{1,0:T(8,128)(2,1)} %reduce-scatter.16.cloned.1.call-done) | copy-start | bytes 1572868
  1497.9 105.4 %copy-start.81 = (f32[128]{0:T(128)S(1)}, f32[128]{0:T(128)}, u32[]{:S(2)}) copy-start(f32[128]{0:T(128)} %copy-done.80) | copy-start | bytes 1540
  1497.9 105.4 %copy-start.98 = (f32[128]{0:T(128)S(1)}, f32[128]{0:T(128)}, u32[]{:S(2)}) copy-start(f32[128]{0:T(128)} %copy-done.97) | copy-start | bytes 1540
  1548.7 54.5 %copy-start.35 = (bf16[128,2048]{1,0:T(8,128)(2,1)S(1)}, bf16[128,2048]{1,0:T(8,128)(2,1)}, u32[]{:S(2)}) copy-start(bf16[128,2048]{1,0:T(8,128)(2,1)} %reduce-scatter.18.cloned.1.call-done) | copy-start | bytes 1572868
  (84 other events, 759.0 us)
Sparse Core Ops, SparseCore 0:
  22.4 48.8 all-gather.10
  331.7 50.5 reduce-scatter.11
  385.8 59.2 all-gather.12
  447.0 61.3 all-gather.24
  542.4 50.5 reduce-scatter.15
  596.7 36.6 all-gather.14
  636.4 60.2 reduce-scatter.23
  699.5 60.2 reduce-scatter.25
  1049.3 35.1 reduce-scatter.21
  1087.3 34.2 reduce-scatter.19
  1123.1 62.4 all-gather.20
  1187.6 62.1 all-gather.22
  1254.1 173.6 all-reduce.46
  1429.3 31.5 all-gather.18
  1463.0 31.6 all-gather.16
  1498.3 50.3 reduce-scatter.17
  1551.9 51.2 reduce-scatter.13
  1606.6 36.0 reduce-scatter.27

commit v2 on v1

v2 whole, which is shorter than its diff:
```python
import functools

import jax
import jax.numpy as jnp
from jax import lax
from jax.experimental import pallas as pl
from jax.experimental.pallas import tpu as pltpu
from jax.sharding import PartitionSpec as P

epsilon = 1e-06
decay_scale = 8.0
GROUP = ("seq", "shard")
ROWS = ("shard", "seq")
f32 = jnp.float32
bf16 = jnp.bfloat16
VM = pl.BlockSpec(memory_space=pltpu.VMEM)


def mm(left, right):
    return jnp.dot(left, right, preferred_element_type=f32)


def mm_nt(left, right):
    return lax.dot_general(left, right, (((1,), (1,)), ((), ())), preferred_element_type=f32)


def mm_tn(left, right):
    return lax.dot_general(left, right, (((0,), (0,)), ((), ())), preferred_element_type=f32)


def gather_rows(part):
    return lax.all_gather(part, ROWS, axis=0, tiled=True)


def scatter_rows(partial):
    return lax.psum_scatter(
        partial.astype(bf16), ROWS, scatter_dimension=0, tiled=True
    ).astype(f32)


def to_columns(weight):
    return lax.all_to_all(weight.astype(bf16), GROUP, split_axis=1, concat_axis=0, tiled=True)


def reduce_rows(grad):
    return lax.psum(grad.astype(bf16), "replica").astype(f32)


def reduce_columns(grad):
    owners = lax.axis_size(GROUP)
    copies = lax.axis_size("replica")
    depth, width = grad.shape
    piece = depth // (owners * copies)
    cut = grad.astype(bf16).reshape(owners, copies, piece, width)
    cut = jnp.swapaxes(cut, 0, 1).reshape(depth, width)
    cut = lax.psum_scatter(cut, "replica", scatter_dimension=0, tiled=True)
    cut = lax.all_to_all(cut, GROUP, split_axis=0, concat_axis=1, tiled=True)
    return lax.all_gather(cut, "replica", axis=0, tiled=True).astype(f32)


def norm_backward(grad_unit, unit, inverse):
    return inverse * (grad_unit - unit * jnp.mean(grad_unit * unit, axis=-1, keepdims=True))


def token_masks(labels, taps):
    length = labels.shape[1]
    masks = [
        (jnp.pad(labels, ((0, 0), (offset, 0)))[:, :length] == labels) for offset in range(taps)
    ]
    return jnp.stack(masks, -1).astype(f32).reshape(-1, taps)


def gelu_parts(x):
    inner = 0.7978845608028654 * (x + 0.044715 * x * x * x)
    t = jnp.tanh(inner)
    value = 0.5 * x * (1.0 + t)
    slope = 0.5 * (1.0 + t) + 0.5 * x * (1.0 - t * t) * 0.7978845608028654 * (
        1.0 + 3.0 * 0.044715 * x * x
    )
    return value, slope


def minus_expm1(y):
    poly = 1.0 + y * (1.0 / 8.0)
    for order in (7.0, 6.0, 5.0, 4.0, 3.0, 2.0):
        poly = 1.0 + y * (1.0 / order) * poly
    return jnp.where(y > -0.5, -y * poly, 1.0 - jnp.exp(y))


def dot_nn(a, b):
    return lax.dot_general(a, b, (((1,), (0,)), ((), ())), preferred_element_type=f32)


def dot_nt(a, b):
    return lax.dot_general(a, b, (((1,), (1,)), ((), ())), preferred_element_type=f32)


def dot_tn(a, b):
    return lax.dot_general(a, b, (((0,), (0,)), ((), ())), preferred_element_type=f32)


def fill_blocks(target, source):
    target[...] = jnp.zeros_like(target)
    count, size = source.shape[0], source.shape[1]
    for h in range(count):
        target[h * size : (h + 1) * size, h * size : (h + 1) * size] = source[h].astype(bf16).astype(f32)


def put_tiles(ref, here, value):
    width = value.shape[1]
    for tile in range(ref.shape[0]):
        lanes = min(128, width - 128 * tile)
        ref[tile, here, 0:lanes] = value[:, 128 * tile : 128 * tile + lanes]


def get_tiles(ref, here, width):
    parts = [ref[tile, here, 0 : min(128, width - 128 * tile)] for tile in range(ref.shape[0])]
    return jnp.concatenate(parts, axis=1)


def clear_tail(ref, width):
    tail = ref.shape[0] * 128 - width
    if tail:
        ref[ref.shape[0] - 1, :, 128 - tail :] = jnp.zeros((ref.shape[1], tail), f32)


def seq_scan(decay_ref, value_ref, sequences, length, reverse):
    tiles = decay_ref.shape[0]
    unroll = 8

    def step(i, states):
        states = list(states)
        for j in range(unroll):
            at = i * unroll + j
            if reverse:
                at = length - 1 - at
            here = pl.ds(at, sequences, stride=length)
            for tile in range(tiles):
                value = value_ref[tile, here, :]
                decay = decay_ref[tile, here, :]
                if reverse:
                    new = value + states[tile]
                    value_ref[tile, here, :] = new
                    states[tile] = decay * new
                else:
                    states[tile] = value + decay * states[tile]
                    value_ref[tile, here, :] = states[tile]
        return tuple(states)

    lax.fori_loop(0, length // unroll, step, (jnp.zeros((sequences, 128), f32),) * tiles)


def mix_forward_kernel(
    sequences, length, n_ref, wb_ref, wi_ref, mask_ref, conv_ref, bias_ref, rw_ref, iw_ref, ow_ref,
    partial_ref, product_ref, pre_ref, conv_in_ref, values_ref, recur_ref, inject_ref, decay_ref, states_ref,
    pad, rbig, ibig,
):
    fill_blocks(rbig, rw_ref)
    fill_blocks(ibig, iw_ref)
    pad[0:8, :] = jnp.zeros((8, pad.shape[1]), f32)
    taps = conv_ref.shape[0]
    width = pad.shape[1]
    clear_tail(decay_ref, width)
    clear_tail(states_ref, width)

    def one(s, _):
        base = pl.multiple_of(s * length, length)
        here = pl.ds(base, length)
        rows = n_ref[here, :]
        pre_ref[here, :] = dot_nn(rows, wb_ref[...])
        conv_in = dot_nn(rows, wi_ref[...]).astype(bf16)
        conv_in_ref[here, :] = conv_in
        pad[8 : 8 + length, :] = conv_in.astype(f32)
        total = bias_ref[0:1, :] + conv_ref[0:1, :] * pad[8 : 8 + length, :]
        for k in range(1, taps):
            total = total + conv_ref[k : k + 1, :] * pad[8 - k : 8 - k + length, :] * mask_ref[here, k : k + 1]
        values = total.astype(bf16)
        values_ref[here, :] = values
        recur = jax.nn.sigmoid(dot_nn(values, rbig[...].astype(bf16)) + bias_ref[1:2, :])
        inject = jax.nn.sigmoid(dot_nn(values, ibig[...].astype(bf16)) + bias_ref[2:3, :])
        recur_ref[here, :] = recur
        inject_ref[here, :] = inject
        log_decay = -decay_scale * bias_ref[3:4, :] * recur
        inside = mask_ref[here, 1:2] > 0.5
        put_tiles(decay_ref, here, jnp.where(inside, jnp.exp(log_decay), 0.0))
        scale = jnp.where(inside, jnp.sqrt(minus_expm1(2.0 * log_decay)), 1.0)
        put_tiles(states_ref, here, scale * inject * values.astype(f32))
        return 0

    lax.fori_loop(0, sequences, one, 0)
    seq_scan(decay_ref, states_ref, sequences, length, False)

    def two(s, _):
        base = pl.multiple_of(s * length, length)
        here = pl.ds(base, length)
        act, _unused = gelu_parts(pre_ref[here, :])
        product = (act * get_tiles(states_ref, here, width)).astype(bf16)
        product_ref[here, :] = product
        partial_ref[here, :] = dot_nn(product, ow_ref[...]).astype(bf16)
        return 0

    lax.fori_loop(0, sequences, two, 0)


def mix_forward(sequences, normed, wb, wi, mask, conv, bias, rw, iw, ow):
    total, width = normed.shape[0], wb.shape[1]
    length = total // sequences
    depth = ow.shape[1]
    shape = jax.ShapeDtypeStruct
    like = lambda dt: shape((total, width), dt)
    tiled = shape((-(-width // 128), total, 128), f32)
    return pl.pallas_call(
        functools.partial(mix_forward_kernel, sequences, length),
        out_shape=(
            shape((total, depth), bf16), like(bf16), like(f32), like(bf16), like(bf16), like(f32), like(f32), tiled, tiled,
        ),
        in_specs=[VM] * 9,
        out_specs=[VM] * 9,
        scratch_shapes=[
            pltpu.VMEM((8 + length, width), f32),
            pltpu.VMEM((width, width), f32),
            pltpu.VMEM((width, width), f32),
        ],
        compiler_params=pltpu.CompilerParams(vmem_limit_bytes=56 * 2**20),
        cost_estimate=pl.CostEstimate(flops=2 * total * width * 3 * depth, bytes_accessed=20 * 2**20, transcendentals=total * width * 5),
    )(normed, wb, wi, mask, conv, bias, rw, iw, ow)


def mix_backward_kernel(
    sequences, length, mid_ref, ow_ref, wb_ref, wi_ref, pre_ref, conv_in_ref, values_ref, recur_ref, inject_ref, decay_ref, states_ref,
    mask_ref, conv_ref, bias_ref, rw_ref, iw_ref,
    partial_ref, branch_low_ref, conv_low_ref, dconv_ref, sums_ref, drw_ref, diw_ref,
    adj, pad, rbig, ibig, dr, di,
):
    fill_blocks(rbig, rw_ref)
    fill_blocks(ibig, iw_ref)
    dr[...] = jnp.zeros_like(dr)
    di[...] = jnp.zeros_like(di)
    sums_ref[...] = jnp.zeros_like(sums_ref)
    dconv_ref[...] = jnp.zeros_like(dconv_ref)
    taps = conv_ref.shape[0]
    width = pad.shape[1]
    clear_tail(adj, width)

    def one(s, _):
        base = pl.multiple_of(s * length, length)
        here = pl.ds(base, length)
        product_grad = dot_nt(mid_ref[here, :], ow_ref[...])
        act, slope = gelu_parts(pre_ref[here, :])
        branch_low_ref[here, :] = (product_grad * get_tiles(states_ref, here, width) * slope).astype(bf16)
        put_tiles(adj, here, product_grad * act)
        return 0

    lax.fori_loop(0, sequences, one, 0)
    seq_scan(decay_ref, adj, sequences, length, True)

    def two(s, _):
        base = pl.multiple_of(s * length, length)
        here = pl.ds(base, length)
        adjoint = get_tiles(adj, here, width)
        recur = recur_ref[here, :]
        inject = inject_ref[here, :]
        decay = get_tiles(decay_ref, here, width)
        values = values_ref[here, :]
        values_f = values.astype(f32)
        inside = mask_ref[here, 1:2] > 0.5
        rate = bias_ref[3:4, :]
        log_decay = -decay_scale * rate * recur
        scale = jnp.where(inside, jnp.sqrt(minus_expm1(2.0 * log_decay)), 1.0)
        pad[0:8, :] = jnp.zeros((8, width), f32)
        pad[8 : 8 + length, :] = get_tiles(states_ref, here, width)
        previous = pad[7 : 7 + length, :]
        driven = adjoint * inject * values_f
        log_grad = jnp.where(inside, adjoint * previous * decay - driven * decay * decay / scale, 0.0)
        recur_low = (log_grad * (-decay_scale * rate) * recur * (1.0 - recur)).astype(bf16)
        inject_low = (driven * scale * (1.0 - inject)).astype(bf16)
        sums_ref[1:2, :] += jnp.sum(recur_low.astype(f32), axis=0, keepdims=True)
        sums_ref[2:3, :] += jnp.sum(inject_low.astype(f32), axis=0, keepdims=True)
        sums_ref[3:4, :] += jnp.sum(log_grad * recur, axis=0, keepdims=True)
        dr[...] += dot_tn(values, recur_low)
        di[...] += dot_tn(values, inject_low)
        grad = adjoint * scale * inject
        grad = grad + dot_nt(recur_low, rbig[...].astype(bf16)) + dot_nt(inject_low, ibig[...].astype(bf16))
        sums_ref[0:1, :] += jnp.sum(grad, axis=0, keepdims=True)
        pad[8 : 8 + length, :] = conv_in_ref[here, :].astype(f32)
        dconv_ref[0:1, :] += jnp.sum(grad * pad[8 : 8 + length, :], axis=0, keepdims=True)
        masked = []
        for k in range(1, taps):
            part = grad * mask_ref[here, k : k + 1]
            masked.append(part)
            dconv_ref[k : k + 1, :] += jnp.sum(part * pad[8 - k : 8 - k + length, :], axis=0, keepdims=True)
        total = grad * conv_ref[0:1, :]
        pad[length : length + 8, :] = jnp.zeros((8, width), f32)
        for k in range(1, taps):
            pad[0:length, :] = masked[k - 1] * conv_ref[k : k + 1, :]
            total = total + pad[k : k + length, :]
        conv_low = total.astype(bf16)
        conv_low_ref[here, :] = conv_low
        partial_ref[here, :] = (dot_nt(branch_low_ref[here, :], wb_ref[...]) + dot_nt(conv_low, wi_ref[...])).astype(bf16)
        return 0

    lax.fori_loop(0, sequences, two, 0)
    size = drw_ref.shape[1]
    for h in range(drw_ref.shape[0]):
        cut = slice(h * size, (h + 1) * size)
        drw_ref[h] = dr[cut, cut]
        diw_ref[h] = di[cut, cut]


def mix_backward(sequences, mid_low, ow, wb, wi, pre, conv_in, values, recur, inject, decay, states, mask, conv, bias, rw, iw):
    total, depth = mid_low.shape
    width = ow.shape[0]
    length = total // sequences
    shape = jax.ShapeDtypeStruct
    return pl.pallas_call(
        functools.partial(mix_backward_kernel, sequences, length),
        out_shape=(
            shape((total, depth), bf16), shape((total, width), bf16), shape((total, width), bf16),
            shape(conv.shape, f32), shape((4, width), f32), shape(rw.shape, f32), shape(iw.shape, f32),
        ),
        in_specs=[VM] * 16,
        out_specs=[VM] * 7,
        scratch_shapes=[
            pltpu.VMEM(states.shape, f32),
            pltpu.VMEM((8 + length, width), f32),
            pltpu.VMEM((width, width), f32),
            pltpu.VMEM((width, width), f32),
            pltpu.VMEM((width, width), f32),
            pltpu.VMEM((width, width), f32),
        ],
        compiler_params=pltpu.CompilerParams(vmem_limit_bytes=56 * 2**20),
        cost_estimate=pl.CostEstimate(flops=2 * total * width * 3 * depth, bytes_accessed=25 * 2**20, transcendentals=total * width * 5),
    )(mid_low, ow, wb, wi, pre, conv_in, values, recur, inject, decay, states, mask, conv, bias, rw, iw)


def body(
    tokens,
    segments,
    cotangent,
    norm_gain,
    branch_weight,
    input_weight,
    conv_weight,
    conv_bias,
    recur_gate_weight,
    recur_gate_bias,
    input_gate_weight,
    input_gate_bias,
    decay_param,
    output_weight,
    mlp_norm_gain,
    gate_weight,
    up_weight,
    down_weight,
):
    def low(item):
        return item.astype(bf16).astype(f32)

    gains = lax.all_gather(
        jnp.stack([norm_gain, mlp_norm_gain]).astype(bf16), GROUP, axis=1, tiled=True
    ).astype(f32)
    gain_f, mlp_gain_f = gains[0], gains[1]
    rows = tokens[0].astype(f32)
    count_rows = rows.shape[0]
    halves = lax.axis_size("seq")
    inverse = lax.rsqrt(jnp.mean(rows * rows, axis=-1, keepdims=True) + epsilon)
    unit = rows * inverse
    normed = (unit * gain_f).astype(bf16)
    normed_all = gather_rows(normed)
    branch_w = to_columns(branch_weight)
    input_w = to_columns(input_weight)
    labels = gather_rows(segments).reshape(-1, halves * count_rows) + 1
    out_low = gather_rows(cotangent[0])
    gate_w = to_columns(gate_weight)
    up_w = to_columns(up_weight)
    output_w = output_weight.astype(bf16)
    down_w = down_weight.astype(bf16)
    sequences = labels.shape[0]

    mask = token_masks(labels, conv_weight.shape[0])
    conv_f = low(conv_weight)
    decay_f = low(decay_param)
    bias = jnp.stack([low(conv_bias), low(recur_gate_bias), low(input_gate_bias), jax.nn.softplus(-decay_f)])
    mixed = mix_forward(
        sequences, normed_all, branch_w, input_w, mask, conv_f, bias, recur_gate_weight, input_gate_weight, output_w
    )
    partial, product = mixed[:2]
    middle = rows + scatter_rows(partial)
    inverse_two = lax.rsqrt(jnp.mean(middle * middle, axis=-1, keepdims=True) + epsilon)
    unit_two = middle * inverse_two
    normed_two = gather_rows((unit_two * mlp_gain_f).astype(bf16))
    gate_pre = mm(normed_two, gate_w)
    up_pre = mm(normed_two, up_w)
    gate_act, gate_pull = jax.vjp(jax.nn.gelu, gate_pre)
    hidden = (gate_act * up_pre).astype(bf16)
    block_out = (middle + scatter_rows(mm(hidden, down_w))).astype(bf16)

    grad_out = cotangent[0].astype(f32)
    hidden_grad = mm_nt(out_low, down_w)
    gate_low = gate_pull(hidden_grad * up_pre)[0].astype(bf16)
    up_low = (hidden_grad * gate_act).astype(bf16)
    down_weight_grad = reduce_rows(mm_tn(hidden, out_low))
    gate_weight_grad = reduce_columns(mm_tn(normed_two, gate_low))
    up_weight_grad = reduce_columns(mm_tn(normed_two, up_low))
    two_grad = scatter_rows(mm_nt(gate_low, gate_w) + mm_nt(up_low, up_w))
    mlp_gain_grad = jnp.sum(two_grad * unit_two, axis=0)
    middle_grad = grad_out + norm_backward(two_grad * mlp_gain_f, unit_two, inverse_two)
    mid_low = gather_rows(middle_grad.astype(bf16))
    output_weight_grad = reduce_rows(mm_tn(product, mid_low))
    back = mix_backward(
        sequences, mid_low, output_w, branch_w, input_w, *mixed[2:], mask, conv_f, bias, recur_gate_weight, input_gate_weight
    )
    partial, branch_low, conv_low, conv_weight_grad, sums, recur_weight_grad, inject_weight_grad = back
    conv_bias_grad, recur_bias_grad, inject_bias_grad = sums[0], sums[1], sums[2]
    decay_param_grad = sums[3] * decay_scale * jax.nn.sigmoid(-decay_f)
    normed_grad = scatter_rows(partial)
    gain_grad = jnp.sum(normed_grad * unit, axis=0)
    tokens_grad = (middle_grad + norm_backward(normed_grad * gain_f, unit, inverse)).astype(bf16)
    branch_weight_grad = reduce_columns(mm_tn(normed_all, branch_low))
    input_weight_grad = reduce_columns(mm_tn(normed_all, conv_low))
    gain_pair = lax.psum_scatter(
        jnp.stack([gain_grad, mlp_gain_grad]), GROUP, scatter_dimension=1, tiled=True
    )
    small = (
        gain_pair,
        conv_weight_grad,
        conv_bias_grad,
        recur_weight_grad,
        recur_bias_grad,
        inject_weight_grad,
        inject_bias_grad,
        decay_param_grad,
    )
    small = lax.psum(tuple(item.astype(bf16) for item in small), "replica")
    small = [item.astype(f32) for item in small]
    return (
        block_out[None],
        tokens_grad[None],
        small[0][0],
        branch_weight_grad,
        input_weight_grad,
        small[1],
        small[2],
        small[3],
        small[4],
        small[5],
        small[6],
        small[7],
        output_weight_grad,
        small[0][1],
        gate_weight_grad,
        up_weight_grad,
        down_weight_grad,
    )


def solution(mesh):
    row3 = P(("shard", "replica"), "seq", None)
    vec = P(("seq", "shard"))
    mat = P(("seq", "shard"), None)
    cube = P(("seq", "shard"), None, None)
    taps = P(None, ("seq", "shard"))
    params = (vec, mat, mat, taps, vec, cube, vec, cube, vec, vec, mat, vec, mat, mat, mat)
    in_specs = (row3, P(("shard", "replica"), "seq"), row3) + params
    out_specs = (row3, row3) + params
    return jax.shard_map(body, mesh=mesh, in_specs=in_specs, out_specs=out_specs, check_vma=False)
```

time: 1690 us -> 1170 us (0.69)
  local copies, waits for them, and re-layouts: 597 us -> 50.4 us
  waiting for transfers between devices: 664 us -> 792 us
  other arithmetic: 144 us -> 50.9 us
  Pallas kernels: 0 us -> 53.4 us
  matrix products: 120 us -> 72.4 us
    pad x28 -> x0, local copies, waits for them, and re-layouts: 382 us -> none  [the longest x14 216 us: body(): lax.associative_scan(link, (shift_up(decay3, 1)[:, ::-1], states_grad[:,...]
    reduce_scatter x4, waiting for transfers between devices: 0.09 us -> 97.4 us  [reduce_columns(): cut = lax.psum_scatter(cut, 'replica', scatter_dimension=0, tiled=True)]
    slice x22 -> x1, local copies, waits for them, and re-layouts: 93.3 us -> 0.03 us  [body(): sums[2]]
    pallas_call x0 -> x2, Pallas kernels: none -> 53.4 us  [the longest x1 29.9 us: mix_backward(): pl.pallas_call(functools.partial(mix_backward_kernel, sequences, length),...]
    add x28 -> x0, other arithmetic: 43.3 us -> none  [the longest x12 17.1 us: link(): return (earlier[0] * later[0], earlier[1] * later[0] + later[1])]
    reshape x13 -> x0, local copies, waits for them, and re-layouts: 30.5 us -> none  [the longest x2 5.34 us: body(): values_grad = values_grad + jnp.einsum('thj,hij->thi', recur_blocks, recu...]
    reduce_sum x2 -> x0, other arithmetic: 20.1 us -> none  [the longest x1 12.2 us: body(): jnp.sum(log_grad * decay_scale * recur_gate, axis=0)]
    unnamed x230 -> x67, local copies, waits for them, and re-layouts: 38.6 us -> 21.1 us
  transfers between devices with their start and end apart: 22 -> 22, of which waited for: 14 -> 18; matrix products, arithmetic and copies ran while one was open for 34% -> 11% of each run, Pallas kernels for 0% -> 3%
where the time goes in v2:
time: 1170 us; the launch traced here: 1160 us
  waiting for transfers between devices  792 us (68%)
  blocking collectives  109 us (9%)
  matrix products  72.4 us (6%)
  Pallas kernels  53.4 us (5%)
  other arithmetic  50.9 us (4%)
  local copies, waits for them, and re-layouts  50.4 us (4%)
  starting transfers between devices  17.6 us (2%)
  between operations  15.2 us (1%)
    reduce_scatter x4, waiting for transfers between devices, scatter_rows(): lax.psum_scatter(partial.astype(bf16), ROWS, scatter_dimension=0, tiled=T...  204 us
    psum x1, waiting for transfers between devices, body(): small = lax.psum(tuple((item.astype(bf16) for item in small)), 'replica')  173 us
    all_gather x4, waiting for transfers between devices, reduce_columns(): return lax.all_gather(cut, 'replica', axis=0, tiled=True).astype(f32)  156 us
    all_to_all x4, waiting for transfers between devices, to_columns(): lax.all_to_all(weight.astype(bf16), GROUP, split_axis=1, concat_axis=0, t...  104 us
    reduce_scatter x4, waiting for transfers between devices, reduce_columns(): cut = lax.psum_scatter(cut, 'replica', scatter_dimension=0, tiled=True)  97.4 us
    all_to_all x4, blocking collectives, reduce_columns(): cut = lax.all_to_all(cut, GROUP, split_axis=0, concat_axis=1, tiled=True)  56.7 us
    unnamed x19, waiting for transfers between devices  37.9 us
    all_gather x1, blocking collectives, gather_rows(): return lax.all_gather(part, ROWS, axis=0, tiled=True)  30.1 us
  transfers between devices with their start and end apart: 22, of which 18 were waited for; matrix products, arithmetic and copies ran while one was open for 11% of the time, Pallas kernels for 3%

profile of v2, /device:TPU:0, one launch (start us, length us, event | category | flops | bytes accessed | tf_op | source)
XLA Modules:
  0.0 1160.7 jit_solution(11708643856258929330)
XLA Ops:
  8.6 10.3 all_gather.30
  25.1 3.6 all-to-all-start
  28.7 30.1 %all-gather.1 = s32[8,1,128]{2,1,0:T(1,128)S(1)} all-gather(s32[1,1,128]{2,1,0:T(1,128)S(1)} %bitcast.169), channel_id=1, replica_groups=mesh['seq'=2,'shard'=4,'replica'=4] {'shard','seq'}, dimensions={0}, use_global_device_ids=true | all-gather | bytes 4608 | tf_op jit(solution)/shard_map/all_gather | solution.py:32
  61.8 4.3 all-to-all-start.1
  72.6 11.9 %all-to-all-done.1 = bf16[256,8,320]{0,2,1:T(8,128)(2,1)} async-done(((bf16[256,8,320]{0,2,1:T(8,128)(2,1)}), bf16[256,8,320]{0,2,1:T(8,128)(2,1)}, u32[]{:S(2)}, u32[]{:S(2)}) %all-to-all-start.1) | async-done | bytes 1310752 | tf_op jit(solution)/shard_map/all_to_all | solution.py:42
  87.0 23.5 %shard_map.305 = (bf16[1024,2048]{1,0:T(8,128)(2,1)}, bf16[1024,320]{1,0:T(8,128)(2,1)}, f32[1024,320]{1,0:T(8,128)}, bf16[1024,320]{1,0:T(8,128)(2,1)}, bf16[10...) custom-call(bf16[1024,2048]{1,0:T(8,128)(2,1)} %all-gather.11.cloned, ...), custom_call_target="tpu_custom_call" | custom-call | flops 4026531840 | bytes 20971520 | tf_op jit(solution)/shard_map/pallas_call | solution.py:212
  110.5 50.7 %reduce-scatter.12.cloned.1.call-done = bf16[128,2048]{1,0:T(8,128)(2,1)} async-done(((bf16[1024,2048]{1,0:T(8,128)(2,1)}), bf16[128,2048]{1,0:T(8,128)(2,1)}) %reduce-scatter.12.cloned.1.call-update) | async-done | bytes 524304 | tf_op jit(solution)/shard_map/reduce_scatter | solution.py:36
  165.2 5.4 copy.76
  170.5 4.5 all-to-all-start.2
  175.0 5.4 copy.78
  180.4 46.2 %all-to-all-done.2 = bf16[256,8,768]{0,2,1:T(8,128)(2,1)} async-done(((bf16[256,8,768]{0,2,1:T(8,128)(2,1)}), bf16[256,8,768]{0,2,1:T(8,128)(2,1)}, u32[]{:S(2)}, u32[]{:S(2)}) %all-to-all-start.2) | async-done | bytes 3145760 | tf_op jit(solution)/shard_map/all_to_all | solution.py:42
  226.5 4.5 all-to-all-start.3
  231.1 4.6 copy.77
  235.7 46.1 %all-to-all-done.3 = bf16[256,8,768]{0,2,1:T(8,128)(2,1)} async-done(((bf16[256,8,768]{0,2,1:T(8,128)(2,1)}), bf16[256,8,768]{0,2,1:T(8,128)(2,1)}, u32[]{:S(2)}, u32[]{:S(2)}) %all-to-all-start.3) | async-done | bytes 3145760 | tf_op jit(solution)/shard_map/all_to_all | solution.py:42
  281.8 5.1 copy.79
  287.0 8.4 fusion.54
  295.3 5.0 fusion.55
  300.4 12.6 %multiply_convert_fusion = (bf16[1024,768]{1,0:T(8,128)(2,1)S(1)}, bf16[1024,768]{1,0:T(8,128)(2,1)S(1)}, bf16[1024,768]{1,0:T(8,128)(2,1)}) fusion(f32[1024,768]{1,0:T(8,128)} %fusion.54, f32[1024,768]{1,0:T(8,128)} %fusion.55, f32[768,2048]{1,0:T(8,128)} %param.35, bf16[1,1024,2048]{2,1,0:T(8,128)(2,1)} %all-gather.25.cloned.1.call-done), kind=kOutput, calls=%fused_computation.18 | convolution fusion | flops 3243245568 | bytes 21495808 | tf_op jit(solution)/shard_map/dot_general | solution.py:24
  316.5 5.2 add_convert_fusion
  321.7 50.7 %reduce-scatter.16.cloned.1.call-done = bf16[128,2048]{1,0:T(8,128)(2,1)} async-done(((bf16[1024,2048]{1,0:T(8,128)(2,1)}), bf16[128,2048]{1,0:T(8,128)(2,1)}) %reduce-scatter.16.cloned.1.call-update) | async-done | bytes 524304 | tf_op jit(solution)/shard_map/reduce_scatter | solution.py:36
  376.3 5.7 convolution_convert_fusion.2
  385.6 5.7 convolution_convert_fusion.1
  393.4 19.7 %all-gather.15.cloned.1.call-done.mid_ref = bf16[1024,2048]{1,0:T(8,128)(2,1)} async-done(((bf16[128,2048]{1,0:T(8,128)(2,1)}), bf16[1024,2048]{1,0:T(8,128)(2,1)}) %all-gather.15.cloned.1.call-update) | async-done | bytes 4194320 | tf_op jit(solution)/shard_map/all_gather | solution.py:32
  413.1 29.9 %shard_map.306 = (bf16[1024,2048]{1,0:T(8,128)(2,1)}, bf16[1024,320]{1,0:T(8,128)(2,1)}, bf16[1024,320]{1,0:T(8,128)(2,1)}, f32[4,320]{1,0:T(4,128)}, f32[4,320]...) custom-call(bf16[1024,2048]{1,0:T(8,128)(2,1)} %all-gather.15.cloned.1.call-done.mid_ref, ...), custom_call_target="tpu_custom_call" | custom-call | flops 4026531840 | bytes 26214400 | tf_op jit(solution)/shard_map/pallas_call | solution.py:315
  443.0 3.8 convolution_convert_fusion.5
  450.0 5.0 convolution_convert_fusion.4
  458.3 18.0 %reduce-scatter.24.cloned.1.call-done = bf16[512,768]{1,0:T(8,128)(2,1)} async-done(((bf16[2048,768]{1,0:T(8,128)(2,1)}), bf16[512,768]{1,0:T(8,128)(2,1)}) %reduce-scatter.24.cloned.1.call-update) | async-done | bytes 786448 | tf_op jit(solution)/shard_map/reduce_scatter | solution.py:56
  476.3 16.2 %all_to_all.152 = bf16[8,64,768]{2,1,0:T(8,128)(2,1)S(1)} all-to-all(bf16[8,64,768]{2,1,0:T(8,128)(2,1)} %bitcast.151), channel_id=1, replica_groups=mesh['seq'=2,'shard'=4,'replica'=4] {'seq','shard'}, dimensions={0} | all-to-all | bytes 1572864 | tf_op jit(solution)/shard_map/all_to_all | solution.py:57
  493.5 46.0 %reduce-scatter.26.cloned.1.call-done = bf16[512,768]{1,0:T(8,128)(2,1)} async-done(((bf16[2048,768]{1,0:T(8,128)(2,1)}), bf16[512,768]{1,0:T(8,128)(2,1)}) %reduce-scatter.26.cloned.1.call-update) | async-done | bytes 786448 | tf_op jit(solution)/shard_map/reduce_scatter | solution.py:56
  539.5 16.2 %all_to_all.153 = bf16[8,64,768]{2,1,0:T(8,128)(2,1)S(1)} all-to-all(bf16[8,64,768]{2,1,0:T(8,128)(2,1)} %bitcast.150), channel_id=1, replica_groups=mesh['seq'=2,'shard'=4,'replica'=4] {'seq','shard'}, dimensions={0} | all-to-all | bytes 1572864 | tf_op jit(solution)/shard_map/all_to_all | solution.py:57
  556.8 7.2 fusion.4
  568.0 9.7 reduce-scatter.20.cloned.1.call-done
  577.7 12.0 %all_to_all.154 = bf16[8,64,320]{2,1,0:T(8,128)(2,1)S(1)} all-to-all(bf16[8,64,320]{2,1,0:T(8,128)(2,1)} %bitcast.153), channel_id=1, replica_groups=mesh['seq'=2,'shard'=4,'replica'=4] {'seq','shard'}, dimensions={0} | all-to-all | bytes 655360 | tf_op jit(solution)/shard_map/all_to_all | solution.py:57
  591.0 23.7 %reduce-scatter.22.cloned.1.call-done = bf16[512,320]{1,0:T(8,128)(2,1)} async-done(((bf16[2048,320]{1,0:T(8,128)(2,1)}), bf16[512,320]{1,0:T(8,128)(2,1)}) %reduce-scatter.22.cloned.1.call-update) | async-done | bytes 327696 | tf_op jit(solution)/shard_map/reduce_scatter | solution.py:56
  614.7 12.3 %all_to_all.155 = bf16[8,64,320]{2,1,0:T(8,128)(2,1)S(1)} all-to-all(bf16[8,64,320]{2,1,0:T(8,128)(2,1)} %bitcast.152), channel_id=1, replica_groups=mesh['seq'=2,'shard'=4,'replica'=4] {'seq','shard'}, dimensions={0} | all-to-all | bytes 655360 | tf_op jit(solution)/shard_map/all_to_all | solution.py:57
  629.6 7.7 convolution_convert_fusion
  637.4 41.9 %all-gather.21.cloned.1.call-done = bf16[256,6144]{1,0:T(8,128)(2,1)} async-done(((bf16[64,6144]{1,0:T(8,128)(2,1)}), bf16[256,6144]{1,0:T(8,128)(2,1)}) %all-gather.21.cloned.1.call-update) | async-done | bytes 3145744 | tf_op jit(solution)/shard_map/all_gather | solution.py:58
  679.4 5.3 convert_element_type.243
  684.7 58.8 %all-gather.23.cloned.1.call-done = bf16[256,6144]{1,0:T(8,128)(2,1)} async-done(((bf16[64,6144]{1,0:T(8,128)(2,1)}), bf16[256,6144]{1,0:T(8,128)(2,1)}) %all-gather.23.cloned.1.call-update) | async-done | bytes 3145744 | tf_op jit(solution)/shard_map/all_gather | solution.py:58
  743.5 5.3 convert_element_type.245
  749.0 172.6 %all-reduce.7.cloned.1.call-done = (bf16[2,160,160]{2,1,0:T(8,128)(2,1)}, bf16[2,160,160]{2,1,0:T(8,128)(2,1)}, bf16[320,2048]{1,0:T(8,128)(2,1)}, bf16[768,2048]{1,0:T(8,128)(2,1)}) async-done(((bf16[2,160,160]{2,1,0:T(8,128)(2,1)}, bf16[2,160,160]{2,1,0:T(8,128)(2,1)}, bf16[320,2048]{1,0:T(8,128)(2,1)}, bf16[768,2048]{1,0:T(8,128)(2,1)}), (bf16[2,160,160]{2,1,0:T(8,128)(2,1)}, ...) | async-done | bytes 4661264 | tf_op jit(solution)/shard_map/psum | solution.py:434
  921.6 5.5 convert_element_type.247
  930.4 24.8 %all-gather.17.cloned.1.call-done = bf16[256,2560]{1,0:T(8,128)(2,1)} async-done(((bf16[64,2560]{1,0:T(8,128)(2,1)}), bf16[256,2560]{1,0:T(8,128)(2,1)}) %all-gather.17.cloned.1.call-update) | async-done | bytes 1310736 | tf_op jit(solution)/shard_map/all_gather | solution.py:58
  958.4 30.7 %all-gather.19.cloned.1.call-done = bf16[256,2560]{1,0:T(8,128)(2,1)} async-done(((bf16[64,2560]{1,0:T(8,128)(2,1)}), bf16[256,2560]{1,0:T(8,128)(2,1)}) %all-gather.19.cloned.1.call-update) | async-done | bytes 1310736 | tf_op jit(solution)/shard_map/all_gather | solution.py:58
  992.2 50.8 %reduce-scatter.18.cloned.1.call-done = bf16[128,2048]{1,0:T(8,128)(2,1)} async-done(((bf16[1024,2048]{1,0:T(8,128)(2,1)}), bf16[128,2048]{1,0:T(8,128)(2,1)}) %reduce-scatter.18.cloned.1.call-update) | async-done | bytes 524304 | tf_op jit(solution)/shard_map/reduce_scatter | solution.py:36
  1046.0 51.6 %reduce-scatter.14.cloned.1.call-done = bf16[128,2048]{1,0:T(8,128)(2,1)} async-done(((bf16[1024,2048]{1,0:T(8,128)(2,1)}), bf16[128,2048]{1,0:T(8,128)(2,1)}) %reduce-scatter.14.cloned.1.call-update) | async-done | bytes 524304 | tf_op jit(solution)/shard_map/reduce_scatter | solution.py:36
  1100.4 36.6 %reduce-scatter.28.cloned.1.call-done = f32[256,2]{1,0:T(8,128)} async-done(((f32[2048,2]{1,0:T(8,128)}), f32[256,2]{1,0:T(8,128)}) %reduce-scatter.28.cloned.1.call-update) | async-done | bytes 2064
  1138.0 11.9 %all-reduce.3 = (bf16[2,256]{1,0:T(2,128)(2,1)S(1)}, bf16[4,320]{1,0:T(4,128)(2,1)S(1)}, bf16[320]{0:T(512)(128)(2,1)S(1)}, bf16[320]{0:T(512)(128)(2,1)S(1)}, b...) all-reduce(bf16[2,256]{1,0:T(2,128)(2,1)S(1)} %copy.91, ...), channel_id=1, replica_groups=mesh['seq'=2,'shard'=4,'replica'=4] {'replica'}, use_global_device_ids=true, to_apply=%region_11.12 | all-reduce | flops 3072 | bytes 12288 | tf_op jit(solution)/shard_map/psum | solution.py:434
  (175 shorter events, 72.9 us)
Async XLA Ops:
  7.2 79.8 %all-gather.11.cloned.1.call-start = ((), (), s32[]{:S(2)}) async-start(), calls=%async_computation.17 | async-start | bytes 4718592 | tf_op jit(solution)/shard_map/all_gather | solution.py:32
  22.3 6.4 copy-start.21
  25.1 36.7 %all-to-all-start = ((bf16[256,8,320]{0,2,1:T(8,128)(2,1)}), bf16[256,8,320]{0,2,1:T(8,128)(2,1)S(1)}, u32[]{:S(2)}, u32[]{:S(2)}) async-start(bf16[256,8,320]{0,2,1:T(8,128)(2,1)} %bitcast.136), calls=%async_computation | async-start | bytes 2621440 | tf_op jit(solution)/shard_map/all_to_all | solution.py:42
  58.9 8.4 copy-start.18
  58.9 8.4 copy-start.19
  58.9 8.4 copy-start.20
  58.9 8.4 copy-start.15
  61.8 8.7 copy-start.17
  61.8 22.7 %all-to-all-start.1 = ((bf16[256,8,320]{0,2,1:T(8,128)(2,1)}), bf16[256,8,320]{0,2,1:T(8,128)(2,1)}, u32[]{:S(2)}, u32[]{:S(2)}) async-start(bf16[256,8,320]{0,2,1:T(8,128)(2,1)} %bitcast.135), calls=%async_computation.1 | async-start | bytes 2621440 | tf_op jit(solution)/shard_map/all_to_all | solution.py:42
  66.0 95.2 %reduce-scatter.12.cloned.1.call-start = ((), (), s32[]{:S(2)}) async-start(), calls=%async_computation.18 | async-start | bytes 4718592 | tf_op jit(solution)/shard_map/reduce_scatter | solution.py:36
  110.5 50.7 %copy-start = (bf16[1,128,2048]{2,1,0:T(8,128)(2,1)S(1)}, bf16[1,128,2048]{2,1,0:T(8,128)(2,1)}, u32[]{:S(2)}) copy-start(bf16[1,128,2048]{2,1,0:T(8,128)(2,1)} %param.18) | copy-start | bytes 1572868
  110.5 176.4 %all-gather.13.cloned.1.call-start = ((), (), s32[]{:S(2)}) async-start(), calls=%async_computation.19 | async-start | bytes 4718592 | tf_op jit(solution)/shard_map/all_gather | solution.py:32
  164.6 135.8 %all-gather.25.cloned.1.call-start = ((), (), s32[]{:S(2)}) async-start(), calls=%async_computation.32 | async-start | bytes 4718592 | tf_op jit(solution)/shard_map/all_gather | solution.py:32
  170.5 56.0 %all-to-all-start.2 = ((bf16[256,8,768]{0,2,1:T(8,128)(2,1)}), bf16[256,8,768]{0,2,1:T(8,128)(2,1)}, u32[]{:S(2)}, u32[]{:S(2)}) async-start(bf16[256,8,768]{0,2,1:T(8,128)(2,1)} %bitcast.125), calls=%async_computation.3 | async-start | bytes 6291456 | tf_op jit(solution)/shard_map/all_to_all | solution.py:42
  226.5 55.3 %all-to-all-start.3 = ((bf16[256,8,768]{0,2,1:T(8,128)(2,1)}), bf16[256,8,768]{0,2,1:T(8,128)(2,1)}, u32[]{:S(2)}, u32[]{:S(2)}) async-start(bf16[256,8,768]{0,2,1:T(8,128)(2,1)} %bitcast.124), calls=%async_computation.4 | async-start | bytes 6291456 | tf_op jit(solution)/shard_map/all_to_all | solution.py:42
  231.0 141.4 %reduce-scatter.16.cloned.1.call-start = ((), (), s32[]{:S(2)}) async-start(), calls=%async_computation.21 | async-start | bytes 4718592 | tf_op jit(solution)/shard_map/reduce_scatter | solution.py:36
  286.9 8.4 copy-start.6
  286.9 8.4 copy-start.23
  300.4 12.6 %copy-start.5 = (bf16[8,256,768]{2,1,0:T(8,128)(2,1)S(1)}, bf16[8,256,768]{2,1,0:T(8,128)(2,1)}, u32[]{:S(2)}) copy-start(bf16[8,256,768]{2,1,0:T(8,128)(2,1)} %copy.77) | copy-start | bytes 9437188
  313.0 3.5 copy-start.27
  313.0 3.5 copy-start.7
  321.7 50.8 %copy-start.1 = (bf16[128,2048]{1,0:T(8,128)(2,1)S(1)}, bf16[128,2048]{1,0:T(8,128)(2,1)}, u32[]{:S(2)}) copy-start(bf16[128,2048]{1,0:T(8,128)(2,1)} %reduce-scatter.12.cloned.1.call-done) | copy-start | bytes 1572868
  321.7 52.3 %copy-start.2 = (bf16[1,128,2048]{2,1,0:T(8,128)(2,1)S(1)}, bf16[1,128,2048]{2,1,0:T(8,128)(2,1)}, u32[]{:S(2)}) copy-start(bf16[1,128,2048]{2,1,0:T(8,128)(2,1)} %param.20) | copy-start | bytes 1572868
  321.7 91.4 %all-gather.15.cloned.1.call-start = ((), (), s32[]{:S(2)}) async-start(), calls=%async_computation.22 | async-start | bytes 4718592 | tf_op jit(solution)/shard_map/all_gather | solution.py:32
  376.3 100.0 %reduce-scatter.24.cloned.1.call-start = ((), (), s32[]{:S(2)}) async-start(), calls=%async_computation.28 | async-start | bytes 3932160 | tf_op jit(solution)/shard_map/reduce_scatter | solution.py:56
  384.1 155.4 %reduce-scatter.26.cloned.1.call-start = ((), (), s32[]{:S(2)}) async-start(), calls=%async_computation.30 | async-start | bytes 3932160 | tf_op jit(solution)/shard_map/reduce_scatter | solution.py:56
  393.4 184.4 %reduce-scatter.20.cloned.1.call-start = ((), (), s32[]{:S(2)}) async-start(), calls=%async_computation.24 | async-start | bytes 1966080 | tf_op jit(solution)/shard_map/reduce_scatter | solution.py:56
  413.1 29.9 %copy-start.22 = (bf16[1024,2048]{1,0:T(8,128)(2,1)S(1)}, bf16[1024,2048]{1,0:T(8,128)(2,1)}, u32[]{:S(2)}) copy-start(bf16[1024,2048]{1,0:T(8,128)(2,1)} %all-gather.11.cloned.1.call-done.n_ref) | copy-start | bytes 12582916
  450.0 164.8 %reduce-scatter.22.cloned.1.call-start = ((), (), s32[]{:S(2)}) async-start(), calls=%async_computation.26 | async-start | bytes 1966080 | tf_op jit(solution)/shard_map/reduce_scatter | solution.py:56
  458.2 221.1 %all-gather.21.cloned.1.call-start = ((), (), s32[]{:S(2)}) async-start(), calls=%async_computation.29 | async-start | bytes 3932160 | tf_op jit(solution)/shard_map/all_gather | solution.py:58
  492.5 64.2 %copy-start.24 = (bf16[1024,768]{1,0:T(8,128)(2,1)S(1)}, bf16[1024,768]{1,0:T(8,128)(2,1)}, u32[]{:S(2)}) copy-start(bf16[1024,768]{1,0:T(8,128)(2,1)} %get-tuple-element.68) | copy-start | bytes 4718596
  493.5 250.1 %all-gather.23.cloned.1.call-start = ((), (), s32[]{:S(2)}) async-start(), calls=%async_computation.31 | async-start | bytes 3932160 | tf_op jit(solution)/shard_map/all_gather | solution.py:58
  556.6 364.9 %all-reduce.7.cloned.1.call-start = ((), (), s32[]{:S(2)}) async-start(), calls=%async_computation.34 | async-start | bytes 9568256 | tf_op jit(solution)/shard_map/psum | solution.py:434
  556.7 7.2 copy-start.11
  556.7 7.9 copy-start.10
  556.7 8.6 copy-start.4
  556.7 8.6 copy-start.26
  568.0 387.3 %all-gather.17.cloned.1.call-start = ((), (), s32[]{:S(2)}) async-start(), calls=%async_computation.25 | async-start | bytes 1638400 | tf_op jit(solution)/shard_map/all_gather | solution.py:58
  591.0 398.1 %all-gather.19.cloned.1.call-start = ((), (), s32[]{:S(2)}) async-start(), calls=%async_computation.27 | async-start | bytes 1638400 | tf_op jit(solution)/shard_map/all_gather | solution.py:58
  628.2 414.8 %reduce-scatter.18.cloned.1.call-start = ((), (), s32[]{:S(2)}) async-start(), calls=%async_computation.23 | async-start | bytes 4718592 | tf_op jit(solution)/shard_map/reduce_scatter | solution.py:36
  628.8 468.8 %reduce-scatter.14.cloned.1.call-start = ((), (), s32[]{:S(2)}) async-start(), calls=%async_computation.20 | async-start | bytes 4718592 | tf_op jit(solution)/shard_map/reduce_scatter | solution.py:36
  637.4 499.6 %reduce-scatter.28.cloned.1.call-start = ((), (), s32[]{:S(2)}) async-start(), calls=%async_computation.33 | async-start | bytes 1179648
  684.7 64.2 %copy-start.14 = (f32[4,320]{1,0:T(4,128)S(1)}, f32[4,320]{1,0:T(4,128)}, u32[]{:S(2)}) copy-start(f32[4,320]{1,0:T(4,128)} %get-tuple-element.45) | copy-start | bytes 15364
  684.7 64.2 %copy-start.16 = (f32[4,320]{1,0:T(4,128)S(1)}, f32[4,320]{1,0:T(4,128)}, u32[]{:S(2)}) copy-start(f32[4,320]{1,0:T(4,128)} %get-tuple-element.44) | copy-start | bytes 15364
  921.6 5.6 copy-start.9
  927.1 2.6 copy-start.12
  958.4 139.2 %copy-start.3 = (bf16[128,2048]{1,0:T(8,128)(2,1)S(1)}, bf16[128,2048]{1,0:T(8,128)(2,1)}, u32[]{:S(2)}) copy-start(bf16[128,2048]{1,0:T(8,128)(2,1)} %reduce-scatter.16.cloned.1.call-done) | copy-start | bytes 1572868
  1043.0 54.5 %copy-start.8 = (bf16[128,2048]{1,0:T(8,128)(2,1)S(1)}, bf16[128,2048]{1,0:T(8,128)(2,1)}, u32[]{:S(2)}) copy-start(bf16[128,2048]{1,0:T(8,128)(2,1)} %reduce-scatter.18.cloned.1.call-done) | copy-start | bytes 1572868
  (3 other events, 4.8 us)
Sparse Core Ops, SparseCore 0:
  22.4 48.7 all-gather.10
  110.6 50.5 reduce-scatter.11
  164.7 59.2 all-gather.12
  225.9 61.4 all-gather.24
  321.8 50.5 reduce-scatter.15
  376.4 36.6 all-gather.14
  416.0 60.2 reduce-scatter.23
  479.2 60.2 reduce-scatter.25
  542.4 35.3 reduce-scatter.19
  580.4 34.2 reduce-scatter.21
  616.9 62.4 all-gather.20
  681.4 62.1 all-gather.22
  747.9 173.6 all-reduce.6
  923.7 31.5 all-gather.16
  957.4 31.6 all-gather.18
  992.7 50.3 reduce-scatter.17
  1046.2 51.2 reduce-scatter.13
  1100.9 36.0 reduce-scatter.27

commit v3 on v2

--- a/solution.py
+++ b/solution.py
@@ -14,6 +14,8 @@
 f32 = jnp.float32
 bf16 = jnp.bfloat16
 VM = pl.BlockSpec(memory_space=pltpu.VMEM)
+ANY = pl.BlockSpec(memory_space=pl.ANY)
+MESH = pl.DeviceIdType.MESH
 
 
 def mm(left, right):
@@ -42,20 +44,14 @@
     return lax.all_to_all(weight.astype(bf16), GROUP, split_axis=1, concat_axis=0, tiled=True)
 
 
-def reduce_rows(grad):
-    return lax.psum(grad.astype(bf16), "replica").astype(f32)
-
-
-def reduce_columns(grad):
+def swap_columns(grad):
     owners = lax.axis_size(GROUP)
-    copies = lax.axis_size("replica")
-    depth, width = grad.shape
-    piece = depth // (owners * copies)
-    cut = grad.astype(bf16).reshape(owners, copies, piece, width)
-    cut = jnp.swapaxes(cut, 0, 1).reshape(depth, width)
-    cut = lax.psum_scatter(cut, "replica", scatter_dimension=0, tiled=True)
-    cut = lax.all_to_all(cut, GROUP, split_axis=0, concat_axis=1, tiled=True)
-    return lax.all_gather(cut, "replica", axis=0, tiled=True).astype(f32)
+    cut = grad.astype(bf16).reshape(owners, grad.shape[0] // owners, grad.shape[1])
+    return lax.all_to_all(cut, GROUP, split_axis=0, concat_axis=0, tiled=True)
+
+
+def side_by_side(cut):
+    return jnp.swapaxes(cut, 0, 1).reshape(1, cut.shape[1], -1)
 
 
 def norm_backward(grad_unit, unit, inverse):
@@ -333,6 +329,195 @@
     )(mid_low, ow, wb, wi, pre, conv_in, values, recur, inject, decay, states, mask, conv, bias, rw, iw)
 
 
+def pieces(rows, most):
+    count = -(-rows // most)
+    while rows % count or (rows // count) % 16:
+        count += 1
+    return count
+
+
+def line_kernel(n, cuts, paired, *refs):
+    ins = len(cuts)
+    own_hbm = refs[:ins]
+    outs = refs[ins : ins + ins + 1]
+    scratch = refs[ins + ins + 1 :]
+    own, from_out, from_in = scratch[:ins], scratch[ins : 2 * ins], scratch[2 * ins : 3 * ins]
+    stage, load_sem, stage_sem, sent_in, sent_out, got_out, got_in = scratch[3 * ins :]
+    me = lax.axis_index("replica")
+    left = me < n // 2
+    inward = jnp.where(left, me + 1, me - 1)
+    outward = jnp.where(left, me - 1, me + 1)
+    has_out = jnp.logical_and(me > 0, me < n - 1)
+    middle = jnp.logical_or(me == n // 2 - 1, me == n // 2)
+
+    loads = [pltpu.make_async_copy(own_hbm[k], own[k], load_sem.at[k]) for k in range(ins)]
+    for load in loads:
+        load.start()
+    barrier = pltpu.get_barrier_semaphore()
+    pl.semaphore_signal(barrier, inc=1, device_id={"replica": inward}, device_id_type=MESH)
+
+    @pl.when(has_out)
+    def _():
+        pl.semaphore_signal(barrier, inc=1, device_id={"replica": outward}, device_id_type=MESH)
+        pl.semaphore_wait(barrier, 2)
+
+    @pl.when(jnp.logical_not(has_out))
+    def _():
+        pl.semaphore_wait(barrier, 1)
+
+    chunks = []
+    for k, (lead, count, rows) in enumerate(cuts):
+        for j in range(lead):
+            for i in range(count):
+                chunks.append((k, j, i * rows, rows))
+    slots = stage.shape[0]
+    ready = set()
+
+    def view(group, c):
+        k, j, start, rows = chunks[c]
+        return group[k].at[j, pl.ds(start, rows), :]
+
+    def push(group, target, c, sent, got, device):
+        return pltpu.make_async_remote_copy(
+            src_ref=view(group, c),
+            dst_ref=view(target, c),
+            send_sem=sent.at[c],
+            recv_sem=got.at[c],
+            device_id={"replica": device},
+            device_id_type=MESH,
+        )
+
+    def add(target, other, c):
+        k, j, start, rows = chunks[c]
+
+        def tile(i, _):
+            here = pl.ds(pl.multiple_of(start + i * 16, 16), 16)
+            total = target[k][j, here, :].astype(f32) + other[k][j, here, :].astype(f32)
+            target[k][j, here, :] = total.astype(bf16)
+            return 0
+
+        lax.fori_loop(0, rows // 16, tile, 0)
+
+    def gather_in(c):
+        k = chunks[c][0]
+        if k not in ready:
+            loads[k].wait()
+            ready.add(k)
+
+        @pl.when(has_out)
+        def _():
+            push(from_out, from_out, c, sent_in, got_out, inward).wait_recv()
+            add(own, from_out, c)
+
+        @pl.when(middle)
+        def _():
+            push(own, from_in, c, sent_in, got_in, inward).start()
+
+        @pl.when(jnp.logical_not(middle))
+        def _():
+            push(own, from_out, c, sent_in, got_out, inward).start()
+
+    def stage_copies(c):
+        k, j, start, rows = chunks[c]
+        slot = c % slots
+        columns = own[k].shape[2]
+        if k == paired:
+            half = columns // 2
+            return [
+                pltpu.make_async_copy(
+                    stage.at[slot, pl.ds(0, rows), pl.ds(side * half, half)],
+                    outs[k + side].at[pl.ds(start, rows), pl.ds(j * half, half)],
+                    stage_sem.at[slot, side],
+                )
+                for side in range(2)
+            ]
+        where = k if k < paired else k + 1
+        return [
+            pltpu.make_async_copy(
+                stage.at[slot, pl.ds(0, rows), pl.ds(0, columns)],
+                outs[where].at[pl.ds(start, rows), :],
+                stage_sem.at[slot, 0],
+            )
+        ]
+
+    def give_back(c):
+        k, j, start, rows = chunks[c]
+        push(own, from_in, c, sent_out, got_in, inward).wait_recv()
+
+        @pl.when(middle)
+        def _():
+            add(from_in, own, c)
+
+        @pl.when(has_out)
+        def _():
+            push(from_in, from_in, c, sent_out, got_in, outward).start()
+
+        if c >= slots:
+            for copy in stage_copies(c - slots):
+                copy.wait()
+        slot = c % slots
+        columns = own[k].shape[2]
+
+        def tile(i, _):
+            step = pl.multiple_of(i * 16, 16)
+            stage[slot, pl.ds(step, 16), 0:columns] = from_in[k][
+                j, pl.ds(pl.multiple_of(start + step, 16), 16), :
+            ].astype(f32)
+            return 0
+
+        lax.fori_loop(0, rows // 16, tile, 0)
+        for copy in stage_copies(c):
+            copy.start()
+
+    lag = 2
+    for c in range(len(chunks) + lag):
+        if c < len(chunks):
+            gather_in(c)
+        if c >= lag:
+            give_back(c - lag)
+    for c in range(max(0, len(chunks) - slots), len(chunks)):
+        for copy in stage_copies(c):
+            copy.wait()
+    for c in range(len(chunks)):
+        push(own, from_in, c, sent_in, got_in, inward).wait_send()
+
+        @pl.when(has_out)
+        def _():
+            push(from_in, from_in, c, sent_out, got_in, outward).wait_send()
+
+
+def replica_sum(arrays, paired, copies):
+    cuts, outs = [], []
+    stage_rows = stage_columns = 0
+    for k, item in enumerate(arrays):
+        lead, rows, columns = item.shape
+        count = pieces(rows, max(16, (210 * 1024) // columns // 16 * 16))
+        cuts.append((lead, count, rows // count))
+        stage_rows, stage_columns = max(stage_rows, rows // count), max(stage_columns, columns)
+        if k == paired:
+            outs += [jax.ShapeDtypeStruct((rows, lead * columns // 2), f32)] * 2
+        else:
+            outs.append(jax.ShapeDtypeStruct((rows, columns), f32))
+    count = sum(lead * cut for lead, cut, _ in cuts)
+    buffers = [pltpu.VMEM(item.shape, bf16) for item in arrays]
+    return pl.pallas_call(
+        functools.partial(line_kernel, copies, tuple(cuts), paired),
+        out_shape=tuple(outs),
+        in_specs=[ANY] * len(arrays),
+        out_specs=[ANY] * len(outs),
+        scratch_shapes=buffers * 3
+        + [
+            pltpu.VMEM((3, stage_rows, stage_columns), f32),
+            pltpu.SemaphoreType.DMA((len(arrays),)),
+            pltpu.SemaphoreType.DMA((3, 2)),
+        ]
+        + [pltpu.SemaphoreType.DMA((count,))] * 4,
+        compiler_params=pltpu.CompilerParams(
+            collective_id=7, has_side_effects=True, vmem_limit_bytes=60 * 2**20
+        ),
+    )(*arrays)
+
+
 def body(
     tokens,
     segments,
@@ -399,14 +584,12 @@
     hidden_grad = mm_nt(out_low, down_w)
     gate_low = gate_pull(hidden_grad * up_pre)[0].astype(bf16)
     up_low = (hidden_grad * gate_act).astype(bf16)
-    down_weight_grad = reduce_rows(mm_tn(hidden, out_low))
-    gate_weight_grad = reduce_columns(mm_tn(normed_two, gate_low))
-    up_weight_grad = reduce_columns(mm_tn(normed_two, up_low))
+    down_partial = mm_tn(hidden, out_low).astype(bf16)[None]
+    pair_partial = swap_columns(mm_tn(normed_two, jnp.concatenate([gate_low, up_low], 1)))
     two_grad = scatter_rows(mm_nt(gate_low, gate_w) + mm_nt(up_low, up_w))
-    mlp_gain_grad = jnp.sum(two_grad * unit_two, axis=0)
     middle_grad = grad_out + norm_backward(two_grad * mlp_gain_f, unit_two, inverse_two)
     mid_low = gather_rows(middle_grad.astype(bf16))
-    output_weight_grad = reduce_rows(mm_tn(product, mid_low))
+    output_partial = mm_tn(product, mid_low).astype(bf16)[None]
     back = mix_backward(
         sequences, mid_low, output_w, branch_w, input_w, *mixed[2:], mask, conv_f, bias, recur_gate_weight, input_gate_weight
     )
@@ -414,15 +597,21 @@
     conv_bias_grad, recur_bias_grad, inject_bias_grad = sums[0], sums[1], sums[2]
     decay_param_grad = sums[3] * decay_scale * jax.nn.sigmoid(-decay_f)
     normed_grad = scatter_rows(partial)
-    gain_grad = jnp.sum(normed_grad * unit, axis=0)
     tokens_grad = (middle_grad + norm_backward(normed_grad * gain_f, unit, inverse)).astype(bf16)
-    branch_weight_grad = reduce_columns(mm_tn(normed_all, branch_low))
-    input_weight_grad = reduce_columns(mm_tn(normed_all, conv_low))
-    gain_pair = lax.psum_scatter(
-        jnp.stack([gain_grad, mlp_gain_grad]), GROUP, scatter_dimension=1, tiled=True
+    branch_partial = side_by_side(swap_columns(mm_tn(normed_all, branch_low)))
+    input_partial = side_by_side(swap_columns(mm_tn(normed_all, conv_low)))
+    down_weight_grad, gate_weight_grad, up_weight_grad, output_weight_grad, branch_weight_grad, input_weight_grad = (
+        replica_sum(
+            [down_partial, pair_partial, output_partial, branch_partial, input_partial], 1, lax.axis_size("replica")
+        )
+    )
+    gain_grad = (
+        jnp.sum(branch_weight_grad * low(branch_weight) + input_weight_grad * low(input_weight), axis=1) / low(norm_gain)
+    )
+    mlp_gain_grad = (
+        jnp.sum(gate_weight_grad * low(gate_weight) + up_weight_grad * low(up_weight), axis=1) / low(mlp_norm_gain)
     )
     small = (
-        gain_pair,
         conv_weight_grad,
         conv_bias_grad,
         recur_weight_grad,
@@ -436,18 +625,18 @@
     return (
         block_out[None],
         tokens_grad[None],
-        small[0][0],
+        gain_grad,
         branch_weight_grad,
         input_weight_grad,
+        small[0],
         small[1],
         small[2],
         small[3],
         small[4],
         small[5],
         small[6],
-        small[7],
         output_weight_grad,
-        small[0][1],
+        mlp_gain_grad,
         gate_weight_grad,
         up_weight_grad,
         down_weight_grad,

time: 1170 us -> 1220 us (1.043)
  Pallas kernels: 53.4 us -> 625 us
  waiting for transfers between devices: 792 us -> 311 us
  blocking collectives: 109 us -> 53.9 us
  starting transfers between devices: 17.6 us -> 30.6 us
  local copies, waits for them, and re-layouts: 50.4 us -> 37.7 us
    pallas_call x0 -> x1, Pallas kernels: none -> 572 us  [replica_sum(): pl.pallas_call(functools.partial(line_kernel, copies, tuple(cuts), paired...]
    psum x1, waiting for transfers between devices: 173 us -> 0.01 us  [body(): small = lax.psum(tuple((item.astype(bf16) for item in small)), 'replica')]
    all_gather x4 -> x0, waiting for transfers between devices: 156 us -> none  [reduce_columns(): return lax.all_gather(cut, 'replica', axis=0, tiled=True).astype(f32)]
    reduce_scatter x4, waiting for transfers between devices: 204 us -> 102 us  [scatter_rows(): lax.psum_scatter(partial.astype(bf16), ROWS, scatter_dimension=0, tiled=T...]
    reduce_scatter x4 -> x0, waiting for transfers between devices: 97.4 us -> none  [reduce_columns(): cut = lax.psum_scatter(cut, 'replica', scatter_dimension=0, tiled=True)]
    all_to_all x0 -> x3, waiting for transfers between devices: none -> 64.3 us  [swap_columns(): return lax.all_to_all(cut, GROUP, split_axis=0, concat_axis=0, tiled=True)]
    all_to_all x4 -> x0, blocking collectives: 56.7 us -> none  [reduce_columns(): cut = lax.all_to_all(cut, GROUP, split_axis=0, concat_axis=1, tiled=True)]
    unnamed x19 -> x9, waiting for transfers between devices: 37.9 us -> 1.33 us
  transfers between devices with their start and end apart: 22 -> 16, of which waited for: 18 -> 9; matrix products, arithmetic and copies ran while one was open for 11% -> 9% of each run, Pallas kernels for 3% -> 47%
where the time goes in v3:
time: 1220 us; the launch traced here: 1210 us
  Pallas kernels  625 us (51%)
  waiting for transfers between devices  311 us (25%)
  matrix products  83.6 us (7%)
  other arithmetic  56.2 us (5%)
  blocking collectives  53.9 us (4%)
  local copies, waits for them, and re-layouts  37.7 us (3%)
  starting transfers between devices  30.6 us (3%)
  between operations  14.7 us (1%)
    pallas_call x1, Pallas kernels, replica_sum(): pl.pallas_call(functools.partial(line_kernel, copies, tuple(cuts), paired...  572 us
    all_to_all x4, waiting for transfers between devices, to_columns(): lax.all_to_all(weight.astype(bf16), GROUP, split_axis=1, concat_axis=0, t...  107 us
    reduce_scatter x4, waiting for transfers between devices, scatter_rows(): lax.psum_scatter(partial.astype(bf16), ROWS, scatter_dimension=0, tiled=T...  102 us
    all_to_all x3, waiting for transfers between devices, swap_columns(): return lax.all_to_all(cut, GROUP, split_axis=0, concat_axis=0, tiled=True)  64.3 us
    all_gather x4, waiting for transfers between devices, gather_rows(): return lax.all_gather(part, ROWS, axis=0, tiled=True)  36.8 us
    dot_general x5, matrix products, mm_tn(): lax.dot_general(left, right, (((0,), (0,)), ((), ())), preferred_element_...  31.9 us
    all_gather x1, blocking collectives, gather_rows(): return lax.all_gather(part, ROWS, axis=0, tiled=True)  31.3 us
    pallas_call x1, Pallas kernels, mix_backward(): pl.pallas_call(functools.partial(mix_backward_kernel, sequences, length),...  29.5 us
  transfers between devices with their start and end apart: 16, of which 9 were waited for; matrix products, arithmetic and copies ran while one was open for 9% of the time, Pallas kernels for 47%

profile of v3, /device:TPU:0, one launch (start us, length us, event | category | flops | bytes accessed | tf_op | source)
XLA Modules:
  0.0 1212.7 jit_solution(13547231886319841119)
XLA Ops:
  9.9 10.4 all_gather.18
  22.3 2.9 convert_element_type.189
  25.2 2.6 copy.52
  27.8 4.3 all-to-all-start
  33.3 2.5 copy.54
  35.8 17.9 %all-to-all-done = bf16[256,8,320]{0,2,1:T(8,128)(2,1)} async-done(((bf16[256,8,320]{0,2,1:T(8,128)(2,1)}), bf16[256,8,320]{0,2,1:T(8,128)(2,1)}, u32[]{:S(2)}, u32[]{:S(2)}) %all-to-all-start) | async-done | bytes 1310752 | tf_op jit(solution)/shard_map/all_to_all | solution.py:44
  53.7 3.7 all-to-all-start.1
  57.5 31.3 %all-gather.1 = s32[8,1,128]{2,1,0:T(1,128)S(1)} all-gather(s32[1,1,128]{2,1,0:T(1,128)S(1)} %bitcast.144), channel_id=1, replica_groups=mesh['seq'=2,'shard'=4,'replica'=4] {'shard','seq'}, dimensions={0}, use_global_device_ids=true | all-gather | bytes 4608 | tf_op jit(solution)/shard_map/all_gather | solution.py:34
  90.2 3.1 convert_element_type.199.ow_ref
  93.9 2.5 copy.53
  98.0 23.5 %shard_map.305 = (bf16[1024,2048]{1,0:T(8,128)(2,1)}, bf16[1024,320]{1,0:T(8,128)(2,1)}, f32[1024,320]{1,0:T(8,128)}, bf16[1024,320]{1,0:T(8,128)(2,1)}, bf16[10...) custom-call(bf16[1024,2048]{1,0:T(8,128)(2,1)} %all-gather.7.cloned., ...), custom_call_target="tpu_custom_call" | custom-call | flops 4026531840 | bytes 20971520 | tf_op jit(solution)/shard_map/pallas_call | solution.py:208
  121.5 51.4 %reduce-scatter.5.cloned.1.call-done = bf16[128,2048]{1,0:T(8,128)(2,1)} async-done(((bf16[1024,2048]{1,0:T(8,128)(2,1)}), bf16[128,2048]{1,0:T(8,128)(2,1)}) %reduce-scatter.5.cloned.1.call-update) | async-done | bytes 524304 | tf_op jit(solution)/shard_map/reduce_scatter | solution.py:38
  176.9 3.2 convert_element_type.203
  182.0 4.5 all-to-all-start.3
  186.4 3.2 convert_element_type.202
  191.5 46.7 %all-to-all-done.3 = bf16[256,8,768]{2,0,1:T(8,128)(2,1)} async-done(((bf16[256,8,768]{2,0,1:T(8,128)(2,1)}), bf16[256,8,768]{2,0,1:T(8,128)(2,1)}, u32[]{:S(2)}, u32[]{:S(2)}) %all-to-all-start.3) | async-done | bytes 3145760 | tf_op jit(solution)/shard_map/all_to_all | solution.py:44
  238.3 4.5 all-to-all-start.2
  243.3 8.3 fusion.54
  251.6 42.0 %all-to-all-done.2 = bf16[256,8,768]{2,0,1:T(8,128)(2,1)} async-done(((bf16[256,8,768]{2,0,1:T(8,128)(2,1)}), bf16[256,8,768]{2,0,1:T(8,128)(2,1)}, u32[]{:S(2)}, u32[]{:S(2)}) %all-to-all-start.2) | async-done | bytes 3145760 | tf_op jit(solution)/shard_map/all_to_all | solution.py:44
  293.6 8.4 fusion.53
  301.9 12.5 %multiply_convert_fusion = (bf16[1024,768]{0,1:T(8,128)(2,1)S(1)}, bf16[1024,768]{0,1:T(8,128)(2,1)S(1)}, bf16[1024,768]{0,1:T(8,128)(2,1)}) fusion(f32[1024,768]{0,1:T(8,128)} %fusion.53, f32[1024,768]{0,1:T(8,128)} %fusion.54, f32[768,2048]{1,0:T(8,128)} %param.35, bf16[1,1024,2048]{2,1,0:T(8,128)(2,1)} %all-gather.13.cloned.1.call-done), kind=kOutput, calls=%fused_computation.23 | convolution fusion | flops 3243245568 | bytes 21495808 | tf_op jit(solution)/shard_map/dot_general | solution.py:26
  314.5 6.7 fusion.55
  321.2 7.1 add_convert_fusion
  328.3 50.7 %reduce-scatter.9.cloned.1.call-done = bf16[128,2048]{1,0:T(8,128)(2,1)} async-done(((bf16[1024,2048]{1,0:T(8,128)(2,1)}), bf16[128,2048]{1,0:T(8,128)(2,1)}) %reduce-scatter.9.cloned.1.call-update) | async-done | bytes 524304 | tf_op jit(solution)/shard_map/reduce_scatter | solution.py:38
  380.5 2.3 fusion.51
  382.8 36.8 %all-gather.11.cloned.1.call-done.mid_ref = bf16[1024,2048]{1,0:T(8,128)(2,1)} async-done(((bf16[128,2048]{1,0:T(8,128)(2,1)}), bf16[1024,2048]{1,0:T(8,128)(2,1)}) %all-gather.11.cloned.1.call-update) | async-done | bytes 4194320 | tf_op jit(solution)/shard_map/all_gather | solution.py:34
  419.6 29.5 %shard_map.306 = (bf16[1024,2048]{1,0:T(8,128)(2,1)}, bf16[1024,320]{1,0:T(8,128)(2,1)}, bf16[1024,320]{1,0:T(8,128)(2,1)}, f32[4,320]{1,0:T(4,128)}, f32[4,320]...) custom-call(bf16[1024,2048]{1,0:T(8,128)(2,1)} %all-gather.11.cloned.1.call-done.mid_ref, ...), custom_call_target="tpu_custom_call" | custom-call | flops 4026531840 | bytes 26214400 | tf_op jit(solution)/shard_map/pallas_call | solution.py:311
  453.2 4.0 convolution_convert_fusion.3
  458.3 3.8 all-to-all-start.5
  462.1 4.0 convolution_convert_fusion.2
  467.2 13.0 %all-to-all-done.5 = bf16[8,256,320]{1,2,0:T(8,128)(2,1)S(1)} async-done(((bf16[8,256,320]{1,2,0:T(8,128)(2,1)}), bf16[8,256,320]{1,2,0:T(8,128)(2,1)S(1)}, u32[]{:S(2)}, u32[]{:S(2)}) %all-to-all-start.5) | async-done | bytes 1310752 | tf_op jit(solution)/shard_map/all_to_all | solution.py:50
  480.2 4.3 all-to-all-start.6
  484.5 11.2 convolution_convert_fusion
  495.7 7.1 all-to-all-done.6
  502.8 4.8 all-to-all-start.4
  507.6 8.8 convolution_convert_fusion.1
  516.4 7.7 fusion.17.refs_0_
  524.3 12.2 %all-reduce.3 = (bf16[4,320]{1,0:T(4,128)(2,1)S(1)}, bf16[320]{0:T(512)(128)(2,1)S(1)}, bf16[320]{0:T(512)(128)(2,1)S(1)}, bf16[320]{0:T(512)(128)(2,1)S(1)}, bf16[320]{0:T(512)(128)(2,1)S(1)}) all-reduce(bf16[4,320]{1,0:T(4,128)(2,1)S(1)} %convert_element_type.225, ...), channel_id=1, replica_groups=mesh['seq'=2,'shard'=4,'replica'=4] {'replica'}, use_global_device_ids=true, to_apply=%region_9.10 | all-reduce | flops 2560 | bytes 10240 | tf_op jit(solution)/shard_map/psum | solution.py:623
  539.4 5.0 fusion.20.refs_2_
  549.3 2.4 copy.62.refs_4_
  551.7 44.2 %all-to-all-done.4.refs_1_ = bf16[8,256,1536]{2,1,0:T(8,128)(2,1)} async-done(((bf16[8,256,1536]{2,1,0:T(8,128)(2,1)}), bf16[8,256,1536]{2,1,0:T(8,128)(2,1)}, u32[]{:S(2)}, u32[]{:S(2)}) %all-to-all-start.4) | async-done | bytes 6291488 | tf_op jit(solution)/shard_map/all_to_all | solution.py:50
  596.0 571.9 %shard_map.307 = (f32[768,2048]{1,0:T(8,128)}, f32[256,6144]{1,0:T(8,128)}, f32[256,6144]{1,0:T(8,128)}, f32[320,2048]{1,0:T(8,128)}, f32[256,2560]{1,0:T(8,128)}, /*index=5*/f32[256,2560]{1,0:T(8,128)}) custom-call(bf16[1,768,2048]{2,1,0:T(8,128)(2,1)} %fusion.17.refs_0_, bf16[8,256,1536]{2,1,0:T(8,128)(2,1)} %all-to-all-done.4.refs_1_, ...), custom_call_target="tpu_custom_call" | custom-call | tf_op jit(solution)/shard_map/pallas_call | solution.py:503
  1167.9 4.6 add_reduce_fusion.1
  1173.1 9.4 add_reduce_fusion
  1184.5 3.2 fusion.35
  1195.1 3.2 copy.89
  1198.4 3.2 copy.90
  1203.0 2.7 copy.91
  (141 shorter events, 45.1 us)
Async XLA Ops:
  7.2 90.8 %all-gather.7.cloned.1.call-start = ((), (), s32[]{:S(2)}) async-start(), calls=%async_computation.11 | async-start | bytes 4718592 | tf_op jit(solution)/shard_map/all_gather | solution.py:34
  25.2 6.9 copy-start.12
  25.2 6.9 copy-start.13
  25.2 6.9 copy-start.4
  27.8 25.9 %all-to-all-start = ((bf16[256,8,320]{0,2,1:T(8,128)(2,1)}), bf16[256,8,320]{0,2,1:T(8,128)(2,1)}, u32[]{:S(2)}, u32[]{:S(2)}) async-start(bf16[256,8,320]{0,2,1:T(8,128)(2,1)} %bitcast.129), calls=%async_computation | async-start | bytes 2621440 | tf_op jit(solution)/shard_map/all_to_all | solution.py:44
  33.3 24.1 %copy-start.14 = (f32[320]{0:T(512)S(1)}, f32[320]{0:T(512)}, u32[]{:S(2)}) copy-start(f32[320]{0:T(512)} %param.29) | copy-start | bytes 3844
  33.3 24.1 %copy-start.9 = (f32[320]{0:T(512)S(1)}, f32[320]{0:T(512)}, u32[]{:S(2)}) copy-start(f32[320]{0:T(512)} %param.30) | copy-start | bytes 3844
  33.3 24.2 %copy-start.17 = (s32[1,128]{1,0:T(1,128)S(1)}, s32[1,128]{1,0:T(1,128)}, u32[]{:S(2)}) copy-start(s32[1,128]{1,0:T(1,128)} %param.19) | copy-start | bytes 1540
  53.7 39.6 %copy-start.11 = (f32[4,320]{1,0:T(4,128)S(1)}, f32[4,320]{1,0:T(4,128)}, u32[]{:S(2)}) copy-start(f32[4,320]{1,0:T(4,128)} %param.24) | copy-start | bytes 15364
  53.7 42.8 %all-to-all-start.1 = ((bf16[256,8,320]{0,2,1:T(8,128)(2,1)}), bf16[256,8,320]{0,2,1:T(8,128)(2,1)S(1)}, u32[]{:S(2)}, u32[]{:S(2)}) async-start(bf16[256,8,320]{0,2,1:T(8,128)(2,1)} %bitcast.6), calls=%async_computation.1 | async-start | bytes 2621440 | tf_op jit(solution)/shard_map/all_to_all | solution.py:44
  57.4 115.5 %reduce-scatter.5.cloned.1.call-start = ((), (), s32[]{:S(2)}) async-start(), calls=%async_computation.12 | async-start | bytes 4718592 | tf_op jit(solution)/shard_map/reduce_scatter | solution.py:38
  121.5 51.4 %copy-start = (bf16[1,128,2048]{2,1,0:T(8,128)(2,1)S(1)}, bf16[1,128,2048]{2,1,0:T(8,128)(2,1)}, u32[]{:S(2)}) copy-start(bf16[1,128,2048]{2,1,0:T(8,128)(2,1)} %param.18) | copy-start | bytes 1572868
  121.5 121.8 %all-gather.9.cloned.1.call-start = ((), (), s32[]{:S(2)}) async-start(), calls=%async_computation.13 | async-start | bytes 4718592 | tf_op jit(solution)/shard_map/all_gather | solution.py:34
  176.3 125.6 %all-gather.13.cloned.1.call-start = ((), (), s32[]{:S(2)}) async-start(), calls=%async_computation.18 | async-start | bytes 4718592 | tf_op jit(solution)/shard_map/all_gather | solution.py:34
  182.0 56.3 %all-to-all-start.3 = ((bf16[256,8,768]{2,0,1:T(8,128)(2,1)}), bf16[256,8,768]{2,0,1:T(8,128)(2,1)}, u32[]{:S(2)}, u32[]{:S(2)}) async-start(bf16[256,8,768]{2,0,1:T(8,128)(2,1)} %bitcast.117), calls=%async_computation.4 | async-start | bytes 6291456 | tf_op jit(solution)/shard_map/all_to_all | solution.py:44
  238.3 55.3 %all-to-all-start.2 = ((bf16[256,8,768]{2,0,1:T(8,128)(2,1)}), bf16[256,8,768]{2,0,1:T(8,128)(2,1)}, u32[]{:S(2)}, u32[]{:S(2)}) async-start(bf16[256,8,768]{2,0,1:T(8,128)(2,1)} %bitcast.116), calls=%async_computation.3 | async-start | bytes 6291456 | tf_op jit(solution)/shard_map/all_to_all | solution.py:44
  242.7 136.3 %reduce-scatter.9.cloned.1.call-start = ((), (), s32[]{:S(2)}) async-start(), calls=%async_computation.15 | async-start | bytes 4718592 | tf_op jit(solution)/shard_map/reduce_scatter | solution.py:38
  314.5 6.7 copy-start.18
  314.5 6.7 copy-start.19
  328.2 50.8 %copy-start.1 = (bf16[128,2048]{1,0:T(8,128)(2,1)S(1)}, bf16[128,2048]{1,0:T(8,128)(2,1)}, u32[]{:S(2)}) copy-start(bf16[128,2048]{1,0:T(8,128)(2,1)} %reduce-scatter.5.cloned.1.call-done) | copy-start | bytes 1572868
  328.2 52.2 %copy-start.5 = (bf16[1,128,2048]{2,1,0:T(8,128)(2,1)S(1)}, bf16[1,128,2048]{2,1,0:T(8,128)(2,1)}, u32[]{:S(2)}) copy-start(bf16[1,128,2048]{2,1,0:T(8,128)(2,1)} %param.20) | copy-start | bytes 1572868
  328.3 91.3 %all-gather.11.cloned.1.call-start = ((), (), s32[]{:S(2)}) async-start(), calls=%async_computation.16 | async-start | bytes 4718592 | tf_op jit(solution)/shard_map/all_gather | solution.py:34
  382.8 161.7 %all-reduce.7.cloned.1.call-start = ((), (), s32[]{:S(2)}) async-start(), calls=%async_computation.19 | async-start | bytes 655360 | tf_op jit(solution)/shard_map/psum | solution.py:623
  452.4 730.6 %reduce-scatter.11.cloned.1.call-start = ((), (), s32[]{:S(2)}) async-start(), calls=%async_computation.17 | async-start | bytes 4718592 | tf_op jit(solution)/shard_map/reduce_scatter | solution.py:38
  458.3 21.9 %all-to-all-start.5 = ((bf16[8,256,320]{1,2,0:T(8,128)(2,1)}), bf16[8,256,320]{1,2,0:T(8,128)(2,1)S(1)}, u32[]{:S(2)}, u32[]{:S(2)}) async-start(bf16[8,256,320]{1,2,0:T(8,128)(2,1)} %bitcast.131), calls=%async_computation.9 | async-start | bytes 2621440 | tf_op jit(solution)/shard_map/all_to_all | solution.py:50
  480.2 22.5 %all-to-all-start.6 = ((bf16[8,256,320]{1,2,0:T(8,128)(2,1)}), bf16[8,256,320]{1,2,0:T(8,128)(2,1)}, u32[]{:S(2)}, u32[]{:S(2)}) async-start(bf16[8,256,320]{1,2,0:T(8,128)(2,1)} %bitcast.130), calls=%async_computation.10 | async-start | bytes 2621440 | tf_op jit(solution)/shard_map/all_to_all | solution.py:50
  502.8 93.2 %all-to-all-start.4 = ((bf16[8,256,1536]{2,1,0:T(8,128)(2,1)}), bf16[8,256,1536]{2,1,0:T(8,128)(2,1)}, u32[]{:S(2)}, u32[]{:S(2)}) async-start(bf16[8,256,1536]{2,1,0:T(8,128)(2,1)} %bitcast.120), calls=%async_computation.8 | async-start | bytes 12582912 | tf_op jit(solution)/shard_map/all_to_all | solution.py:50
  507.6 676.9 %reduce-scatter.7.cloned.1.call-start = ((), (), s32[]{:S(2)}) async-start(), calls=%async_computation.14 | async-start | bytes 4718592 | tf_op jit(solution)/shard_map/reduce_scatter | solution.py:38
  516.4 7.8 copy-start.8
  516.4 7.8 copy-start.10
  1167.9 4.6 copy-start.15
  1173.0 9.4 copy-start.16
  1173.1 11.4 copy-start.6
  1184.5 3.2 copy-start.3
  1187.6 2.7 copy-start.2
  1187.6 4.2 copy-start.7
  1187.7 6.6 slice-start.2
  1190.3 4.7 slice-start.3
  1191.8 6.4 slice-start
  1195.1 3.3 slice-start.1
  1195.1 6.5 slice-start.4
  1198.4 4.7 slice-start.5
Sparse Core Ops, SparseCore 0:
  22.4 58.1 all-gather.6
  121.6 51.2 reduce-scatter.4
  176.4 59.5 all-gather.8
  237.9 61.1 all-gather.12
  328.4 50.5 reduce-scatter.8
  382.9 36.6 all-gather.10
  452.6 36.3 all-reduce.6
  492.9 78.5 reduce-scatter.10
  575.9 65.0 reduce-scatter.6

commit v4 on v3

--- a/solution.py
+++ b/solution.py
@@ -30,18 +30,8 @@
     return lax.dot_general(left, right, (((0,), (0,)), ((), ())), preferred_element_type=f32)
 
 
-def gather_rows(part):
-    return lax.all_gather(part, ROWS, axis=0, tiled=True)
-
-
-def scatter_rows(partial):
-    return lax.psum_scatter(
-        partial.astype(bf16), ROWS, scatter_dimension=0, tiled=True
-    ).astype(f32)
-
-
-def to_columns(weight):
-    return lax.all_to_all(weight.astype(bf16), GROUP, split_axis=1, concat_axis=0, tiled=True)
+def low(item):
+    return item.astype(bf16).astype(f32)
 
 
 def swap_columns(grad):
@@ -54,16 +44,12 @@
     return jnp.swapaxes(cut, 0, 1).reshape(1, cut.shape[1], -1)
 
 
-def norm_backward(grad_unit, unit, inverse):
-    return inverse * (grad_unit - unit * jnp.mean(grad_unit * unit, axis=-1, keepdims=True))
-
-
-def token_masks(labels, taps):
-    length = labels.shape[1]
-    masks = [
-        (jnp.pad(labels, ((0, 0), (offset, 0)))[:, :length] == labels) for offset in range(taps)
-    ]
-    return jnp.stack(masks, -1).astype(f32).reshape(-1, taps)
+def to_columns(weights, gain):
+    owners = lax.axis_size(GROUP)
+    rows = weights[0].shape[0]
+    scaled = [(low(item) * gain).astype(bf16).reshape(rows, owners, -1) for item in weights]
+    cut = jnp.swapaxes(jnp.concatenate(scaled, 2), 0, 1)
+    return lax.all_to_all(cut, GROUP, split_axis=0, concat_axis=0, tiled=True).reshape(rows * owners, -1)
 
 
 def gelu_parts(x):
@@ -118,6 +104,17 @@
     tail = ref.shape[0] * 128 - width
     if tail:
         ref[ref.shape[0] - 1, :, 128 - tail :] = jnp.zeros((ref.shape[1], tail), f32)
+
+
+def label_masks(label_ref, here, length, width, taps, lines):
+    own = label_ref[here, :].astype(f32)
+    lines[0:8, :] = jnp.full((8, 128), -1.0, f32)
+    lines[8 : 8 + length, :] = own
+    masks = []
+    for k in range(1, taps):
+        same = jnp.where(lines[8 - k : 8 - k + length, :] == own, 1.0, 0.0)
+        masks.append(jnp.concatenate([same] * -(-width // 128), axis=1)[:, :width])
+    return masks
 
 
 def seq_scan(decay_ref, value_ref, sequences, length, reverse):
@@ -147,9 +144,9 @@
 
 
 def mix_forward_kernel(
-    sequences, length, n_ref, wb_ref, wi_ref, mask_ref, conv_ref, bias_ref, rw_ref, iw_ref, ow_ref,
+    sequences, length, n_ref, wb_ref, wi_ref, label_ref, conv_ref, bias_ref, rw_ref, iw_ref, ow_ref,
     partial_ref, product_ref, pre_ref, conv_in_ref, values_ref, recur_ref, inject_ref, decay_ref, states_ref,
-    pad, rbig, ibig,
+    pad, lines, rbig, ibig,
 ):
     fill_blocks(rbig, rw_ref)
     fill_blocks(ibig, iw_ref)
@@ -163,13 +160,14 @@
         base = pl.multiple_of(s * length, length)
         here = pl.ds(base, length)
         rows = n_ref[here, :]
+        masks = label_masks(label_ref, here, length, width, taps, lines)
         pre_ref[here, :] = dot_nn(rows, wb_ref[...])
         conv_in = dot_nn(rows, wi_ref[...]).astype(bf16)
         conv_in_ref[here, :] = conv_in
         pad[8 : 8 + length, :] = conv_in.astype(f32)
         total = bias_ref[0:1, :] + conv_ref[0:1, :] * pad[8 : 8 + length, :]
         for k in range(1, taps):
-            total = total + conv_ref[k : k + 1, :] * pad[8 - k : 8 - k + length, :] * mask_ref[here, k : k + 1]
+            total = total + conv_ref[k : k + 1, :] * pad[8 - k : 8 - k + length, :] * masks[k - 1]
         values = total.astype(bf16)
         values_ref[here, :] = values
         recur = jax.nn.sigmoid(dot_nn(values, rbig[...].astype(bf16)) + bias_ref[1:2, :])
@@ -177,7 +175,7 @@
         recur_ref[here, :] = recur
         inject_ref[here, :] = inject
         log_decay = -decay_scale * bias_ref[3:4, :] * recur
-        inside = mask_ref[here, 1:2] > 0.5
+        inside = masks[0] > 0.5
         put_tiles(decay_ref, here, jnp.where(inside, jnp.exp(log_decay), 0.0))
         scale = jnp.where(inside, jnp.sqrt(minus_expm1(2.0 * log_decay)), 1.0)
         put_tiles(states_ref, here, scale * inject * values.astype(f32))
@@ -198,7 +196,7 @@
     lax.fori_loop(0, sequences, two, 0)
 
 
-def mix_forward(sequences, normed, wb, wi, mask, conv, bias, rw, iw, ow):
+def mix_forward(sequences, normed, wb, wi, labels, conv, bias, rw, iw, ow):
     total, width = normed.shape[0], wb.shape[1]
     length = total // sequences
     depth = ow.shape[1]
@@ -214,19 +212,20 @@
         out_specs=[VM] * 9,
         scratch_shapes=[
             pltpu.VMEM((8 + length, width), f32),
+            pltpu.VMEM((8 + length, 128), f32),
             pltpu.VMEM((width, width), f32),
             pltpu.VMEM((width, width), f32),
         ],
         compiler_params=pltpu.CompilerParams(vmem_limit_bytes=56 * 2**20),
         cost_estimate=pl.CostEstimate(flops=2 * total * width * 3 * depth, bytes_accessed=20 * 2**20, transcendentals=total * width * 5),
-    )(normed, wb, wi, mask, conv, bias, rw, iw, ow)
+    )(normed, wb, wi, labels, conv, bias, rw, iw, ow)
 
 
 def mix_backward_kernel(
     sequences, length, mid_ref, ow_ref, wb_ref, wi_ref, pre_ref, conv_in_ref, values_ref, recur_ref, inject_ref, decay_ref, states_ref,
-    mask_ref, conv_ref, bias_ref, rw_ref, iw_ref,
+    label_ref, conv_ref, bias_ref, rw_ref, iw_ref,
     partial_ref, branch_low_ref, conv_low_ref, dconv_ref, sums_ref, drw_ref, diw_ref,
-    adj, pad, rbig, ibig, dr, di,
+    adj, pad, lines, rbig, ibig, dr, di,
 ):
     fill_blocks(rbig, rw_ref)
     fill_blocks(ibig, iw_ref)
@@ -259,7 +258,8 @@
         decay = get_tiles(decay_ref, here, width)
         values = values_ref[here, :]
         values_f = values.astype(f32)
-        inside = mask_ref[here, 1:2] > 0.5
+        masks = label_masks(label_ref, here, length, width, taps, lines)
+        inside = masks[0] > 0.5
         rate = bias_ref[3:4, :]
         log_decay = -decay_scale * rate * recur
         scale = jnp.where(inside, jnp.sqrt(minus_expm1(2.0 * log_decay)), 1.0)
@@ -282,7 +282,7 @@
         dconv_ref[0:1, :] += jnp.sum(grad * pad[8 : 8 + length, :], axis=0, keepdims=True)
         masked = []
         for k in range(1, taps):
-            part = grad * mask_ref[here, k : k + 1]
+            part = grad * masks[k - 1]
             masked.append(part)
             dconv_ref[k : k + 1, :] += jnp.sum(part * pad[8 - k : 8 - k + length, :], axis=0, keepdims=True)
         total = grad * conv_ref[0:1, :]
@@ -303,7 +303,7 @@
         diw_ref[h] = di[cut, cut]
 
 
-def mix_backward(sequences, mid_low, ow, wb, wi, pre, conv_in, values, recur, inject, decay, states, mask, conv, bias, rw, iw):
+def mix_backward(sequences, mid_low, ow, wb, wi, pre, conv_in, values, recur, inject, decay, states, labels, conv, bias, rw, iw):
     total, depth = mid_low.shape
     width = ow.shape[0]
     length = total // sequences
@@ -319,6 +319,7 @@
         scratch_shapes=[
             pltpu.VMEM(states.shape, f32),
             pltpu.VMEM((8 + length, width), f32),
+            pltpu.VMEM((8 + length, 128), f32),
             pltpu.VMEM((width, width), f32),
             pltpu.VMEM((width, width), f32),
             pltpu.VMEM((width, width), f32),
@@ -326,7 +327,228 @@
         ],
         compiler_params=pltpu.CompilerParams(vmem_limit_bytes=56 * 2**20),
         cost_estimate=pl.CostEstimate(flops=2 * total * width * 3 * depth, bytes_accessed=25 * 2**20, transcendentals=total * width * 5),
-    )(mid_low, ow, wb, wi, pre, conv_in, values, recur, inject, decay, states, mask, conv, bias, rw, iw)
+    )(mid_low, ow, wb, wi, pre, conv_in, values, recur, inject, decay, states, labels, conv, bias, rw, iw)
+
+
+def plane():
+    halves, shards = lax.axis_size("seq"), lax.axis_size("shard")
+    y, s = lax.axis_index("seq"), lax.axis_index("shard")
+    offsets = [(dy, ds) for ds in range(0, shards, 2) for dy in range(halves)]
+
+    def at(dy, ds):
+        return {"seq": jnp.bitwise_xor(y, dy), "shard": jnp.bitwise_xor(s, ds)}
+
+    def block(dy, ds):
+        return jnp.bitwise_xor(s, ds) * halves + jnp.bitwise_xor(y, dy)
+
+    return offsets, at, block
+
+
+def greet(offsets, at):
+    barrier = pltpu.get_barrier_semaphore()
+    partners = [(0, 1)] + offsets[1:]
+    for dy, ds in partners:
+        pl.semaphore_signal(barrier, inc=1, device_id=at(dy, ds), device_id_type=MESH)
+    pl.semaphore_wait(barrier, len(partners))
+
+
+def remote(src, dst, sent, got, device):
+    return pltpu.make_async_remote_copy(
+        src_ref=src, dst_ref=dst, send_sem=sent, recv_sem=got, device_id=device, device_id_type=MESH
+    )
+
+
+def row_block(ref, index, rows):
+    return ref.at[pl.ds(pl.multiple_of(index * rows, rows), rows), :]
+
+
+def scatter_sum(rows, partial, near, far, stage, acc, sems):
+    offsets, at, block = plane()
+    near_sent, near_got, far_sent, far_got = sems
+    count = len(offsets)
+    order = list(range(count - 1, -1, -1))
+    firsts = {}
+    for q in order:
+        dy, ds = offsets[q]
+        firsts[q] = remote(
+            row_block(partial, block(dy, ds ^ 1), rows), near.at[q], near_sent.at[q], near_got.at[q], at(0, 1)
+        )
+        firsts[q].start()
+    seconds = {}
+    for q in order:
+        dy, ds = offsets[q]
+        firsts[q].wait_recv()
+        base = block(dy, ds) * rows
+
+        def tile(i, _):
+            step = pl.multiple_of(i * 16, 16)
+            here = pl.ds(step, 16)
+            total = partial[pl.ds(pl.multiple_of(base + step, 16), 16), :].astype(f32) + near[q, here, :].astype(f32)
+            if q:
+                stage[q - 1, here, :] = total.astype(bf16)
+            else:
+                acc[here, :] = total
+            return 0
+
+        lax.fori_loop(0, rows // 16, tile, 0)
+        if q:
+            seconds[q] = remote(stage.at[q - 1], far.at[q - 1], far_sent.at[q - 1], far_got.at[q - 1], at(dy, ds))
+            seconds[q].start()
+    for q in order[:-1]:
+        seconds[q].wait_recv()
+
+        def more(i, _):
+            here = pl.ds(pl.multiple_of(i * 16, 16), 16)
+            acc[here, :] += far[q - 1, here, :].astype(f32)
+            return 0
+
+        lax.fori_loop(0, rows // 16, more, 0)
+    return [firsts[q].wait_send for q in order] + [seconds[q].wait_send for q in order[:-1]]
+
+
+def gather_blocks(rows, whole, sems):
+    offsets, at, block = plane()
+    near_sent, near_got, far_sent, far_got = sems
+    count = len(offsets)
+    own = row_block(whole, block(0, 0), rows)
+    sends = []
+    outs = {}
+    for q in range(count - 1, 0, -1):
+        dy, ds = offsets[q]
+        outs[q] = remote(own, own, far_sent.at[q - 1], far_got.at[q - 1], at(dy, ds))
+        outs[q].start()
+        sends.append(outs[q].wait_send)
+    hand = remote(own, own, near_sent.at[0], near_got.at[0], at(0, 1))
+    hand.start()
+    sends.append(hand.wait_send)
+    arrivals = [hand.wait_recv]
+    for q in list(range(1, count)):
+        dy, ds = offsets[q]
+        outs[q].wait_recv()
+        block_q = row_block(whole, block(dy, ds), rows)
+        hand = remote(block_q, block_q, near_sent.at[q], near_got.at[q], at(0, 1))
+        hand.start()
+        sends.append(hand.wait_send)
+        arrivals.append(hand.wait_recv)
+    return arrivals + sends
+
+
+def root_mean(rows):
+    return lax.rsqrt(jnp.mean(rows * rows, axis=-1, keepdims=True) + epsilon)
+
+
+def norm_backward(grad_unit, unit, inverse):
+    return inverse * (grad_unit - unit * jnp.mean(grad_unit * unit, axis=-1, keepdims=True))
+
+
+def by_tiles(rows, work):
+    def tile(i, _):
+        work(pl.ds(pl.multiple_of(i * 16, 16), 16), i)
+        return 0
+
+    lax.fori_loop(0, rows // 16, tile, 0)
+
+
+def start_kernel(x_ref, label_ref, unit_ref, labels_ref, *sems):
+    rows = x_ref.shape[0]
+    offsets, at, block = plane()
+    greet(offsets, at)
+    base = block(0, 0) * rows
+
+    def unit(here, i):
+        value = x_ref[here, :].astype(f32)
+        there = pl.ds(pl.multiple_of(base + i * 16, 16), 16)
+        unit_ref[there, :] = (value * root_mean(value)).astype(bf16)
+        labels_ref[there, :] = label_ref[here, :]
+
+    by_tiles(rows, unit)
+    waits = gather_blocks(rows, labels_ref, sems[4:])
+    waits = waits + gather_blocks(rows, unit_ref, sems[:4])
+    for wait in waits:
+        wait()
+
+
+def forward_kernel(partial, x_ref, unit_ref, middle_ref, near, far, stage, acc, *sems):
+    rows = x_ref.shape[0]
+    offsets, at, block = plane()
+    greet(offsets, at)
+    waits = scatter_sum(rows, partial, near, far, stage, acc, sems[:4])
+    base = block(0, 0) * rows
+
+    def norm(here, i):
+        middle = x_ref[here, :].astype(f32) + acc[here, :]
+        middle_ref[here, :] = middle
+        there = pl.ds(pl.multiple_of(base + i * 16, 16), 16)
+        unit_ref[there, :] = (middle * root_mean(middle)).astype(bf16)
+
+    by_tiles(rows, norm)
+    waits = waits + gather_blocks(rows, unit_ref, sems[4:])
+    for wait in waits:
+        wait()
+
+
+def backward_kernel(partial, middle_ref, cot_ref, low_ref, grad_ref, near, far, stage, acc, *sems):
+    rows = middle_ref.shape[0]
+    offsets, at, block = plane()
+    greet(offsets, at)
+    waits = scatter_sum(rows, partial, near, far, stage, acc, sems[:4])
+    base = block(0, 0) * rows
+
+    def norm(here, i):
+        middle = middle_ref[here, :]
+        inverse = root_mean(middle)
+        grad = cot_ref[here, :].astype(f32) + norm_backward(acc[here, :], middle * inverse, inverse)
+        grad_ref[here, :] = grad
+        there = pl.ds(pl.multiple_of(base + i * 16, 16), 16)
+        low_ref[there, :] = grad.astype(bf16)
+
+    by_tiles(rows, norm)
+    waits = waits + gather_blocks(rows, low_ref, sems[4:])
+    for wait in waits:
+        wait()
+
+
+def last_kernel(partial, grad_ref, x_ref, out_ref, near, far, stage, acc, *sems):
+    rows = x_ref.shape[0]
+    offsets, at, block = plane()
+    greet(offsets, at)
+    waits = scatter_sum(rows, partial, near, far, stage, acc, sems[:4])
+
+    def norm(here, i):
+        value = x_ref[here, :].astype(f32)
+        inverse = root_mean(value)
+        grad = grad_ref[here, :] + norm_backward(acc[here, :], value * inverse, inverse)
+        out_ref[here, :] = grad.astype(bf16)
+
+    by_tiles(rows, norm)
+    for wait in waits:
+        wait()
+
+
+def exchange(kernel, identity, inputs, outs, rows, depth, gathers, scatters):
+    count = lax.axis_size("seq") * lax.axis_size("shard") // 2
+    block = (rows, depth)
+    scratch = []
+    if scatters:
+        scratch = [
+            pltpu.VMEM((count,) + block, bf16),
+            pltpu.VMEM((count - 1,) + block, bf16),
+            pltpu.VMEM((count - 1,) + block, bf16),
+            pltpu.VMEM(block, f32),
+        ]
+    for _ in range(scatters + gathers):
+        scratch += [pltpu.SemaphoreType.DMA((count,))] * 2 + [pltpu.SemaphoreType.DMA((count - 1,))] * 2
+    return pl.pallas_call(
+        kernel,
+        out_shape=tuple(jax.ShapeDtypeStruct(shape, kind) for shape, kind in outs),
+        in_specs=[VM] * len(inputs),
+        out_specs=[VM] * len(outs),
+        scratch_shapes=scratch,
+        compiler_params=pltpu.CompilerParams(
+            collective_id=identity, has_side_effects=True, vmem_limit_bytes=40 * 2**20
+        ),
+        cost_estimate=pl.CostEstimate(flops=10**6, bytes_accessed=60 * 2**20, transcendentals=0),
+    )(*inputs)
 
 
 def pieces(rows, most):
@@ -398,17 +620,7 @@
 
         lax.fori_loop(0, rows // 16, tile, 0)
 
-    def gather_in(c):
-        k = chunks[c][0]
-        if k not in ready:
-            loads[k].wait()
-            ready.add(k)
-
-        @pl.when(has_out)
-        def _():
-            push(from_out, from_out, c, sent_in, got_out, inward).wait_recv()
-            add(own, from_out, c)
-
+    def pass_in(c):
         @pl.when(middle)
         def _():
             push(own, from_in, c, sent_in, got_in, inward).start()
@@ -416,6 +628,25 @@
         @pl.when(jnp.logical_not(middle))
         def _():
             push(own, from_out, c, sent_in, got_out, inward).start()
+
+    def gather_in(c):
+        @pl.when(has_out)
+        def _():
+            if chunks[c][0] not in ready:
+                loads[chunks[c][0]].wait()
+                ready.add(chunks[c][0])
+            push(from_out, from_out, c, sent_in, got_out, inward).wait_recv()
+            add(own, from_out, c)
+            pass_in(c)
+
+    @pl.when(jnp.logical_not(has_out))
+    def _():
+        seen = set()
+        for c in range(len(chunks)):
+            if chunks[c][0] not in seen:
+                loads[chunks[c][0]].wait()
+                seen.add(chunks[c][0])
+            pass_in(c)
 
     def stage_copies(c):
         k, j, start, rows = chunks[c]
@@ -538,108 +769,83 @@
     up_weight,
     down_weight,
 ):
-    def low(item):
-        return item.astype(bf16).astype(f32)
-
-    gains = lax.all_gather(
-        jnp.stack([norm_gain, mlp_norm_gain]).astype(bf16), GROUP, axis=1, tiled=True
-    ).astype(f32)
-    gain_f, mlp_gain_f = gains[0], gains[1]
-    rows = tokens[0].astype(f32)
-    count_rows = rows.shape[0]
-    halves = lax.axis_size("seq")
-    inverse = lax.rsqrt(jnp.mean(rows * rows, axis=-1, keepdims=True) + epsilon)
-    unit = rows * inverse
-    normed = (unit * gain_f).astype(bf16)
-    normed_all = gather_rows(normed)
-    branch_w = to_columns(branch_weight)
-    input_w = to_columns(input_weight)
-    labels = gather_rows(segments).reshape(-1, halves * count_rows) + 1
-    out_low = gather_rows(cotangent[0])
-    gate_w = to_columns(gate_weight)
-    up_w = to_columns(up_weight)
+    x, cot = tokens[0], cotangent[0]
+    rows, depth = x.shape
+    members = lax.axis_size(GROUP)
+    sequences = lax.axis_size("shard")
+    total = members * rows
+    gain, mlp_gain = low(norm_gain)[:, None], low(mlp_norm_gain)[:, None]
+    own_labels = jnp.broadcast_to(segments[0].astype(bf16)[:, None], (rows, 128))
+    unit_all, labels = exchange(
+        start_kernel, 1, (x, own_labels), (((total, depth), bf16), ((total, 128), bf16)), rows, depth, 2, 0
+    )
+    mix_w = to_columns([branch_weight, input_weight], gain)
+    pair_w = to_columns([gate_weight, up_weight], mlp_gain)
+    width = branch_weight.shape[1] // members
+    branch_w, input_w = mix_w[:, :width], mix_w[:, width:]
+    out_low = lax.all_gather(cot, ROWS, axis=0, tiled=True)
     output_w = output_weight.astype(bf16)
     down_w = down_weight.astype(bf16)
-    sequences = labels.shape[0]
-
-    mask = token_masks(labels, conv_weight.shape[0])
+
     conv_f = low(conv_weight)
     decay_f = low(decay_param)
     bias = jnp.stack([low(conv_bias), low(recur_gate_bias), low(input_gate_bias), jax.nn.softplus(-decay_f)])
     mixed = mix_forward(
-        sequences, normed_all, branch_w, input_w, mask, conv_f, bias, recur_gate_weight, input_gate_weight, output_w
+        sequences, unit_all, branch_w, input_w, labels, conv_f, bias, recur_gate_weight, input_gate_weight, output_w
     )
     partial, product = mixed[:2]
-    middle = rows + scatter_rows(partial)
-    inverse_two = lax.rsqrt(jnp.mean(middle * middle, axis=-1, keepdims=True) + epsilon)
-    unit_two = middle * inverse_two
-    normed_two = gather_rows((unit_two * mlp_gain_f).astype(bf16))
-    gate_pre = mm(normed_two, gate_w)
-    up_pre = mm(normed_two, up_w)
-    gate_act, gate_pull = jax.vjp(jax.nn.gelu, gate_pre)
+    whole = ((total, depth), bf16)
+    unit_two, middle = exchange(
+        forward_kernel, 2, (partial, x), (whole, ((rows, depth), f32)), rows, depth, 1, 1
+    )
+    ff = pair_w.shape[1] // 2
+    gate_pre = mm(unit_two, pair_w[:, :ff])
+    up_pre = mm(unit_two, pair_w[:, ff:])
+    hidden_grad = mm_nt(out_low, down_w)
+    gate_act, gate_slope = gelu_parts(gate_pre)
     hidden = (gate_act * up_pre).astype(bf16)
-    block_out = (middle + scatter_rows(mm(hidden, down_w))).astype(bf16)
-
-    grad_out = cotangent[0].astype(f32)
-    hidden_grad = mm_nt(out_low, down_w)
-    gate_low = gate_pull(hidden_grad * up_pre)[0].astype(bf16)
+    gate_low = (hidden_grad * up_pre * gate_slope).astype(bf16)
     up_low = (hidden_grad * gate_act).astype(bf16)
+    pair_low = jnp.concatenate([gate_low, up_low], 1)
+    partial = mm_nt(pair_low, pair_w).astype(bf16)
+    mid_low, middle_grad = exchange(
+        backward_kernel, 3, (partial, middle, cot), (whole, ((rows, depth), f32)), rows, depth, 1, 1
+    )
+    pair_partial = swap_columns(mm_tn(unit_two, pair_low))
     down_partial = mm_tn(hidden, out_low).astype(bf16)[None]
-    pair_partial = swap_columns(mm_tn(normed_two, jnp.concatenate([gate_low, up_low], 1)))
-    two_grad = scatter_rows(mm_nt(gate_low, gate_w) + mm_nt(up_low, up_w))
-    middle_grad = grad_out + norm_backward(two_grad * mlp_gain_f, unit_two, inverse_two)
-    mid_low = gather_rows(middle_grad.astype(bf16))
+    block_sum = lax.psum_scatter(mm(hidden, down_w).astype(bf16), ROWS, scatter_dimension=0, tiled=True)
+    block_out = (middle + block_sum.astype(f32)).astype(bf16)
     output_partial = mm_tn(product, mid_low).astype(bf16)[None]
     back = mix_backward(
-        sequences, mid_low, output_w, branch_w, input_w, *mixed[2:], mask, conv_f, bias, recur_gate_weight, input_gate_weight
+        sequences, mid_low, output_w, branch_w, input_w, *mixed[2:], labels, conv_f, bias, recur_gate_weight, input_gate_weight
     )
     partial, branch_low, conv_low, conv_weight_grad, sums, recur_weight_grad, inject_weight_grad = back
-    conv_bias_grad, recur_bias_grad, inject_bias_grad = sums[0], sums[1], sums[2]
+    branch_partial = side_by_side(swap_columns(mm_tn(unit_all, branch_low)))
+    input_partial = side_by_side(swap_columns(mm_tn(unit_all, conv_low)))
+    (tokens_grad,) = exchange(
+        last_kernel, 4, (partial, middle_grad, x), (((rows, depth), bf16),), rows, depth, 0, 1
+    )
     decay_param_grad = sums[3] * decay_scale * jax.nn.sigmoid(-decay_f)
-    normed_grad = scatter_rows(partial)
-    tokens_grad = (middle_grad + norm_backward(normed_grad * gain_f, unit, inverse)).astype(bf16)
-    branch_partial = side_by_side(swap_columns(mm_tn(normed_all, branch_low)))
-    input_partial = side_by_side(swap_columns(mm_tn(normed_all, conv_low)))
-    down_weight_grad, gate_weight_grad, up_weight_grad, output_weight_grad, branch_weight_grad, input_weight_grad = (
-        replica_sum(
-            [down_partial, pair_partial, output_partial, branch_partial, input_partial], 1, lax.axis_size("replica")
-        )
-    )
-    gain_grad = (
-        jnp.sum(branch_weight_grad * low(branch_weight) + input_weight_grad * low(input_weight), axis=1) / low(norm_gain)
-    )
-    mlp_gain_grad = (
-        jnp.sum(gate_weight_grad * low(gate_weight) + up_weight_grad * low(up_weight), axis=1) / low(mlp_norm_gain)
-    )
-    small = (
-        conv_weight_grad,
-        conv_bias_grad,
-        recur_weight_grad,
-        recur_bias_grad,
-        inject_weight_grad,
-        inject_bias_grad,
-        decay_param_grad,
-    )
+    small = (conv_weight_grad, sums[0], recur_weight_grad, sums[1], inject_weight_grad, sums[2], decay_param_grad)
     small = lax.psum(tuple(item.astype(bf16) for item in small), "replica")
     small = [item.astype(f32) for item in small]
+    down_grad, gate_grad, up_grad, output_grad, branch_grad, input_grad = replica_sum(
+        [down_partial, pair_partial, output_partial, branch_partial, input_partial], 1, lax.axis_size("replica")
+    )
+    gain_grad = jnp.sum(branch_grad * low(branch_weight) + input_grad * low(input_weight), axis=1)
+    mlp_gain_grad = jnp.sum(gate_grad * low(gate_weight) + up_grad * low(up_weight), axis=1)
     return (
         block_out[None],
         tokens_grad[None],
         gain_grad,
-        branch_weight_grad,
-        input_weight_grad,
-        small[0],
-        small[1],
-        small[2],
-        small[3],
-        small[4],
-        small[5],
-        small[6],
-        output_weight_grad,
+        branch_grad * gain,
+        input_grad * gain,
+        *small,
+        output_grad,
         mlp_gain_grad,
-        gate_weight_grad,
-        up_weight_grad,
-        down_weight_grad,
+        gate_grad * mlp_gain,
+        up_grad * mlp_gain,
+        down_grad,
     )
 
 

time: 1220 us -> 946 us (0.78)
  waiting for transfers between devices: 311 us -> 50.6 us
  Pallas kernels: 625 us -> 676 us
  blocking collectives: 53.9 us -> 12.9 us
  matrix products: 83.6 us -> 70.7 us
    pallas_call x0 -> x4, Pallas kernels: none -> 305 us  [exchange(): pl.pallas_call(kernel, out_shape=tuple((jax.ShapeDtypeStruct(shape, kind)...]
    pallas_call x1, Pallas kernels: 572 us -> 317 us  [replica_sum(): pl.pallas_call(functools.partial(line_kernel, copies, tuple(cuts), paired...]
    reduce_scatter x4 -> x1, waiting for transfers between devices: 102 us -> 0.01 us  [body(): lax.psum_scatter(mm(hidden, down_w).astype(bf16), ROWS, scatter_dimension...]
    all_to_all x4 -> x2, waiting for transfers between devices: 107 us -> 29.7 us  [to_columns(): lax.all_to_all(cut, GROUP, split_axis=0, concat_axis=0, tiled=True)]
    all_to_all x3, waiting for transfers between devices: 64.3 us -> 20.2 us  [swap_columns(): return lax.all_to_all(cut, GROUP, split_axis=0, concat_axis=0, tiled=True)]
    all_gather x2 -> x0, blocking collectives: 41.7 us -> none  [the longest x1 31.3 us: gather_rows(): return lax.all_gather(part, ROWS, axis=0, tiled=True)]
    all_gather x4 -> x1, waiting for transfers between devices: 36.8 us -> 0.01 us  [body(): out_low = lax.all_gather(cot, ROWS, axis=0, tiled=True)]
    reduce_sum x6 -> x0, other arithmetic: 19.3 us -> none  [the longest x1 9.41 us: body(): jnp.sum(gate_weight_grad * low(gate_weight) + up_weight_grad * low(up_wei...]
  transfers between devices with their start and end apart: 16 -> 8, of which waited for: 9 -> 3; matrix products, arithmetic and copies ran while one was open for 9% -> 12% of each run, Pallas kernels for 47% -> 62%
where the time goes in v4:
time: 946 us; the launch traced here: 941 us
  Pallas kernels  676 us (71%)
  matrix products  70.7 us (7%)
  other arithmetic  50.7 us (5%)
  waiting for transfers between devices  50.6 us (5%)
  local copies, waits for them, and re-layouts  42 us (4%)
  starting transfers between devices  23.9 us (3%)
  between operations  14.4 us (2%)
  blocking collectives  12.9 us (1%)
    pallas_call x1, Pallas kernels, replica_sum(): pl.pallas_call(functools.partial(line_kernel, copies, tuple(cuts), paired...  317 us
    pallas_call x4, Pallas kernels, exchange(): pl.pallas_call(kernel, out_shape=tuple((jax.ShapeDtypeStruct(shape, kind)...  305 us
    all_to_all x2, waiting for transfers between devices, to_columns(): lax.all_to_all(cut, GROUP, split_axis=0, concat_axis=0, tiled=True)  29.7 us
    pallas_call x1, Pallas kernels, mix_backward(): pl.pallas_call(functools.partial(mix_backward_kernel, sequences, length),...  29.7 us
    dot_general x5, matrix products, mm_tn(): lax.dot_general(left, right, (((0,), (0,)), ((), ())), preferred_element_...  27.7 us
    dot_general x3, matrix products, mm(): return jnp.dot(left, right, preferred_element_type=f32)  26 us
    pallas_call x1, Pallas kernels, mix_forward(): pl.pallas_call(functools.partial(mix_forward_kernel, sequences, length),...  23.6 us
    all_to_all x3, waiting for transfers between devices, swap_columns(): return lax.all_to_all(cut, GROUP, split_axis=0, concat_axis=0, tiled=True)  20.2 us
  transfers between devices with their start and end apart: 8, of which 3 were waited for; matrix products, arithmetic and copies ran while one was open for 12% of the time, Pallas kernels for 62%

profile of v4, /device:TPU:0, one launch (start us, length us, event | category | flops | bytes accessed | tf_op | source)
XLA Modules:
  0.0 941.3 jit_solution(1092404198118054689)
XLA Ops:
  8.6 4.6 fusion.25
  14.8 2.4 copy.39
  17.3 3.0 maximum_bitcast_fusion.1
  20.2 5.4 all-to-all-start
  25.6 6.3 fusion
  32.0 2.3 copy_bitcast_fusion
  34.3 5.2 maximum_bitcast_fusion
  39.5 29.7 %all-to-all-done = bf16[8,256,640]{1,2,0:T(8,128)(2,1)} async-done(((bf16[8,256,640]{1,2,0:T(8,128)(2,1)}), bf16[8,256,640]{1,2,0:T(8,128)(2,1)}, u32[]{:S(2)}, u32[]{:S(2)}) %all-to-all-start) | async-done | bytes 2621472 | tf_op jit(solution)/shard_map/all_to_all | solution.py:52
  69.2 4.9 all-to-all-start.1
  74.3 3.0 convert_element_type.194.ow_ref
  77.4 96.4 %shard_map.305 = (bf16[1024,2048]{1,0:T(8,128)(2,1)S(1)}, bf16[1024,128]{1,0:T(8,128)(2,1)S(1)}) custom-call(bf16[128,2048]{1,0:T(8,128)(2,1)S(1)} %bitcast.61, bf16[128,128]{1,0:T(8,128)(2,1)S(1)} %broadcast_in_dim.20.label_ref), custom_call_target="tpu_custom_call" | custom-call | flops 1000000 | bytes 62914560 | tf_op jit(solution)/shard_map/pallas_call | solution.py:541
  174.6 2.0 copy-done.6
  177.2 4.4 copy.40
  181.6 4.4 fusion.43
  186.0 23.6 %shard_map.306 = (bf16[1024,2048]{1,0:T(8,128)(2,1)}, bf16[1024,320]{1,0:T(8,128)(2,1)}, f32[1024,320]{1,0:T(8,128)}, bf16[1024,320]{1,0:T(8,128)(2,1)}, bf16[10...) custom-call(bf16[1024,2048]{1,0:T(8,128)(2,1)} %copy-done.6, ...), custom_call_target="tpu_custom_call" | custom-call | flops 4026531840 | bytes 20971520 | tf_op jit(solution)/shard_map/pallas_call | solution.py:206
  209.6 2.2 copy-done.3
  211.8 56.9 %shard_map.307 = (bf16[1024,2048]{1,0:T(8,128)(2,1)S(1)}, f32[128,2048]{1,0:T(8,128)S(1)}) custom-call(bf16[1024,2048]{1,0:T(8,128)(2,1)S(1)} %copy-done.3, bf16[128,2048]{1,0:T(8,128)(2,1)S(1)} %bitcast.62), custom_call_target="tpu_custom_call" | custom-call | flops 1000000 | bytes 62914560 | tf_op jit(solution)/shard_map/pallas_call | solution.py:541
  268.7 2.0 copy-done.8
  270.7 8.3 fusion.18
  279.0 7.0 fusion.6
  286.0 8.9 fusion.17
  294.9 10.0 %convolution_convert_fusion.1.partial = bf16[1024,2048]{1,0:T(8,128)(2,1)S(1)} fusion(bf16[2048,1536]{1,0:T(8,128)(2,1)} %bitcast.7, bf16[1024,768]{0,1:T(8,128)(2,1)S(1)} %get-tuple-element.87, bf16[1024,768]{0,1:T(8,128)(2,1)S(1)} %get-tuple-element.86), kind=kOutput, calls=%fused_computation.16 | convolution fusion | flops 6450839552 | bytes 13631488 | tf_op jit(solution)/shard_map/dot_general | solution.py:26
  305.0 58.2 %shard_map.308 = (bf16[1024,2048]{1,0:T(8,128)(2,1)S(1)}, f32[128,2048]{1,0:T(8,128)S(1)}) custom-call(bf16[1024,2048]{1,0:T(8,128)(2,1)S(1)} %convolution_convert_fusion.1.partial, f32[128,2048]{1,0:T(8,128)S(1)} %get-tuple-element.48.middle_ref, bf16[128,2048]{1,0:T(8,128)(2,1)S(1)} %bitcast.65), custom_call_target="tpu_custom_call" | custom-call | flops 1000000 | bytes 62914560 | tf_op jit(solution)/shard_map/pallas_call | solution.py:541
  363.1 2.0 copy-done.1
  365.2 29.7 %shard_map.309 = (bf16[1024,2048]{1,0:T(8,128)(2,1)}, bf16[1024,320]{1,0:T(8,128)(2,1)}, bf16[1024,320]{1,0:T(8,128)(2,1)}, f32[4,320]{1,0:T(4,128)}, f32[4,320]...) custom-call(bf16[1024,2048]{1,0:T(8,128)(2,1)} %copy-done.1, ...), custom_call_target="tpu_custom_call" | custom-call | flops 4026531840 | bytes 26214400 | tf_op jit(solution)/shard_map/pallas_call | solution.py:311
  394.9 2.7 convolution_convert_fusion.4
  398.7 4.3 all-to-all-start.3
  403.0 4.0 convolution_convert_fusion.3
  408.1 13.1 %all-to-all-done.3 = bf16[8,256,320]{1,2,0:T(8,128)(2,1)} async-done(((bf16[8,256,320]{1,2,0:T(8,128)(2,1)}), bf16[8,256,320]{1,2,0:T(8,128)(2,1)}, u32[]{:S(2)}, u32[]{:S(2)}) %all-to-all-start.3) | async-done | bytes 1310752 | tf_op jit(solution)/shard_map/all_to_all | solution.py:40
  421.2 4.3 all-to-all-start.4
  425.5 11.2 %convolution_convert_fusion = bf16[2048,1536]{1,0:T(8,128)(2,1)} fusion(bf16[1024,2048]{1,0:T(8,128)(2,1)} %copy-done.8, bf16[1024,768]{0,1:T(8,128)(2,1)} %copy-done.26, bf16[1024,768]{0,1:T(8,128)(2,1)} %copy-done.25), kind=kOutput, calls=%fused_computation.4 | convolution fusion | flops 6451888128 | bytes 13631488 | tf_op jit(solution)/shard_map/dot_general | solution.py:30
  436.6 7.1 all-to-all-done.4
  443.7 4.9 all-to-all-start.2
  450.1 8.8 convolution_convert_fusion.2
  458.9 2.2 copy-done.2
  461.2 93.8 %shard_map.310 = bf16[128,2048]{1,0:T(8,128)(2,1)S(1)} custom-call(bf16[1024,2048]{1,0:T(8,128)(2,1)S(1)} %copy-done.2, f32[128,2048]{1,0:T(8,128)S(1)} %get-tuple-element.59.grad_ref, bf16[128,2048]{1,0:T(8,128)(2,1)S(1)} %bitcast.63), custom_call_target="tpu_custom_call" | custom-call | flops 1000000 | bytes 62914560 | tf_op jit(solution)/shard_map/pallas_call | solution.py:541
  555.1 12.9 %all-reduce = (bf16[4,320]{1,0:T(4,128)(2,1)S(1)}, bf16[320]{0:T(512)(128)(2,1)S(1)}, bf16[320]{0:T(512)(128)(2,1)S(1)}, bf16[320]{0:T(512)(128)(2,1)S(1)}, bf16[320]{0:T(512)(128)(2,1)S(1)}) all-reduce(bf16[4,320]{1,0:T(4,128)(2,1)S(1)} %convert_element_type.216, ...), channel_id=1, replica_groups=mesh['seq'=2,'shard'=4,'replica'=4] {'replica'}, use_global_device_ids=true, to_apply=%region_2.3 | all-reduce | flops 2560 | bytes 10240 | tf_op jit(solution)/shard_map/psum | solution.py:830
  571.0 5.2 fusion.29.refs_2_
  576.2 4.7 fusion.22.refs_0_
  580.9 1.7 convert_element_type.221
  584.3 2.4 copy.45.refs_3_
  586.7 2.4 copy.46.refs_4_
  589.1 317.4 %shard_map.311 = (f32[768,2048]{1,0:T(8,128)}, f32[256,6144]{1,0:T(8,128)}, f32[256,6144]{1,0:T(8,128)}, f32[320,2048]{1,0:T(8,128)}, f32[256,2560]{1,0:T(8,128)}, /*index=5*/f32[256,2560]{1,0:T(8,128)}) custom-call(bf16[1,768,2048]{2,1,0:T(8,128)(2,1)} %fusion.22.refs_0_, bf16[8,256,1536]{2,1,0:T(8,128)(2,1)} %all-to-all-done.2.refs_1_, ...), custom_call_target="tpu_custom_call" | custom-call | tf_op jit(solution)/shard_map/pallas_call | solution.py:734
  906.6 8.2 broadcast_multiply_fusion.2
  915.6 9.5 %broadcast_multiply_fusion = (f32[256,6144]{1,0:T(8,128)}, f32[256]{0:T(256)}, f32[256,6144]{1,0:T(8,128)}) fusion(f32[256,6144]{1,0:T(8,128)} %get-tuple-element.71, f32[256]{0:T(256)S(1)} %convert_convert_fusion.4, f32[256,6144]{1,0:T(8,128)S(1)} %bitcast.69, f32[256,6144]{1,0:T(8,128)} %get-tuple-element.70, f32[256,6144]{1,0:T(8,128)S(1)} %bitcast.67), kind=kLoop, calls=%fused_computation.39 | loop fusion | flops 15728384 | bytes 37750784 | tf_op jit(solution)/shard_map/mul | solution.py:847
  925.1 1.9 fusion.32
  927.8 4.1 copy.63
  931.9 2.7 copy.64
  (100 shorter events, 14.5 us)
Async XLA Ops:
  7.2 271.8 %all-gather.3.cloned.1.call-start = ((), (), s32[]{:S(2)}) async-start(), calls=%async_computation.7 | async-start | bytes 4718592 | tf_op jit(solution)/shard_map/all_gather | solution.py:786
  20.2 5.4 copy-start.20
  20.2 48.9 %all-to-all-start = ((bf16[8,256,640]{1,2,0:T(8,128)(2,1)}), bf16[8,256,640]{1,2,0:T(8,128)(2,1)}, u32[]{:S(2)}, u32[]{:S(2)}) async-start(bf16[8,256,640]{1,2,0:T(8,128)(2,1)} %maximum_bitcast_fusion.1), calls=%async_computation | async-start | bytes 5242880 | tf_op jit(solution)/shard_map/all_to_all | solution.py:52
  39.5 34.7 %copy-start.17 = (f32[320]{0:T(512)S(1)}, f32[320]{0:T(512)}, u32[]{:S(2)}) copy-start(f32[320]{0:T(512)} %param.25) | copy-start | bytes 3844
  39.5 34.7 %copy-start.18 = (f32[320]{0:T(512)S(1)}, f32[320]{0:T(512)}, u32[]{:S(2)}) copy-start(f32[320]{0:T(512)} %param.27) | copy-start | bytes 3844
  39.5 34.8 %copy-start.19 = (f32[320]{0:T(512)S(1)}, f32[320]{0:T(512)}, u32[]{:S(2)}) copy-start(f32[320]{0:T(512)} %param.29) | copy-start | bytes 3844
  39.5 34.8 %copy-start.14 = (f32[320]{0:T(512)S(1)}, f32[320]{0:T(512)}, u32[]{:S(2)}) copy-start(f32[320]{0:T(512)} %param.30) | copy-start | bytes 3844
  69.2 201.5 %all-to-all-start.1 = ((bf16[8,256,1536]{2,1,0:T(8,128)(2,1)}), bf16[8,256,1536]{2,1,0:T(8,128)(2,1)}, u32[]{:S(2)}, u32[]{:S(2)}) async-start(bf16[8,256,1536]{2,1,0:T(8,128)(2,1)} %maximum_bitcast_fusion), calls=%async_computation.1 | async-start | bytes 12582912 | tf_op jit(solution)/shard_map/all_to_all | solution.py:52
  74.1 3.2 copy-start.22
  74.2 3.3 copy-start
  74.2 102.4 %copy-start.16 = (f32[4,320]{1,0:T(4,128)S(1)}, f32[4,320]{1,0:T(4,128)}, u32[]{:S(2)}) copy-start(f32[4,320]{1,0:T(4,128)} %param.24) | copy-start | bytes 15364
  173.9 0.7 copy-start.5
  174.6 2.0 copy-start.6
  209.6 2.2 copy-start.3
  268.7 2.0 copy-start.8
  279.0 7.0 copy-start.9
  279.0 7.0 copy-start.24
  294.9 10.0 %copy-start.25 = (bf16[1024,768]{0,1:T(8,128)(2,1)}, bf16[1024,768]{0,1:T(8,128)(2,1)S(1)}, u32[]{:S(2)}) copy-start(bf16[1024,768]{0,1:T(8,128)(2,1)S(1)} %get-tuple-element.86) | copy-start | bytes 4718596
  294.9 10.0 %copy-start.26 = (bf16[1024,768]{0,1:T(8,128)(2,1)}, bf16[1024,768]{0,1:T(8,128)(2,1)S(1)}, u32[]{:S(2)}) copy-start(bf16[1024,768]{0,1:T(8,128)(2,1)S(1)} %get-tuple-element.87) | copy-start | bytes 4718596
  294.9 10.0 %copy-start.4 = (bf16[1,128,2048]{2,1,0:T(8,128)(2,1)S(1)}, bf16[1,128,2048]{2,1,0:T(8,128)(2,1)}, u32[]{:S(2)}) copy-start(bf16[1,128,2048]{2,1,0:T(8,128)(2,1)} %param.20) | copy-start | bytes 1572868
  363.1 2.0 copy-start.1
  365.2 29.7 %copy-start.7 = (bf16[1024,2048]{1,0:T(8,128)(2,1)S(1)}, bf16[1024,2048]{1,0:T(8,128)(2,1)}, u32[]{:S(2)}) copy-start(bf16[1024,2048]{1,0:T(8,128)(2,1)} %copy-done.6) | copy-start | bytes 12582916
  398.7 22.5 %all-to-all-start.3 = ((bf16[8,256,320]{1,2,0:T(8,128)(2,1)}), bf16[8,256,320]{1,2,0:T(8,128)(2,1)}, u32[]{:S(2)}, u32[]{:S(2)}) async-start(bf16[8,256,320]{1,2,0:T(8,128)(2,1)} %bitcast.77), calls=%async_computation.4 | async-start | bytes 2621440 | tf_op jit(solution)/shard_map/all_to_all | solution.py:40
  421.2 22.5 %all-to-all-start.4 = ((bf16[8,256,320]{1,2,0:T(8,128)(2,1)}), bf16[8,256,320]{1,2,0:T(8,128)(2,1)}, u32[]{:S(2)}, u32[]{:S(2)}) async-start(bf16[8,256,320]{1,2,0:T(8,128)(2,1)} %bitcast.76), calls=%async_computation.5 | async-start | bytes 2621440 | tf_op jit(solution)/shard_map/all_to_all | solution.py:40
  443.7 5.0 copy-start.12
  443.7 5.6 copy-start.11
  443.7 145.4 %all-to-all-start.2 = ((bf16[8,256,1536]{2,1,0:T(8,128)(2,1)}), bf16[8,256,1536]{2,1,0:T(8,128)(2,1)}, u32[]{:S(2)}, u32[]{:S(2)}) async-start(bf16[8,256,1536]{2,1,0:T(8,128)(2,1)} %bitcast.73), calls=%async_computation.3 | async-start | bytes 12582912 | tf_op jit(solution)/shard_map/all_to_all | solution.py:40
  448.6 132.3 %all-reduce.4.cloned.1.call-start = ((), (), s32[]{:S(2)}) async-start(), calls=%async_computation.8 | async-start | bytes 655360 | tf_op jit(solution)/shard_map/psum | solution.py:830
  450.1 475.0 %reduce-scatter.2.cloned.1.call-start = ((), (), s32[]{:S(2)}) async-start(), calls=%async_computation.6 | async-start | bytes 4718592 | tf_op jit(solution)/shard_map/reduce_scatter | solution.py:816
  458.9 2.2 copy-start.2
  461.2 93.9 %copy-start.13 = (f32[4,320]{1,0:T(4,128)S(1)}, f32[4,320]{1,0:T(4,128)}, u32[]{:S(2)}) copy-start(f32[4,320]{1,0:T(4,128)} %get-tuple-element.66) | copy-start | bytes 15364
  461.2 93.9 %copy-start.15 = (f32[4,320]{1,0:T(4,128)S(1)}, f32[4,320]{1,0:T(4,128)}, u32[]{:S(2)}) copy-start(f32[4,320]{1,0:T(4,128)} %get-tuple-element.65) | copy-start | bytes 15364
  571.0 5.2 copy-start.21
  571.0 5.2 copy-start.23
  589.1 325.7 %slice-start.2 = ((s8[6291456]{0:T(1024)(128)(4,1)}), s8[2097152]{0:T(1024)(128)(4,1)S(1)}, s32[]{:S(2)}) async-start(s8[6291456]{0:T(1024)(128)(4,1)} %bitcast.68), calls=%async_computation.11 | async-start | bytes 4194304
  906.5 8.2 slice-start
  906.6 8.2 slice-start.1
  906.6 9.0 slice-start.3
  927.0 4.9 copy-start.10
Sparse Core Ops, SparseCore 0:
  9.9 52.9 all-gather.2
  453.0 38.4 all-reduce.3
  494.9 73.6 reduce-scatter.1

commit v5 on v4

--- a/solution.py
+++ b/solution.py
@@ -561,8 +561,9 @@
 def line_kernel(n, cuts, paired, *refs):
     ins = len(cuts)
     own_hbm = refs[:ins]
-    outs = refs[ins : ins + ins + 1]
-    scratch = refs[ins + ins + 1 :]
+    made = ins if paired is None else ins + 1
+    outs = refs[ins : ins + made]
+    scratch = refs[ins + made :]
     own, from_out, from_in = scratch[:ins], scratch[ins : 2 * ins], scratch[2 * ins : 3 * ins]
     stage, load_sem, stage_sem, sent_in, sent_out, got_out, got_in = scratch[3 * ins :]
     me = lax.axis_index("replica")
@@ -662,7 +663,7 @@
                 )
                 for side in range(2)
             ]
-        where = k if k < paired else k + 1
+        where = k if paired is None or k < paired else k + 1
         return [
             pltpu.make_async_copy(
                 stage.at[slot, pl.ds(0, rows), pl.ds(0, columns)],
@@ -808,11 +809,11 @@
     up_low = (hidden_grad * gate_act).astype(bf16)
     pair_low = jnp.concatenate([gate_low, up_low], 1)
     partial = mm_nt(pair_low, pair_w).astype(bf16)
+    down_sum = lax.psum(mm_tn(hidden, out_low).astype(bf16), "replica")
+    pair_partial = swap_columns(mm_tn(unit_two, pair_low))
     mid_low, middle_grad = exchange(
         backward_kernel, 3, (partial, middle, cot), (whole, ((rows, depth), f32)), rows, depth, 1, 1
     )
-    pair_partial = swap_columns(mm_tn(unit_two, pair_low))
-    down_partial = mm_tn(hidden, out_low).astype(bf16)[None]
     block_sum = lax.psum_scatter(mm(hidden, down_w).astype(bf16), ROWS, scatter_dimension=0, tiled=True)
     block_out = (middle + block_sum.astype(f32)).astype(bf16)
     output_partial = mm_tn(product, mid_low).astype(bf16)[None]
@@ -820,18 +821,34 @@
         sequences, mid_low, output_w, branch_w, input_w, *mixed[2:], labels, conv_f, bias, recur_gate_weight, input_gate_weight
     )
     partial, branch_low, conv_low, conv_weight_grad, sums, recur_weight_grad, inject_weight_grad = back
+    down_sum, pair_partial, branch_low = lax.optimization_barrier((down_sum, pair_partial, branch_low))
+    pair_sum = lax.psum(pair_partial, "replica").astype(f32)
+    gate_grad = jnp.swapaxes(pair_sum[:, :, :ff], 0, 1).reshape(-1, members * ff)
+    up_grad = jnp.swapaxes(pair_sum[:, :, ff:], 0, 1).reshape(-1, members * ff)
     branch_partial = side_by_side(swap_columns(mm_tn(unit_all, branch_low)))
     input_partial = side_by_side(swap_columns(mm_tn(unit_all, conv_low)))
     (tokens_grad,) = exchange(
         last_kernel, 4, (partial, middle_grad, x), (((rows, depth), bf16),), rows, depth, 0, 1
     )
-    decay_param_grad = sums[3] * decay_scale * jax.nn.sigmoid(-decay_f)
-    small = (conv_weight_grad, sums[0], recur_weight_grad, sums[1], inject_weight_grad, sums[2], decay_param_grad)
-    small = lax.psum(tuple(item.astype(bf16) for item in small), "replica")
-    small = [item.astype(f32) for item in small]
-    down_grad, gate_grad, up_grad, output_grad, branch_grad, input_grad = replica_sum(
-        [down_partial, pair_partial, output_partial, branch_partial, input_partial], 1, lax.axis_size("replica")
-    )
+    size = recur_gate_weight.shape[1]
+    gates = jnp.concatenate([recur_weight_grad, inject_weight_grad], 2).reshape(width, 2 * size)
+    lanes = -(-max(width, 2 * size) // 128) * 128
+    lines = jnp.concatenate([conv_weight_grad, sums], 0)
+    packed = jnp.concatenate(
+        [
+            jnp.pad(gates, ((0, 0), (0, lanes - 2 * size))),
+            jnp.pad(lines, ((0, 16 - lines.shape[0]), (0, lanes - width))),
+        ],
+        0,
+    ).astype(bf16)[None]
+    output_grad, branch_grad, input_grad, packed = replica_sum(
+        [output_partial, branch_partial, input_partial, packed], None, lax.axis_size("replica")
+    )
+    recur_weight_grad = packed[:width, :size].reshape(-1, size, size)
+    inject_weight_grad = packed[:width, size : 2 * size].reshape(-1, size, size)
+    conv_weight_grad = packed[width : width + conv_weight.shape[0], :width]
+    conv_bias_grad, recur_bias_grad, inject_bias_grad, rate_grad = [packed[width + conv_weight.shape[0] + i, :width] for i in range(4)]
+    decay_param_grad = rate_grad * decay_scale * jax.nn.sigmoid(-decay_f)
     gain_grad = jnp.sum(branch_grad * low(branch_weight) + input_grad * low(input_weight), axis=1)
     mlp_gain_grad = jnp.sum(gate_grad * low(gate_weight) + up_grad * low(up_weight), axis=1)
     return (
@@ -840,12 +857,18 @@
         gain_grad,
         branch_grad * gain,
         input_grad * gain,
-        *small,
+        conv_weight_grad,
+        conv_bias_grad,
+        recur_weight_grad,
+        recur_bias_grad,
+        inject_weight_grad,
+        inject_bias_grad,
+        decay_param_grad,
         output_grad,
         mlp_gain_grad,
         gate_grad * mlp_gain,
         up_grad * mlp_gain,
-        down_grad,
+        down_sum.astype(f32),
     )
 
 

time: 946 us -> 900 us (0.951)
  Pallas kernels: 676 us -> 603 us
  local copies, waits for them, and re-layouts: 42 us -> 93.5 us
  waiting for transfers between devices: 50.6 us -> 32.5 us
  blocking collectives: 12.9 us -> 0 us
    pallas_call x1, Pallas kernels: 317 us -> 245 us  [replica_sum(): pl.pallas_call(functools.partial(line_kernel, copies, tuple(cuts), paired...]
    transpose x0 -> x3, local copies, waits for them, and re-layouts: none -> 23.8 us  [the longest x2 17.2 us: body(): jnp.swapaxes(pair_sum[:, :, :ff], 0, 1).reshape(-1, members * ff)]
    unnamed x65 -> x58, local copies, waits for them, and re-layouts: 19.7 us -> 40.5 us
    all_to_all x3, waiting for transfers between devices: 20.2 us -> 2.56 us  [swap_columns(): return lax.all_to_all(cut, GROUP, split_axis=0, concat_axis=0, tiled=True)]
    psum x1 -> x0, blocking collectives: 12.9 us -> none  [body(): small = lax.psum(tuple((item.astype(bf16) for item in small)), 'replica')]
  transfers between devices with their start and end apart: 8 -> 9, of which waited for: 3 -> 2; matrix products, arithmetic and copies ran while one was open for 12% -> 14% of each run, Pallas kernels for 62% -> 67%
where the time goes in v5:
time: 900 us; the launch traced here: 895 us
  Pallas kernels  603 us (67%)
  local copies, waits for them, and re-layouts  93.5 us (10%)
  matrix products  71.9 us (8%)
  other arithmetic  56.3 us (6%)
  waiting for transfers between devices  32.5 us (4%)
  starting transfers between devices  23.3 us (3%)
  between operations  14.5 us (2%)
    pallas_call x4, Pallas kernels, exchange(): pl.pallas_call(kernel, out_shape=tuple((jax.ShapeDtypeStruct(shape, kind)...  305 us
    pallas_call x1, Pallas kernels, replica_sum(): pl.pallas_call(functools.partial(line_kernel, copies, tuple(cuts), paired...  245 us
    unnamed x58, local copies, waits for them, and re-layouts  40.5 us
    pallas_call x1, Pallas kernels, mix_backward(): pl.pallas_call(functools.partial(mix_backward_kernel, sequences, length),...  29.3 us
    all_to_all x2, waiting for transfers between devices, to_columns(): lax.all_to_all(cut, GROUP, split_axis=0, concat_axis=0, tiled=True)  29.2 us
    dot_general x5, matrix products, mm_tn(): lax.dot_general(left, right, (((0,), (0,)), ((), ())), preferred_element_...  26.6 us
    dot_general x3, matrix products, mm(): return jnp.dot(left, right, preferred_element_type=f32)  25.9 us
    pallas_call x1, Pallas kernels, mix_forward(): pl.pallas_call(functools.partial(mix_forward_kernel, sequences, length),...  23.6 us
  transfers between devices with their start and end apart: 9, of which 2 were waited for; matrix products, arithmetic and copies ran while one was open for 14% of the time, Pallas kernels for 67%

profile of v5, /device:TPU:0, one launch (start us, length us, event | category | flops | bytes accessed | tf_op | source)
XLA Modules:
  0.0 895.5 jit_solution(7996600466727447997)
XLA Ops:
  8.6 4.2 fusion.22
  16.7 5.2 all-to-all-start
  21.9 4.0 copy.52
  25.9 6.5 copy.53
  32.4 3.1 fusion
  35.5 3.1 maximum_bitcast_fusion
  38.6 29.2 %all-to-all-done = bf16[8,256,640]{1,2,0:T(8,128)(2,1)} async-done(((bf16[8,256,640]{1,2,0:T(8,128)(2,1)}), bf16[8,256,640]{1,2,0:T(8,128)(2,1)}, u32[]{:S(2)}, u32[]{:S(2)}) %all-to-all-start) | async-done | bytes 2621472 | tf_op jit(solution)/shard_map/all_to_all | solution.py:52
  67.9 4.8 all-to-all-start.1
  73.1 3.0 convert_element_type.167.ow_ref
  76.3 96.0 %shard_map.305 = (bf16[1024,2048]{1,0:T(8,128)(2,1)S(1)}, bf16[1024,128]{1,0:T(8,128)(2,1)S(1)}) custom-call(bf16[128,2048]{1,0:T(8,128)(2,1)S(1)} %bitcast.70, bf16[128,128]{1,0:T(8,128)(2,1)S(1)} %broadcast_in_dim.8.label_ref), custom_call_target="tpu_custom_call" | custom-call | flops 1000000 | bytes 62914560 | tf_op jit(solution)/shard_map/pallas_call | solution.py:541
  173.1 2.0 copy-done.6
  175.7 4.4 copy.51
  180.1 4.4 fusion.46
  184.5 23.6 %shard_map.306 = (bf16[1024,2048]{1,0:T(8,128)(2,1)}, bf16[1024,320]{1,0:T(8,128)(2,1)}, f32[1024,320]{1,0:T(8,128)}, bf16[1024,320]{1,0:T(8,128)(2,1)}, bf16[10...) custom-call(bf16[1024,2048]{1,0:T(8,128)(2,1)} %copy-done.6, ...), custom_call_target="tpu_custom_call" | custom-call | flops 4026531840 | bytes 20971520 | tf_op jit(solution)/shard_map/pallas_call | solution.py:206
  208.1 2.2 copy-done.3
  210.3 56.9 %shard_map.307 = (bf16[1024,2048]{1,0:T(8,128)(2,1)S(1)}, f32[128,2048]{1,0:T(8,128)S(1)}) custom-call(bf16[1024,2048]{1,0:T(8,128)(2,1)S(1)} %copy-done.3, bf16[128,2048]{1,0:T(8,128)(2,1)S(1)} %bitcast.71), custom_call_target="tpu_custom_call" | custom-call | flops 1000000 | bytes 62914560 | tf_op jit(solution)/shard_map/pallas_call | solution.py:541
  267.2 2.0 copy-done.8
  269.3 8.6 copy.54
  277.9 8.3 fusion.18
  286.1 9.3 %fusion.6 = f32[1024,768]{0,1:T(8,128)} fusion(bf16[1,1024,2048]{2,1,0:T(8,128)(2,1)} %all-gather.3.cloned.1.call-done, f32[768,2048]{1,0:T(8,128)} %param.35), kind=kOutput, calls=%fused_computation.18 | convolution fusion | flops 3222798336 | bytes 13631488 | tf_op jit(solution)/shard_map/dot_general | solution.py:26
  295.5 9.8 %fusion.17 = (bf16[1024,768]{0,1:T(8,128)(2,1)}, bf16[1024,768]{0,1:T(8,128)(2,1)}, bf16[1024,768]{0,1:T(8,128)(2,1)S(1)}) fusion(f32[1024,768]{0,1:T(8,128)} %fusion.6, f32[1024,768]{0,1:T(8,128)} %fusion.18, bf16[1024,2048]{1,0:T(8,128)(2,1)S(1)} %copy-done.9, bf16[2048,1536]{1,0:T(8,128)(2,1)S(1)} %bitcast.80), kind=kOutput, calls=%fused_computation.33 | convolution fusion | flops 3240886272 | bytes 18350080 | tf_op jit(solution)/shard_map/dot_general | solution.py:22
  305.2 4.8 fusion.8
  310.2 7.8 convolution_convert_fusion.2
  319.4 11.2 %convolution_convert_fusion = bf16[2048,1536]{1,0:T(8,128)(2,1)} fusion(bf16[1024,2048]{1,0:T(8,128)(2,1)} %copy-done.8, bf16[1024,768]{0,1:T(8,128)(2,1)} %get-tuple-element.102, bf16[1024,768]{0,1:T(8,128)(2,1)S(1)} %copy-done.25), kind=kOutput, calls=%fused_computation.4 | convolution fusion | flops 6451888128 | bytes 13631488 | tf_op jit(solution)/shard_map/dot_general | solution.py:30
  330.6 4.8 all-to-all-start.2
  335.5 10.1 %convolution_convert_fusion.1.partial = bf16[1024,2048]{1,0:T(8,128)(2,1)S(1)} fusion(bf16[2048,1536]{1,0:T(8,128)(2,1)} %bitcast.79, bf16[1024,768]{0,1:T(8,128)(2,1)} %get-tuple-element.102, bf16[1024,768]{0,1:T(8,128)(2,1)} %get-tuple-element.101), kind=kOutput, calls=%fused_computation.20 | convolution fusion | flops 6450839552 | bytes 13631488 | tf_op jit(solution)/shard_map/dot_general | solution.py:26
  345.6 112.8 %shard_map.308 = (bf16[1024,2048]{1,0:T(8,128)(2,1)S(1)}, f32[128,2048]{1,0:T(8,128)S(1)}) custom-call(bf16[1024,2048]{1,0:T(8,128)(2,1)S(1)} %convolution_convert_fusion.1.partial, f32[128,2048]{1,0:T(8,128)S(1)} %get-tuple-element.49.middle_ref, bf16[128,2048]{1,0:T(8,128)(2,1)S(1)} %bitcast.74), custom_call_target="tpu_custom_call" | custom-call | flops 1000000 | bytes 62914560 | tf_op jit(solution)/shard_map/pallas_call | solution.py:541
  458.4 2.0 copy-done.1
  460.4 29.3 %shard_map.309 = (bf16[1024,2048]{1,0:T(8,128)(2,1)}, bf16[1024,320]{1,0:T(8,128)(2,1)}, bf16[1024,320]{1,0:T(8,128)(2,1)}, f32[4,320]{1,0:T(4,128)}, f32[4,320]...) custom-call(bf16[1024,2048]{1,0:T(8,128)(2,1)} %copy-done.1, ...), custom_call_target="tpu_custom_call" | custom-call | flops 4026531840 | bytes 26214400 | tf_op jit(solution)/shard_map/pallas_call | solution.py:311
  489.7 4.0 convolution_convert_fusion.3
  494.8 4.3 all-to-all-start.4
  499.1 2.2 copy-done.2
  501.3 39.6 %shard_map.310 = bf16[128,2048]{1,0:T(8,128)(2,1)S(1)} custom-call(bf16[1024,2048]{1,0:T(8,128)(2,1)S(1)} %copy-done.2, f32[128,2048]{1,0:T(8,128)S(1)} %get-tuple-element.60.grad_ref, bf16[128,2048]{1,0:T(8,128)(2,1)S(1)} %bitcast.72), custom_call_target="tpu_custom_call" | custom-call | flops 1000000 | bytes 62914560 | tf_op jit(solution)/shard_map/pallas_call | solution.py:541
  543.9 3.8 all-to-all-start.3
  548.5 5.0 fusion.26.refs_0_
  553.5 2.4 copy.58.refs_2_
  555.9 5.4 convert_element_type.190
  563.3 2.6 all-to-all-done.3
  567.5 245.2 %shard_map.311 = (f32[320,2048]{1,0:T(8,128)}, f32[256,2560]{1,0:T(8,128)}, f32[256,2560]{1,0:T(8,128)}, f32[336,384]{1,0:T(8,128)}) custom-call(bf16[1,320,2048]{2,1,0:T(8,128)(2,1)} %fusion.26.refs_0_, bf16[1,256,2560]{2,1,0:T(8,128)(2,1)} %copy.57.refs_1_, bf16[1,256,2560]{2,1,0:T(8,128)(2,1)} %copy.58.refs_2_, bf16[1,336,384]{2,1,0:T(8,128)(2,1)} %pad_maximum_fusion.3.refs_3_), custom_call_target="tpu_custom_call" | custom-call | tf_op jit(solution)/shard_map/pallas_call | solution.py:735
  818.0 7.7 broadcast_multiply_fusion
  825.8 9.0 %convert_element_type.189 = f32[8,256,1536]{2,1,0:T(8,128)} convert(bf16[8,256,1536]{2,1,0:T(8,128)(2,1)} %all-reduce.7.cloned.1.call-done) | non-fusion elementwise | flops 3145728 | bytes 18874368 | tf_op jit(solution)/shard_map/convert_element_type | solution.py:825
  834.8 10.6 %slice_bitcast_fusion.1 = (f32[256,8,768]{2,0,1:T(8,128)}, f32[256,8,768]{2,0,1:T(8,128)}) fusion(f32[8,256,1536]{2,1,0:T(8,128)} %convert_element_type.189), kind=kLoop, calls=%fused_computation.10 | loop fusion | bytes 25165824 | tf_op jit(solution)/shard_map/transpose | solution.py:826
  845.4 6.6 copy.59
  852.0 6.6 copy.60
  858.5 12.7 %bitcast_multiply_fusion = (f32[256,6144]{0,1:T(8,128)}, f32[256]{0:T(256)}, f32[256,6144]{0,1:T(8,128)}) fusion(f32[256,8,768]{0,2,1:T(8,128)} %copy.60, f32[256]{0:T(256)S(1)} %convert_convert_fusion.4, bf16[256,6144]{0,1:T(8,128)(2,1)} %copy.53, bf16[256,6144]{0,1:T(8,128)(2,1)} %copy-done.10, f32[256,8,768]{0,2,1:T(8,128)} %copy.59), kind=kLoop, calls=%fused_computation.12 | loop fusion | flops 12582656 | bytes 31459328 | tf_op jit(solution)/shard_map/mul | solution.py:870
  871.3 6.6 copy.62
  877.8 6.6 copy.61
  885.2 3.5 copy.74
  (96 shorter events, 23.1 us)
Async XLA Ops:
  7.2 279.0 %all-gather.3.cloned.1.call-start = ((), (), s32[]{:S(2)}) async-start(), calls=%async_computation.9 | async-start | bytes 4718592 | tf_op jit(solution)/shard_map/all_gather | solution.py:787
  16.7 51.1 %all-to-all-start = ((bf16[8,256,640]{1,2,0:T(8,128)(2,1)}), bf16[8,256,640]{1,2,0:T(8,128)(2,1)}, u32[]{:S(2)}, u32[]{:S(2)}) async-start(bf16[8,256,640]{1,2,0:T(8,128)(2,1)} %maximum_bitcast_fusion.1), calls=%async_computation | async-start | bytes 5242880 | tf_op jit(solution)/shard_map/all_to_all | solution.py:52
  25.8 6.5 copy-start.10
  25.9 6.5 copy-start.21
  38.6 34.4 %copy-start.18 = (f32[320]{0:T(512)S(1)}, f32[320]{0:T(512)}, u32[]{:S(2)}) copy-start(f32[320]{0:T(512)} %param.25) | copy-start | bytes 3844
  38.6 34.4 %copy-start.19 = (f32[320]{0:T(512)S(1)}, f32[320]{0:T(512)}, u32[]{:S(2)}) copy-start(f32[320]{0:T(512)} %param.27) | copy-start | bytes 3844
  38.6 34.5 %copy-start.20 = (f32[320]{0:T(512)S(1)}, f32[320]{0:T(512)}, u32[]{:S(2)}) copy-start(f32[320]{0:T(512)} %param.29) | copy-start | bytes 3844
  38.6 34.5 %copy-start.14 = (f32[320]{0:T(512)S(1)}, f32[320]{0:T(512)}, u32[]{:S(2)}) copy-start(f32[320]{0:T(512)} %param.30) | copy-start | bytes 3844
  67.9 201.4 %all-to-all-start.1 = ((bf16[8,256,1536]{1,2,0:T(8,128)(2,1)}), bf16[8,256,1536]{1,2,0:T(8,128)(2,1)}, u32[]{:S(2)}, u32[]{:S(2)}) async-start(bf16[8,256,1536]{1,2,0:T(8,128)(2,1)} %maximum_bitcast_fusion), calls=%async_computation.1 | async-start | bytes 12582912 | tf_op jit(solution)/shard_map/all_to_all | solution.py:52
  72.6 3.6 copy-start.24
  72.6 3.6 copy-start
  72.7 102.4 %copy-start.17 = (f32[4,320]{1,0:T(4,128)S(1)}, f32[4,320]{1,0:T(4,128)}, u32[]{:S(2)}) copy-start(f32[4,320]{1,0:T(4,128)} %param.24) | copy-start | bytes 15364
  72.7 417.0 %all-reduce.5.cloned.1.call-start = ((), (), s32[]{:S(2)}) async-start(), calls=%async_computation.7 | async-start | bytes 6291456 | tf_op jit(solution)/shard_map/psum | solution.py:812
  172.3 0.7 copy-start.5
  173.1 2.0 copy-start.6
  208.1 2.2 copy-start.3
  267.2 2.0 copy-start.8
  286.1 9.3 %copy-start.9 = (bf16[1024,2048]{1,0:T(8,128)(2,1)S(1)}, bf16[1024,2048]{1,0:T(8,128)(2,1)}, u32[]{:S(2)}) copy-start(bf16[1024,2048]{1,0:T(8,128)(2,1)} %copy-done.8) | copy-start | bytes 12582916
  286.1 9.3 %copy-start.11 = (bf16[8,256,1536]{2,1,0:T(8,128)(2,1)S(1)}, bf16[8,256,1536]{2,1,0:T(8,128)(2,1)}, u32[]{:S(2)}) copy-start(bf16[8,256,1536]{2,1,0:T(8,128)(2,1)} %copy.54) | copy-start | bytes 18874372
  295.5 9.8 %copy-start.22 = (bf16[1,1024,2048]{2,1,0:T(8,128)(2,1)S(1)}, bf16[1,1024,2048]{2,1,0:T(8,128)(2,1)}, u32[]{:S(2)}) copy-start(bf16[1,1024,2048]{2,1,0:T(8,128)(2,1)} %all-gather.3.cloned.1.call-done) | copy-start | bytes 12582916
  310.1 251.3 %reduce-scatter.2.cloned.1.call-start = ((), (), s32[]{:S(2)}) async-start(), calls=%async_computation.6 | async-start | bytes 4718592 | tf_op jit(solution)/shard_map/reduce_scatter | solution.py:817
  318.0 1.4 copy-start.25
  330.6 159.1 %all-to-all-start.2 = ((bf16[8,256,1536]{2,1,0:T(8,128)(2,1)}), bf16[8,256,1536]{2,1,0:T(8,128)(2,1)}, u32[]{:S(2)}, u32[]{:S(2)}) async-start(bf16[8,256,1536]{2,1,0:T(8,128)(2,1)} %bitcast.81), calls=%async_computation.3 | async-start | bytes 12582912 | tf_op jit(solution)/shard_map/all_to_all | solution.py:40
  335.4 10.1 %copy-start.4 = (bf16[1,128,2048]{2,1,0:T(8,128)(2,1)S(1)}, bf16[1,128,2048]{2,1,0:T(8,128)(2,1)}, u32[]{:S(2)}) copy-start(bf16[1,128,2048]{2,1,0:T(8,128)(2,1)} %param.20) | copy-start | bytes 1572868
  335.4 490.3 %all-reduce.7.cloned.1.call-start = ((), (), s32[]{:S(2)}) async-start(), calls=%async_computation.8 | async-start | bytes 12582912 | tf_op jit(solution)/shard_map/psum | solution.py:825
  458.4 2.0 copy-start.1
  494.8 49.1 %all-to-all-start.4 = ((bf16[8,256,320]{1,2,0:T(8,128)(2,1)}), bf16[8,256,320]{1,2,0:T(8,128)(2,1)}, u32[]{:S(2)}, u32[]{:S(2)}) async-start(bf16[8,256,320]{1,2,0:T(8,128)(2,1)} %bitcast.85), calls=%async_computation.5 | async-start | bytes 2621440 | tf_op jit(solution)/shard_map/all_to_all | solution.py:40
  499.1 2.2 copy-start.2
  501.3 39.6 %copy-start.16 = (f32[4,320]{1,0:T(4,128)S(1)}, f32[4,320]{1,0:T(4,128)}, u32[]{:S(2)}) copy-start(f32[4,320]{1,0:T(4,128)} %get-tuple-element.67) | copy-start | bytes 15364
  501.3 39.7 %copy-start.15 = (f32[4,320]{1,0:T(4,128)S(1)}, f32[4,320]{1,0:T(4,128)}, u32[]{:S(2)}) copy-start(f32[4,320]{1,0:T(4,128)} %get-tuple-element.68) | copy-start | bytes 15364
  501.3 39.7 %copy-start.13 = (f32[2,160,160]{2,1,0:T(8,128)S(1)}, f32[2,160,160]{2,1,0:T(8,128)}, u32[]{:S(2)}) copy-start(f32[2,160,160]{2,1,0:T(8,128)} %get-tuple-element.65) | copy-start | bytes 614404
  501.3 39.7 %copy-start.12 = (f32[2,160,160]{2,1,0:T(8,128)S(1)}, f32[2,160,160]{2,1,0:T(8,128)}, u32[]{:S(2)}) copy-start(f32[2,160,160]{2,1,0:T(8,128)} %get-tuple-element.66) | copy-start | bytes 614404
  501.3 39.9 %copy-start.7 = (bf16[1024,2048]{1,0:T(8,128)(2,1)S(1)}, bf16[1024,2048]{1,0:T(8,128)(2,1)}, u32[]{:S(2)}) copy-start(bf16[1024,2048]{1,0:T(8,128)(2,1)} %copy-done.6) | copy-start | bytes 12582916
  501.3 39.9 %copy-start.23 = (bf16[1024,320]{1,0:T(8,128)(2,1)S(1)}, bf16[1024,320]{1,0:T(8,128)(2,1)}, u32[]{:S(2)}) copy-start(bf16[1024,320]{1,0:T(8,128)(2,1)} %get-tuple-element.63) | copy-start | bytes 1966084
  543.9 21.9 %all-to-all-start.3 = ((bf16[8,256,320]{1,2,0:T(8,128)(2,1)}), bf16[8,256,320]{1,2,0:T(8,128)(2,1)S(1)}, u32[]{:S(2)}, u32[]{:S(2)}) async-start(bf16[8,256,320]{1,2,0:T(8,128)(2,1)} %bitcast.69), calls=%async_computation.4 | async-start | bytes 2621440 | tf_op jit(solution)/shard_map/all_to_all | solution.py:40
Sparse Core Ops, SparseCore 0:
  9.9 59.8 all-gather.2
  310.2 121.0 all-reduce.4
  434.7 50.3 reduce-scatter.1
  489.8 302.1 all-reduce.6

commit v6 on v5

--- a/solution.py
+++ b/solution.py
@@ -34,22 +34,14 @@
     return item.astype(bf16).astype(f32)
 
 
-def swap_columns(grad):
+def by_owner(weight, gain):
     owners = lax.axis_size(GROUP)
-    cut = grad.astype(bf16).reshape(owners, grad.shape[0] // owners, grad.shape[1])
+    scaled = (low(weight) * gain).astype(bf16)
+    return jnp.swapaxes(scaled.reshape(weight.shape[0], owners, -1), 0, 1)
+
+
+def swap(cut):
     return lax.all_to_all(cut, GROUP, split_axis=0, concat_axis=0, tiled=True)
-
-
-def side_by_side(cut):
-    return jnp.swapaxes(cut, 0, 1).reshape(1, cut.shape[1], -1)
-
-
-def to_columns(weights, gain):
-    owners = lax.axis_size(GROUP)
-    rows = weights[0].shape[0]
-    scaled = [(low(item) * gain).astype(bf16).reshape(rows, owners, -1) for item in weights]
-    cut = jnp.swapaxes(jnp.concatenate(scaled, 2), 0, 1)
-    return lax.all_to_all(cut, GROUP, split_axis=0, concat_axis=0, tiled=True).reshape(rows * owners, -1)
 
 
 def gelu_parts(x):
@@ -79,6 +71,11 @@
 
 def dot_tn(a, b):
     return lax.dot_general(a, b, (((0,), (0,)), ((), ())), preferred_element_type=f32)
+
+
+def whole_weight(ref, part):
+    owners, _, rows, width = ref.shape
+    return ref[:, part].reshape(owners * rows, width)
 
 
 def fill_blocks(target, source):
@@ -144,7 +141,7 @@
 
 
 def mix_forward_kernel(
-    sequences, length, n_ref, wb_ref, wi_ref, label_ref, conv_ref, bias_ref, rw_ref, iw_ref, ow_ref,
+    sequences, length, n_ref, w_ref, label_ref, conv_ref, bias_ref, rw_ref, iw_ref, ow_ref,
     partial_ref, product_ref, pre_ref, conv_in_ref, values_ref, recur_ref, inject_ref, decay_ref, states_ref,
     pad, lines, rbig, ibig,
 ):
@@ -161,8 +158,8 @@
         here = pl.ds(base, length)
         rows = n_ref[here, :]
         masks = label_masks(label_ref, here, length, width, taps, lines)
-        pre_ref[here, :] = dot_nn(rows, wb_ref[...])
-        conv_in = dot_nn(rows, wi_ref[...]).astype(bf16)
+        pre_ref[here, :] = dot_nn(rows, whole_weight(w_ref, 0))
+        conv_in = dot_nn(rows, whole_weight(w_ref, 1)).astype(bf16)
         conv_in_ref[here, :] = conv_in
         pad[8 : 8 + length, :] = conv_in.astype(f32)
         total = bias_ref[0:1, :] + conv_ref[0:1, :] * pad[8 : 8 + length, :]
@@ -196,8 +193,8 @@
     lax.fori_loop(0, sequences, two, 0)
 
 
-def mix_forward(sequences, normed, wb, wi, labels, conv, bias, rw, iw, ow):
-    total, width = normed.shape[0], wb.shape[1]
+def mix_forward(sequences, normed, weights, labels, conv, bias, rw, iw, ow):
+    total, width = normed.shape[0], weights.shape[3]
     length = total // sequences
     depth = ow.shape[1]
     shape = jax.ShapeDtypeStruct
@@ -208,7 +205,7 @@
         out_shape=(
             shape((total, depth), bf16), like(bf16), like(f32), like(bf16), like(bf16), like(f32), like(f32), tiled, tiled,
         ),
-        in_specs=[VM] * 9,
+        in_specs=[VM] * 8,
         out_specs=[VM] * 9,
         scratch_shapes=[
             pltpu.VMEM((8 + length, width), f32),
@@ -218,11 +215,11 @@
         ],
         compiler_params=pltpu.CompilerParams(vmem_limit_bytes=56 * 2**20),
         cost_estimate=pl.CostEstimate(flops=2 * total * width * 3 * depth, bytes_accessed=20 * 2**20, transcendentals=total * width * 5),
-    )(normed, wb, wi, labels, conv, bias, rw, iw, ow)
+    )(normed, weights, labels, conv, bias, rw, iw, ow)
 
 
 def mix_backward_kernel(
-    sequences, length, mid_ref, ow_ref, wb_ref, wi_ref, pre_ref, conv_in_ref, values_ref, recur_ref, inject_ref, decay_ref, states_ref,
+    sequences, length, mid_ref, ow_ref, w_ref, pre_ref, conv_in_ref, values_ref, recur_ref, inject_ref, decay_ref, states_ref,
     label_ref, conv_ref, bias_ref, rw_ref, iw_ref,
     partial_ref, branch_low_ref, conv_low_ref, dconv_ref, sums_ref, drw_ref, diw_ref,
     adj, pad, lines, rbig, ibig, dr, di,
@@ -292,7 +289,7 @@
             total = total + pad[k : k + length, :]
         conv_low = total.astype(bf16)
         conv_low_ref[here, :] = conv_low
-        partial_ref[here, :] = (dot_nt(branch_low_ref[here, :], wb_ref[...]) + dot_nt(conv_low, wi_ref[...])).astype(bf16)
+        partial_ref[here, :] = (dot_nt(branch_low_ref[here, :], whole_weight(w_ref, 0)) + dot_nt(conv_low, whole_weight(w_ref, 1))).astype(bf16)
         return 0
 
     lax.fori_loop(0, sequences, two, 0)
@@ -303,7 +300,7 @@
         diw_ref[h] = di[cut, cut]
 
 
-def mix_backward(sequences, mid_low, ow, wb, wi, pre, conv_in, values, recur, inject, decay, states, labels, conv, bias, rw, iw):
+def mix_backward(sequences, mid_low, ow, weights, pre, conv_in, values, recur, inject, decay, states, labels, conv, bias, rw, iw):
     total, depth = mid_low.shape
     width = ow.shape[0]
     length = total // sequences
@@ -314,7 +311,7 @@
             shape((total, depth), bf16), shape((total, width), bf16), shape((total, width), bf16),
             shape(conv.shape, f32), shape((4, width), f32), shape(rw.shape, f32), shape(iw.shape, f32),
         ),
-        in_specs=[VM] * 16,
+        in_specs=[VM] * 15,
         out_specs=[VM] * 7,
         scratch_shapes=[
             pltpu.VMEM(states.shape, f32),
@@ -327,7 +324,7 @@
         ],
         compiler_params=pltpu.CompilerParams(vmem_limit_bytes=56 * 2**20),
         cost_estimate=pl.CostEstimate(flops=2 * total * width * 3 * depth, bytes_accessed=25 * 2**20, transcendentals=total * width * 5),
-    )(mid_low, ow, wb, wi, pre, conv_in, values, recur, inject, decay, states, labels, conv, bias, rw, iw)
+    )(mid_low, ow, weights, pre, conv_in, values, recur, inject, decay, states, labels, conv, bias, rw, iw)
 
 
 def plane():
@@ -362,7 +359,7 @@
     return ref.at[pl.ds(pl.multiple_of(index * rows, rows), rows), :]
 
 
-def scatter_sum(rows, partial, near, far, stage, acc, sems):
+def scatter_steps(rows, partial, near, far, stage, acc, sems):
     offsets, at, block = plane()
     near_sent, near_got, far_sent, far_got = sems
     count = len(offsets)
@@ -394,6 +391,7 @@
         if q:
             seconds[q] = remote(stage.at[q - 1], far.at[q - 1], far_sent.at[q - 1], far_got.at[q - 1], at(dy, ds))
             seconds[q].start()
+    yield None
     for q in order[:-1]:
         seconds[q].wait_recv()
 
@@ -403,10 +401,15 @@
             return 0
 
         lax.fori_loop(0, rows // 16, more, 0)
-    return [firsts[q].wait_send for q in order] + [seconds[q].wait_send for q in order[:-1]]
-
-
-def gather_blocks(rows, whole, sems):
+    yield [firsts[q].wait_send for q in order] + [seconds[q].wait_send for q in order[:-1]]
+
+
+def scatter_sum(*args):
+    *_, waits = scatter_steps(*args)
+    return waits
+
+
+def gather_steps(rows, whole, sems):
     offsets, at, block = plane()
     near_sent, near_got, far_sent, far_got = sems
     count = len(offsets)
@@ -422,6 +425,7 @@
     hand.start()
     sends.append(hand.wait_send)
     arrivals = [hand.wait_recv]
+    yield None
     for q in list(range(1, count)):
         dy, ds = offsets[q]
         outs[q].wait_recv()
@@ -430,7 +434,12 @@
         hand.start()
         sends.append(hand.wait_send)
         arrivals.append(hand.wait_recv)
-    return arrivals + sends
+    yield arrivals + sends
+
+
+def gather_blocks(*args):
+    *_, waits = gather_steps(*args)
+    return waits
 
 
 def root_mean(rows):
@@ -487,11 +496,13 @@
         wait()
 
 
-def backward_kernel(partial, middle_ref, cot_ref, low_ref, grad_ref, near, far, stage, acc, *sems):
+def backward_steps(partial, middle_ref, cot_ref, low_ref, grad_ref, near, far, stage, acc, *sems):
     rows = middle_ref.shape[0]
     offsets, at, block = plane()
-    greet(offsets, at)
-    waits = scatter_sum(rows, partial, near, far, stage, acc, sems[:4])
+    scatter = scatter_steps(rows, partial, near, far, stage, acc, sems[:4])
+    next(scatter)
+    yield
+    waits = next(scatter)
     base = block(0, 0) * rows
 
     def norm(here, i):
@@ -503,16 +514,21 @@
         low_ref[there, :] = grad.astype(bf16)
 
     by_tiles(rows, norm)
-    waits = waits + gather_blocks(rows, low_ref, sems[4:])
+    gather = gather_steps(rows, low_ref, sems[4:])
+    next(gather)
+    yield
+    waits = waits + next(gather)
+    yield
     for wait in waits:
         wait()
 
 
-def last_kernel(partial, grad_ref, x_ref, out_ref, near, far, stage, acc, *sems):
+def last_steps(partial, grad_ref, x_ref, out_ref, near, far, stage, acc, *sems):
     rows = x_ref.shape[0]
-    offsets, at, block = plane()
-    greet(offsets, at)
-    waits = scatter_sum(rows, partial, near, far, stage, acc, sems[:4])
+    scatter = scatter_steps(rows, partial, near, far, stage, acc, sems[:4])
+    next(scatter)
+    yield
+    waits = next(scatter)
 
     def norm(here, i):
         value = x_ref[here, :].astype(f32)
@@ -521,11 +537,12 @@
         out_ref[here, :] = grad.astype(bf16)
 
     by_tiles(rows, norm)
+    yield
     for wait in waits:
         wait()
 
 
-def exchange(kernel, identity, inputs, outs, rows, depth, gathers, scatters):
+def plane_scratch(rows, depth, gathers, scatters):
     count = lax.axis_size("seq") * lax.axis_size("shard") // 2
     block = (rows, depth)
     scratch = []
@@ -538,12 +555,16 @@
         ]
     for _ in range(scatters + gathers):
         scratch += [pltpu.SemaphoreType.DMA((count,))] * 2 + [pltpu.SemaphoreType.DMA((count - 1,))] * 2
+    return scratch
+
+
+def exchange(kernel, identity, inputs, outs, rows, depth, gathers, scatters):
     return pl.pallas_call(
         kernel,
         out_shape=tuple(jax.ShapeDtypeStruct(shape, kind) for shape, kind in outs),
         in_specs=[VM] * len(inputs),
         out_specs=[VM] * len(outs),
-        scratch_shapes=scratch,
+        scratch_shapes=plane_scratch(rows, depth, gathers, scatters),
         compiler_params=pltpu.CompilerParams(
             collective_id=identity, has_side_effects=True, vmem_limit_bytes=40 * 2**20
         ),
@@ -558,65 +579,82 @@
     return count
 
 
-def line_kernel(n, cuts, paired, *refs):
+def line_kernel(n, kinds, cuts, beside, turns, extra, *refs):
     ins = len(cuts)
-    own_hbm = refs[:ins]
-    made = ins if paired is None else ins + 1
-    outs = refs[ins : ins + made]
-    scratch = refs[ins + made :]
+    made = ins + kinds.count("pair")
+    extra_ins, extra_outs, extra_scratch = extra
+    refs = list(refs)
+
+    def take(count):
+        taken = refs[:count]
+        del refs[:count]
+        return taken
+
+    own_hbm, side_in = take(ins), take(extra_ins)
+    outs, side_out = take(made), take(extra_outs)
+    side_scratch, scratch = take(extra_scratch), refs
     own, from_out, from_in = scratch[:ins], scratch[ins : 2 * ins], scratch[2 * ins : 3 * ins]
-    stage, load_sem, stage_sem, sent_in, sent_out, got_out, got_in = scratch[3 * ins :]
+    columns = [k for k in range(ins) if kinds[k] != "row"]
+    swapped = dict(zip(columns, scratch[3 * ins :]))
+    load_sem, sent_in, sent_out, got_out, got_in, sent_x, got_x, out_sem = scratch[3 * ins + len(columns) :]
     me = lax.axis_index("replica")
+    y, s = lax.axis_index("seq"), lax.axis_index("shard")
+    shards = lax.axis_size("shard")
+    owners = shards * lax.axis_size("seq")
     left = me < n // 2
     inward = jnp.where(left, me + 1, me - 1)
     outward = jnp.where(left, me - 1, me + 1)
     has_out = jnp.logical_and(me > 0, me < n - 1)
     middle = jnp.logical_or(me == n // 2 - 1, me == n // 2)
 
+    def peer(i):
+        return {"seq": jnp.bitwise_xor(y, i // shards), "shard": jnp.bitwise_xor(s, i % shards)}
+
+    def place(i):
+        return jnp.bitwise_xor(y, i // shards) * shards + jnp.bitwise_xor(s, i % shards)
+
     loads = [pltpu.make_async_copy(own_hbm[k], own[k], load_sem.at[k]) for k in range(ins)]
     for load in loads:
         load.start()
     barrier = pltpu.get_barrier_semaphore()
+    for i in range(1, owners):
+        pl.semaphore_signal(barrier, inc=1, device_id=peer(i), device_id_type=MESH)
     pl.semaphore_signal(barrier, inc=1, device_id={"replica": inward}, device_id_type=MESH)
 
     @pl.when(has_out)
     def _():
         pl.semaphore_signal(barrier, inc=1, device_id={"replica": outward}, device_id_type=MESH)
-        pl.semaphore_wait(barrier, 2)
+        pl.semaphore_wait(barrier, owners + 1)
 
     @pl.when(jnp.logical_not(has_out))
     def _():
-        pl.semaphore_wait(barrier, 1)
+        pl.semaphore_wait(barrier, owners)
 
     chunks = []
     for k, (lead, count, rows) in enumerate(cuts):
-        for j in range(lead):
+        for step in range(lead):
             for i in range(count):
-                chunks.append((k, j, i * rows, rows))
-    slots = stage.shape[0]
+                chunks.append((k, step if kinds[k] == "row" else (step + 1) % lead, i * rows, rows))
+    total = len(chunks)
     ready = set()
 
-    def view(group, c):
-        k, j, start, rows = chunks[c]
-        return group[k].at[j, pl.ds(start, rows), :]
+    def view(group, c, index=None):
+        k, i, start, rows = chunks[c]
+        if index is None:
+            index = 0 if kinds[k] == "row" else place(i)
+        return group[k].at[index, pl.ds(start, rows), :]
 
     def push(group, target, c, sent, got, device):
-        return pltpu.make_async_remote_copy(
-            src_ref=view(group, c),
-            dst_ref=view(target, c),
-            send_sem=sent.at[c],
-            recv_sem=got.at[c],
-            device_id={"replica": device},
-            device_id_type=MESH,
-        )
+        return remote(view(group, c), view(target, c), sent.at[c], got.at[c], {"replica": device})
 
     def add(target, other, c):
-        k, j, start, rows = chunks[c]
-
-        def tile(i, _):
-            here = pl.ds(pl.multiple_of(start + i * 16, 16), 16)
-            total = target[k][j, here, :].astype(f32) + other[k][j, here, :].astype(f32)
-            target[k][j, here, :] = total.astype(bf16)
+        k, i, start, rows = chunks[c]
+        index = 0 if kinds[k] == "row" else place(i)
+
+        def tile(t, _):
+            here = pl.ds(pl.multiple_of(start + t * 16, 16), 16)
+            both = target[k][index, here, :].astype(f32) + other[k][index, here, :].astype(f32)
+            target[k][index, here, :] = both.astype(bf16)
             return 0
 
         lax.fori_loop(0, rows // 16, tile, 0)
@@ -643,37 +681,41 @@
     @pl.when(jnp.logical_not(has_out))
     def _():
         seen = set()
-        for c in range(len(chunks)):
+        for c in range(total):
             if chunks[c][0] not in seen:
                 loads[chunks[c][0]].wait()
                 seen.add(chunks[c][0])
             pass_in(c)
 
-    def stage_copies(c):
-        k, j, start, rows = chunks[c]
-        slot = c % slots
-        columns = own[k].shape[2]
-        if k == paired:
-            half = columns // 2
-            return [
-                pltpu.make_async_copy(
-                    stage.at[slot, pl.ds(0, rows), pl.ds(side * half, half)],
-                    outs[k + side].at[pl.ds(start, rows), pl.ds(j * half, half)],
-                    stage_sem.at[slot, side],
-                )
-                for side in range(2)
-            ]
-        where = k if paired is None or k < paired else k + 1
+    def crosses(c):
+        return kinds[chunks[c][0]] != "row" and chunks[c][1] != 0
+
+    def hand_over(c):
+        k, i, start, rows = chunks[c]
+        return remote(
+            view(from_in, c), view(swapped, c, place(0)), sent_x.at[c], got_x.at[c], peer(i)
+        )
+
+    def stores(c):
+        k, i, start, rows = chunks[c]
+        here = pl.ds(start, rows)
+        first = k + kinds[:k].count("pair")
+        if kinds[k] == "row":
+            return [pltpu.make_async_copy(from_in[k].at[0, here, :], outs[first].at[here, :], out_sem.at[c, 0])]
+        source = swapped[k] if i else from_in[k]
+        index = place(i)
+        if kinds[k] == "side":
+            return [pltpu.make_async_copy(source.at[index, here, :], outs[first].at[index, here, :], out_sem.at[c, 0])]
+        half = source.shape[2] // 2
+        there = pl.ds(pl.multiple_of(index * half, half), half)
         return [
             pltpu.make_async_copy(
-                stage.at[slot, pl.ds(0, rows), pl.ds(0, columns)],
-                outs[where].at[pl.ds(start, rows), :],
-                stage_sem.at[slot, 0],
+                source.at[index, here, pl.ds(part * half, half)], outs[first + part].at[here, there], out_sem.at[c, part]
             )
+            for part in range(2)
         ]
 
     def give_back(c):
-        k, j, start, rows = chunks[c]
         push(own, from_in, c, sent_out, got_in, inward).wait_recv()
 
         @pl.when(middle)
@@ -684,33 +726,37 @@
         def _():
             push(from_in, from_in, c, sent_out, got_in, outward).start()
 
-        if c >= slots:
-            for copy in stage_copies(c - slots):
-                copy.wait()
-        slot = c % slots
-        columns = own[k].shape[2]
-
-        def tile(i, _):
-            step = pl.multiple_of(i * 16, 16)
-            stage[slot, pl.ds(step, 16), 0:columns] = from_in[k][
-                j, pl.ds(pl.multiple_of(start + step, 16), 16), :
-            ].astype(f32)
-            return 0
-
-        lax.fori_loop(0, rows // 16, tile, 0)
-        for copy in stage_copies(c):
-            copy.start()
-
-    lag = 2
-    for c in range(len(chunks) + lag):
-        if c < len(chunks):
+        if crosses(c):
+            hand_over(c).start()
+        else:
+            for copy in stores(c):
+                copy.start()
+
+    def finish(c):
+        if crosses(c):
+            hand_over(c).wait_recv()
+            for copy in stores(c):
+                copy.start()
+
+    lag, later = 2, 5
+    work = beside(*side_in, *side_out, *side_scratch)
+    for c in range(total + later):
+        for turn in turns:
+            if turn == c:
+                next(work)
+        if c < total:
             gather_in(c)
-        if c >= lag:
+        if 0 <= c - lag < total:
             give_back(c - lag)
-    for c in range(max(0, len(chunks) - slots), len(chunks)):
-        for copy in stage_copies(c):
+        if 0 <= c - later < total:
+            finish(c - later)
+    for _ in work:
+        pass
+    for c in range(total):
+        for copy in stores(c):
             copy.wait()
-    for c in range(len(chunks)):
+        if crosses(c):
+            hand_over(c).wait_send()
         push(own, from_in, c, sent_in, got_in, inward).wait_send()
 
         @pl.when(has_out)
@@ -718,36 +764,118 @@
             push(from_in, from_in, c, sent_out, got_in, outward).wait_send()
 
 
-def replica_sum(arrays, paired, copies):
-    cuts, outs = [], []
-    stage_rows = stage_columns = 0
-    for k, item in enumerate(arrays):
-        lead, rows, columns = item.shape
-        count = pieces(rows, max(16, (210 * 1024) // columns // 16 * 16))
-        cuts.append((lead, count, rows // count))
-        stage_rows, stage_columns = max(stage_rows, rows // count), max(stage_columns, columns)
-        if k == paired:
-            outs += [jax.ShapeDtypeStruct((rows, lead * columns // 2), f32)] * 2
+def replica_sum(arrays, kinds, identity, beside, turns, inputs, results, rows, depth, gathers):
+    cuts, outs, swaps = [], [], []
+    for item, kind in zip(arrays, kinds):
+        lead, height, columns = item.shape
+        count = pieces(height, max(16, (210 * 1024) // columns // 16 * 16))
+        cuts.append((lead, count, height // count))
+        if kind == "pair":
+            outs += [jax.ShapeDtypeStruct((height, lead * columns // 2), bf16)] * 2
+        elif kind == "side":
+            outs.append(jax.ShapeDtypeStruct(item.shape, bf16))
         else:
-            outs.append(jax.ShapeDtypeStruct((rows, columns), f32))
+            outs.append(jax.ShapeDtypeStruct((height, columns), bf16))
+        if kind != "row":
+            swaps.append(pltpu.VMEM(item.shape, bf16))
     count = sum(lead * cut for lead, cut, _ in cuts)
     buffers = [pltpu.VMEM(item.shape, bf16) for item in arrays]
+    side_scratch = plane_scratch(rows, depth, gathers, 1)
     return pl.pallas_call(
-        functools.partial(line_kernel, copies, tuple(cuts), paired),
-        out_shape=tuple(outs),
-        in_specs=[ANY] * len(arrays),
-        out_specs=[ANY] * len(outs),
-        scratch_shapes=buffers * 3
-        + [
-            pltpu.VMEM((3, stage_rows, stage_columns), f32),
-            pltpu.SemaphoreType.DMA((len(arrays),)),
-            pltpu.SemaphoreType.DMA((3, 2)),
-        ]
-        + [pltpu.SemaphoreType.DMA((count,))] * 4,
+        functools.partial(
+            line_kernel, lax.axis_size("replica"), tuple(kinds), tuple(cuts), beside, turns,
+            (len(inputs), len(results), len(side_scratch)),
+        ),
+        out_shape=tuple(outs) + tuple(jax.ShapeDtypeStruct(shape, kind) for shape, kind in results),
+        in_specs=[ANY] * len(arrays) + [VM] * len(inputs),
+        out_specs=[ANY] * len(outs) + [VM] * len(results),
+        scratch_shapes=side_scratch
+        + buffers * 3
+        + swaps
+        + [pltpu.SemaphoreType.DMA((len(arrays),))]
+        + [pltpu.SemaphoreType.DMA((count,))] * 6
+        + [pltpu.SemaphoreType.DMA((count, 2))],
         compiler_params=pltpu.CompilerParams(
-            collective_id=7, has_side_effects=True, vmem_limit_bytes=60 * 2**20
+            collective_id=identity, has_side_effects=True, vmem_limit_bytes=60 * 2**20
         ),
-    )(*arrays)
+        cost_estimate=pl.CostEstimate(flops=10**6, bytes_accessed=200 * 2**20, transcendentals=0),
+    )(*arrays, *inputs)
+
+
+def finish_pair_kernel(gain_ref, a_ref, b_ref, wa_ref, wb_ref, outa_ref, outb_ref, grad_ref):
+    grad = jnp.zeros(gain_ref.shape, f32)
+    for sum_ref, weight_ref, out_ref in ((a_ref, wa_ref, outa_ref), (b_ref, wb_ref, outb_ref)):
+        total = sum_ref[...].astype(f32)
+        out_ref[...] = total * gain_ref[...]
+        grad = grad + jnp.sum(total * low(weight_ref[...]), axis=1, keepdims=True)
+    grad_ref[...] = grad
+
+
+def finish_pair(gain, a, b, wa, wb):
+    rows, columns = wa.shape
+    cut = min(rows, 32)
+    wide = pl.BlockSpec((cut, columns), lambda i: (i, 0))
+    thin = pl.BlockSpec((cut, 1), lambda i: (i, 0))
+    out = jax.ShapeDtypeStruct((rows, columns), f32)
+    return pl.pallas_call(
+        finish_pair_kernel,
+        grid=(rows // cut,),
+        out_shape=(out, out, jax.ShapeDtypeStruct((rows, 1), f32)),
+        in_specs=[thin, wide, wide, wide, wide],
+        out_specs=[wide, wide, thin],
+        compiler_params=pltpu.CompilerParams(vmem_limit_bytes=40 * 2**20),
+        cost_estimate=pl.CostEstimate(flops=6 * rows * columns, bytes_accessed=20 * rows * columns, transcendentals=0),
+    )(gain, a, b, wa, wb)
+
+
+def finish_rest_kernel(gain_ref, mix_ref, wa_ref, wb_ref, out_sum_ref, down_sum_ref, outa_ref, outb_ref, grad_ref, out_ref, down_ref):
+    owners, _, width = mix_ref.shape
+    width = width // 2
+    grad = jnp.zeros(gain_ref.shape, f32)
+    for part, (weight_ref, target_ref) in enumerate(((wa_ref, outa_ref), (wb_ref, outb_ref))):
+        total = jnp.concatenate(
+            [mix_ref[j, :, part * width : (part + 1) * width].astype(f32) for j in range(owners)], axis=1
+        )
+        target_ref[...] = total * gain_ref[...]
+        grad = grad + jnp.sum(total * low(weight_ref[...]), axis=1, keepdims=True)
+    grad_ref[...] = grad
+    out_ref[...] = out_sum_ref[...].astype(f32)
+    down_ref[...] = down_sum_ref[...].astype(f32)
+
+
+def finish_rest(gain, mix, wa, wb, out_sum, down_sum):
+    rows, columns = wa.shape
+    steps = 4
+    while out_sum.shape[0] % (16 * steps) or down_sum.shape[0] % (16 * steps) or rows % (16 * steps):
+        steps //= 2
+
+    def tall(item):
+        return pl.BlockSpec((item.shape[0] // steps, item.shape[1]), lambda i: (i, 0))
+
+    owners, _, both = mix.shape
+    wide, thin = tall(wa), tall(gain)
+    return pl.pallas_call(
+        finish_rest_kernel,
+        grid=(steps,),
+        out_shape=(
+            jax.ShapeDtypeStruct(wa.shape, f32),
+            jax.ShapeDtypeStruct(wa.shape, f32),
+            jax.ShapeDtypeStruct((rows, 1), f32),
+            jax.ShapeDtypeStruct(out_sum.shape, f32),
+            jax.ShapeDtypeStruct(down_sum.shape, f32),
+        ),
+        in_specs=[
+            thin,
+            pl.BlockSpec((owners, rows // steps, both), lambda i: (0, i, 0)),
+            wide,
+            wide,
+            tall(out_sum),
+            tall(down_sum),
+        ],
+        out_specs=[wide, wide, thin, tall(out_sum), tall(down_sum)],
+        compiler_params=pltpu.CompilerParams(vmem_limit_bytes=40 * 2**20),
+        cost_estimate=pl.CostEstimate(flops=10**7, bytes_accessed=40 * 2**20, transcendentals=0),
+    )(gain, mix, wa, wb, out_sum, down_sum)
 
 
 def body(
@@ -780,10 +908,11 @@
     unit_all, labels = exchange(
         start_kernel, 1, (x, own_labels), (((total, depth), bf16), ((total, 128), bf16)), rows, depth, 2, 0
     )
-    mix_w = to_columns([branch_weight, input_weight], gain)
-    pair_w = to_columns([gate_weight, up_weight], mlp_gain)
+    mix_w = swap(jnp.stack([by_owner(branch_weight, gain), by_owner(input_weight, gain)], 1))
+    pair_cut = jnp.concatenate([by_owner(gate_weight, mlp_gain), by_owner(up_weight, mlp_gain)], 2)
+    unit_all, pair_cut = lax.optimization_barrier((unit_all, pair_cut))
+    pair_w = swap(pair_cut).reshape(depth, -1)
     width = branch_weight.shape[1] // members
-    branch_w, input_w = mix_w[:, :width], mix_w[:, width:]
     out_low = lax.all_gather(cot, ROWS, axis=0, tiled=True)
     output_w = output_weight.astype(bf16)
     down_w = down_weight.astype(bf16)
@@ -792,7 +921,7 @@
     decay_f = low(decay_param)
     bias = jnp.stack([low(conv_bias), low(recur_gate_bias), low(input_gate_bias), jax.nn.softplus(-decay_f)])
     mixed = mix_forward(
-        sequences, unit_all, branch_w, input_w, labels, conv_f, bias, recur_gate_weight, input_gate_weight, output_w
+        sequences, unit_all, mix_w, labels, conv_f, bias, recur_gate_weight, input_gate_weight, output_w
     )
     partial, product = mixed[:2]
     whole = ((total, depth), bf16)
@@ -809,27 +938,24 @@
     up_low = (hidden_grad * gate_act).astype(bf16)
     pair_low = jnp.concatenate([gate_low, up_low], 1)
     partial = mm_nt(pair_low, pair_w).astype(bf16)
-    down_sum = lax.psum(mm_tn(hidden, out_low).astype(bf16), "replica")
-    pair_partial = swap_columns(mm_tn(unit_two, pair_low))
-    mid_low, middle_grad = exchange(
-        backward_kernel, 3, (partial, middle, cot), (whole, ((rows, depth), f32)), rows, depth, 1, 1
+    pair_partial = mm_tn(unit_two, pair_low).astype(bf16).reshape(members, -1, 2 * ff)
+    down_partial = mm_tn(hidden, out_low).astype(bf16)
+    gate_sum, up_sum, mid_low, middle_grad = replica_sum(
+        [pair_partial], ["pair"], 3, backward_steps, (0, 3, 6),
+        (partial, middle, cot), (whole, ((rows, depth), f32)), rows, depth, 1,
     )
+    mid_low, down_partial = lax.optimization_barrier((mid_low, down_partial))
+    down_sum = lax.psum(down_partial, "replica")
+    gate_grad, up_grad, mlp_gain_grad = finish_pair(mlp_gain, gate_sum, up_sum, gate_weight, up_weight)
     block_sum = lax.psum_scatter(mm(hidden, down_w).astype(bf16), ROWS, scatter_dimension=0, tiled=True)
     block_out = (middle + block_sum.astype(f32)).astype(bf16)
     output_partial = mm_tn(product, mid_low).astype(bf16)[None]
     back = mix_backward(
-        sequences, mid_low, output_w, branch_w, input_w, *mixed[2:], labels, conv_f, bias, recur_gate_weight, input_gate_weight
+        sequences, mid_low, output_w, mix_w, *mixed[2:], labels, conv_f, bias, recur_gate_weight, input_gate_weight
     )
     partial, branch_low, conv_low, conv_weight_grad, sums, recur_weight_grad, inject_weight_grad = back
-    down_sum, pair_partial, branch_low = lax.optimization_barrier((down_sum, pair_partial, branch_low))
-    pair_sum = lax.psum(pair_partial, "replica").astype(f32)
-    gate_grad = jnp.swapaxes(pair_sum[:, :, :ff], 0, 1).reshape(-1, members * ff)
-    up_grad = jnp.swapaxes(pair_sum[:, :, ff:], 0, 1).reshape(-1, members * ff)
-    branch_partial = side_by_side(swap_columns(mm_tn(unit_all, branch_low)))
-    input_partial = side_by_side(swap_columns(mm_tn(unit_all, conv_low)))
-    (tokens_grad,) = exchange(
-        last_kernel, 4, (partial, middle_grad, x), (((rows, depth), bf16),), rows, depth, 0, 1
-    )
+    mix_low = jnp.concatenate([branch_low, conv_low], 1)
+    mix_partial = mm_tn(unit_all, mix_low).astype(bf16).reshape(members, -1, 2 * width)
     size = recur_gate_weight.shape[1]
     gates = jnp.concatenate([recur_weight_grad, inject_weight_grad], 2).reshape(width, 2 * size)
     lanes = -(-max(width, 2 * size) // 128) * 128
@@ -841,22 +967,25 @@
         ],
         0,
     ).astype(bf16)[None]
-    output_grad, branch_grad, input_grad, packed = replica_sum(
-        [output_partial, branch_partial, input_partial, packed], None, lax.axis_size("replica")
+    output_sum, mix_sum, packed, tokens_grad = replica_sum(
+        [output_partial, mix_partial, packed], ["row", "side", "row"], 4, last_steps, (0, 3),
+        (partial, middle_grad, x), (((rows, depth), bf16),), rows, depth, 0,
+    )
+    packed = packed.astype(f32)
+    branch_grad, input_grad, gain_grad, output_grad, down_grad = finish_rest(
+        gain, mix_sum, branch_weight, input_weight, output_sum, down_sum
     )
     recur_weight_grad = packed[:width, :size].reshape(-1, size, size)
     inject_weight_grad = packed[:width, size : 2 * size].reshape(-1, size, size)
     conv_weight_grad = packed[width : width + conv_weight.shape[0], :width]
     conv_bias_grad, recur_bias_grad, inject_bias_grad, rate_grad = [packed[width + conv_weight.shape[0] + i, :width] for i in range(4)]
     decay_param_grad = rate_grad * decay_scale * jax.nn.sigmoid(-decay_f)
-    gain_grad = jnp.sum(branch_grad * low(branch_weight) + input_grad * low(input_weight), axis=1)
-    mlp_gain_grad = jnp.sum(gate_grad * low(gate_weight) + up_grad * low(up_weight), axis=1)
     return (
         block_out[None],
         tokens_grad[None],
-        gain_grad,
-        branch_grad * gain,
-        input_grad * gain,
+        gain_grad[:, 0],
+        branch_grad,
+        input_grad,
         conv_weight_grad,
         conv_bias_grad,
         recur_weight_grad,
@@ -865,10 +994,10 @@
         inject_bias_grad,
         decay_param_grad,
         output_grad,
-        mlp_gain_grad,
-        gate_grad * mlp_gain,
-        up_grad * mlp_gain,
-        down_sum.astype(f32),
+        mlp_gain_grad[:, 0],
+        gate_grad,
+        up_grad,
+        down_grad,
     )
 
 

time: 900 us -> 747 us (0.83)
  local copies, waits for them, and re-layouts: 93.5 us -> 54.3 us
  Pallas kernels: 603 us -> 571 us
  waiting for transfers between devices: 32.5 us -> 0.72 us
  other arithmetic: 56.3 us -> 25.7 us
  starting transfers between devices: 23.3 us -> 10.5 us
    pallas_call x4 -> x2, Pallas kernels: 305 us -> 149 us  [exchange(): pl.pallas_call(kernel, out_shape=tuple((jax.ShapeDtypeStruct(shape, kind)...]
    pallas_call x1 -> x4, Pallas kernels: 245 us -> 369 us  [the longest x2 353 us: replica_sum(): pl.pallas_call(functools.partial(line_kernel, lax.axis_size('replica'), t...]
    all_to_all x5 -> x2, waiting for transfers between devices: 31.8 us -> 0.01 us  [swap(): return lax.all_to_all(cut, GROUP, split_axis=0, concat_axis=0, tiled=True)]
    transpose x3 -> x0, local copies, waits for them, and re-layouts: 23.8 us -> none  [the longest x2 17.2 us: body(): jnp.swapaxes(pair_sum[:, :, :ff], 0, 1).reshape(-1, members * ff)]
    mul x2 -> x0, other arithmetic: 20.4 us -> none  [the longest x1 12.7 us: body(): up_grad * mlp_gain]
    convert_element_type x4 -> x3, other arithmetic: 21.8 us -> 8.12 us  [the longest x2 6.35 us: by_owner(): scaled = (low(weight) * gain).astype(bf16)]
    all_to_all x5 -> x2, starting transfers between devices: 22.8 us -> 10.2 us  [swap(): return lax.all_to_all(cut, GROUP, split_axis=0, concat_axis=0, tiled=True)]
    dot_general x5 -> x4, matrix products: 26.6 us -> 24.1 us  [mm_tn(): lax.dot_general(left, right, (((0,), (0,)), ((), ())), preferred_element_...]
  transfers between devices with their start and end apart: 9 -> 5, of which waited for: 2 -> 0; matrix products, arithmetic and copies ran while one was open for 14% -> 11% of each run, Pallas kernels for 67% -> 54%
where the time goes in v6:
time: 747 us; the launch traced here: 742 us
  Pallas kernels  571 us (76%)
  matrix products  64.4 us (9%)
  local copies, waits for them, and re-layouts  54.3 us (7%)
  other arithmetic  25.7 us (3%)
  between operations  14.6 us (2%)
  starting transfers between devices  10.5 us (1%)
    pallas_call x2, Pallas kernels, replica_sum(): pl.pallas_call(functools.partial(line_kernel, lax.axis_size('replica'), t...  353 us
    pallas_call x2, Pallas kernels, exchange(): pl.pallas_call(kernel, out_shape=tuple((jax.ShapeDtypeStruct(shape, kind)...  149 us
    unnamed x71, local copies, waits for them, and re-layouts  38.7 us
    pallas_call x1, Pallas kernels, mix_backward(): pl.pallas_call(functools.partial(mix_backward_kernel, sequences, length),...  29.3 us
    dot_general x4, matrix products, mm_tn(): lax.dot_general(left, right, (((0,), (0,)), ((), ())), preferred_element_...  24.1 us
    pallas_call x1, Pallas kernels, mix_forward(): pl.pallas_call(functools.partial(mix_forward_kernel, sequences, length),...  23.5 us
    dot_general x3, matrix products, mm(): return jnp.dot(left, right, preferred_element_type=f32)  23.4 us
    dot_general x2, matrix products, mm_nt(): lax.dot_general(left, right, (((1,), (1,)), ((), ())), preferred_element_...  16.9 us
  transfers between devices with their start and end apart: 5, of which 0 were waited for; matrix products, arithmetic and copies ran while one was open for 11% of the time, Pallas kernels for 54%

profile of v6, /device:TPU:0, one launch (start us, length us, event | category | flops | bytes accessed | tf_op | source)
XLA Modules:
  0.0 741.5 jit_solution(15053996260912658123)
XLA Ops:
  8.7 2.8 copy.52
  11.4 1.5 copy.53
  13.0 2.2 multiply_convert_fusion.5
  15.4 1.7 copy.54
  17.1 5.3 all-to-all-start
  22.4 5.4 copy.50
  27.8 5.3 copy.51
  33.2 4.1 multiply_convert_fusion.1
  37.4 59.9 %shard_map.305 = (bf16[1024,2048]{1,0:T(8,128)(2,1)S(1)}, bf16[1024,128]{1,0:T(8,128)(2,1)S(1)}) custom-call(bf16[128,2048]{1,0:T(8,128)(2,1)S(1)} %bitcast.54, bf16[128,128]{1,0:T(8,128)(2,1)S(1)} %broadcast_in_dim.22.label_ref), custom_call_target="tpu_custom_call" | custom-call | flops 1000000 | bytes 62914560 | tf_op jit(solution)/shard_map/pallas_call | solution.py:562
  98.1 2.0 copy-done.13
  100.1 3.1 pad_maximum_fusion
  103.2 4.9 all-to-all-start.1
  108.5 3.0 convert_element_type.161.ow_ref
  112.1 2.8 copy.55.w_ref
  114.9 23.5 %shard_map.306 = (bf16[1024,2048]{1,0:T(8,128)(2,1)}, bf16[1024,320]{1,0:T(8,128)(2,1)}, f32[1024,320]{1,0:T(8,128)}, bf16[1024,320]{1,0:T(8,128)(2,1)}, bf16[10...) custom-call(bf16[1024,2048]{1,0:T(8,128)(2,1)} %copy-done.13, ...), custom_call_target="tpu_custom_call" | custom-call | flops 4026531840 | bytes 20971520 | tf_op jit(solution)/shard_map/pallas_call | solution.py:203
  138.4 2.2 copy-done.6
  140.6 89.5 %shard_map.307 = (bf16[1024,2048]{1,0:T(8,128)(2,1)S(1)}, f32[128,2048]{1,0:T(8,128)S(1)}) custom-call(bf16[1024,2048]{1,0:T(8,128)(2,1)S(1)} %copy-done.6, bf16[128,2048]{1,0:T(8,128)(2,1)S(1)} %bitcast.55), custom_call_target="tpu_custom_call" | custom-call | flops 1000000 | bytes 62914560 | tf_op jit(solution)/shard_map/pallas_call | solution.py:562
  230.1 1.0 copy-done.5
  231.1 2.0 copy-done.15
  233.1 8.6 %copy.56 = bf16[8,256,1536]{2,1,0:T(8,128)(2,1)} copy(bf16[8,256,1536]{1,2,0:T(8,128)(2,1)} %all-to-all-done.1) | data formatting | bytes 12582912 | tf_op jit(solution)/shard_map/all_to_all | solution.py:44
  241.7 8.3 %fusion.14 = f32[1024,768]{0,1:T(8,128)} fusion(bf16[1024,2048]{1,0:T(8,128)(2,1)} %copy-done.15, bf16[2048,1536]{1,0:T(8,128)(2,1)} %bitcast.58), kind=kOutput, calls=%fused_computation.21 | convolution fusion | flops 3221225472 | bytes 10485760 | tf_op jit(solution)/shard_map/dot_general | solution.py:22
  250.0 7.0 fusion.2
  257.1 0.9 copy-done.31
  258.0 6.9 fusion.13
  264.9 10.0 %convolution_convert_fusion.1.refs_1_ = bf16[1024,2048]{1,0:T(8,128)(2,1)} fusion(bf16[2048,1536]{1,0:T(8,128)(2,1)S(1)} %bitcast.60, bf16[1024,768]{0,1:T(8,128)(2,1)} %get-tuple-element.102, bf16[1024,768]{0,1:T(8,128)(2,1)S(1)} %get-tuple-element.101), kind=kOutput, calls=%fused_computation.10 | convolution fusion | flops 6450839552 | bytes 13631488 | tf_op jit(solution)/shard_map/dot_general | solution.py:26
  274.9 9.4 %convolution_convert_fusion = bf16[2048,1536]{1,0:T(8,128)(2,1)} fusion(bf16[1024,2048]{1,0:T(8,128)(2,1)S(1)} %copy-done.16, bf16[1024,768]{0,1:T(8,128)(2,1)S(1)} %copy-done.32, bf16[1024,768]{0,1:T(8,128)(2,1)S(1)} %get-tuple-element.101), kind=kOutput, calls=%fused_computation | convolution fusion | flops 6451888128 | bytes 13631488 | tf_op jit(solution)/shard_map/dot_general | solution.py:30
  284.4 174.5 %shard_map.308 = (bf16[256,6144]{1,0:T(8,128)(2,1)}, bf16[256,6144]{1,0:T(8,128)(2,1)}, bf16[1024,2048]{1,0:T(8,128)(2,1)}, f32[128,2048]{1,0:T(8,128)}) custom-call(bf16[8,256,1536]{2,1,0:T(8,128)(2,1)} %bitcast.61, bf16[1024,2048]{1,0:T(8,128)(2,1)} %convolution_convert_fusion.1.refs_1_, f32[128,2048]{1,0:T(8,128)} %copy-done.5, bf16[128,2048]{1,0:T(8,128)(2,1)} %bitcast.65), custom_call_target="tpu_custom_call" | custom-call | flops 1000000 | bytes 209715200 | tf_op jit(solution)/shard_map/pallas_call | solution.py:784
  458.9 6.9 fusion.4
  465.9 8.1 %convolution_convert_fusion.2 = bf16[1024,2048]{1,0:T(8,128)(2,1)} fusion(bf16[1024,768]{0,1:T(8,128)(2,1)S(1)} %get-tuple-element.103, f32[768,2048]{1,0:T(8,128)} %param.35), kind=kOutput, calls=%fused_computation.11 | convolution fusion | flops 3224895488 | bytes 12058624 | tf_op jit(solution)/shard_map/dot_general | solution.py:22
  474.3 29.3 %shard_map.309 = (bf16[1024,2048]{1,0:T(8,128)(2,1)}, bf16[1024,320]{1,0:T(8,128)(2,1)}, bf16[1024,320]{1,0:T(8,128)(2,1)}, f32[4,320]{1,0:T(4,128)}, f32[4,320]...) custom-call(bf16[1024,2048]{1,0:T(8,128)(2,1)} %get-tuple-element.66.mid_ref, ...), custom_call_target="tpu_custom_call" | custom-call | flops 4026531840 | bytes 26214400 | tf_op jit(solution)/shard_map/pallas_call | solution.py:308
  505.0 1.0 convert.24
  506.0 1.0 convert.25
  508.0 2.6 fusion.18.refs_0_
  510.9 5.1 convolution_convert_fusion.3
  516.0 178.8 %shard_map.310 = (bf16[320,2048]{1,0:T(8,128)(2,1)}, bf16[8,256,640]{2,1,0:T(8,128)(2,1)}, bf16[336,384]{1,0:T(8,128)(2,1)}, bf16[128,2048]{1,0:T(8,128)(2,1)}) custom-call(bf16[1,320,2048]{2,1,0:T(8,128)(2,1)} %fusion.18.refs_0_, bf16[8,256,640]{2,1,0:T(8,128)(2,1)} %bitcast.64, bf16[1,336,384]{2,1,0:T(8,128)(2,1)} %pad_maximum_fusion.5.refs_2_, ...), custom_call_target="tpu_custom_call" | custom-call | flops 1000000 | bytes 209715200 | tf_op jit(solution)/shard_map/pallas_call | solution.py:784
  694.9 1.3 slice.38
  696.2 1.8 convert_element_type.174
  697.9 2.8 copy-done
  700.7 2.2 copy-done.7
  703.0 1.9 copy-done.8
  704.8 10.0 %shard_map.312 = (f32[256,6144]{1,0:T(8,128)}, f32[256,6144]{1,0:T(8,128)}, f32[256,1]{1,0:T(8,128)S(1)}) custom-call(f32[256,1]{1,0:T(8,128)S(1)} %copy.59.gain_ref, bf16[256,6144]{1,0:T(8,128)(2,1)S(1)} %copy-done.7, bf16[256,6144]{1,0:T(8,128)(2,1)S(1)} %copy-done.8, f32[256,6144]{1,0:T(8,128)S(1)} %copy-done, f32[256,6144]{1,0:T(8,128)} %wb_ref.3), custom_call_target="tpu_custom_call" | custom-call | flops 9437184 | bytes 31457280 | tf_op jit(solution)/shard_map/pallas_call | solution.py:820
  715.5 1.5 fusion.39
  718.5 1.7 copy-done.3
  720.2 1.9 copy-done.9
  722.1 1.7 copy-done.10
  723.8 1.3 copy-done.11
  725.2 5.6 shard_map.311
  731.5 2.3 fusion.24
  (92 shorter events, 10.1 us)
Async XLA Ops:
  7.2 4.3 copy-start.2
  7.2 242.8 %all-gather.3.cloned.1.call-start = ((), (), s32[]{:S(2)}) async-start(), calls=%async_computation.5 | async-start | bytes 4718592 | tf_op jit(solution)/shard_map/all_gather | solution.py:916
  17.1 5.3 copy-start.26
  17.1 86.1 %all-to-all-start = ((bf16[8,2,256,320]{2,3,1,0:T(8,128)(2,1)}), bf16[8,2,256,320]{2,3,1,0:T(8,128)(2,1)S(1)}, u32[]{:S(2)}, u32[]{:S(2)}) async-start(bf16[8,2,256,320]{2,3,1,0:T(8,128)(2,1)} %copy.54), calls=%async_computation | async-start | bytes 5242880 | tf_op jit(solution)/shard_map/all_to_all | solution.py:44
  33.2 4.1 copy-start.29
  33.2 4.2 copy-start.4
  97.4 0.7 copy-start.12
  98.1 2.0 copy-start.13
  103.2 5.2 copy-start.23
  103.2 5.2 copy-start.24
  103.2 5.2 copy-start.25
  103.2 5.3 copy-start.21
  103.2 129.9 %all-to-all-start.1 = ((bf16[8,256,1536]{1,2,0:T(8,128)(2,1)}), bf16[8,256,1536]{1,2,0:T(8,128)(2,1)}, u32[]{:S(2)}, u32[]{:S(2)}) async-start(bf16[8,256,1536]{1,2,0:T(8,128)(2,1)} %pad_maximum_fusion), calls=%async_computation.1 | async-start | bytes 12582912 | tf_op jit(solution)/shard_map/all_to_all | solution.py:44
  108.1 3.4 copy-start.22
  108.1 610.3 %all-reduce.4.cloned.1.call-start = ((), (), s32[]{:S(2)}) async-start(), calls=%async_computation.4 | async-start | bytes 6291456 | tf_op jit(solution)/shard_map/psum | solution.py:948
  138.4 2.2 copy-start.6
  230.1 1.0 copy-start.5
  231.1 2.0 copy-start.15
  250.0 7.0 copy-start.16
  250.0 7.1 copy-start.17
  250.0 8.0 %copy-start.31 = (f32[1024,768]{0,1:T(8,128)S(1)}, f32[1024,768]{0,1:T(8,128)}, u32[]{:S(2)}) copy-start(f32[1024,768]{0,1:T(8,128)} %fusion.14) | copy-start | bytes 9437188
  264.9 10.0 %copy-start.32 = (bf16[1024,768]{0,1:T(8,128)(2,1)S(1)}, bf16[1024,768]{0,1:T(8,128)(2,1)}, u32[]{:S(2)}) copy-start(bf16[1024,768]{0,1:T(8,128)(2,1)} %get-tuple-element.102) | copy-start | bytes 4718596
  465.8 265.6 %reduce-scatter.2.cloned.1.call-start = ((), (), s32[]{:S(2)}) async-start(), calls=%async_computation.3 | async-start | bytes 4718592 | tf_op jit(solution)/shard_map/reduce_scatter | solution.py:950
  474.3 33.6 %copy-start.18 = (bf16[1024,2048]{1,0:T(8,128)(2,1)S(1)}, bf16[1024,2048]{1,0:T(8,128)(2,1)}, u32[]{:S(2)}) copy-start(bf16[1024,2048]{1,0:T(8,128)(2,1)} %get-tuple-element.66.mid_ref) | copy-start | bytes 12582916
  474.3 33.6 %copy-start.30 = (bf16[1024,320]{1,0:T(8,128)(2,1)S(1)}, bf16[1024,320]{1,0:T(8,128)(2,1)}, u32[]{:S(2)}) copy-start(bf16[1024,320]{1,0:T(8,128)(2,1)} %get-tuple-element.64) | copy-start | bytes 1966084
  508.0 2.6 copy-start.14
  508.0 2.6 copy-start.27
  508.0 3.0 copy-start.28
  697.9 2.8 copy-start
  700.7 2.2 copy-start.7
  703.0 1.9 copy-start.8
  704.8 12.7 %copy-start.19 = (bf16[336,384]{1,0:T(8,128)(2,1)S(1)}, bf16[336,384]{1,0:T(8,128)(2,1)}, u32[]{:S(2)}) copy-start(bf16[336,384]{1,0:T(8,128)(2,1)} %get-tuple-element.89) | copy-start | bytes 774148
  704.8 13.6 %copy-start.1 = (f32[256,2560]{1,0:T(8,128)S(1)}, f32[256,2560]{1,0:T(8,128)}, u32[]{:S(2)}) copy-start(f32[256,2560]{1,0:T(8,128)} %wa_ref.2) | copy-start | bytes 7864324
  718.5 1.7 copy-start.3
  720.2 1.9 copy-start.9
  722.1 1.7 copy-start.10
  723.8 1.3 copy-start.11
  725.2 8.6 %copy-start.20 = (bf16[128,2048]{1,0:T(8,128)(2,1)S(1)}, bf16[128,2048]{1,0:T(8,128)(2,1)}, u32[]{:S(2)}) copy-start(bf16[128,2048]{1,0:T(8,128)(2,1)} %get-tuple-element.82) | copy-start | bytes 1572868
Sparse Core Ops, SparseCore 0:
  9.9 61.4 all-gather.2
  466.0 170.4 all-reduce.3
  639.9 70.7 reduce-scatter.1

commit v7 on v6

--- a/solution.py
+++ b/solution.py
@@ -138,84 +138,6 @@
         return tuple(states)
 
     lax.fori_loop(0, length // unroll, step, (jnp.zeros((sequences, 128), f32),) * tiles)
-
-
-def mix_forward_kernel(
-    sequences, length, n_ref, w_ref, label_ref, conv_ref, bias_ref, rw_ref, iw_ref, ow_ref,
-    partial_ref, product_ref, pre_ref, conv_in_ref, values_ref, recur_ref, inject_ref, decay_ref, states_ref,
-    pad, lines, rbig, ibig,
-):
-    fill_blocks(rbig, rw_ref)
-    fill_blocks(ibig, iw_ref)
-    pad[0:8, :] = jnp.zeros((8, pad.shape[1]), f32)
-    taps = conv_ref.shape[0]
-    width = pad.shape[1]
-    clear_tail(decay_ref, width)
-    clear_tail(states_ref, width)
-
-    def one(s, _):
-        base = pl.multiple_of(s * length, length)
-        here = pl.ds(base, length)
-        rows = n_ref[here, :]
-        masks = label_masks(label_ref, here, length, width, taps, lines)
-        pre_ref[here, :] = dot_nn(rows, whole_weight(w_ref, 0))
-        conv_in = dot_nn(rows, whole_weight(w_ref, 1)).astype(bf16)
-        conv_in_ref[here, :] = conv_in
-        pad[8 : 8 + length, :] = conv_in.astype(f32)
-        total = bias_ref[0:1, :] + conv_ref[0:1, :] * pad[8 : 8 + length, :]
-        for k in range(1, taps):
-            total = total + conv_ref[k : k + 1, :] * pad[8 - k : 8 - k + length, :] * masks[k - 1]
-        values = total.astype(bf16)
-        values_ref[here, :] = values
-        recur = jax.nn.sigmoid(dot_nn(values, rbig[...].astype(bf16)) + bias_ref[1:2, :])
-        inject = jax.nn.sigmoid(dot_nn(values, ibig[...].astype(bf16)) + bias_ref[2:3, :])
-        recur_ref[here, :] = recur
-        inject_ref[here, :] = inject
-        log_decay = -decay_scale * bias_ref[3:4, :] * recur
-        inside = masks[0] > 0.5
-        put_tiles(decay_ref, here, jnp.where(inside, jnp.exp(log_decay), 0.0))
-        scale = jnp.where(inside, jnp.sqrt(minus_expm1(2.0 * log_decay)), 1.0)
-        put_tiles(states_ref, here, scale * inject * values.astype(f32))
-        return 0
-
-    lax.fori_loop(0, sequences, one, 0)
-    seq_scan(decay_ref, states_ref, sequences, length, False)
-
-    def two(s, _):
-        base = pl.multiple_of(s * length, length)
-        here = pl.ds(base, length)
-        act, _unused = gelu_parts(pre_ref[here, :])
-        product = (act * get_tiles(states_ref, here, width)).astype(bf16)
-        product_ref[here, :] = product
-        partial_ref[here, :] = dot_nn(product, ow_ref[...]).astype(bf16)
-        return 0
-
-    lax.fori_loop(0, sequences, two, 0)
-
-
-def mix_forward(sequences, normed, weights, labels, conv, bias, rw, iw, ow):
-    total, width = normed.shape[0], weights.shape[3]
-    length = total // sequences
-    depth = ow.shape[1]
-    shape = jax.ShapeDtypeStruct
-    like = lambda dt: shape((total, width), dt)
-    tiled = shape((-(-width // 128), total, 128), f32)
-    return pl.pallas_call(
-        functools.partial(mix_forward_kernel, sequences, length),
-        out_shape=(
-            shape((total, depth), bf16), like(bf16), like(f32), like(bf16), like(bf16), like(f32), like(f32), tiled, tiled,
-        ),
-        in_specs=[VM] * 8,
-        out_specs=[VM] * 9,
-        scratch_shapes=[
-            pltpu.VMEM((8 + length, width), f32),
-            pltpu.VMEM((8 + length, 128), f32),
-            pltpu.VMEM((width, width), f32),
-            pltpu.VMEM((width, width), f32),
-        ],
-        compiler_params=pltpu.CompilerParams(vmem_limit_bytes=56 * 2**20),
-        cost_estimate=pl.CostEstimate(flops=2 * total * width * 3 * depth, bytes_accessed=20 * 2**20, transcendentals=total * width * 5),
-    )(normed, weights, labels, conv, bias, rw, iw, ow)
 
 
 def mix_backward_kernel(
@@ -341,14 +263,6 @@
     return offsets, at, block
 
 
-def greet(offsets, at):
-    barrier = pltpu.get_barrier_semaphore()
-    partners = [(0, 1)] + offsets[1:]
-    for dy, ds in partners:
-        pl.semaphore_signal(barrier, inc=1, device_id=at(dy, ds), device_id_type=MESH)
-    pl.semaphore_wait(barrier, len(partners))
-
-
 def remote(src, dst, sent, got, device):
     return pltpu.make_async_remote_copy(
         src_ref=src, dst_ref=dst, send_sem=sent, recv_sem=got, device_id=device, device_id_type=MESH
@@ -359,7 +273,7 @@
     return ref.at[pl.ds(pl.multiple_of(index * rows, rows), rows), :]
 
 
-def scatter_steps(rows, partial, near, far, stage, acc, sems):
+def scatter_steps(rows, partial, near, far, acc, sems):
     offsets, at, block = plane()
     near_sent, near_got, far_sent, far_got = sems
     count = len(offsets)
@@ -382,14 +296,14 @@
             here = pl.ds(step, 16)
             total = partial[pl.ds(pl.multiple_of(base + step, 16), 16), :].astype(f32) + near[q, here, :].astype(f32)
             if q:
-                stage[q - 1, here, :] = total.astype(bf16)
+                near[q, here, :] = total.astype(bf16)
             else:
                 acc[here, :] = total
             return 0
 
         lax.fori_loop(0, rows // 16, tile, 0)
         if q:
-            seconds[q] = remote(stage.at[q - 1], far.at[q - 1], far_sent.at[q - 1], far_got.at[q - 1], at(dy, ds))
+            seconds[q] = remote(near.at[q], far.at[q - 1], far_sent.at[q - 1], far_got.at[q - 1], at(dy, ds))
             seconds[q].start()
     yield None
     for q in order[:-1]:
@@ -402,11 +316,6 @@
 
         lax.fori_loop(0, rows // 16, more, 0)
     yield [firsts[q].wait_send for q in order] + [seconds[q].wait_send for q in order[:-1]]
-
-
-def scatter_sum(*args):
-    *_, waits = scatter_steps(*args)
-    return waits
 
 
 def gather_steps(rows, whole, sems):
@@ -437,11 +346,6 @@
     yield arrivals + sends
 
 
-def gather_blocks(*args):
-    *_, waits = gather_steps(*args)
-    return waits
-
-
 def root_mean(rows):
     return lax.rsqrt(jnp.mean(rows * rows, axis=-1, keepdims=True) + epsilon)
 
@@ -458,48 +362,10 @@
     lax.fori_loop(0, rows // 16, tile, 0)
 
 
-def start_kernel(x_ref, label_ref, unit_ref, labels_ref, *sems):
-    rows = x_ref.shape[0]
-    offsets, at, block = plane()
-    greet(offsets, at)
-    base = block(0, 0) * rows
-
-    def unit(here, i):
-        value = x_ref[here, :].astype(f32)
-        there = pl.ds(pl.multiple_of(base + i * 16, 16), 16)
-        unit_ref[there, :] = (value * root_mean(value)).astype(bf16)
-        labels_ref[there, :] = label_ref[here, :]
-
-    by_tiles(rows, unit)
-    waits = gather_blocks(rows, labels_ref, sems[4:])
-    waits = waits + gather_blocks(rows, unit_ref, sems[:4])
-    for wait in waits:
-        wait()
-
-
-def forward_kernel(partial, x_ref, unit_ref, middle_ref, near, far, stage, acc, *sems):
-    rows = x_ref.shape[0]
-    offsets, at, block = plane()
-    greet(offsets, at)
-    waits = scatter_sum(rows, partial, near, far, stage, acc, sems[:4])
-    base = block(0, 0) * rows
-
-    def norm(here, i):
-        middle = x_ref[here, :].astype(f32) + acc[here, :]
-        middle_ref[here, :] = middle
-        there = pl.ds(pl.multiple_of(base + i * 16, 16), 16)
-        unit_ref[there, :] = (middle * root_mean(middle)).astype(bf16)
-
-    by_tiles(rows, norm)
-    waits = waits + gather_blocks(rows, unit_ref, sems[4:])
-    for wait in waits:
-        wait()
-
-
-def backward_steps(partial, middle_ref, cot_ref, low_ref, grad_ref, near, far, stage, acc, *sems):
+def backward_steps(partial, middle_ref, cot_ref, low_ref, grad_ref, near, far, acc, *sems):
     rows = middle_ref.shape[0]
     offsets, at, block = plane()
-    scatter = scatter_steps(rows, partial, near, far, stage, acc, sems[:4])
+    scatter = scatter_steps(rows, partial, near, far, acc, sems[:4])
     next(scatter)
     yield
     waits = next(scatter)
@@ -523,9 +389,9 @@
         wait()
 
 
-def last_steps(partial, grad_ref, x_ref, out_ref, near, far, stage, acc, *sems):
+def last_steps(partial, grad_ref, x_ref, out_ref, near, far, acc, *sems):
     rows = x_ref.shape[0]
-    scatter = scatter_steps(rows, partial, near, far, stage, acc, sems[:4])
+    scatter = scatter_steps(rows, partial, near, far, acc, sems[:4])
     next(scatter)
     yield
     waits = next(scatter)
@@ -550,7 +416,6 @@
         scratch = [
             pltpu.VMEM((count,) + block, bf16),
             pltpu.VMEM((count - 1,) + block, bf16),
-            pltpu.VMEM((count - 1,) + block, bf16),
             pltpu.VMEM(block, f32),
         ]
     for _ in range(scatters + gathers):
@@ -558,18 +423,348 @@
     return scratch
 
 
-def exchange(kernel, identity, inputs, outs, rows, depth, gathers, scatters):
+def cut_columns(weight_ref, gain, target, start, lanes):
+    owners = weight_ref.shape[1] // lanes
+
+    def tile(i, _):
+        step = pl.multiple_of(i * 16, 16)
+        here = pl.ds(step, 16)
+        scaled = low(weight_ref[here, :]) * gain(step)
+        for j in range(owners):
+            target(j)[here, start : start + lanes] = scaled[:, j * lanes : (j + 1) * lanes].astype(bf16)
+        return 0
+
+    lax.fori_loop(0, weight_ref.shape[0] // 16, tile, 0)
+
+
+def quarter_steps(n, part, whole, sems):
+    me = lax.axis_index("replica")
+    right_sent, right_got, left_sent, left_got = sems
+
+    def rows(q):
+        return whole.at[:, pl.ds(pl.multiple_of(q * part, 16), part), :]
+
+    def to_right(hop):
+        block = rows(me - hop)
+        return remote(block, block, right_sent.at[hop], right_got.at[hop], {"replica": me + 1})
+
+    def to_left(hop):
+        block = rows(me + hop)
+        return remote(block, block, left_sent.at[hop], left_got.at[hop], {"replica": me - 1})
+
+    def from_left(hop):
+        block = rows(me - hop - 1)
+        return remote(block, block, right_sent.at[hop], right_got.at[hop], {"replica": me + 1})
+
+    def from_right(hop):
+        block = rows(me + hop + 1)
+        return remote(block, block, left_sent.at[hop], left_got.at[hop], {"replica": me - 1})
+
+    for hop in range(n - 1):
+        if hop:
+
+            @pl.when(me >= hop)
+            def _():
+                from_left(hop - 1).wait_recv()
+
+            @pl.when(me + hop < n)
+            def _():
+                from_right(hop - 1).wait_recv()
+
+        @pl.when(jnp.logical_and(me >= hop, me < n - 1))
+        def _():
+            to_right(hop).start()
+
+        @pl.when(jnp.logical_and(me + hop < n, me > 0))
+        def _():
+            to_left(hop).start()
+
+        yield
+
+    @pl.when(me >= n - 1)
+    def _():
+        from_left(n - 2).wait_recv()
+
+    @pl.when(me + n - 1 < n)
+    def _():
+        from_right(n - 2).wait_recv()
+
+    for hop in range(n - 1):
+
+        @pl.when(jnp.logical_and(me >= hop, me < n - 1))
+        def _():
+            to_right(hop).wait_send()
+
+        @pl.when(jnp.logical_and(me + hop < n, me > 0))
+        def _():
+            to_left(hop).wait_send()
+
+    yield
+
+
+def front_kernel(
+    n, sequences, length,
+    x_ref, label_ref, cot_ref, gains_ref, conv_ref, bias_ref, rw_ref, iw_ref,
+    branch_hbm, input_hbm, gate_hbm, up_hbm, ow_hbm,
+    unit_out, labels_out, low_out, product_out, pre_out, conv_in_out, values_out, recur_out, inject_out, decay_out,
+    states_out, mix_out, ow_out, two_out, middle_out, pair_out,
+    unit_ref, labels_ref, product_ref, pre_ref, conv_in_ref, values_ref, recur_ref, inject_ref, decay_ref,
+    states_ref, mix_ref, ow_ref, two_ref, middle_ref,
+    wide, tall, ow_f, mix_cut, pair_cut, pad, lines, rbig, ibig, partial,
+    near, far, acc, *sems,
+):
+    rows = x_ref.shape[0]
+    scatter_sems, sems = sems[:4], sems[4:]
+    unit_sems, label_sems, low_sems, two_sems, sems = sems[:4], sems[4:8], sems[8:12], sems[12:16], sems[16:]
+    load_sem, save_sem, mix_sent, mix_got, pair_sent, pair_got = sems[:6]
+    line_sems = sems[6:]
+    offsets, at, block = plane()
+    z = lax.axis_index("replica")
+    y, s = lax.axis_index("seq"), lax.axis_index("shard")
+    shards = lax.axis_size("shard")
+    owners = shards * lax.axis_size("seq")
+    part = gate_hbm.shape[0] // n
+    width = pad.shape[1]
+    ff = gate_hbm.shape[1] // owners
+
+    def peer(i):
+        return {"seq": jnp.bitwise_xor(y, i // shards), "shard": jnp.bitwise_xor(s, i % shards)}
+
+    def place(i):
+        return jnp.bitwise_xor(y, i // shards) * shards + jnp.bitwise_xor(s, i % shards)
+
+    own_rows = pl.ds(pl.multiple_of(z * part, 16), part)
+    loads = [
+        pltpu.make_async_copy(gate_hbm.at[own_rows, :], tall.at[0], load_sem.at[0]),
+        pltpu.make_async_copy(up_hbm.at[own_rows, :], tall.at[1], load_sem.at[1]),
+        pltpu.make_async_copy(branch_hbm, wide.at[0], load_sem.at[2]),
+        pltpu.make_async_copy(input_hbm, wide.at[1], load_sem.at[3]),
+        pltpu.make_async_copy(ow_hbm, ow_f, load_sem.at[4]),
+    ]
+    for load in loads:
+        load.start()
+    saves = []
+
+    def save(source, target):
+        copy = pltpu.make_async_copy(source, target, save_sem.at[len(saves)])
+        copy.start()
+        saves.append(copy)
+
+    low_own = pltpu.make_async_copy(cot_ref, row_block(low_out, block(0, 0), rows), load_sem.at[5])
+    low_own.start()
+    barrier = pltpu.get_barrier_semaphore()
+    for i in range(1, owners):
+        pl.semaphore_signal(barrier, inc=1, device_id=peer(i), device_id_type=MESH)
+
+    @pl.when(z > 0)
+    def _():
+        pl.semaphore_signal(barrier, inc=1, device_id={"replica": z - 1}, device_id_type=MESH)
+
+    @pl.when(z < n - 1)
+    def _():
+        pl.semaphore_signal(barrier, inc=1, device_id={"replica": z + 1}, device_id_type=MESH)
+
+    base = block(0, 0) * rows
+
+    def unit(here, i):
+        value = x_ref[here, :].astype(f32)
+        there = pl.ds(pl.multiple_of(base + i * 16, 16), 16)
+        unit_ref[there, :] = (value * root_mean(value)).astype(bf16)
+        labels_ref[there, :] = label_ref[here, :]
+
+    by_tiles(rows, unit)
+    inside_line = jnp.logical_and(z > 0, z < n - 1)
+
+    @pl.when(inside_line)
+    def _():
+        pl.semaphore_wait(barrier, owners + 1)
+
+    @pl.when(jnp.logical_not(inside_line))
+    def _():
+        pl.semaphore_wait(barrier, owners)
+
+    label_gather = gather_steps(rows, labels_ref, label_sems)
+    unit_gather = gather_steps(rows, unit_ref, unit_sems)
+    next(label_gather)
+    next(unit_gather)
+
+    for side in range(2):
+        loads[side].wait()
+
+        cut_columns(
+            tall.at[side],
+            lambda step: gains_ref[pl.ds(pl.multiple_of(z * part + step, 16), 16), 1:2],
+            lambda j: pair_cut.at[j],
+            side * ff,
+            ff,
+        )
+    me = place(0)
+    pair_there = pair_out.at[me, own_rows, :]
+    pair_moves = [
+        remote(pair_cut.at[place(i)], pair_there, pair_sent.at[i], pair_got.at[i], peer(i)) for i in range(1, owners)
+    ]
+    for move in pair_moves:
+        move.start()
+    pair_own = pltpu.make_async_copy(pair_cut.at[me], pair_there, pair_sent.at[0])
+    pair_own.start()
+
+    for side in range(2):
+        loads[2 + side].wait()
+        cut_columns(
+            wide.at[side], lambda step: gains_ref[pl.ds(step, 16), 0:1], lambda j: mix_cut.at[j, side], 0, width
+        )
+    mix_moves = [
+        remote(mix_cut.at[place(i)], mix_ref.at[me], mix_sent.at[i], mix_got.at[i], peer(i)) for i in range(1, owners)
+    ]
+    for move in mix_moves:
+        move.start()
+    mix_own = pltpu.make_async_copy(mix_cut.at[me], mix_ref.at[me], mix_sent.at[0])
+    mix_own.start()
+    loads[4].wait()
+    ow_ref[...] = ow_f[...].astype(bf16)
+    save(ow_ref, ow_out)
+    fill_blocks(rbig, rw_ref)
+    fill_blocks(ibig, iw_ref)
+    pad[0:8, :] = jnp.zeros((8, width), f32)
+    taps = conv_ref.shape[0]
+    clear_tail(decay_ref, width)
+    clear_tail(states_ref, width)
+
+    waits = next(label_gather)
+    waits = waits + next(unit_gather)
+    pair_own.wait()
+    for move in pair_moves:
+        move.wait_recv()
+    line = quarter_steps(n, part, pair_out, line_sems)
+    next(line)
+    for wait in waits:
+        wait()
+    mix_own.wait()
+    for move in mix_moves:
+        move.wait_recv()
+    save(unit_ref, unit_out)
+    save(labels_ref, labels_out)
+    save(mix_ref, mix_out)
+
+    low_own.wait()
+    low_gather = gather_steps(rows, low_out, low_sems)
+    next(low_gather)
+
+    def one(q, _):
+        here = pl.ds(pl.multiple_of(q * length, length), length)
+        sequence = unit_ref[here, :]
+        masks = label_masks(labels_ref, here, length, width, taps, lines)
+        pre_ref[here, :] = dot_nn(sequence, whole_weight(mix_ref, 0))
+        conv_in = dot_nn(sequence, whole_weight(mix_ref, 1)).astype(bf16)
+        conv_in_ref[here, :] = conv_in
+        pad[8 : 8 + length, :] = conv_in.astype(f32)
+        total = bias_ref[0:1, :] + conv_ref[0:1, :] * pad[8 : 8 + length, :]
+        for k in range(1, taps):
+            total = total + conv_ref[k : k + 1, :] * pad[8 - k : 8 - k + length, :] * masks[k - 1]
+        values = total.astype(bf16)
+        values_ref[here, :] = values
+        recur = jax.nn.sigmoid(dot_nn(values, rbig[...].astype(bf16)) + bias_ref[1:2, :])
+        inject = jax.nn.sigmoid(dot_nn(values, ibig[...].astype(bf16)) + bias_ref[2:3, :])
+        recur_ref[here, :] = recur
+        inject_ref[here, :] = inject
+        log_decay = -decay_scale * bias_ref[3:4, :] * recur
+        inside = masks[0] > 0.5
+        put_tiles(decay_ref, here, jnp.where(inside, jnp.exp(log_decay), 0.0))
+        scale = jnp.where(inside, jnp.sqrt(minus_expm1(2.0 * log_decay)), 1.0)
+        put_tiles(states_ref, here, scale * inject * values.astype(f32))
+        return 0
+
+    lax.fori_loop(0, sequences, one, 0)
+    seq_scan(decay_ref, states_ref, sequences, length, False)
+
+    def two(q, _):
+        here = pl.ds(pl.multiple_of(q * length, length), length)
+        act, _unused = gelu_parts(pre_ref[here, :])
+        product = (act * get_tiles(states_ref, here, width)).astype(bf16)
+        product_ref[here, :] = product
+        partial[here, :] = dot_nn(product, ow_ref[...]).astype(bf16)
+        return 0
+
+    lax.fori_loop(0, sequences, two, 0)
+    scatter = scatter_steps(rows, partial, near, far, acc, scatter_sems)
+    next(scatter)
+    for source, target in (
+        (product_ref, product_out), (pre_ref, pre_out), (conv_in_ref, conv_in_out), (values_ref, values_out),
+        (recur_ref, recur_out), (inject_ref, inject_out), (decay_ref, decay_out), (states_ref, states_out),
+    ):
+        save(source, target)
+    next(line)
+    waits = next(low_gather)
+    waits = waits + next(scatter)
+
+    def norm(here, i):
+        middle = x_ref[here, :].astype(f32) + acc[here, :]
+        middle_ref[here, :] = middle
+        there = pl.ds(pl.multiple_of(base + i * 16, 16), 16)
+        two_ref[there, :] = (middle * root_mean(middle)).astype(bf16)
+
+    by_tiles(rows, norm)
+    two_gather = gather_steps(rows, two_ref, two_sems)
+    next(two_gather)
+    save(middle_ref, middle_out)
+    for _ in range(n - 3):
+        next(line)
+    for wait in waits:
+        wait()
+    waits = next(two_gather)
+    for wait in waits:
+        wait()
+    save(two_ref, two_out)
+    for _ in line:
+        pass
+    for move in pair_moves + mix_moves:
+        move.wait_send()
+    for copy in saves:
+        copy.wait()
+
+
+def front(sequences, x, label, cot, gains, conv, bias, rw, iw, branch_w, input_w, gate_w, up_w, output_w):
+    rows, depth = x.shape
+    own, n = branch_w.shape[0], lax.axis_size("replica")
+    owners = lax.axis_size(GROUP)
+    total, width, ff = owners * rows, branch_w.shape[1] // owners, gate_w.shape[1] // owners
+    part = own // n
+    length = total // sequences
+    tiles = -(-width // 128)
+    kept = [
+        ((total, depth), bf16), ((total, 128), bf16), ((total, depth), bf16), ((total, width), bf16),
+        ((total, width), f32), ((total, width), bf16), ((total, width), bf16), ((total, width), f32),
+        ((total, width), f32), ((tiles, total, 128), f32), ((tiles, total, 128), f32), ((owners, 2, own, width), bf16),
+        ((width, depth), bf16), ((total, depth), bf16), ((rows, depth), f32),
+    ]
+    vm = pltpu.VMEM
+    dma = pltpu.SemaphoreType.DMA
+    scratch = [vm(*item) for k, item in enumerate(kept) if k != 2] + [
+        vm((2,) + branch_w.shape, f32),
+        vm((2, part, gate_w.shape[1]), f32),
+        vm(output_w.shape, f32),
+        vm((owners, 2, own, width), bf16),
+        vm((owners, part, 2 * ff), bf16),
+        vm((8 + length, width), f32),
+        vm((8 + length, 128), f32),
+        vm((width, width), f32),
+        vm((width, width), f32),
+        vm((total, depth), bf16),
+    ]
+    scratch += plane_scratch(rows, depth, 4, 1)
+    scratch += [dma((6,)), dma((len(kept),))] + [dma((owners,))] * 4 + [dma((n - 1,))] * 4
+    outs = kept + [((owners, own, 2 * ff), bf16)]
     return pl.pallas_call(
-        kernel,
-        out_shape=tuple(jax.ShapeDtypeStruct(shape, kind) for shape, kind in outs),
-        in_specs=[VM] * len(inputs),
-        out_specs=[VM] * len(outs),
-        scratch_shapes=plane_scratch(rows, depth, gathers, scatters),
+        functools.partial(front_kernel, n, sequences, length),
+        out_shape=tuple(jax.ShapeDtypeStruct(*item) for item in outs),
+        in_specs=[VM] * 8 + [ANY] * 5,
+        out_specs=[ANY] * len(outs),
+        scratch_shapes=scratch,
         compiler_params=pltpu.CompilerParams(
-            collective_id=identity, has_side_effects=True, vmem_limit_bytes=40 * 2**20
+            collective_id=1, has_side_effects=True, vmem_limit_bytes=60 * 2**20
         ),
-        cost_estimate=pl.CostEstimate(flops=10**6, bytes_accessed=60 * 2**20, transcendentals=0),
-    )(*inputs)
+        cost_estimate=pl.CostEstimate(flops=10**6, bytes_accessed=200 * 2**20, transcendentals=0),
+    )(x, label, cot, gains, conv, bias, rw, iw, branch_w, input_w, gate_w, up_w, output_w)
 
 
 def pieces(rows, most):
@@ -905,29 +1100,19 @@
     total = members * rows
     gain, mlp_gain = low(norm_gain)[:, None], low(mlp_norm_gain)[:, None]
     own_labels = jnp.broadcast_to(segments[0].astype(bf16)[:, None], (rows, 128))
-    unit_all, labels = exchange(
-        start_kernel, 1, (x, own_labels), (((total, depth), bf16), ((total, 128), bf16)), rows, depth, 2, 0
-    )
-    mix_w = swap(jnp.stack([by_owner(branch_weight, gain), by_owner(input_weight, gain)], 1))
-    pair_cut = jnp.concatenate([by_owner(gate_weight, mlp_gain), by_owner(up_weight, mlp_gain)], 2)
-    unit_all, pair_cut = lax.optimization_barrier((unit_all, pair_cut))
-    pair_w = swap(pair_cut).reshape(depth, -1)
     width = branch_weight.shape[1] // members
-    out_low = lax.all_gather(cot, ROWS, axis=0, tiled=True)
-    output_w = output_weight.astype(bf16)
-    down_w = down_weight.astype(bf16)
-
     conv_f = low(conv_weight)
     decay_f = low(decay_param)
     bias = jnp.stack([low(conv_bias), low(recur_gate_bias), low(input_gate_bias), jax.nn.softplus(-decay_f)])
-    mixed = mix_forward(
-        sequences, unit_all, mix_w, labels, conv_f, bias, recur_gate_weight, input_gate_weight, output_w
+    (
+        unit_all, labels, out_low, product, *mixed, mix_w, output_w, unit_two, middle, pair_w,
+    ) = front(
+        sequences, x, own_labels, cot, low(jnp.stack([norm_gain, mlp_norm_gain], 1)), conv_f, bias,
+        recur_gate_weight, input_gate_weight, branch_weight, input_weight, gate_weight, up_weight, output_weight,
     )
-    partial, product = mixed[:2]
+    pair_w = pair_w.reshape(depth, -1)
+    down_w = down_weight.astype(bf16)
     whole = ((total, depth), bf16)
-    unit_two, middle = exchange(
-        forward_kernel, 2, (partial, x), (whole, ((rows, depth), f32)), rows, depth, 1, 1
-    )
     ff = pair_w.shape[1] // 2
     gate_pre = mm(unit_two, pair_w[:, :ff])
     up_pre = mm(unit_two, pair_w[:, ff:])
@@ -951,7 +1136,7 @@
     block_out = (middle + block_sum.astype(f32)).astype(bf16)
     output_partial = mm_tn(product, mid_low).astype(bf16)[None]
     back = mix_backward(
-        sequences, mid_low, output_w, mix_w, *mixed[2:], labels, conv_f, bias, recur_gate_weight, input_gate_weight
+        sequences, mid_low, output_w, mix_w, *mixed, labels, conv_f, bias, recur_gate_weight, input_gate_weight
     )
     partial, branch_low, conv_low, conv_weight_grad, sums, recur_weight_grad, inject_weight_grad = back
     mix_low = jnp.concatenate([branch_low, conv_low], 1)

time: 747 us -> 690 us (0.924)
  local copies, waits for them, and re-layouts: 54.3 us -> 18.5 us
  starting transfers between devices: 10.5 us -> 0.08 us
  other arithmetic: 25.7 us -> 17.7 us
    unnamed x71 -> x45, local copies, waits for them, and re-layouts: 38.7 us -> 14.5 us
    all_to_all x2 -> x0, local copies, waits for them, and re-layouts: 11.4 us -> none  [swap(): return lax.all_to_all(cut, GROUP, split_axis=0, concat_axis=0, tiled=True)]
    all_to_all x2 -> x0, starting transfers between devices: 10.2 us -> none  [swap(): return lax.all_to_all(cut, GROUP, split_axis=0, concat_axis=0, tiled=True)]
    convert_element_type x3 -> x0, other arithmetic: 9.35 us -> none  [the longest x2 6.35 us: by_owner(): scaled = (low(weight) * gain).astype(bf16)]
    pallas_call x3 -> x1, Pallas kernels: 173 us -> 173 us  [front(): pl.pallas_call(functools.partial(front_kernel, n, sequences, length), out...]
  transfers between devices with their start and end apart: 5 -> 2, of which waited for: 0 -> 0; matrix products, arithmetic and copies ran while one was open for 11% -> 4% of each run, Pallas kernels for 54% -> 32%
where the time goes in v7:
time: 690 us; the launch traced here: 682 us
  Pallas kernels  569 us (82%)
  matrix products  61 us (9%)
  local copies, waits for them, and re-layouts  18.5 us (3%)
  other arithmetic  17.7 us (3%)
  between operations  15.9 us (2%)
    pallas_call x2, Pallas kernels, replica_sum(): pl.pallas_call(functools.partial(line_kernel, lax.axis_size('replica'), t...  349 us
    pallas_call x1, Pallas kernels, front(): pl.pallas_call(functools.partial(front_kernel, n, sequences, length), out...  173 us
    pallas_call x1, Pallas kernels, mix_backward(): pl.pallas_call(functools.partial(mix_backward_kernel, sequences, length),...  30.7 us
    dot_general x3, matrix products, mm(): return jnp.dot(left, right, preferred_element_type=f32)  25.7 us
    dot_general x4, matrix products, mm_tn(): lax.dot_general(left, right, (((0,), (0,)), ((), ())), preferred_element_...  21.9 us
    unnamed x45, local copies, waits for them, and re-layouts  14.5 us
  transfers between devices with their start and end apart: 2, of which 0 were waited for; matrix products, arithmetic and copies ran while one was open for 4% of the time, Pallas kernels for 32%

profile of v7, /device:TPU:0, one launch (start us, length us, event | category | flops | bytes accessed | tf_op | source)
XLA Modules:
  0.0 682.3 jit_solution(4938963672409345288)
XLA Ops:
  8.1 0.7 convert.34
  8.7 0.7 convert.35
  9.4 0.7 convert_bitcast_fusion
  10.1 0.7 convert_convert_fusion.3
  10.8 0.7 convert_convert_fusion.2
  11.5 0.7 convert_convert_fusion.1
  12.2 0.7 compare_select_fusion
  12.9 0.8 copy.42.gains_ref
  13.7 1.3 pad_maximum_fusion.5
  15.0 0.7 broadcast_in_dim.22.label_ref
  15.7 173.3 %shard_map.305 = (bf16[1024,2048]{1,0:T(8,128)(2,1)}, bf16[1024,128]{1,0:T(8,128)(2,1)}, bf16[1024,2048]{1,0:T(8,128)(2,1)}, bf16[1024,320]{1,0:T(8,128)(2,1)}, ...) custom-call(bf16[128,2048]{1,0:T(8,128)(2,1)} %bitcast.34, ...), custom_call_target="tpu_custom_call" | custom-call | flops 1000000 | bytes 209715200 | tf_op jit(solution)/shard_map/pallas_call | solution.py:757
  189.1 8.4 %fusion.7 = f32[1024,768]{0,1:T(8,128)} fusion(bf16[1024,2048]{1,0:T(8,128)(2,1)} %get-tuple-element.59, bf16[2048,1536]{1,0:T(8,128)(2,1)} %bitcast.42), kind=kOutput, calls=%fused_computation.14 | convolution fusion | flops 3221225472 | bytes 10485760 | tf_op jit(solution)/shard_map/dot_general | solution.py:22
  197.5 5.2 fusion.12
  202.7 9.3 %fusion.6 = (bf16[1024,768]{0,1:T(8,128)(2,1)S(1)}, bf16[1024,768]{0,1:T(8,128)(2,1)S(1)}, bf16[1024,768]{0,1:T(8,128)(2,1)S(1)}) fusion(f32[1024,768]{0,1:T(8,128)} %fusion.12, f32[1024,768]{0,1:T(8,128)} %fusion.7, bf16[1024,2048]{1,0:T(8,128)(2,1)} %get-tuple-element.59, bf16[2048,1536]{1,0:T(8,128)(2,1)S(1)} %bitcast.45), kind=kOutput, calls=%fused_computation.13 | convolution fusion | flops 3240886272 | bytes 18350080 | tf_op jit(solution)/shard_map/dot_general | solution.py:22
  212.0 8.3 %convolution_convert_fusion.1.refs_1_ = bf16[1024,2048]{1,0:T(8,128)(2,1)} fusion(bf16[2048,1536]{1,0:T(8,128)(2,1)S(1)} %bitcast.46, bf16[1024,768]{0,1:T(8,128)(2,1)S(1)} %get-tuple-element.104, bf16[1024,768]{0,1:T(8,128)(2,1)S(1)} %get-tuple-element.103), kind=kOutput, calls=%fused_computation.3 | convolution fusion | flops 6450839552 | bytes 13631488 | tf_op jit(solution)/shard_map/dot_general | solution.py:26
  220.3 9.4 %convolution_convert_fusion = bf16[2048,1536]{1,0:T(8,128)(2,1)} fusion(bf16[1024,2048]{1,0:T(8,128)(2,1)S(1)} %copy-done.14, bf16[1024,768]{0,1:T(8,128)(2,1)S(1)} %get-tuple-element.104, bf16[1024,768]{0,1:T(8,128)(2,1)S(1)} %get-tuple-element.103), kind=kOutput, calls=%fused_computation | convolution fusion | flops 6451888128 | bytes 13631488 | tf_op jit(solution)/shard_map/dot_general | solution.py:30
  229.7 4.8 convolution_convert_fusion.3
  234.5 178.9 %shard_map.306 = (bf16[256,6144]{1,0:T(8,128)(2,1)}, bf16[256,6144]{1,0:T(8,128)(2,1)}, bf16[1024,2048]{1,0:T(8,128)(2,1)}, f32[128,2048]{1,0:T(8,128)}) custom-call(bf16[8,256,1536]{2,1,0:T(8,128)(2,1)} %bitcast.30, bf16[1024,2048]{1,0:T(8,128)(2,1)} %convolution_convert_fusion.1.refs_1_, f32[128,2048]{1,0:T(8,128)} %get-tuple-element.58.refs_2_, ...), custom_call_target="tpu_custom_call" | custom-call | flops 1000000 | bytes 209715200 | tf_op jit(solution)/shard_map/pallas_call | solution.py:979
  413.5 8.0 %convolution_convert_fusion.2 = bf16[1024,2048]{1,0:T(8,128)(2,1)} fusion(bf16[1024,768]{0,1:T(8,128)(2,1)S(1)} %get-tuple-element.105, f32[768,2048]{1,0:T(8,128)} %param.35), kind=kOutput, calls=%fused_computation.4 | convolution fusion | flops 3224895488 | bytes 12058624 | tf_op jit(solution)/shard_map/dot_general | solution.py:22
  421.5 30.7 %shard_map.307 = (bf16[1024,2048]{1,0:T(8,128)(2,1)}, bf16[1024,320]{1,0:T(8,128)(2,1)}, bf16[1024,320]{1,0:T(8,128)(2,1)}, f32[4,320]{1,0:T(4,128)}, f32[4,320]...) custom-call(bf16[1024,2048]{1,0:T(8,128)(2,1)} %get-tuple-element.64.mid_ref, ...), custom_call_target="tpu_custom_call" | custom-call | flops 4026531840 | bytes 26214400 | tf_op jit(solution)/shard_map/pallas_call | solution.py:230
  452.2 0.7 convert.38
  452.9 0.7 convert.39
  453.6 1.0 convert.36
  454.6 1.0 convert.37
  455.8 0.7 pad_maximum_fusion.3.refs_2_
  456.6 2.6 fusion.11.refs_0_
  459.2 0.4 copy-done.17
  459.6 5.1 convolution_convert_fusion.4
  464.7 170.3 %shard_map.308 = (bf16[320,2048]{1,0:T(8,128)(2,1)}, bf16[8,256,640]{2,1,0:T(8,128)(2,1)}, bf16[336,384]{1,0:T(8,128)(2,1)}, bf16[128,2048]{1,0:T(8,128)(2,1)}) custom-call(bf16[1,320,2048]{2,1,0:T(8,128)(2,1)} %fusion.11.refs_0_, bf16[8,256,640]{2,1,0:T(8,128)(2,1)} %bitcast.31, bf16[1,336,384]{2,1,0:T(8,128)(2,1)} %pad_maximum_fusion.3.refs_2_, ...), custom_call_target="tpu_custom_call" | custom-call | flops 1000000 | bytes 209715200 | tf_op jit(solution)/shard_map/pallas_call | solution.py:979
  635.0 1.3 slice.38
  636.3 1.8 convert_element_type.115
  638.1 0.1 copy.43.gain_ref
  638.4 2.8 copy-done
  641.2 1.9 copy-done.3
  643.0 1.9 copy-done.4
  644.9 10.0 %shard_map.310 = (f32[256,6144]{1,0:T(8,128)}, f32[256,6144]{1,0:T(8,128)}, f32[256,1]{1,0:T(8,128)S(1)}) custom-call(f32[256,1]{1,0:T(8,128)S(1)} %copy.44.gain_ref, bf16[256,6144]{1,0:T(8,128)(2,1)S(1)} %copy-done.3, bf16[256,6144]{1,0:T(8,128)(2,1)S(1)} %copy-done.4, f32[256,6144]{1,0:T(8,128)S(1)} %copy-done, f32[256,6144]{1,0:T(8,128)} %wb_ref.3), custom_call_target="tpu_custom_call" | custom-call | flops 9437184 | bytes 31457280 | tf_op jit(solution)/shard_map/pallas_call | solution.py:1015
  655.0 0.7 reduce.5
  655.7 1.5 fusion.33
  657.1 0.6 divide_multiply_fusion
  657.7 0.9 fusion.37
  658.6 1.7 copy-done.2
  660.4 1.9 copy-done.5
  662.2 1.7 copy-done.6
  664.0 1.3 copy-done.7
  665.3 5.6 shard_map.309
  670.9 0.7 reduce
  671.6 2.3 fusion.18
  673.9 0.8 copy.47
  (57 shorter events, 0.5 us)
Async XLA Ops:
  8.0 650.6 %all-reduce.4.cloned.1.call-start = ((), (), s32[]{:S(2)}) async-start(), calls=%async_computation.2 | async-start | bytes 6291456 | tf_op jit(solution)/shard_map/psum | solution.py:1133
  15.7 181.8 %slice-start = ((s8[6291456]{0:T(1024)(128)(4,1)}), s8[2097152]{0:T(1024)(128)(4,1)S(1)}, s32[]{:S(2)}) async-start(s8[6291456]{0:T(1024)(128)(4,1)} %bitcast.40), calls=%async_computation.3 | async-start | bytes 4194304
  189.0 8.5 %slice-start.1 = ((s8[6291456]{0:T(1024)(128)(4,1)}), s8[4194304]{0:T(1024)(128)(4,1)S(1)}, s32[]{:S(2)}) async-start(s8[6291456]{0:T(1024)(128)(4,1)} %bitcast.40), calls=%async_computation.4 | async-start | bytes 8388608
  189.1 8.5 %copy-start.13 = (bf16[1024,2048]{1,0:T(8,128)(2,1)S(1)}, bf16[1024,2048]{1,0:T(8,128)(2,1)}, u32[]{:S(2)}) copy-start(bf16[1024,2048]{1,0:T(8,128)(2,1)} %get-tuple-element.62) | copy-start | bytes 12582916
  189.1 13.6 %slice-start.2 = ((s8[6291456]{0:T(1024)(128)(4,1)}), s8[4194304]{0:T(1024)(128)(4,1)S(1)}, s32[]{:S(2)}) async-start(s8[6291456]{0:T(1024)(128)(4,1)} %bitcast.43), calls=%async_computation.5 | async-start | bytes 8388608
  197.5 5.2 slice-start.3
  212.0 8.3 %copy-start.14 = (bf16[1024,2048]{1,0:T(8,128)(2,1)S(1)}, bf16[1024,2048]{1,0:T(8,128)(2,1)}, u32[]{:S(2)}) copy-start(bf16[1024,2048]{1,0:T(8,128)(2,1)} %get-tuple-element.59) | copy-start | bytes 12582916
  413.4 258.2 %reduce-scatter.2.cloned.1.call-start = ((), (), s32[]{:S(2)}) async-start(), calls=%async_computation.1 | async-start | bytes 4718592 | tf_op jit(solution)/shard_map/reduce_scatter | solution.py:1135
  421.5 35.0 %copy-start.8 = (bf16[1024,2048]{1,0:T(8,128)(2,1)S(1)}, bf16[1024,2048]{1,0:T(8,128)(2,1)}, u32[]{:S(2)}) copy-start(bf16[1024,2048]{1,0:T(8,128)(2,1)} %get-tuple-element.64.mid_ref) | copy-start | bytes 12582916
  421.5 35.0 %copy-start.15 = (bf16[1024,320]{1,0:T(8,128)(2,1)S(1)}, bf16[1024,320]{1,0:T(8,128)(2,1)}, u32[]{:S(2)}) copy-start(bf16[1024,320]{1,0:T(8,128)(2,1)} %get-tuple-element.61) | copy-start | bytes 1966084
  456.5 2.6 copy-start.12
  456.5 2.6 copy-start.16
  456.5 3.0 copy-start.17
  638.4 2.8 copy-start
  641.2 1.9 copy-start.3
  643.0 1.9 copy-start.4
  644.9 12.2 %copy-start.11 = (f32[320]{0:T(512)S(1)}, f32[320]{0:T(512)}, u32[]{:S(2)}) copy-start(f32[320]{0:T(512)} %param.30) | copy-start | bytes 3844
  644.9 12.8 %copy-start.9 = (bf16[336,384]{1,0:T(8,128)(2,1)S(1)}, bf16[336,384]{1,0:T(8,128)(2,1)}, u32[]{:S(2)}) copy-start(bf16[336,384]{1,0:T(8,128)(2,1)} %get-tuple-element.91) | copy-start | bytes 774148
  644.9 13.7 %copy-start.1 = (f32[256,2560]{1,0:T(8,128)S(1)}, f32[256,2560]{1,0:T(8,128)}, u32[]{:S(2)}) copy-start(f32[256,2560]{1,0:T(8,128)} %wa_ref.2) | copy-start | bytes 7864324
  658.6 1.7 copy-start.2
  660.4 1.9 copy-start.5
  662.2 1.7 copy-start.6
  664.0 1.3 copy-start.7
  665.3 8.6 %copy-start.10 = (bf16[128,2048]{1,0:T(8,128)(2,1)S(1)}, bf16[128,2048]{1,0:T(8,128)(2,1)}, u32[]{:S(2)}) copy-start(bf16[128,2048]{1,0:T(8,128)(2,1)} %get-tuple-element.84) | copy-start | bytes 1572868
Sparse Core Ops, SparseCore 0:
  413.5 166.8 all-reduce.3
Sparse Core Ops, SparseCore 1:
  421.6 48.2 reduce-scatter.1

commit v8 on v7

--- a/solution.py
+++ b/solution.py
@@ -138,115 +138,6 @@
         return tuple(states)
 
     lax.fori_loop(0, length // unroll, step, (jnp.zeros((sequences, 128), f32),) * tiles)
-
-
-def mix_backward_kernel(
-    sequences, length, mid_ref, ow_ref, w_ref, pre_ref, conv_in_ref, values_ref, recur_ref, inject_ref, decay_ref, states_ref,
-    label_ref, conv_ref, bias_ref, rw_ref, iw_ref,
-    partial_ref, branch_low_ref, conv_low_ref, dconv_ref, sums_ref, drw_ref, diw_ref,
-    adj, pad, lines, rbig, ibig, dr, di,
-):
-    fill_blocks(rbig, rw_ref)
-    fill_blocks(ibig, iw_ref)
-    dr[...] = jnp.zeros_like(dr)
-    di[...] = jnp.zeros_like(di)
-    sums_ref[...] = jnp.zeros_like(sums_ref)
-    dconv_ref[...] = jnp.zeros_like(dconv_ref)
-    taps = conv_ref.shape[0]
-    width = pad.shape[1]
-    clear_tail(adj, width)
-
-    def one(s, _):
-        base = pl.multiple_of(s * length, length)
-        here = pl.ds(base, length)
-        product_grad = dot_nt(mid_ref[here, :], ow_ref[...])
-        act, slope = gelu_parts(pre_ref[here, :])
-        branch_low_ref[here, :] = (product_grad * get_tiles(states_ref, here, width) * slope).astype(bf16)
-        put_tiles(adj, here, product_grad * act)
-        return 0
-
-    lax.fori_loop(0, sequences, one, 0)
-    seq_scan(decay_ref, adj, sequences, length, True)
-
-    def two(s, _):
-        base = pl.multiple_of(s * length, length)
-        here = pl.ds(base, length)
-        adjoint = get_tiles(adj, here, width)
-        recur = recur_ref[here, :]
-        inject = inject_ref[here, :]
-        decay = get_tiles(decay_ref, here, width)
-        values = values_ref[here, :]
-        values_f = values.astype(f32)
-        masks = label_masks(label_ref, here, length, width, taps, lines)
-        inside = masks[0] > 0.5
-        rate = bias_ref[3:4, :]
-        log_decay = -decay_scale * rate * recur
-        scale = jnp.where(inside, jnp.sqrt(minus_expm1(2.0 * log_decay)), 1.0)
-        pad[0:8, :] = jnp.zeros((8, width), f32)
-        pad[8 : 8 + length, :] = get_tiles(states_ref, here, width)
-        previous = pad[7 : 7 + length, :]
-        driven = adjoint * inject * values_f
-        log_grad = jnp.where(inside, adjoint * previous * decay - driven * decay * decay / scale, 0.0)
-        recur_low = (log_grad * (-decay_scale * rate) * recur * (1.0 - recur)).astype(bf16)
-        inject_low = (driven * scale * (1.0 - inject)).astype(bf16)
-        sums_ref[1:2, :] += jnp.sum(recur_low.astype(f32), axis=0, keepdims=True)
-        sums_ref[2:3, :] += jnp.sum(inject_low.astype(f32), axis=0, keepdims=True)
-        sums_ref[3:4, :] += jnp.sum(log_grad * recur, axis=0, keepdims=True)
-        dr[...] += dot_tn(values, recur_low)
-        di[...] += dot_tn(values, inject_low)
-        grad = adjoint * scale * inject
-        grad = grad + dot_nt(recur_low, rbig[...].astype(bf16)) + dot_nt(inject_low, ibig[...].astype(bf16))
-        sums_ref[0:1, :] += jnp.sum(grad, axis=0, keepdims=True)
-        pad[8 : 8 + length, :] = conv_in_ref[here, :].astype(f32)
-        dconv_ref[0:1, :] += jnp.sum(grad * pad[8 : 8 + length, :], axis=0, keepdims=True)
-        masked = []
-        for k in range(1, taps):
-            part = grad * masks[k - 1]
-            masked.append(part)
-            dconv_ref[k : k + 1, :] += jnp.sum(part * pad[8 - k : 8 - k + length, :], axis=0, keepdims=True)
-        total = grad * conv_ref[0:1, :]
-        pad[length : length + 8, :] = jnp.zeros((8, width), f32)
-        for k in range(1, taps):
-            pad[0:length, :] = masked[k - 1] * conv_ref[k : k + 1, :]
-            total = total + pad[k : k + length, :]
-        conv_low = total.astype(bf16)
-        conv_low_ref[here, :] = conv_low
-        partial_ref[here, :] = (dot_nt(branch_low_ref[here, :], whole_weight(w_ref, 0)) + dot_nt(conv_low, whole_weight(w_ref, 1))).astype(bf16)
-        return 0
-
-    lax.fori_loop(0, sequences, two, 0)
-    size = drw_ref.shape[1]
-    for h in range(drw_ref.shape[0]):
-        cut = slice(h * size, (h + 1) * size)
-        drw_ref[h] = dr[cut, cut]
-        diw_ref[h] = di[cut, cut]
-
-
-def mix_backward(sequences, mid_low, ow, weights, pre, conv_in, values, recur, inject, decay, states, labels, conv, bias, rw, iw):
-    total, depth = mid_low.shape
-    width = ow.shape[0]
-    length = total // sequences
-    shape = jax.ShapeDtypeStruct
-    return pl.pallas_call(
-        functools.partial(mix_backward_kernel, sequences, length),
-        out_shape=(
-            shape((total, depth), bf16), shape((total, width), bf16), shape((total, width), bf16),
-            shape(conv.shape, f32), shape((4, width), f32), shape(rw.shape, f32), shape(iw.shape, f32),
-        ),
-        in_specs=[VM] * 15,
-        out_specs=[VM] * 7,
-        scratch_shapes=[
-            pltpu.VMEM(states.shape, f32),
-            pltpu.VMEM((8 + length, width), f32),
-            pltpu.VMEM((8 + length, 128), f32),
-            pltpu.VMEM((width, width), f32),
-            pltpu.VMEM((width, width), f32),
-            pltpu.VMEM((width, width), f32),
-            pltpu.VMEM((width, width), f32),
-        ],
-        compiler_params=pltpu.CompilerParams(vmem_limit_bytes=56 * 2**20),
-        cost_estimate=pl.CostEstimate(flops=2 * total * width * 3 * depth, bytes_accessed=25 * 2**20, transcendentals=total * width * 5),
-    )(mid_low, ow, weights, pre, conv_in, values, recur, inject, decay, states, labels, conv, bias, rw, iw)
 
 
 def plane():
@@ -360,52 +251,6 @@
         return 0
 
     lax.fori_loop(0, rows // 16, tile, 0)
-
-
-def backward_steps(partial, middle_ref, cot_ref, low_ref, grad_ref, near, far, acc, *sems):
-    rows = middle_ref.shape[0]
-    offsets, at, block = plane()
-    scatter = scatter_steps(rows, partial, near, far, acc, sems[:4])
-    next(scatter)
-    yield
-    waits = next(scatter)
-    base = block(0, 0) * rows
-
-    def norm(here, i):
-        middle = middle_ref[here, :]
-        inverse = root_mean(middle)
-        grad = cot_ref[here, :].astype(f32) + norm_backward(acc[here, :], middle * inverse, inverse)
-        grad_ref[here, :] = grad
-        there = pl.ds(pl.multiple_of(base + i * 16, 16), 16)
-        low_ref[there, :] = grad.astype(bf16)
-
-    by_tiles(rows, norm)
-    gather = gather_steps(rows, low_ref, sems[4:])
-    next(gather)
-    yield
-    waits = waits + next(gather)
-    yield
-    for wait in waits:
-        wait()
-
-
-def last_steps(partial, grad_ref, x_ref, out_ref, near, far, acc, *sems):
-    rows = x_ref.shape[0]
-    scatter = scatter_steps(rows, partial, near, far, acc, sems[:4])
-    next(scatter)
-    yield
-    waits = next(scatter)
-
-    def norm(here, i):
-        value = x_ref[here, :].astype(f32)
-        inverse = root_mean(value)
-        grad = grad_ref[here, :] + norm_backward(acc[here, :], value * inverse, inverse)
-        out_ref[here, :] = grad.astype(bf16)
-
-    by_tiles(rows, norm)
-    yield
-    for wait in waits:
-        wait()
 
 
 def plane_scratch(rows, depth, gathers, scatters):
@@ -767,6 +612,187 @@
     )(x, label, cot, gains, conv, bias, rw, iw, branch_w, input_w, gate_w, up_w, output_w)
 
 
+def turn_steps(
+    sequences, length,
+    partial_hbm, middle_ref, cot_ref, label_ref, conv_ref, bias_ref, rw_ref, iw_ref, *rest,
+):
+    kept_hbm, rest = rest[:9], rest[9:]
+    low_out, grad_out, partial_out, branch_low_out, conv_low_out, dconv_ref, sums_ref, drw_ref, diw_ref = rest[:9]
+    scatter_sems, gather_sems = rest[9 + 3 : 9 + 7], rest[9 + 7 : 9 + 11]
+    near, far, acc = rest[9:12]
+    rest = rest[20:]
+    kept, rest = rest[:9], rest[9:]
+    ow_ref, w_ref, pre_ref, conv_in_ref, values_ref, recur_ref, inject_ref, decay_ref, states_ref = kept
+    partial, low_ref, grad_ref, branch_low_ref, conv_low_ref, adj, pad, lines, rbig, ibig, dr, di, load_sem, save_sem = rest
+    rows = middle_ref.shape[0]
+    offsets, at, block = plane()
+    first = pltpu.make_async_copy(partial_hbm, partial, load_sem.at[9])
+    first.start()
+    loads = [pltpu.make_async_copy(kept_hbm[k], kept[k], load_sem.at[k]) for k in range(9)]
+    for load in loads:
+        load.start()
+    first.wait()
+    scatter = scatter_steps(rows, partial, near, far, acc, scatter_sems)
+    next(scatter)
+    yield
+    waits = next(scatter)
+    base = block(0, 0) * rows
+
+    def norm(here, i):
+        middle = middle_ref[here, :]
+        inverse = root_mean(middle)
+        grad = cot_ref[here, :].astype(f32) + norm_backward(acc[here, :], middle * inverse, inverse)
+        grad_ref[here, :] = grad
+        there = pl.ds(pl.multiple_of(base + i * 16, 16), 16)
+        low_ref[there, :] = grad.astype(bf16)
+
+    by_tiles(rows, norm)
+    gather = gather_steps(rows, low_ref, gather_sems)
+    next(gather)
+    yield
+    waits = waits + next(gather)
+    yield
+    for wait in waits:
+        wait()
+    for load in loads:
+        load.wait()
+    saves = [pltpu.make_async_copy(low_ref, low_out, save_sem.at[0]), pltpu.make_async_copy(grad_ref, grad_out, save_sem.at[1])]
+    for save in saves:
+        save.start()
+    fill_blocks(rbig, rw_ref)
+    fill_blocks(ibig, iw_ref)
+    dr[...] = jnp.zeros_like(dr)
+    di[...] = jnp.zeros_like(di)
+    sums_ref[...] = jnp.zeros_like(sums_ref)
+    dconv_ref[...] = jnp.zeros_like(dconv_ref)
+    taps = conv_ref.shape[0]
+    width = pad.shape[1]
+    clear_tail(adj, width)
+
+    def one(s):
+        here = pl.ds(s * length, length)
+        product_grad = dot_nt(low_ref[here, :], ow_ref[...])
+        act, slope = gelu_parts(pre_ref[here, :])
+        branch_low_ref[here, :] = (product_grad * get_tiles(states_ref, here, width) * slope).astype(bf16)
+        put_tiles(adj, here, product_grad * act)
+
+    for s in range(sequences):
+        one(s)
+        yield
+    seq_scan(decay_ref, adj, sequences, length, True)
+    yield
+
+    def two(s):
+        here = pl.ds(s * length, length)
+        adjoint = get_tiles(adj, here, width)
+        recur = recur_ref[here, :]
+        inject = inject_ref[here, :]
+        decay = get_tiles(decay_ref, here, width)
+        values = values_ref[here, :]
+        values_f = values.astype(f32)
+        masks = label_masks(label_ref, here, length, width, taps, lines)
+        inside = masks[0] > 0.5
+        rate = bias_ref[3:4, :]
+        log_decay = -decay_scale * rate * recur
+        scale = jnp.where(inside, jnp.sqrt(minus_expm1(2.0 * log_decay)), 1.0)
+        pad[0:8, :] = jnp.zeros((8, width), f32)
+        pad[8 : 8 + length, :] = get_tiles(states_ref, here, width)
+        previous = pad[7 : 7 + length, :]
+        driven = adjoint * inject * values_f
+        log_grad = jnp.where(inside, adjoint * previous * decay - driven * decay * decay / scale, 0.0)
+        recur_low = (log_grad * (-decay_scale * rate) * recur * (1.0 - recur)).astype(bf16)
+        inject_low = (driven * scale * (1.0 - inject)).astype(bf16)
+        sums_ref[1:2, :] += jnp.sum(recur_low.astype(f32), axis=0, keepdims=True)
+        sums_ref[2:3, :] += jnp.sum(inject_low.astype(f32), axis=0, keepdims=True)
+        sums_ref[3:4, :] += jnp.sum(log_grad * recur, axis=0, keepdims=True)
+        dr[...] += dot_tn(values, recur_low)
+        di[...] += dot_tn(values, inject_low)
+        grad = adjoint * scale * inject
+        grad = grad + dot_nt(recur_low, rbig[...].astype(bf16)) + dot_nt(inject_low, ibig[...].astype(bf16))
+        sums_ref[0:1, :] += jnp.sum(grad, axis=0, keepdims=True)
+        pad[8 : 8 + length, :] = conv_in_ref[here, :].astype(f32)
+        dconv_ref[0:1, :] += jnp.sum(grad * pad[8 : 8 + length, :], axis=0, keepdims=True)
+        masked = []
+        for k in range(1, taps):
+            part = grad * masks[k - 1]
+            masked.append(part)
+            dconv_ref[k : k + 1, :] += jnp.sum(part * pad[8 - k : 8 - k + length, :], axis=0, keepdims=True)
+        total = grad * conv_ref[0:1, :]
+        pad[length : length + 8, :] = jnp.zeros((8, width), f32)
+        for k in range(1, taps):
+            pad[0:length, :] = masked[k - 1] * conv_ref[k : k + 1, :]
+            total = total + pad[k : k + length, :]
+        conv_low = total.astype(bf16)
+        conv_low_ref[here, :] = conv_low
+        partial[here, :] = (dot_nt(branch_low_ref[here, :], whole_weight(w_ref, 0)) + dot_nt(conv_low, whole_weight(w_ref, 1))).astype(bf16)
+
+    for s in range(sequences):
+        two(s)
+        yield
+    size = drw_ref.shape[1]
+    for h in range(drw_ref.shape[0]):
+        cut = slice(h * size, (h + 1) * size)
+        drw_ref[h] = dr[cut, cut]
+        diw_ref[h] = di[cut, cut]
+    ends = [(partial, partial_out), (branch_low_ref, branch_low_out), (conv_low_ref, conv_low_out)]
+    for k, pair in enumerate(ends):
+        saves.append(pltpu.make_async_copy(*pair, save_sem.at[2 + k]))
+        saves[-1].start()
+    yield
+    for save in saves:
+        save.wait()
+
+
+def end_steps(
+    partial_hbm, grad_ref, x_ref, middle_ref, hidden_hbm, down_hbm, tokens_ref, block_ref, *rest,
+):
+    near, far, acc = rest[:3]
+    scatter_sems = rest[3:7]
+    more_sems = rest[7:11]
+    near_two, far_two, partial, partial_two, hidden, down, load_sem = rest[11:]
+    rows = x_ref.shape[0]
+    loads = [
+        pltpu.make_async_copy(source, target, load_sem.at[k])
+        for k, (source, target) in enumerate(((partial_hbm, partial), (hidden_hbm, hidden), (down_hbm, down)))
+    ]
+    for load in loads:
+        load.start()
+    loads[0].wait()
+    scatter = scatter_steps(rows, partial, near, far, acc, scatter_sems)
+    next(scatter)
+    yield
+    loads[1].wait()
+    loads[2].wait()
+    pieces_of = 4
+    height = hidden.shape[0] // pieces_of
+    for k in range(pieces_of):
+        here = pl.ds(k * height, height)
+        partial_two[here, :] = dot_nn(hidden[here, :], down[...]).astype(bf16)
+        yield
+    waits = next(scatter)
+
+    def norm(here, i):
+        value = x_ref[here, :].astype(f32)
+        inverse = root_mean(value)
+        grad = grad_ref[here, :] + norm_backward(acc[here, :], value * inverse, inverse)
+        tokens_ref[here, :] = grad.astype(bf16)
+
+    by_tiles(rows, norm)
+    yield
+    scatter = scatter_steps(rows, partial_two, near_two, far_two, acc, more_sems)
+    next(scatter)
+    yield
+    waits = waits + next(scatter)
+
+    def out(here, i):
+        block_ref[here, :] = (middle_ref[here, :] + acc[here, :]).astype(bf16)
+
+    by_tiles(rows, out)
+    yield
+    for wait in waits:
+        wait()
+
+
 def pieces(rows, most):
     count = -(-rows // most)
     while rows % count or (rows // count) % 16:
@@ -787,11 +813,10 @@
 
     own_hbm, side_in = take(ins), take(extra_ins)
     outs, side_out = take(made), take(extra_outs)
-    side_scratch, scratch = take(extra_scratch), refs
-    own, from_out, from_in = scratch[:ins], scratch[ins : 2 * ins], scratch[2 * ins : 3 * ins]
-    columns = [k for k in range(ins) if kinds[k] != "row"]
-    swapped = dict(zip(columns, scratch[3 * ins :]))
-    load_sem, sent_in, sent_out, got_out, got_in, sent_x, got_x, out_sem = scratch[3 * ins + len(columns) :]
+    side_scratch = take(extra_scratch)
+    from_out, from_in = take(ins), take(ins)
+    slots, whole_sem, slot_sem, sent_in, sent_out, got_out, got_in, sent_x, got_x = refs
+    depth = slots.shape[0]
     me = lax.axis_index("replica")
     y, s = lax.axis_index("seq"), lax.axis_index("shard")
     shards = lax.axis_size("shard")
@@ -800,6 +825,7 @@
     inward = jnp.where(left, me + 1, me - 1)
     outward = jnp.where(left, me - 1, me + 1)
     has_out = jnp.logical_and(me > 0, me < n - 1)
+    at_end = jnp.logical_not(has_out)
     middle = jnp.logical_or(me == n // 2 - 1, me == n // 2)
 
     def peer(i):
@@ -807,23 +833,6 @@
 
     def place(i):
         return jnp.bitwise_xor(y, i // shards) * shards + jnp.bitwise_xor(s, i % shards)
-
-    loads = [pltpu.make_async_copy(own_hbm[k], own[k], load_sem.at[k]) for k in range(ins)]
-    for load in loads:
-        load.start()
-    barrier = pltpu.get_barrier_semaphore()
-    for i in range(1, owners):
-        pl.semaphore_signal(barrier, inc=1, device_id=peer(i), device_id_type=MESH)
-    pl.semaphore_signal(barrier, inc=1, device_id={"replica": inward}, device_id_type=MESH)
-
-    @pl.when(has_out)
-    def _():
-        pl.semaphore_signal(barrier, inc=1, device_id={"replica": outward}, device_id_type=MESH)
-        pl.semaphore_wait(barrier, owners + 1)
-
-    @pl.when(jnp.logical_not(has_out))
-    def _():
-        pl.semaphore_wait(barrier, owners)
 
     chunks = []
     for k, (lead, count, rows) in enumerate(cuts):
@@ -831,25 +840,54 @@
             for i in range(count):
                 chunks.append((k, step if kinds[k] == "row" else (step + 1) % lead, i * rows, rows))
     total = len(chunks)
-    ready = set()
-
-    def view(group, c, index=None):
+
+    def view(group, c):
         k, i, start, rows = chunks[c]
-        if index is None:
-            index = 0 if kinds[k] == "row" else place(i)
-        return group[k].at[index, pl.ds(start, rows), :]
+        return group[k].at[0 if kinds[k] == "row" else place(i), pl.ds(start, rows), :]
+
+    def slot(c):
+        k, i, start, rows = chunks[c]
+        return slots.at[c % depth, pl.ds(0, rows), pl.ds(0, from_in[k].shape[2])]
+
+    def load(c):
+        return pltpu.make_async_copy(view(own_hbm, c), slot(c), slot_sem.at[c % depth])
+
+    wholes = [pltpu.make_async_copy(own_hbm[k], from_out[k], whole_sem.at[k]) for k in range(ins)]
+
+    @pl.when(at_end)
+    def _():
+        for item in wholes:
+            item.start()
+
+    @pl.when(has_out)
+    def _():
+        for c in range(min(depth - 1, total)):
+            load(c).start()
+
+    barrier = pltpu.get_barrier_semaphore()
+    for i in range(1, owners):
+        pl.semaphore_signal(barrier, inc=1, device_id=peer(i), device_id_type=MESH)
+    pl.semaphore_signal(barrier, inc=1, device_id={"replica": inward}, device_id_type=MESH)
+
+    @pl.when(has_out)
+    def _():
+        pl.semaphore_signal(barrier, inc=1, device_id={"replica": outward}, device_id_type=MESH)
+        pl.semaphore_wait(barrier, owners + 1)
+
+    @pl.when(at_end)
+    def _():
+        pl.semaphore_wait(barrier, owners)
 
     def push(group, target, c, sent, got, device):
         return remote(view(group, c), view(target, c), sent.at[c], got.at[c], {"replica": device})
 
     def add(target, other, c):
         k, i, start, rows = chunks[c]
-        index = 0 if kinds[k] == "row" else place(i)
+        into, more = view(target, c), slot(c) if other is None else view(other, c)
 
         def tile(t, _):
-            here = pl.ds(pl.multiple_of(start + t * 16, 16), 16)
-            both = target[k][index, here, :].astype(f32) + other[k][index, here, :].astype(f32)
-            target[k][index, here, :] = both.astype(bf16)
+            here = pl.ds(pl.multiple_of(t * 16, 16), 16)
+            into[here, :] = (into[here, :].astype(f32) + more[here, :].astype(f32)).astype(bf16)
             return 0
 
         lax.fori_loop(0, rows // 16, tile, 0)
@@ -857,144 +895,125 @@
     def pass_in(c):
         @pl.when(middle)
         def _():
-            push(own, from_in, c, sent_in, got_in, inward).start()
+            push(from_out, from_in, c, sent_in, got_in, inward).start()
 
         @pl.when(jnp.logical_not(middle))
         def _():
-            push(own, from_out, c, sent_in, got_out, inward).start()
+            push(from_out, from_out, c, sent_in, got_out, inward).start()
 
     def gather_in(c):
         @pl.when(has_out)
         def _():
-            if chunks[c][0] not in ready:
-                loads[chunks[c][0]].wait()
-                ready.add(chunks[c][0])
+            load(c).wait()
             push(from_out, from_out, c, sent_in, got_out, inward).wait_recv()
-            add(own, from_out, c)
+            add(from_out, None, c)
             pass_in(c)
-
-    @pl.when(jnp.logical_not(has_out))
+            if c + depth - 1 < total:
+                load(c + depth - 1).start()
+
+    work = beside(*side_in, *side_out, *side_scratch)
+    next(work)
+
+    @pl.when(at_end)
     def _():
-        seen = set()
         for c in range(total):
-            if chunks[c][0] not in seen:
-                loads[chunks[c][0]].wait()
-                seen.add(chunks[c][0])
+            if c == 0 or chunks[c][0] != chunks[c - 1][0]:
+                wholes[chunks[c][0]].wait()
             pass_in(c)
 
-    def crosses(c):
-        return kinds[chunks[c][0]] != "row" and chunks[c][1] != 0
-
-    def hand_over(c):
-        k, i, start, rows = chunks[c]
-        return remote(
-            view(from_in, c), view(swapped, c, place(0)), sent_x.at[c], got_x.at[c], peer(i)
-        )
-
-    def stores(c):
+    def deliveries(c):
         k, i, start, rows = chunks[c]
         here = pl.ds(start, rows)
         first = k + kinds[:k].count("pair")
+        source = view(from_in, c)
         if kinds[k] == "row":
-            return [pltpu.make_async_copy(from_in[k].at[0, here, :], outs[first].at[here, :], out_sem.at[c, 0])]
-        source = swapped[k] if i else from_in[k]
-        index = place(i)
-        if kinds[k] == "side":
-            return [pltpu.make_async_copy(source.at[index, here, :], outs[first].at[index, here, :], out_sem.at[c, 0])]
-        half = source.shape[2] // 2
-        there = pl.ds(pl.multiple_of(index * half, half), half)
-        return [
-            pltpu.make_async_copy(
-                source.at[index, here, pl.ds(part * half, half)], outs[first + part].at[here, there], out_sem.at[c, part]
-            )
-            for part in range(2)
-        ]
+            ends = [(source, outs[first].at[here, :])]
+        elif kinds[k] == "side":
+            ends = [(source, outs[first].at[place(0), here, :])]
+        else:
+            half = source.shape[1] // 2
+            there = pl.ds(pl.multiple_of(place(0) * half, half), half)
+            ends = [
+                (source.at[:, pl.ds(part * half, half)], outs[first + part].at[here, there]) for part in range(2)
+            ]
+        if kinds[k] == "row" or i == 0:
+            return [pltpu.make_async_copy(*pair, sent_x.at[c, p]) for p, pair in enumerate(ends)], False
+        return [remote(*pair, sent_x.at[c, p], got_x.at[c, p], peer(i)) for p, pair in enumerate(ends)], True
 
     def give_back(c):
-        push(own, from_in, c, sent_out, got_in, inward).wait_recv()
+        push(from_out, from_in, c, sent_out, got_in, inward).wait_recv()
 
         @pl.when(middle)
         def _():
-            add(from_in, own, c)
+            add(from_in, from_out, c)
 
         @pl.when(has_out)
         def _():
             push(from_in, from_in, c, sent_out, got_in, outward).start()
 
-        if crosses(c):
-            hand_over(c).start()
-        else:
-            for copy in stores(c):
-                copy.start()
-
-    def finish(c):
-        if crosses(c):
-            hand_over(c).wait_recv()
-            for copy in stores(c):
-                copy.start()
-
-    lag, later = 2, 5
-    work = beside(*side_in, *side_out, *side_scratch)
-    for c in range(total + later):
-        for turn in turns:
-            if turn == c:
-                next(work)
+        for copy in deliveries(c)[0]:
+            copy.start()
+
+    lag = 2
+    for c in range(total + lag):
+        for _ in range(turns.count(c)):
+            next(work)
         if c < total:
             gather_in(c)
-        if 0 <= c - lag < total:
+        if c >= lag:
             give_back(c - lag)
-        if 0 <= c - later < total:
-            finish(c - later)
     for _ in work:
         pass
     for c in range(total):
-        for copy in stores(c):
-            copy.wait()
-        if crosses(c):
-            hand_over(c).wait_send()
-        push(own, from_in, c, sent_in, got_in, inward).wait_send()
+        copies, away = deliveries(c)
+        for copy in copies:
+            if away:
+                copy.wait_recv()
+                copy.wait_send()
+            else:
+                copy.wait()
+        push(from_out, from_in, c, sent_in, got_in, inward).wait_send()
 
         @pl.when(has_out)
         def _():
             push(from_in, from_in, c, sent_out, got_in, outward).wait_send()
 
 
-def replica_sum(arrays, kinds, identity, beside, turns, inputs, results, rows, depth, gathers):
-    cuts, outs, swaps = [], [], []
+def replica_sum(arrays, kinds, identity, beside, turns, inputs, results, side_scratch):
+    cuts, outs = [], []
+    tall = broad = 0
     for item, kind in zip(arrays, kinds):
         lead, height, columns = item.shape
-        count = pieces(height, max(16, (210 * 1024) // columns // 16 * 16))
+        count = pieces(height, max(16, (105 * 1024) // columns // 16 * 16))
         cuts.append((lead, count, height // count))
+        tall, broad = max(tall, height // count), max(broad, columns)
         if kind == "pair":
             outs += [jax.ShapeDtypeStruct((height, lead * columns // 2), bf16)] * 2
         elif kind == "side":
             outs.append(jax.ShapeDtypeStruct(item.shape, bf16))
         else:
             outs.append(jax.ShapeDtypeStruct((height, columns), bf16))
-        if kind != "row":
-            swaps.append(pltpu.VMEM(item.shape, bf16))
     count = sum(lead * cut for lead, cut, _ in cuts)
     buffers = [pltpu.VMEM(item.shape, bf16) for item in arrays]
-    side_scratch = plane_scratch(rows, depth, gathers, 1)
+    dma = pltpu.SemaphoreType.DMA
     return pl.pallas_call(
         functools.partial(
             line_kernel, lax.axis_size("replica"), tuple(kinds), tuple(cuts), beside, turns,
             (len(inputs), len(results), len(side_scratch)),
         ),
-        out_shape=tuple(outs) + tuple(jax.ShapeDtypeStruct(shape, kind) for shape, kind in results),
-        in_specs=[ANY] * len(arrays) + [VM] * len(inputs),
-        out_specs=[ANY] * len(outs) + [VM] * len(results),
-        scratch_shapes=side_scratch
-        + buffers * 3
-        + swaps
-        + [pltpu.SemaphoreType.DMA((len(arrays),))]
-        + [pltpu.SemaphoreType.DMA((count,))] * 6
-        + [pltpu.SemaphoreType.DMA((count, 2))],
+        out_shape=tuple(outs) + tuple(jax.ShapeDtypeStruct(shape, kind) for shape, kind, _ in results),
+        in_specs=[ANY] * len(arrays) + [spec for _, spec in inputs],
+        out_specs=[ANY] * len(outs) + [spec for _, _, spec in results],
+        scratch_shapes=list(side_scratch)
+        + buffers * 2
+        + [pltpu.VMEM((4, tall, broad), bf16), dma((len(arrays),)), dma((4,))]
+        + [dma((count,))] * 4
+        + [dma((count, 2))] * 2,
         compiler_params=pltpu.CompilerParams(
-            collective_id=identity, has_side_effects=True, vmem_limit_bytes=60 * 2**20
+            collective_id=identity, has_side_effects=True, vmem_limit_bytes=61 * 2**20
         ),
         cost_estimate=pl.CostEstimate(flops=10**6, bytes_accessed=200 * 2**20, transcendentals=0),
-    )(*arrays, *inputs)
+    )(*arrays, *[item for item, _ in inputs])
 
 
 def finish_pair_kernel(gain_ref, a_ref, b_ref, wa_ref, wb_ref, outa_ref, outb_ref, grad_ref):
@@ -1018,14 +1037,14 @@
         out_shape=(out, out, jax.ShapeDtypeStruct((rows, 1), f32)),
         in_specs=[thin, wide, wide, wide, wide],
         out_specs=[wide, wide, thin],
-        compiler_params=pltpu.CompilerParams(vmem_limit_bytes=40 * 2**20),
+        compiler_params=pltpu.CompilerParams(vmem_limit_bytes=61 * 2**20),
         cost_estimate=pl.CostEstimate(flops=6 * rows * columns, bytes_accessed=20 * rows * columns, transcendentals=0),
     )(gain, a, b, wa, wb)
 
 
 def finish_rest_kernel(gain_ref, mix_ref, wa_ref, wb_ref, out_sum_ref, down_sum_ref, outa_ref, outb_ref, grad_ref, out_ref, down_ref):
-    owners, _, width = mix_ref.shape
-    width = width // 2
+    owners = mix_ref.shape[0]
+    width = wa_ref.shape[1] // owners
     grad = jnp.zeros(gain_ref.shape, f32)
     for part, (weight_ref, target_ref) in enumerate(((wa_ref, outa_ref), (wb_ref, outb_ref))):
         total = jnp.concatenate(
@@ -1068,7 +1087,7 @@
             tall(down_sum),
         ],
         out_specs=[wide, wide, thin, tall(out_sum), tall(down_sum)],
-        compiler_params=pltpu.CompilerParams(vmem_limit_bytes=40 * 2**20),
+        compiler_params=pltpu.CompilerParams(vmem_limit_bytes=61 * 2**20),
         cost_estimate=pl.CostEstimate(flops=10**7, bytes_accessed=40 * 2**20, transcendentals=0),
     )(gain, mix, wa, wb, out_sum, down_sum)
 
@@ -1124,23 +1143,33 @@
     pair_low = jnp.concatenate([gate_low, up_low], 1)
     partial = mm_nt(pair_low, pair_w).astype(bf16)
     pair_partial = mm_tn(unit_two, pair_low).astype(bf16).reshape(members, -1, 2 * ff)
-    down_partial = mm_tn(hidden, out_low).astype(bf16)
-    gate_sum, up_sum, mid_low, middle_grad = replica_sum(
-        [pair_partial], ["pair"], 3, backward_steps, (0, 3, 6),
-        (partial, middle, cot), (whole, ((rows, depth), f32)), rows, depth, 1,
+    down_partial = mm_tn(hidden, out_low).astype(bf16)[None]
+    kept = (output_w, mix_w, *mixed)
+    narrow = ((total, width), bf16)
+    vm, dma = pltpu.VMEM, pltpu.SemaphoreType.DMA
+    length = total // sequences
+    back = replica_sum(
+        [down_partial, pair_partial], ["row", "pair"], 3,
+        functools.partial(turn_steps, sequences, length),
+        (6, 12) + tuple(range(14, 14 + 2 * sequences + 2)),
+        [(partial, ANY)] + [(item, VM) for item in (middle, cot, labels, conv_f, bias, recur_gate_weight, input_gate_weight)]
+        + [(item, ANY) for item in kept],
+        [whole + (ANY,), ((rows, depth), f32, ANY), whole + (ANY,), narrow + (ANY,), narrow + (ANY,)]
+        + [(conv_f.shape, f32, VM), ((4, width), f32, VM), (recur_gate_weight.shape, f32, VM), (input_gate_weight.shape, f32, VM)],
+        plane_scratch(rows, depth, 1, 1)
+        + [vm(item.shape, item.dtype) for item in kept]
+        + [vm(*whole), vm(*whole), vm((rows, depth), f32), vm(*narrow), vm(*narrow), vm(mixed[-1].shape, f32)]
+        + [vm((8 + length, width), f32), vm((8 + length, 128), f32)]
+        + [vm((width, width), f32)] * 4
+        + [dma((10,)), dma((5,))],
     )
-    mid_low, down_partial = lax.optimization_barrier((mid_low, down_partial))
-    down_sum = lax.psum(down_partial, "replica")
+    down_sum, gate_sum, up_sum, mid_low, middle_grad, partial, branch_low, conv_low = back[:8]
+    conv_weight_grad, sums, recur_weight_grad, inject_weight_grad = back[8:]
     gate_grad, up_grad, mlp_gain_grad = finish_pair(mlp_gain, gate_sum, up_sum, gate_weight, up_weight)
-    block_sum = lax.psum_scatter(mm(hidden, down_w).astype(bf16), ROWS, scatter_dimension=0, tiled=True)
-    block_out = (middle + block_sum.astype(f32)).astype(bf16)
     output_partial = mm_tn(product, mid_low).astype(bf16)[None]
-    back = mix_backward(
-        sequences, mid_low, output_w, mix_w, *mixed, labels, conv_f, bias, recur_gate_weight, input_gate_weight
-    )
-    partial, branch_low, conv_low, conv_weight_grad, sums, recur_weight_grad, inject_weight_grad = back
     mix_low = jnp.concatenate([branch_low, conv_low], 1)
-    mix_partial = mm_tn(unit_all, mix_low).astype(bf16).reshape(members, -1, 2 * width)
+    mix_low = jnp.pad(mix_low, ((0, 0), (0, -2 * width % 128)))
+    mix_partial = mm_tn(unit_all, mix_low).astype(bf16).reshape(members, -1, mix_low.shape[1])
     size = recur_gate_weight.shape[1]
     gates = jnp.concatenate([recur_weight_grad, inject_weight_grad], 2).reshape(width, 2 * size)
     lanes = -(-max(width, 2 * size) // 128) * 128
@@ -1152,9 +1181,12 @@
         ],
         0,
     ).astype(bf16)[None]
-    output_sum, mix_sum, packed, tokens_grad = replica_sum(
-        [output_partial, mix_partial, packed], ["row", "side", "row"], 4, last_steps, (0, 3),
-        (partial, middle_grad, x), (((rows, depth), bf16),), rows, depth, 0,
+    again = plane_scratch(rows, depth, 1, 1)
+    output_sum, mix_sum, packed, tokens_grad, block_out = replica_sum(
+        [output_partial, mix_partial, packed], ["row", "side", "row"], 4, end_steps, (1, 2, 3, 4, 6, 7, 14),
+        [(partial, ANY), (middle_grad, VM), (x, VM), (middle, VM), (hidden, ANY), (down_w, ANY)],
+        [((rows, depth), bf16, VM), ((rows, depth), bf16, VM)],
+        again + again[:2] + [vm(*whole), vm(*whole), vm(hidden.shape, bf16), vm(down_w.shape, bf16), dma((3,))],
     )
     packed = packed.astype(f32)
     branch_grad, input_grad, gain_grad, output_grad, down_grad = finish_rest(

time: 690 us -> 638 us (0.925)
  between operations: 15.9 us -> 1.33 us
  Pallas kernels: 569 us -> 555 us
  local copies, waits for them, and re-layouts: 18.5 us -> 9.82 us
  matrix products: 61 us -> 52.8 us
    pallas_call x1 -> x0, Pallas kernels: 30.7 us -> none  [mix_backward(): pl.pallas_call(functools.partial(mix_backward_kernel, sequences, length),...]
    dot_general x3 -> x2, matrix products: 25.7 us -> 15.3 us  [mm(): return jnp.dot(left, right, preferred_element_type=f32)]
    unnamed x45 -> x46, local copies, waits for them, and re-layouts: 14.5 us -> 5.17 us
    pallas_call x2, Pallas kernels: 349 us -> 358 us  [replica_sum(): pl.pallas_call(functools.partial(line_kernel, lax.axis_size('replica'), t...]
  transfers between devices with their start and end apart: 2 -> 0, of which waited for: 0 -> 0; matrix products, arithmetic and copies ran while one was open for 4% -> 0% of each run, Pallas kernels for 32% -> 0%
where the time goes in v8:
time: 638 us; the launch traced here: 630 us
  Pallas kernels  555 us (87%)
  matrix products  52.8 us (8%)
  other arithmetic  11.9 us (2%)
  local copies, waits for them, and re-layouts  9.82 us (2%)
    pallas_call x2, Pallas kernels, replica_sum(): pl.pallas_call(functools.partial(line_kernel, lax.axis_size('replica'), t...  358 us
    pallas_call x1, Pallas kernels, front(): pl.pallas_call(functools.partial(front_kernel, n, sequences, length), out...  173 us
    dot_general x4, matrix products, mm_tn(): lax.dot_general(left, right, (((0,), (0,)), ((), ())), preferred_element_...  23.8 us
    dot_general x2, matrix products, mm(): return jnp.dot(left, right, preferred_element_type=f32)  15.3 us
    dot_general x2, matrix products, mm_nt(): lax.dot_general(left, right, (((1,), (1,)), ((), ())), preferred_element_...  13.7 us
    pallas_call x1, Pallas kernels, finish_pair(): pl.pallas_call(finish_pair_kernel, grid=(rows // cut,), out_shape=(out, o...  13.6 us

profile of v8, /device:TPU:0, one launch (start us, length us, event | category | flops | bytes accessed | tf_op | source)
XLA Modules:
  0.0 630.4 jit_solution(6346774228650568030)
XLA Ops:
  0.7 0.7 convert.34
  1.3 0.7 convert.35
  2.0 0.8 copy.75.gains_ref
  2.8 0.7 convert_convert_fusion.1
  3.5 0.7 convert_convert_fusion.3
  4.2 0.7 convert_convert_fusion.2
  4.9 0.7 compare_select_fusion
  5.6 1.3 pad_maximum_fusion.5
  6.9 0.7 convert_bitcast_fusion
  7.6 0.7 broadcast_in_dim.25.label_ref
  8.3 173.3 %shard_map.305 = (bf16[1024,2048]{1,0:T(8,128)(2,1)}, bf16[1024,128]{1,0:T(8,128)(2,1)}, bf16[1024,2048]{1,0:T(8,128)(2,1)}, bf16[1024,320]{1,0:T(8,128)(2,1)}, ...) custom-call(bf16[128,2048]{1,0:T(8,128)(2,1)} %bitcast.37, ...), custom_call_target="tpu_custom_call" | custom-call | flops 1000000 | bytes 209715200 | tf_op jit(solution)/shard_map/pallas_call | solution.py:602
  181.6 0.0 slice-start.1
  181.6 8.4 %fusion.7 = f32[1024,768]{1,0:T(8,128)} fusion(bf16[1024,2048]{1,0:T(8,128)(2,1)} %get-tuple-element.59, bf16[2048,1536]{1,0:T(8,128)(2,1)} %bitcast.44), kind=kOutput, calls=%fused_computation.13 | convolution fusion | flops 3221225472 | bytes 10485760 | tf_op jit(solution)/shard_map/dot_general | solution.py:22
  190.0 0.0 slice-done
  190.0 0.0 slice-done.1
  190.0 0.0 slice-start.2
  190.0 0.5 convert_element_type.96.refs_8_
  190.5 0.0 copy-start
  190.5 1.6 copy-done
  192.2 1.2 copy-done.11
  193.4 3.5 fusion.35
  196.8 0.0 slice-done.2
  196.8 0.0 slice-done.3
  196.8 0.0 copy-done.12
  196.8 0.7 copy-done.16
  197.5 6.9 %fusion.6 = (bf16[1024,768]{1,0:T(8,128)(2,1)S(1)}, bf16[1024,768]{1,0:T(8,128)(2,1)}, bf16[1024,768]{1,0:T(8,128)(2,1)S(1)}) fusion(f32[1024,768]{1,0:T(8,128)S(1)} %fusion.35, f32[1024,768]{1,0:T(8,128)S(1)} %copy-done.16, bf16[1024,2048]{1,0:T(8,128)(2,1)S(1)} %copy-done.12, bf16[2048,1536]{1,0:T(8,128)(2,1)S(1)} %bitcast.47), kind=kOutput, calls=%fused_computation.12 | convolution fusion | flops 3240886272 | bytes 18350080 | tf_op jit(solution)/shard_map/dot_general | solution.py:22
  204.5 10.2 %convolution_convert_fusion.1.refs_2_ = bf16[1024,2048]{1,0:T(8,128)(2,1)} fusion(bf16[2048,1536]{1,0:T(8,128)(2,1)S(1)} %bitcast.48, bf16[1024,768]{1,0:T(8,128)(2,1)} %get-tuple-element.104, bf16[1024,768]{1,0:T(8,128)(2,1)S(1)} %get-tuple-element.103), kind=kOutput, calls=%fused_computation.3 | convolution fusion | flops 6450839552 | bytes 13631488 | tf_op jit(solution)/shard_map/dot_general | solution.py:26
  214.7 8.9 %convolution_convert_fusion = bf16[2048,1536]{1,0:T(8,128)(2,1)} fusion(bf16[1024,2048]{1,0:T(8,128)(2,1)S(1)} %copy-done.12, bf16[1024,768]{1,0:T(8,128)(2,1)S(1)} %copy-done.17, bf16[1024,768]{1,0:T(8,128)(2,1)S(1)} %get-tuple-element.103), kind=kOutput, calls=%fused_computation | convolution fusion | flops 6451888128 | bytes 13631488 | tf_op jit(solution)/shard_map/dot_general | solution.py:30
  223.6 4.8 fusion.11.refs_0_
  228.5 235.9 %shard_map.306 = (bf16[768,2048]{1,0:T(8,128)(2,1)}, bf16[256,6144]{1,0:T(8,128)(2,1)}, bf16[256,6144]{1,0:T(8,128)(2,1)}, bf16[1024,2048]{1,0:T(8,128)(2,1)}, f...) custom-call(bf16[1,768,2048]{2,1,0:T(8,128)(2,1)} %fusion.11.refs_0_, ...), custom_call_target="tpu_custom_call" | custom-call | flops 1000000 | bytes 209715200 | tf_op jit(solution)/shard_map/pallas_call | solution.py:999
  464.3 0.8 copy.88.gain_ref
  465.2 13.6 %shard_map.309 = (f32[256,6144]{1,0:T(8,128)}, f32[256,6144]{1,0:T(8,128)}, f32[256,1]{1,0:T(8,128)}) custom-call(f32[256,1]{1,0:T(8,128)} %copy.88.gain_ref, bf16[256,6144]{1,0:T(8,128)(2,1)} %get-tuple-element.93.a_ref, bf16[256,6144]{1,0:T(8,128)(2,1)} %get-tuple-element.94.b_ref, f32[256,6144]{1,0:T(8,128)} %wa_ref.3, f32[256,6144]{1,0:T(8,128)} %wb_ref.3), custom_call_target="tpu_custom_call" | custom-call | flops 9437184 | bytes 31457280 | tf_op jit(solution)/shard_map/pallas_call | solution.py:1034
  478.7 1.6 reduce.5
  480.4 0.1 pad_maximum_fusion.4
  480.6 0.7 pad_maximum_fusion.3.refs_2_
  481.3 7.4 %convolution_convert_fusion.3 = bf16[2048,640]{1,0:T(8,128)(2,1)} fusion(bf16[1024,2048]{1,0:T(8,128)(2,1)} %get-tuple-element.74, bf16[1024,320]{1,0:T(8,128)(2,1)S(1)} %copy-done.15, bf16[1024,320]{1,0:T(8,128)(2,1)S(1)} %copy-done.14), kind=kOutput, calls=%fused_computation.5 | convolution fusion | flops 2688286720 | bytes 8126464 | tf_op jit(solution)/shard_map/dot_general | solution.py:30
  488.8 0.0 copy-done.13
  488.8 2.6 fusion.12.refs_0_
  491.4 121.8 %shard_map.307 = (bf16[320,2048]{1,0:T(8,128)(2,1)}, bf16[8,256,640]{2,1,0:T(8,128)(2,1)}, bf16[336,384]{1,0:T(8,128)(2,1)}, bf16[128,2048]{1,0:T(8,128)(2,1)}, bf16[128,2048]{1,0:T(8,128)(2,1)}) custom-call(bf16[1,320,2048]{2,1,0:T(8,128)(2,1)} %fusion.12.refs_0_, bf16[8,256,640]{2,1,0:T(8,128)(2,1)} %bitcast.34, ...), custom_call_target="tpu_custom_call" | custom-call | flops 1000000 | bytes 209715200 | tf_op jit(solution)/shard_map/pallas_call | solution.py:999
  613.2 0.8 copy.87.gain_ref
  614.0 10.0 %shard_map.308 = (f32[256,2560]{1,0:T(8,128)}, f32[256,2560]{1,0:T(8,128)}, f32[256,1]{1,0:T(8,128)}, f32[320,2048]{1,0:T(8,128)}, f32[768,2048]{1,0:T(8,128)}) custom-call(f32[256,1]{1,0:T(8,128)} %copy.87.gain_ref, bf16[8,256,640]{2,1,0:T(8,128)(2,1)} %get-tuple-element.85.mix_ref, f32[256,2560]{1,0:T(8,128)} %wa_ref.2, f32[256,2560]{1,0:T(8,128)} %wb_ref.2, ...), custom_call_target="tpu_custom_call" | custom-call | flops 10000000 | bytes 41943040 | tf_op jit(solution)/shard_map/pallas_call | solution.py:1071
  624.0 1.6 reduce
  625.7 0.9 fusion.34
  626.6 0.6 fusion.30
  627.2 0.6 divide_multiply_fusion
  627.8 0.6 slice.38
  628.4 0.8 copy.94
  629.2 0.8 copy.95
  (50 shorter events, 0.2 us)
Async XLA Ops:
  8.3 181.7 %slice-start = ((s8[6291456]{0:T(1024)(128)(4,1)}), s8[2097152]{0:T(1024)(128)(4,1)S(1)}, s32[]{:S(2)}) async-start(s8[6291456]{0:T(1024)(128)(4,1)} %bitcast.31), calls=%async_computation | async-start | bytes 4194304
  181.6 8.4 %slice-start.1 = ((s8[6291456]{0:T(1024)(128)(4,1)}), s8[4194304]{0:T(1024)(128)(4,1)S(1)}, s32[]{:S(2)}) async-start(s8[6291456]{0:T(1024)(128)(4,1)} %bitcast.31), calls=%async_computation.1 | async-start | bytes 8388608
  190.0 3.3 copy-start.11
  190.0 6.8 %slice-start.2 = ((s8[6291456]{0:T(1024)(128)(4,1)}), s8[4194304]{0:T(1024)(128)(4,1)S(1)}, s32[]{:S(2)}) async-start(s8[6291456]{0:T(1024)(128)(4,1)} %bitcast.45), calls=%async_computation.2 | async-start | bytes 8388608
  190.5 1.7 copy-start
  193.3 3.5 slice-start.3
  193.3 3.5 copy-start.12
  193.4 4.2 copy-start.16
  204.5 19.2 %copy-start.2 = (bf16[1024,768]{1,0:T(8,128)(2,1)}, bf16[1024,768]{1,0:T(8,128)(2,1)S(1)}, u32[]{:S(2)}) copy-start(bf16[1024,768]{1,0:T(8,128)(2,1)S(1)} %get-tuple-element.105.refs_7_) | copy-start | bytes 4718596
  204.5 10.2 %copy-start.17 = (bf16[1024,768]{1,0:T(8,128)(2,1)S(1)}, bf16[1024,768]{1,0:T(8,128)(2,1)}, u32[]{:S(2)}) copy-start(bf16[1024,768]{1,0:T(8,128)(2,1)} %get-tuple-element.104) | copy-start | bytes 4718596
  465.1 15.2 %copy-start.6 = (f32[2,160,160]{2,1,0:T(8,128)S(1)}, f32[2,160,160]{2,1,0:T(8,128)}, u32[]{:S(2)}) copy-start(f32[2,160,160]{2,1,0:T(8,128)} %get-tuple-element.77) | copy-start | bytes 614404
  465.2 15.2 %copy-start.5 = (f32[2,160,160]{2,1,0:T(8,128)S(1)}, f32[2,160,160]{2,1,0:T(8,128)}, u32[]{:S(2)}) copy-start(f32[2,160,160]{2,1,0:T(8,128)} %get-tuple-element.78) | copy-start | bytes 614404
  465.2 15.4 %copy-start.9 = (f32[4,320]{1,0:T(4,128)S(1)}, f32[4,320]{1,0:T(4,128)}, u32[]{:S(2)}) copy-start(f32[4,320]{1,0:T(4,128)} %get-tuple-element.79) | copy-start | bytes 15364
  465.2 15.4 %copy-start.8 = (f32[4,320]{1,0:T(4,128)S(1)}, f32[4,320]{1,0:T(4,128)}, u32[]{:S(2)}) copy-start(f32[4,320]{1,0:T(4,128)} %get-tuple-element.80) | copy-start | bytes 15364
  465.2 16.2 %copy-start.14 = (bf16[1024,320]{1,0:T(8,128)(2,1)S(1)}, bf16[1024,320]{1,0:T(8,128)(2,1)}, u32[]{:S(2)}) copy-start(bf16[1024,320]{1,0:T(8,128)(2,1)} %get-tuple-element.75) | copy-start | bytes 1966084
  465.2 16.2 %copy-start.15 = (bf16[1024,320]{1,0:T(8,128)(2,1)S(1)}, bf16[1024,320]{1,0:T(8,128)(2,1)}, u32[]{:S(2)}) copy-start(bf16[1024,320]{1,0:T(8,128)(2,1)} %get-tuple-element.76) | copy-start | bytes 1966084
  481.3 7.4 %copy-start.10 = (bf16[1024,2048]{1,0:T(8,128)(2,1)S(1)}, bf16[1024,2048]{1,0:T(8,128)(2,1)}, u32[]{:S(2)}) copy-start(bf16[1024,2048]{1,0:T(8,128)(2,1)} %get-tuple-element.73) | copy-start | bytes 12582916
  481.3 7.4 %copy-start.13 = (bf16[1024,320]{1,0:T(8,128)(2,1)S(1)}, bf16[1024,320]{1,0:T(8,128)(2,1)}, u32[]{:S(2)}) copy-start(bf16[1024,320]{1,0:T(8,128)(2,1)} %get-tuple-element.58) | copy-start | bytes 1966084
  614.0 11.7 %copy-start.1 = (bf16[336,384]{1,0:T(8,128)(2,1)S(1)}, bf16[336,384]{1,0:T(8,128)(2,1)}, u32[]{:S(2)}) copy-start(bf16[336,384]{1,0:T(8,128)(2,1)} %get-tuple-element.91) | copy-start | bytes 774148
  614.0 13.2 %copy-start.7 = (f32[320]{0:T(512)S(1)}, f32[320]{0:T(512)}, u32[]{:S(2)}) copy-start(f32[320]{0:T(512)} %param.30) | copy-start | bytes 3844
  614.0 14.4 %copy-start.4 = (bf16[128,2048]{1,0:T(8,128)(2,1)S(1)}, bf16[128,2048]{1,0:T(8,128)(2,1)}, u32[]{:S(2)}) copy-start(bf16[128,2048]{1,0:T(8,128)(2,1)} %get-tuple-element.83) | copy-start | bytes 1572868
  624.0 5.2 copy-start.3

commit v9 on v8

--- a/solution.py
+++ b/solution.py
@@ -213,27 +213,53 @@
     offsets, at, block = plane()
     near_sent, near_got, far_sent, far_got = sems
     count = len(offsets)
+    half = rows // 2
+
+    def piece(q, part):
+        start = pl.multiple_of(block(*offsets[q]) * rows + part * half, 16)
+        return whole.at[pl.ds(start, half), :]
+
     own = row_block(whole, block(0, 0), rows)
-    sends = []
+    straight = [q for q in range(1, count) if offsets[q][0] == 0 or offsets[q][1] == 0]
+    across = [q for q in range(1, count) if q not in straight]
+    upright = [q for q in straight if offsets[q][0]]
+    sends, arrivals = [], []
     outs = {}
-    for q in range(count - 1, 0, -1):
-        dy, ds = offsets[q]
-        outs[q] = remote(own, own, far_sent.at[q - 1], far_got.at[q - 1], at(dy, ds))
+    for q in straight:
+        outs[q] = remote(own, own, far_sent.at[q], far_got.at[q], at(*offsets[q]))
         outs[q].start()
         sends.append(outs[q].wait_send)
-    hand = remote(own, own, near_sent.at[0], near_got.at[0], at(0, 1))
-    hand.start()
-    sends.append(hand.wait_send)
-    arrivals = [hand.wait_recv]
+
+    def hand(q, part=None):
+        source = row_block(whole, block(*offsets[q]), rows) if part is None else piece(q, part)
+        place = q if part is None or part == 0 else count + q
+        copy = remote(source, source, near_sent.at[place], near_got.at[place], at(0, 1))
+        copy.start()
+        sends.append(copy.wait_send)
+        arrivals.append(copy.wait_recv)
+
+    hand(0)
     yield None
-    for q in list(range(1, count)):
-        dy, ds = offsets[q]
+    onward = {}
+    for q in straight:
         outs[q].wait_recv()
-        block_q = row_block(whole, block(dy, ds), rows)
-        hand = remote(block_q, block_q, near_sent.at[q], near_got.at[q], at(0, 1))
-        hand.start()
-        sends.append(hand.wait_send)
-        arrivals.append(hand.wait_recv)
+        if q in upright:
+            targets = [(1, t) for t in straight if t not in upright]
+        else:
+            targets = [(0, t) for t in upright]
+        for part, t in targets:
+            dy, ds = offsets[q][0] | offsets[t][0], offsets[q][1] | offsets[t][1]
+            a = offsets.index((dy, ds))
+            source = piece(q, part)
+            onward[a, part] = remote(source, source, far_sent.at[part * count + a], far_got.at[part * count + a], at(*offsets[t]))
+            onward[a, part].start()
+            sends.append(onward[a, part].wait_send)
+        hand(q)
+    yield None
+    for a in across:
+        for part in range(2):
+            onward[a, part].wait_recv()
+            hand(a, part)
     yield arrivals + sends
 
 
@@ -263,8 +289,11 @@
             pltpu.VMEM((count - 1,) + block, bf16),
             pltpu.VMEM(block, f32),
         ]
-    for _ in range(scatters + gathers):
-        scratch += [pltpu.SemaphoreType.DMA((count,))] * 2 + [pltpu.SemaphoreType.DMA((count - 1,))] * 2
+    dma = pltpu.SemaphoreType.DMA
+    for _ in range(scatters):
+        scratch += [dma((count,))] * 2 + [dma((count - 1,))] * 2
+    for _ in range(gathers):
+        scratch += [dma((2 * count,))] * 4
     return scratch
 
 
@@ -409,30 +438,6 @@
     def _():
         pl.semaphore_signal(barrier, inc=1, device_id={"replica": z + 1}, device_id_type=MESH)
 
-    base = block(0, 0) * rows
-
-    def unit(here, i):
-        value = x_ref[here, :].astype(f32)
-        there = pl.ds(pl.multiple_of(base + i * 16, 16), 16)
-        unit_ref[there, :] = (value * root_mean(value)).astype(bf16)
-        labels_ref[there, :] = label_ref[here, :]
-
-    by_tiles(rows, unit)
-    inside_line = jnp.logical_and(z > 0, z < n - 1)
-
-    @pl.when(inside_line)
-    def _():
-        pl.semaphore_wait(barrier, owners + 1)
-
-    @pl.when(jnp.logical_not(inside_line))
-    def _():
-        pl.semaphore_wait(barrier, owners)
-
-    label_gather = gather_steps(rows, labels_ref, label_sems)
-    unit_gather = gather_steps(rows, unit_ref, unit_sems)
-    next(label_gather)
-    next(unit_gather)
-
     for side in range(2):
         loads[side].wait()
 
@@ -443,6 +448,17 @@
             side * ff,
             ff,
         )
+
+    inside_line = jnp.logical_and(z > 0, z < n - 1)
+
+    @pl.when(inside_line)
+    def _():
+        pl.semaphore_wait(barrier, owners + 1)
+
+    @pl.when(jnp.logical_not(inside_line))
+    def _():
+        pl.semaphore_wait(barrier, owners)
+
     me = place(0)
     pair_there = pair_out.at[me, own_rows, :]
     pair_moves = [
@@ -452,6 +468,20 @@
         move.start()
     pair_own = pltpu.make_async_copy(pair_cut.at[me], pair_there, pair_sent.at[0])
     pair_own.start()
+
+    base = block(0, 0) * rows
+
+    def unit(here, i):
+        value = x_ref[here, :].astype(f32)
+        there = pl.ds(pl.multiple_of(base + i * 16, 16), 16)
+        unit_ref[there, :] = (value * root_mean(value)).astype(bf16)
+        labels_ref[there, :] = label_ref[here, :]
+
+    by_tiles(rows, unit)
+    label_gather = gather_steps(rows, labels_ref, label_sems)
+    unit_gather = gather_steps(rows, unit_ref, unit_sems)
+    next(label_gather)
+    next(unit_gather)
 
     for side in range(2):
         loads[2 + side].wait()
@@ -475,13 +505,14 @@
     clear_tail(decay_ref, width)
     clear_tail(states_ref, width)
 
-    waits = next(label_gather)
-    waits = waits + next(unit_gather)
     pair_own.wait()
     for move in pair_moves:
         move.wait_recv()
     line = quarter_steps(n, part, pair_out, line_sems)
     next(line)
+    next(label_gather)
+    next(unit_gather)
+    waits = next(label_gather) + next(unit_gather)
     for wait in waits:
         wait()
     mix_own.wait()
@@ -494,6 +525,7 @@
     low_own.wait()
     low_gather = gather_steps(rows, low_out, low_sems)
     next(low_gather)
+    next(line)
 
     def one(q, _):
         here = pl.ds(pl.multiple_of(q * length, length), length)
@@ -539,8 +571,8 @@
     ):
         save(source, target)
     next(line)
-    waits = next(low_gather)
-    waits = waits + next(scatter)
+    next(low_gather)
+    waits = next(low_gather) + next(scatter)
 
     def norm(here, i):
         middle = x_ref[here, :].astype(f32) + acc[here, :]
@@ -552,12 +584,12 @@
     two_gather = gather_steps(rows, two_ref, two_sems)
     next(two_gather)
     save(middle_ref, middle_out)
-    for _ in range(n - 3):
+    for _ in range(n - 4):
         next(line)
     for wait in waits:
         wait()
-    waits = next(two_gather)
-    for wait in waits:
+    next(two_gather)
+    for wait in next(two_gather):
         wait()
     save(two_ref, two_out)
     for _ in line:
@@ -648,6 +680,8 @@
 
     by_tiles(rows, norm)
     gather = gather_steps(rows, low_ref, gather_sems)
+    next(gather)
+    yield
     next(gather)
     yield
     waits = waits + next(gather)
@@ -911,15 +945,15 @@
             if c + depth - 1 < total:
                 load(c + depth - 1).start()
 
-    work = beside(*side_in, *side_out, *side_scratch)
-    next(work)
-
     @pl.when(at_end)
     def _():
         for c in range(total):
             if c == 0 or chunks[c][0] != chunks[c - 1][0]:
                 wholes[chunks[c][0]].wait()
             pass_in(c)
+
+    work = beside(*side_in, *side_out, *side_scratch)
+    next(work)
 
     def deliveries(c):
         k, i, start, rows = chunks[c]
@@ -1151,7 +1185,7 @@
     back = replica_sum(
         [down_partial, pair_partial], ["row", "pair"], 3,
         functools.partial(turn_steps, sequences, length),
-        (6, 12) + tuple(range(14, 14 + 2 * sequences + 2)),
+        (6, 9, 12) + tuple(range(14, 14 + 2 * sequences + 2)),
         [(partial, ANY)] + [(item, VM) for item in (middle, cot, labels, conv_f, bias, recur_gate_weight, input_gate_weight)]
         + [(item, ANY) for item in kept],
         [whole + (ANY,), ((rows, depth), f32, ANY), whole + (ANY,), narrow + (ANY,), narrow + (ANY,)]

time: 638 us -> 610 us (0.956)
  Pallas kernels: 555 us -> 526 us
    pallas_call x1, Pallas kernels: 173 us -> 153 us  [front(): pl.pallas_call(functools.partial(front_kernel, n, sequences, length), out...]
    pallas_call x2, Pallas kernels: 358 us -> 349 us  [replica_sum(): pl.pallas_call(functools.partial(line_kernel, lax.axis_size('replica'), t...]
where the time goes in v9:
time: 610 us; the launch traced here: 601 us
  Pallas kernels  526 us (86%)
  matrix products  52.8 us (9%)
  other arithmetic  11.9 us (2%)
  local copies, waits for them, and re-layouts  9.82 us (2%)
    pallas_call x2, Pallas kernels, replica_sum(): pl.pallas_call(functools.partial(line_kernel, lax.axis_size('replica'), t...  349 us
    pallas_call x1, Pallas kernels, front(): pl.pallas_call(functools.partial(front_kernel, n, sequences, length), out...  153 us
    dot_general x4, matrix products, mm_tn(): lax.dot_general(left, right, (((0,), (0,)), ((), ())), preferred_element_...  23.8 us
    dot_general x2, matrix products, mm(): return jnp.dot(left, right, preferred_element_type=f32)  15.3 us
    dot_general x2, matrix products, mm_nt(): lax.dot_general(left, right, (((1,), (1,)), ((), ())), preferred_element_...  13.7 us
    pallas_call x1, Pallas kernels, finish_pair(): pl.pallas_call(finish_pair_kernel, grid=(rows // cut,), out_shape=(out, o...  13.6 us

profile of v9, /device:TPU:0, one launch (start us, length us, event | category | flops | bytes accessed | tf_op | source)
XLA Modules:
  0.0 601.4 jit_solution(7281859066446057476)
XLA Ops:
  0.7 0.7 convert.34
  1.3 0.7 convert.35
  2.0 0.8 copy.75.gains_ref
  2.8 0.7 convert_convert_fusion.1
  3.5 0.7 convert_convert_fusion.3
  4.2 0.7 convert_convert_fusion.2
  4.9 0.7 compare_select_fusion
  5.6 1.3 pad_maximum_fusion.5
  6.9 0.7 convert_bitcast_fusion
  7.6 0.7 broadcast_in_dim.25.label_ref
  8.3 152.9 %shard_map.305 = (bf16[1024,2048]{1,0:T(8,128)(2,1)}, bf16[1024,128]{1,0:T(8,128)(2,1)}, bf16[1024,2048]{1,0:T(8,128)(2,1)}, bf16[1024,320]{1,0:T(8,128)(2,1)}, ...) custom-call(bf16[128,2048]{1,0:T(8,128)(2,1)} %bitcast.37, ...), custom_call_target="tpu_custom_call" | custom-call | flops 1000000 | bytes 209715200 | tf_op jit(solution)/shard_map/pallas_call | solution.py:634
  161.2 0.0 slice-start.1
  161.2 8.4 %fusion.7 = f32[1024,768]{1,0:T(8,128)} fusion(bf16[1024,2048]{1,0:T(8,128)(2,1)} %get-tuple-element.59, bf16[2048,1536]{1,0:T(8,128)(2,1)} %bitcast.44), kind=kOutput, calls=%fused_computation.13 | convolution fusion | flops 3221225472 | bytes 10485760 | tf_op jit(solution)/shard_map/dot_general | solution.py:22
  169.6 0.0 slice-done.1
  169.6 0.0 slice-start.2
  169.6 0.5 convert_element_type.96.refs_8_
  170.1 1.6 copy-done
  171.7 1.2 copy-done.11
  172.9 3.5 fusion.35
  176.4 0.7 copy-done.16
  177.1 6.9 %fusion.6 = (bf16[1024,768]{1,0:T(8,128)(2,1)S(1)}, bf16[1024,768]{1,0:T(8,128)(2,1)}, bf16[1024,768]{1,0:T(8,128)(2,1)S(1)}) fusion(f32[1024,768]{1,0:T(8,128)S(1)} %fusion.35, f32[1024,768]{1,0:T(8,128)S(1)} %copy-done.16, bf16[1024,2048]{1,0:T(8,128)(2,1)S(1)} %copy-done.12, bf16[2048,1536]{1,0:T(8,128)(2,1)S(1)} %bitcast.47), kind=kOutput, calls=%fused_computation.12 | convolution fusion | flops 3240886272 | bytes 18350080 | tf_op jit(solution)/shard_map/dot_general | solution.py:22
  184.0 10.2 %convolution_convert_fusion.1.refs_2_ = bf16[1024,2048]{1,0:T(8,128)(2,1)} fusion(bf16[2048,1536]{1,0:T(8,128)(2,1)S(1)} %bitcast.48, bf16[1024,768]{1,0:T(8,128)(2,1)} %get-tuple-element.104, bf16[1024,768]{1,0:T(8,128)(2,1)S(1)} %get-tuple-element.103), kind=kOutput, calls=%fused_computation.3 | convolution fusion | flops 6450839552 | bytes 13631488 | tf_op jit(solution)/shard_map/dot_general | solution.py:26
  194.3 8.9 %convolution_convert_fusion = bf16[2048,1536]{1,0:T(8,128)(2,1)} fusion(bf16[1024,2048]{1,0:T(8,128)(2,1)S(1)} %copy-done.12, bf16[1024,768]{1,0:T(8,128)(2,1)S(1)} %copy-done.17, bf16[1024,768]{1,0:T(8,128)(2,1)S(1)} %get-tuple-element.103), kind=kOutput, calls=%fused_computation | convolution fusion | flops 6451888128 | bytes 13631488 | tf_op jit(solution)/shard_map/dot_general | solution.py:30
  203.2 4.8 fusion.11.refs_0_
  208.0 227.7 %shard_map.306 = (bf16[768,2048]{1,0:T(8,128)(2,1)}, bf16[256,6144]{1,0:T(8,128)(2,1)}, bf16[256,6144]{1,0:T(8,128)(2,1)}, bf16[1024,2048]{1,0:T(8,128)(2,1)}, f...) custom-call(bf16[1,768,2048]{2,1,0:T(8,128)(2,1)} %fusion.11.refs_0_, ...), custom_call_target="tpu_custom_call" | custom-call | flops 1000000 | bytes 209715200 | tf_op jit(solution)/shard_map/pallas_call | solution.py:1033
  435.8 0.8 copy.88.gain_ref
  436.6 0.0 copy-start.14
  436.6 0.0 copy-start.15
  436.6 13.6 %shard_map.309 = (f32[256,6144]{1,0:T(8,128)}, f32[256,6144]{1,0:T(8,128)}, f32[256,1]{1,0:T(8,128)}) custom-call(f32[256,1]{1,0:T(8,128)} %copy.88.gain_ref, bf16[256,6144]{1,0:T(8,128)(2,1)} %get-tuple-element.93.a_ref, bf16[256,6144]{1,0:T(8,128)(2,1)} %get-tuple-element.94.b_ref, f32[256,6144]{1,0:T(8,128)} %wa_ref.3, f32[256,6144]{1,0:T(8,128)} %wb_ref.3), custom_call_target="tpu_custom_call" | custom-call | flops 9437184 | bytes 31457280 | tf_op jit(solution)/shard_map/pallas_call | solution.py:1068
  450.2 1.6 reduce.5
  451.8 0.0 copy-done.5
  451.8 0.1 pad_maximum_fusion.4
  452.0 0.7 pad_maximum_fusion.3.refs_2_
  452.8 0.0 copy-done.14
  452.8 7.4 %convolution_convert_fusion.3 = bf16[2048,640]{1,0:T(8,128)(2,1)} fusion(bf16[1024,2048]{1,0:T(8,128)(2,1)} %get-tuple-element.74, bf16[1024,320]{1,0:T(8,128)(2,1)S(1)} %copy-done.15, bf16[1024,320]{1,0:T(8,128)(2,1)S(1)} %copy-done.14), kind=kOutput, calls=%fused_computation.5 | convolution fusion | flops 2688286720 | bytes 8126464 | tf_op jit(solution)/shard_map/dot_general | solution.py:30
  460.2 0.0 copy-done.10
  460.2 2.6 fusion.12.refs_0_
  462.8 121.4 %shard_map.307 = (bf16[320,2048]{1,0:T(8,128)(2,1)}, bf16[8,256,640]{2,1,0:T(8,128)(2,1)}, bf16[336,384]{1,0:T(8,128)(2,1)}, bf16[128,2048]{1,0:T(8,128)(2,1)}, bf16[128,2048]{1,0:T(8,128)(2,1)}) custom-call(bf16[1,320,2048]{2,1,0:T(8,128)(2,1)} %fusion.12.refs_0_, bf16[8,256,640]{2,1,0:T(8,128)(2,1)} %bitcast.34, ...), custom_call_target="tpu_custom_call" | custom-call | flops 1000000 | bytes 209715200 | tf_op jit(solution)/shard_map/pallas_call | solution.py:1033
  584.2 0.8 copy.87.gain_ref
  585.0 10.0 %shard_map.308 = (f32[256,2560]{1,0:T(8,128)}, f32[256,2560]{1,0:T(8,128)}, f32[256,1]{1,0:T(8,128)}, f32[320,2048]{1,0:T(8,128)}, f32[768,2048]{1,0:T(8,128)}) custom-call(f32[256,1]{1,0:T(8,128)} %copy.87.gain_ref, bf16[8,256,640]{2,1,0:T(8,128)(2,1)} %get-tuple-element.85.mix_ref, f32[256,2560]{1,0:T(8,128)} %wa_ref.2, f32[256,2560]{1,0:T(8,128)} %wb_ref.2, ...), custom_call_target="tpu_custom_call" | custom-call | flops 10000000 | bytes 41943040 | tf_op jit(solution)/shard_map/pallas_call | solution.py:1105
  595.0 1.6 reduce
  596.7 0.9 fusion.34
  597.6 0.6 fusion.30
  598.2 0.0 copy-done.7
  598.2 0.6 divide_multiply_fusion
  598.8 0.6 slice.38
  599.4 0.8 copy.94
  600.2 0.8 copy.95
  (50 shorter events, 0.2 us)
Async XLA Ops:
  8.3 161.3 %slice-start = ((s8[6291456]{0:T(1024)(128)(4,1)}), s8[2097152]{0:T(1024)(128)(4,1)S(1)}, s32[]{:S(2)}) async-start(s8[6291456]{0:T(1024)(128)(4,1)} %bitcast.31), calls=%async_computation | async-start | bytes 4194304
  161.2 8.4 %slice-start.1 = ((s8[6291456]{0:T(1024)(128)(4,1)}), s8[4194304]{0:T(1024)(128)(4,1)S(1)}, s32[]{:S(2)}) async-start(s8[6291456]{0:T(1024)(128)(4,1)} %bitcast.31), calls=%async_computation.1 | async-start | bytes 8388608
  169.6 3.3 copy-start.11
  169.6 6.8 %slice-start.2 = ((s8[6291456]{0:T(1024)(128)(4,1)}), s8[4194304]{0:T(1024)(128)(4,1)S(1)}, s32[]{:S(2)}) async-start(s8[6291456]{0:T(1024)(128)(4,1)} %bitcast.45), calls=%async_computation.2 | async-start | bytes 8388608
  170.1 1.7 copy-start
  172.9 3.5 slice-start.3
  172.9 3.5 copy-start.12
  172.9 4.2 copy-start.16
  184.0 19.2 %copy-start.2 = (bf16[1024,768]{1,0:T(8,128)(2,1)}, bf16[1024,768]{1,0:T(8,128)(2,1)S(1)}, u32[]{:S(2)}) copy-start(bf16[1024,768]{1,0:T(8,128)(2,1)S(1)} %get-tuple-element.105.refs_7_) | copy-start | bytes 4718596
  184.0 10.2 %copy-start.17 = (bf16[1024,768]{1,0:T(8,128)(2,1)S(1)}, bf16[1024,768]{1,0:T(8,128)(2,1)}, u32[]{:S(2)}) copy-start(bf16[1024,768]{1,0:T(8,128)(2,1)} %get-tuple-element.104) | copy-start | bytes 4718596
  436.6 15.2 %copy-start.6 = (f32[2,160,160]{2,1,0:T(8,128)S(1)}, f32[2,160,160]{2,1,0:T(8,128)}, u32[]{:S(2)}) copy-start(f32[2,160,160]{2,1,0:T(8,128)} %get-tuple-element.77) | copy-start | bytes 614404
  436.6 15.2 %copy-start.5 = (f32[2,160,160]{2,1,0:T(8,128)S(1)}, f32[2,160,160]{2,1,0:T(8,128)}, u32[]{:S(2)}) copy-start(f32[2,160,160]{2,1,0:T(8,128)} %get-tuple-element.78) | copy-start | bytes 614404
  436.6 15.4 %copy-start.9 = (f32[4,320]{1,0:T(4,128)S(1)}, f32[4,320]{1,0:T(4,128)}, u32[]{:S(2)}) copy-start(f32[4,320]{1,0:T(4,128)} %get-tuple-element.79) | copy-start | bytes 15364
  436.6 15.4 %copy-start.8 = (f32[4,320]{1,0:T(4,128)S(1)}, f32[4,320]{1,0:T(4,128)}, u32[]{:S(2)}) copy-start(f32[4,320]{1,0:T(4,128)} %get-tuple-element.80) | copy-start | bytes 15364
  436.6 16.2 %copy-start.14 = (bf16[1024,320]{1,0:T(8,128)(2,1)S(1)}, bf16[1024,320]{1,0:T(8,128)(2,1)}, u32[]{:S(2)}) copy-start(bf16[1024,320]{1,0:T(8,128)(2,1)} %get-tuple-element.75) | copy-start | bytes 1966084
  436.6 16.2 %copy-start.15 = (bf16[1024,320]{1,0:T(8,128)(2,1)S(1)}, bf16[1024,320]{1,0:T(8,128)(2,1)}, u32[]{:S(2)}) copy-start(bf16[1024,320]{1,0:T(8,128)(2,1)} %get-tuple-element.76) | copy-start | bytes 1966084
  452.8 7.4 %copy-start.10 = (bf16[1024,2048]{1,0:T(8,128)(2,1)S(1)}, bf16[1024,2048]{1,0:T(8,128)(2,1)}, u32[]{:S(2)}) copy-start(bf16[1024,2048]{1,0:T(8,128)(2,1)} %get-tuple-element.73) | copy-start | bytes 12582916
  452.8 7.4 %copy-start.13 = (bf16[1024,320]{1,0:T(8,128)(2,1)S(1)}, bf16[1024,320]{1,0:T(8,128)(2,1)}, u32[]{:S(2)}) copy-start(bf16[1024,320]{1,0:T(8,128)(2,1)} %get-tuple-element.58) | copy-start | bytes 1966084
  585.0 11.7 %copy-start.1 = (bf16[336,384]{1,0:T(8,128)(2,1)S(1)}, bf16[336,384]{1,0:T(8,128)(2,1)}, u32[]{:S(2)}) copy-start(bf16[336,384]{1,0:T(8,128)(2,1)} %get-tuple-element.91) | copy-start | bytes 774148
  585.0 13.2 %copy-start.7 = (f32[320]{0:T(512)S(1)}, f32[320]{0:T(512)}, u32[]{:S(2)}) copy-start(f32[320]{0:T(512)} %param.30) | copy-start | bytes 3844
  585.0 14.4 %copy-start.4 = (bf16[128,2048]{1,0:T(8,128)(2,1)S(1)}, bf16[128,2048]{1,0:T(8,128)(2,1)}, u32[]{:S(2)}) copy-start(bf16[128,2048]{1,0:T(8,128)(2,1)} %get-tuple-element.83) | copy-start | bytes 1572868
  595.0 5.2 copy-start.3

commit v10 on v9

--- a/solution.py
+++ b/solution.py
@@ -827,6 +827,100 @@
         wait()
 
 
+def mlp_kernel(
+    two_hbm, low_hbm, pair_hbm, down_hbm, hidden_out, partial_out, down_out, pair_out,
+    two, low_rows, pair_w, down_w, hidden, pair_low, partial, down_grad, pair_grad, load_sem, save_sem, pair_sem,
+):
+    total, depth = two.shape
+    ff = down_w.shape[0]
+    tile = 256 if ff % 256 == 0 else 128
+    height = 256
+    steps = total // height
+
+    def rows_of(hbm, ref, r, which):
+        here = pl.ds(r * height, height)
+        return pltpu.make_async_copy(hbm.at[here, :], ref.at[here, :], load_sem.at[which, r])
+
+    weights = [
+        pltpu.make_async_copy(pair_hbm, pair_w, load_sem.at[2, 0]),
+        pltpu.make_async_copy(down_hbm, down_w, load_sem.at[2, 1]),
+    ]
+    rows_of(two_hbm, two, 0, 0).start()
+    weights[0].start()
+    rows_of(low_hbm, low_rows, 0, 1).start()
+    weights[1].start()
+    for r in range(1, steps):
+        rows_of(two_hbm, two, r, 0).start()
+        rows_of(low_hbm, low_rows, r, 1).start()
+    weights[0].wait()
+    weights[1].wait()
+
+    def row_step(r, _):
+        here = pl.ds(pl.multiple_of(r * height, height), height)
+        pltpu.make_async_copy(two_hbm.at[here, :], two.at[here, :], load_sem.at[0, r]).wait()
+        pltpu.make_async_copy(low_hbm.at[here, :], low_rows.at[here, :], load_sem.at[1, r]).wait()
+        for f in range(ff // tile):
+            cut = slice(f * tile, (f + 1) * tile)
+            more = slice(ff + f * tile, ff + (f + 1) * tile)
+            gate = dot_nn(two[here, :], pair_w[:, cut])
+            up = dot_nn(two[here, :], pair_w[:, more])
+            grad = dot_nt(low_rows[here, :], down_w[cut, :])
+            act, slope = gelu_parts(gate)
+            hidden[here, cut] = (act * up).astype(bf16)
+            pair_low[here, cut] = (grad * up * slope).astype(bf16)
+            pair_low[here, more] = (grad * act).astype(bf16)
+        for d in range(0, depth, 512):
+            partial[here, d : d + 512] = dot_nt(pair_low[here, :], pair_w[d : d + 512, :]).astype(bf16)
+        return 0
+
+    lax.fori_loop(0, steps, row_step, 0)
+    saves = [
+        pltpu.make_async_copy(partial, partial_out, save_sem.at[0]),
+        pltpu.make_async_copy(hidden, hidden_out, save_sem.at[1]),
+    ]
+    for save in saves:
+        save.start()
+    for f in range(ff // tile):
+        cut = slice(f * tile, (f + 1) * tile)
+        down_grad[cut, :] = dot_tn(hidden[:, cut], low_rows[...]).astype(bf16)
+    saves.append(pltpu.make_async_copy(down_grad, down_out, save_sem.at[2]))
+    saves[-1].start()
+
+    def column_step(d, _):
+        here = pl.ds(pl.multiple_of(d * height, height), height)
+        pair_grad[here, :] = dot_tn(two[:, here], pair_low[...]).astype(bf16)
+        pltpu.make_async_copy(pair_grad.at[here, :], pair_out.at[here, :], pair_sem.at[d]).start()
+        return 0
+
+    lax.fori_loop(0, depth // height, column_step, 0)
+    for d in range(depth // height):
+        here = pl.ds(d * height, height)
+        pltpu.make_async_copy(pair_grad.at[here, :], pair_out.at[here, :], pair_sem.at[d]).wait()
+    for save in saves:
+        save.wait()
+
+
+def mlp(unit_two, out_low, pair_w, down_w):
+    total, depth = unit_two.shape
+    ff = down_w.shape[0]
+    kept = [((total, ff), bf16), ((total, depth), bf16), ((ff, depth), bf16), ((depth, 2 * ff), bf16)]
+    vm, dma = pltpu.VMEM, pltpu.SemaphoreType.DMA
+    return pl.pallas_call(
+        mlp_kernel,
+        out_shape=tuple(jax.ShapeDtypeStruct(*item) for item in kept),
+        in_specs=[ANY] * 4,
+        out_specs=[ANY] * 4,
+        scratch_shapes=[vm(item.shape, bf16) for item in (unit_two, out_low, pair_w, down_w)]
+        + [vm((total, ff), bf16), vm((total, 2 * ff), bf16)]
+        + [vm(*item) for item in kept[1:]]
+        + [dma((3, total // 256)), dma((3,)), dma((depth // 256,))],
+        compiler_params=pltpu.CompilerParams(vmem_limit_bytes=60 * 2**20),
+        cost_estimate=pl.CostEstimate(
+            flops=2 * total * depth * ff * 8, bytes_accessed=36 * 2**20, transcendentals=total * ff
+        ),
+    )(unit_two, out_low, pair_w, down_w)
+
+
 def pieces(rows, most):
     count = -(-rows // most)
     while rows % count or (rows // count) % 16:
@@ -988,7 +1082,7 @@
         for copy in deliveries(c)[0]:
             copy.start()
 
-    lag = 2
+    lag = 1
     for c in range(total + lag):
         for _ in range(turns.count(c)):
             next(work)
@@ -1166,18 +1260,9 @@
     pair_w = pair_w.reshape(depth, -1)
     down_w = down_weight.astype(bf16)
     whole = ((total, depth), bf16)
-    ff = pair_w.shape[1] // 2
-    gate_pre = mm(unit_two, pair_w[:, :ff])
-    up_pre = mm(unit_two, pair_w[:, ff:])
-    hidden_grad = mm_nt(out_low, down_w)
-    gate_act, gate_slope = gelu_parts(gate_pre)
-    hidden = (gate_act * up_pre).astype(bf16)
-    gate_low = (hidden_grad * up_pre * gate_slope).astype(bf16)
-    up_low = (hidden_grad * gate_act).astype(bf16)
-    pair_low = jnp.concatenate([gate_low, up_low], 1)
-    partial = mm_nt(pair_low, pair_w).astype(bf16)
-    pair_partial = mm_tn(unit_two, pair_low).astype(bf16).reshape(members, -1, 2 * ff)
-    down_partial = mm_tn(hidden, out_low).astype(bf16)[None]
+    hidden, partial, down_partial, pair_partial = mlp(unit_two, out_low, pair_w, down_w)
+    down_partial = down_partial[None]
+    pair_partial = pair_partial.reshape(members, -1, pair_w.shape[1])
     kept = (output_w, mix_w, *mixed)
     narrow = ((total, width), bf16)
     vm, dma = pltpu.VMEM, pltpu.SemaphoreType.DMA

time: 610 us -> 604 us (level)
  matrix products: 52.8 us -> 10 us
  Pallas kernels: 526 us -> 561 us
    pallas_call x0 -> x1, Pallas kernels: none -> 37.4 us  [mlp(): pl.pallas_call(mlp_kernel, out_shape=tuple((jax.ShapeDtypeStruct(*item) f...]
    dot_general x4 -> x0, matrix products: 29 us -> none  [the longest x2 15.3 us: mm(): return jnp.dot(left, right, preferred_element_type=f32)]
    dot_general x4 -> x2, matrix products: 23.8 us -> 10 us  [mm_tn(): lax.dot_general(left, right, (((0,), (0,)), ((), ())), preferred_element_...]
where the time goes in v10:
time: 604 us; the launch traced here: 595 us
  Pallas kernels  561 us (93%)
  other arithmetic  16.4 us (3%)
  matrix products  10 us (2%)
  local copies, waits for them, and re-layouts  6.28 us (1%)
    pallas_call x2, Pallas kernels, replica_sum(): pl.pallas_call(functools.partial(line_kernel, lax.axis_size('replica'), t...  347 us
    pallas_call x1, Pallas kernels, front(): pl.pallas_call(functools.partial(front_kernel, n, sequences, length), out...  153 us
    pallas_call x1, Pallas kernels, mlp(): pl.pallas_call(mlp_kernel, out_shape=tuple((jax.ShapeDtypeStruct(*item) f...  37.4 us
    pallas_call x1, Pallas kernels, finish_pair(): pl.pallas_call(finish_pair_kernel, grid=(rows // cut,), out_shape=(out, o...  13.6 us

profile of v10, /device:TPU:0, one launch (start us, length us, event | category | flops | bytes accessed | tf_op | source)
XLA Modules:
  0.0 594.5 jit_solution(9030914781019585799)
XLA Ops:
  0.7 0.7 convert.34
  1.3 0.7 convert.35
  2.0 0.8 copy.42.gains_ref
  2.8 0.7 convert_convert_fusion.1
  3.5 0.7 convert_convert_fusion.3
  4.2 0.7 convert_convert_fusion.2
  4.9 0.7 compare_select_fusion
  5.6 1.3 pad_maximum_fusion.2
  6.9 0.7 convert_bitcast_fusion
  7.6 0.7 broadcast_in_dim.25.label_ref
  8.3 152.8 %shard_map.305 = (bf16[1024,2048]{1,0:T(8,128)(2,1)}, bf16[1024,128]{1,0:T(8,128)(2,1)}, bf16[1024,2048]{1,0:T(8,128)(2,1)}, bf16[1024,320]{1,0:T(8,128)(2,1)}, ...) custom-call(bf16[128,2048]{1,0:T(8,128)(2,1)} %bitcast.27, ...), custom_call_target="tpu_custom_call" | custom-call | flops 1000000 | bytes 209715200 | tf_op jit(solution)/shard_map/pallas_call | solution.py:634
  161.0 4.9 convert_element_type.76.down_hbm.refs_8_
  166.0 37.4 %shard_map.306 = (bf16[1024,768]{1,0:T(8,128)(2,1)}, bf16[1024,2048]{1,0:T(8,128)(2,1)}, bf16[768,2048]{1,0:T(8,128)(2,1)}, bf16[2048,1536]{1,0:T(8,128)(2,1)}) custom-call(bf16[1024,2048]{1,0:T(8,128)(2,1)} %get-tuple-element.63.two_hbm, bf16[1024,2048]{1,0:T(8,128)(2,1)} %get-tuple-element.64.low_hbm, bf16[2048,1536]{1,0:T(8,128)(2,1)} %bitcast.34, ...), custom_call_target="tpu_custom_call" | custom-call | flops 25769803776 | bytes 37748736 | tf_op jit(solution)/shard_map/pallas_call | solution.py:908
  203.4 228.8 %shard_map.307 = (bf16[768,2048]{1,0:T(8,128)(2,1)}, bf16[256,6144]{1,0:T(8,128)(2,1)}, bf16[256,6144]{1,0:T(8,128)(2,1)}, bf16[1024,2048]{1,0:T(8,128)(2,1)}, f...) custom-call(bf16[1,768,2048]{2,1,0:T(8,128)(2,1)} %bitcast.23, ...), custom_call_target="tpu_custom_call" | custom-call | flops 1000000 | bytes 209715200 | tf_op jit(solution)/shard_map/pallas_call | solution.py:1127
  432.2 0.8 copy.44.gain_ref
  433.0 0.0 copy-start.4
  433.0 0.0 copy-start.7
  433.0 0.0 copy-start.6
  433.0 0.0 copy-start.10
  433.0 0.0 copy-start.11
  433.0 13.6 %shard_map.310 = (f32[256,6144]{1,0:T(8,128)}, f32[256,6144]{1,0:T(8,128)}, f32[256,1]{1,0:T(8,128)}) custom-call(f32[256,1]{1,0:T(8,128)} %copy.44.gain_ref, bf16[256,6144]{1,0:T(8,128)(2,1)} %get-tuple-element.101.a_ref, bf16[256,6144]{1,0:T(8,128)(2,1)} %get-tuple-element.102.b_ref, f32[256,6144]{1,0:T(8,128)} %wa_ref.3, f32[256,6144]{1,0:T(8,128)} %wb_ref.3), custom_call_target="tpu_custom_call" | custom-call | flops 9437184 | bytes 31457280 | tf_op jit(solution)/shard_map/pallas_call | solution.py:1162
  446.6 1.6 reduce.5
  448.2 0.0 copy-done.4
  448.2 0.0 copy-done.3
  448.2 0.1 pad_maximum_fusion.1
  448.4 0.0 copy-done.7
  448.4 0.0 copy-done.6
  448.4 0.7 pad_maximum_fusion.refs_2_
  449.2 0.0 copy-done.10
  449.2 0.0 copy-done.11
  449.2 7.4 %convolution_convert_fusion = bf16[2048,640]{1,0:T(8,128)(2,1)} fusion(bf16[1024,2048]{1,0:T(8,128)(2,1)} %get-tuple-element.81, bf16[1024,320]{1,0:T(8,128)(2,1)S(1)} %copy-done.11, bf16[1024,320]{1,0:T(8,128)(2,1)S(1)} %copy-done.10), kind=kOutput, calls=%fused_computation | convolution fusion | flops 2688286720 | bytes 8126464 | tf_op jit(solution)/shard_map/dot_general | solution.py:30
  456.6 0.0 copy-done.8
  456.6 0.0 copy-done.9
  456.6 2.6 fusion.refs_0_
  459.2 118.3 %shard_map.308 = (bf16[320,2048]{1,0:T(8,128)(2,1)}, bf16[8,256,640]{2,1,0:T(8,128)(2,1)}, bf16[336,384]{1,0:T(8,128)(2,1)}, bf16[128,2048]{1,0:T(8,128)(2,1)}, bf16[128,2048]{1,0:T(8,128)(2,1)}) custom-call(bf16[1,320,2048]{2,1,0:T(8,128)(2,1)} %fusion.refs_0_, bf16[8,256,640]{2,1,0:T(8,128)(2,1)} %bitcast.24, ...), custom_call_target="tpu_custom_call" | custom-call | flops 1000000 | bytes 209715200 | tf_op jit(solution)/shard_map/pallas_call | solution.py:1127
  577.5 0.8 copy.43.gain_ref
  578.3 10.0 %shard_map.309 = (f32[256,2560]{1,0:T(8,128)}, f32[256,2560]{1,0:T(8,128)}, f32[256,1]{1,0:T(8,128)}, f32[320,2048]{1,0:T(8,128)}, f32[768,2048]{1,0:T(8,128)}) custom-call(f32[256,1]{1,0:T(8,128)} %copy.43.gain_ref, bf16[8,256,640]{2,1,0:T(8,128)(2,1)} %get-tuple-element.93.mix_ref, f32[256,2560]{1,0:T(8,128)} %wa_ref.2, f32[256,2560]{1,0:T(8,128)} %wb_ref.2, ...), custom_call_target="tpu_custom_call" | custom-call | flops 10000000 | bytes 41943040 | tf_op jit(solution)/shard_map/pallas_call | solution.py:1199
  588.4 1.6 reduce
  590.0 0.0 copy-done
  590.0 0.9 fusion.20
  590.9 0.6 fusion.18
  591.5 0.0 copy-done.5
  591.5 0.6 divide_multiply_fusion
  592.1 0.6 slice.28
  592.7 0.0 copy-done.2
  592.7 0.8 copy.47
  593.5 0.0 copy-done.1
  593.5 0.8 copy.48
  (23 shorter events, 0.2 us)
Async XLA Ops:
  433.0 15.2 %copy-start.4 = (f32[2,160,160]{2,1,0:T(8,128)S(1)}, f32[2,160,160]{2,1,0:T(8,128)}, u32[]{:S(2)}) copy-start(f32[2,160,160]{2,1,0:T(8,128)} %get-tuple-element.84) | copy-start | bytes 614404
  433.0 15.2 %copy-start.3 = (f32[2,160,160]{2,1,0:T(8,128)S(1)}, f32[2,160,160]{2,1,0:T(8,128)}, u32[]{:S(2)}) copy-start(f32[2,160,160]{2,1,0:T(8,128)} %get-tuple-element.85) | copy-start | bytes 614404
  433.0 15.4 %copy-start.7 = (f32[4,320]{1,0:T(4,128)S(1)}, f32[4,320]{1,0:T(4,128)}, u32[]{:S(2)}) copy-start(f32[4,320]{1,0:T(4,128)} %get-tuple-element.86) | copy-start | bytes 15364
  433.0 15.4 %copy-start.6 = (f32[4,320]{1,0:T(4,128)S(1)}, f32[4,320]{1,0:T(4,128)}, u32[]{:S(2)}) copy-start(f32[4,320]{1,0:T(4,128)} %get-tuple-element.87) | copy-start | bytes 15364
  433.0 16.2 %copy-start.10 = (bf16[1024,320]{1,0:T(8,128)(2,1)S(1)}, bf16[1024,320]{1,0:T(8,128)(2,1)}, u32[]{:S(2)}) copy-start(bf16[1024,320]{1,0:T(8,128)(2,1)} %get-tuple-element.82) | copy-start | bytes 1966084
  433.0 16.2 %copy-start.11 = (bf16[1024,320]{1,0:T(8,128)(2,1)S(1)}, bf16[1024,320]{1,0:T(8,128)(2,1)}, u32[]{:S(2)}) copy-start(bf16[1024,320]{1,0:T(8,128)(2,1)} %get-tuple-element.83) | copy-start | bytes 1966084
  449.2 7.4 %copy-start.8 = (bf16[1024,2048]{1,0:T(8,128)(2,1)S(1)}, bf16[1024,2048]{1,0:T(8,128)(2,1)}, u32[]{:S(2)}) copy-start(bf16[1024,2048]{1,0:T(8,128)(2,1)} %get-tuple-element.80) | copy-start | bytes 12582916
  449.2 7.4 %copy-start.9 = (bf16[1024,320]{1,0:T(8,128)(2,1)S(1)}, bf16[1024,320]{1,0:T(8,128)(2,1)}, u32[]{:S(2)}) copy-start(bf16[1024,320]{1,0:T(8,128)(2,1)} %get-tuple-element.62) | copy-start | bytes 1966084
  578.3 11.7 %copy-start = (bf16[336,384]{1,0:T(8,128)(2,1)S(1)}, bf16[336,384]{1,0:T(8,128)(2,1)}, u32[]{:S(2)}) copy-start(bf16[336,384]{1,0:T(8,128)(2,1)} %get-tuple-element.99) | copy-start | bytes 774148
  578.3 13.2 %copy-start.5 = (f32[320]{0:T(512)S(1)}, f32[320]{0:T(512)}, u32[]{:S(2)}) copy-start(f32[320]{0:T(512)} %param.30) | copy-start | bytes 3844
  578.3 14.4 %copy-start.2 = (bf16[128,2048]{1,0:T(8,128)(2,1)S(1)}, bf16[128,2048]{1,0:T(8,128)(2,1)}, u32[]{:S(2)}) copy-start(bf16[128,2048]{1,0:T(8,128)(2,1)} %get-tuple-element.91) | copy-start | bytes 1572868
  588.4 5.2 copy-start.1

commit v11 on v10

--- a/solution.py
+++ b/solution.py
@@ -101,6 +101,13 @@
     tail = ref.shape[0] * 128 - width
     if tail:
         ref[ref.shape[0] - 1, :, 128 - tail :] = jnp.zeros((ref.shape[1], tail), f32)
+
+
+def fill_small(conv, bias, raw_conv, raw_a, raw_b, raw_c, rate):
+    conv[0 : raw_conv.shape[0], :] = low(raw_conv[...])
+    for row, ref in enumerate((raw_a, raw_b, raw_c)):
+        bias[row : row + 1, :] = low(ref[...])
+    bias[3:4, :] = rate[...]
 
 
 def label_masks(label_ref, here, length, width, taps, lines):
@@ -378,20 +385,20 @@
 
 def front_kernel(
     n, sequences, length,
-    x_ref, label_ref, cot_ref, gains_ref, conv_ref, bias_ref, rw_ref, iw_ref,
-    branch_hbm, input_hbm, gate_hbm, up_hbm, ow_hbm,
+    x_ref, label_ref, cot_ref, gains_ref, raw_conv, raw_a, raw_b, raw_c, rate_ref, rw_ref, iw_ref,
+    branch_hbm, input_hbm, gate_hbm, up_hbm, ow_hbm, down_hbm,
     unit_out, labels_out, low_out, product_out, pre_out, conv_in_out, values_out, recur_out, inject_out, decay_out,
-    states_out, mix_out, ow_out, two_out, middle_out, pair_out,
+    states_out, mix_out, ow_out, two_out, middle_out, pair_out, down_out,
     unit_ref, labels_ref, product_ref, pre_ref, conv_in_ref, values_ref, recur_ref, inject_ref, decay_ref,
     states_ref, mix_ref, ow_ref, two_ref, middle_ref,
-    wide, tall, ow_f, mix_cut, pair_cut, pad, lines, rbig, ibig, partial,
+    wide, tall, ow_f, mix_cut, pair_cut, pad, lines, rbig, ibig, partial, conv_ref, bias_ref, down_f, down_low,
     near, far, acc, *sems,
 ):
     rows = x_ref.shape[0]
     scatter_sems, sems = sems[:4], sems[4:]
     unit_sems, label_sems, low_sems, two_sems, sems = sems[:4], sems[4:8], sems[8:12], sems[12:16], sems[16:]
-    load_sem, save_sem, mix_sent, mix_got, pair_sent, pair_got = sems[:6]
-    line_sems = sems[6:]
+    load_sem, save_sem, mix_sent, mix_got, pair_sent, pair_got, down_sem = sems[:7]
+    line_sems = sems[7:]
     offsets, at, block = plane()
     z = lax.axis_index("replica")
     y, s = lax.axis_index("seq"), lax.axis_index("shard")
@@ -498,13 +505,34 @@
     loads[4].wait()
     ow_ref[...] = ow_f[...].astype(bf16)
     save(ow_ref, ow_out)
+    fill_small(conv_ref, bias_ref, raw_conv, raw_a, raw_b, raw_c, rate_ref)
     fill_blocks(rbig, rw_ref)
     fill_blocks(ibig, iw_ref)
     pad[0:8, :] = jnp.zeros((8, width), f32)
-    taps = conv_ref.shape[0]
+    taps = raw_conv.shape[0]
     clear_tail(decay_ref, width)
     clear_tail(states_ref, width)
 
+    cuts = down_hbm.shape[0] // down_low.shape[1]
+    height = down_low.shape[1]
+
+    def down_load(k):
+        return pltpu.make_async_copy(down_hbm.at[pl.ds(k * height, height), :], down_f.at[k % 2], down_sem.at[k % 2])
+
+    def down_save(k):
+        return pltpu.make_async_copy(down_low.at[k % 2], down_out.at[pl.ds(k * height, height), :], down_sem.at[2 + k % 2])
+
+    def down_cast(k):
+        down_load(k).wait()
+        if k >= 2:
+            down_save(k - 2).wait()
+        down_low[k % 2] = down_f[k % 2].astype(bf16)
+        down_save(k).start()
+        if k + 2 < cuts:
+            down_load(k + 2).start()
+
+    for k in range(2):
+        down_load(k).start()
     pair_own.wait()
     for move in pair_moves:
         move.wait_recv()
@@ -516,6 +544,10 @@
     for wait in waits:
         wait()
     mix_own.wait()
+    for k in range(cuts):
+        down_cast(k)
+    for k in range(cuts - 2, cuts):
+        down_save(k).wait()
     for move in mix_moves:
         move.wait_recv()
     save(unit_ref, unit_out)
@@ -600,7 +632,7 @@
         copy.wait()
 
 
-def front(sequences, x, label, cot, gains, conv, bias, rw, iw, branch_w, input_w, gate_w, up_w, output_w):
+def front(sequences, x, label, cot, gains, small, rw, iw, branch_w, input_w, gate_w, up_w, output_w, down_w):
     rows, depth = x.shape
     own, n = branch_w.shape[0], lax.axis_size("replica")
     owners = lax.axis_size(GROUP)
@@ -627,26 +659,30 @@
         vm((width, width), f32),
         vm((width, width), f32),
         vm((total, depth), bf16),
+        vm((8, width), f32),
+        vm((8, width), f32),
+        vm((2, down_w.shape[0] // 8, depth), f32),
+        vm((2, down_w.shape[0] // 8, depth), bf16),
     ]
     scratch += plane_scratch(rows, depth, 4, 1)
-    scratch += [dma((6,)), dma((len(kept),))] + [dma((owners,))] * 4 + [dma((n - 1,))] * 4
-    outs = kept + [((owners, own, 2 * ff), bf16)]
+    scratch += [dma((6,)), dma((len(kept),))] + [dma((owners,))] * 4 + [dma((4,))] + [dma((n - 1,))] * 4
+    outs = kept + [((owners, own, 2 * ff), bf16), (down_w.shape, bf16)]
     return pl.pallas_call(
         functools.partial(front_kernel, n, sequences, length),
         out_shape=tuple(jax.ShapeDtypeStruct(*item) for item in outs),
-        in_specs=[VM] * 8 + [ANY] * 5,
+        in_specs=[VM] * 11 + [ANY] * 6,
         out_specs=[ANY] * len(outs),
         scratch_shapes=scratch,
         compiler_params=pltpu.CompilerParams(
-            collective_id=1, has_side_effects=True, vmem_limit_bytes=60 * 2**20
+            collective_id=1, has_side_effects=True, vmem_limit_bytes=62 * 2**20
         ),
         cost_estimate=pl.CostEstimate(flops=10**6, bytes_accessed=200 * 2**20, transcendentals=0),
-    )(x, label, cot, gains, conv, bias, rw, iw, branch_w, input_w, gate_w, up_w, output_w)
+    )(x, label, cot, gains, *small, rw, iw, branch_w, input_w, gate_w, up_w, output_w, down_w)
 
 
 def turn_steps(
     sequences, length,
-    partial_hbm, middle_ref, cot_ref, label_ref, conv_ref, bias_ref, rw_ref, iw_ref, *rest,
+    partial_hbm, middle_ref, cot_ref, label_ref, raw_conv, raw_a, raw_b, raw_c, rate_ref, rw_ref, iw_ref, *rest,
 ):
     kept_hbm, rest = rest[:9], rest[9:]
     low_out, grad_out, partial_out, branch_low_out, conv_low_out, dconv_ref, sums_ref, drw_ref, diw_ref = rest[:9]
@@ -655,7 +691,7 @@
     rest = rest[20:]
     kept, rest = rest[:9], rest[9:]
     ow_ref, w_ref, pre_ref, conv_in_ref, values_ref, recur_ref, inject_ref, decay_ref, states_ref = kept
-    partial, low_ref, grad_ref, branch_low_ref, conv_low_ref, adj, pad, lines, rbig, ibig, dr, di, load_sem, save_sem = rest
+    partial, low_ref, grad_ref, branch_low_ref, conv_low_ref, adj, pad, lines, rbig, ibig, dr, di, conv_ref, bias_ref, load_sem, save_sem = rest
     rows = middle_ref.shape[0]
     offsets, at, block = plane()
     first = pltpu.make_async_copy(partial_hbm, partial, load_sem.at[9])
@@ -699,7 +735,8 @@
     di[...] = jnp.zeros_like(di)
     sums_ref[...] = jnp.zeros_like(sums_ref)
     dconv_ref[...] = jnp.zeros_like(dconv_ref)
-    taps = conv_ref.shape[0]
+    taps = raw_conv.shape[0]
+    fill_small(conv_ref, bias_ref, raw_conv, raw_a, raw_b, raw_c, rate_ref)
     width = pad.shape[1]
     clear_tail(adj, width)
 
@@ -778,31 +815,53 @@
 
 
 def end_steps(
-    partial_hbm, grad_ref, x_ref, middle_ref, hidden_hbm, down_hbm, tokens_ref, block_ref, *rest,
+    outputs_at, mixes_at,
+    partial_hbm, grad_ref, x_ref, middle_ref, hidden_hbm, down_hbm, product_hbm, mid_hbm, unit_hbm, branch_hbm, conv_hbm,
+    tokens_ref, block_ref, *rest,
 ):
     near, far, acc = rest[:3]
-    scatter_sems = rest[3:7]
-    more_sems = rest[7:11]
-    near_two, far_two, partial, partial_two, hidden, down, load_sem = rest[11:]
+    scatter_sems, more_sems = rest[3:7], rest[7:11]
+    near_two, far_two, partial, hidden, down, product, tokens_wide, branch_low, conv_low, mix_low, load_sem = rest[11:22]
+    output_made, mix_made = rest[22:]
     rows = x_ref.shape[0]
+    depth = down.shape[1]
+
+    def load(k, source, target):
+        copy = pltpu.make_async_copy(source, target, load_sem.at[k])
+        copy.start()
+        return copy
+
+    first = load(0, mid_hbm, tokens_wide), load(1, product_hbm, product)
     loads = [
-        pltpu.make_async_copy(source, target, load_sem.at[k])
-        for k, (source, target) in enumerate(((partial_hbm, partial), (hidden_hbm, hidden), (down_hbm, down)))
+        load(2, partial_hbm, partial), load(3, branch_hbm, branch_low), load(4, conv_hbm, conv_low),
+        load(5, hidden_hbm, hidden), load(6, down_hbm, down),
     ]
-    for load in loads:
-        load.start()
+    for copy in first:
+        copy.wait()
+    for d in range(0, depth, 512):
+        output_made[0, :, d : d + 512] = dot_tn(product[...], tokens_wide[:, d : d + 512]).astype(bf16)
+    again = load(7, unit_hbm, tokens_wide)
+    yield outputs_at
     loads[0].wait()
     scatter = scatter_steps(rows, partial, near, far, acc, scatter_sems)
     next(scatter)
-    yield
+    yield None
     loads[1].wait()
     loads[2].wait()
-    pieces_of = 4
-    height = hidden.shape[0] // pieces_of
-    for k in range(pieces_of):
-        here = pl.ds(k * height, height)
-        partial_two[here, :] = dot_nn(hidden[here, :], down[...]).astype(bf16)
-        yield
+    width = branch_low.shape[1]
+    if mix_low.shape[1] > 2 * width:
+        mix_low[...] = jnp.zeros_like(mix_low)
+
+    def pack(here, i):
+        mix_low[here, 0 : 2 * width] = jnp.concatenate([branch_low[here, :], conv_low[here, :]], axis=1)
+
+    by_tiles(mix_low.shape[0], pack)
+    again.wait()
+    owners, own = mix_made.shape[:2]
+    for part in range(4):
+        for j in range(part * owners // 4, (part + 1) * owners // 4):
+            mix_made[j] = dot_tn(tokens_wide[:, j * own : (j + 1) * own], mix_low[...]).astype(bf16)
+        yield mixes_at if part == 3 else None
     waits = next(scatter)
 
     def norm(here, i):
@@ -812,17 +871,27 @@
         tokens_ref[here, :] = grad.astype(bf16)
 
     by_tiles(rows, norm)
-    yield
-    scatter = scatter_steps(rows, partial_two, near_two, far_two, acc, more_sems)
+    for wait in waits:
+        wait()
+    yield None
+    loads[3].wait()
+    loads[4].wait()
+    pieces_of = 4
+    height = hidden.shape[0] // pieces_of
+    for k in range(pieces_of):
+        here = pl.ds(k * height, height)
+        partial[here, :] = dot_nn(hidden[here, :], down[...]).astype(bf16)
+        yield None
+    scatter = scatter_steps(rows, partial, near_two, far_two, acc, more_sems)
     next(scatter)
-    yield
-    waits = waits + next(scatter)
+    yield None
+    waits = next(scatter)
 
     def out(here, i):
         block_ref[here, :] = (middle_ref[here, :] + acc[here, :]).astype(bf16)
 
     by_tiles(rows, out)
-    yield
+    yield None
     for wait in waits:
         wait()
 
@@ -928,7 +997,7 @@
     return count
 
 
-def line_kernel(n, kinds, cuts, beside, turns, extra, *refs):
+def line_kernel(n, kinds, cuts, made_here, beside, turns, extra, *refs):
     ins = len(cuts)
     made = ins + kinds.count("pair")
     extra_ins, extra_outs, extra_scratch = extra
@@ -939,10 +1008,12 @@
         del refs[:count]
         return taken
 
-    own_hbm, side_in = take(ins), take(extra_ins)
+    given = [k for k in range(ins) if k not in made_here]
+    own_hbm, side_in = dict(zip(given, take(len(given)))), take(extra_ins)
     outs, side_out = take(made), take(extra_outs)
     side_scratch = take(extra_scratch)
     from_out, from_in = take(ins), take(ins)
+    own_made = dict(zip(made_here, take(len(made_here))))
     slots, whole_sem, slot_sem, sent_in, sent_out, got_out, got_in, sent_x, got_x = refs
     depth = slots.shape[0]
     me = lax.axis_index("replica")
@@ -980,16 +1051,17 @@
     def load(c):
         return pltpu.make_async_copy(view(own_hbm, c), slot(c), slot_sem.at[c % depth])
 
-    wholes = [pltpu.make_async_copy(own_hbm[k], from_out[k], whole_sem.at[k]) for k in range(ins)]
+    wholes = {k: pltpu.make_async_copy(own_hbm[k], from_out[k], whole_sem.at[k]) for k in given}
+    loaded = [c for c in range(total) if chunks[c][0] in given]
 
     @pl.when(at_end)
     def _():
-        for item in wholes:
-            item.start()
+        for k in given:
+            wholes[k].start()
 
     @pl.when(has_out)
     def _():
-        for c in range(min(depth - 1, total)):
+        for c in loaded[: depth - 1]:
             load(c).start()
 
     barrier = pltpu.get_barrier_semaphore()
@@ -1011,7 +1083,11 @@
 
     def add(target, other, c):
         k, i, start, rows = chunks[c]
-        into, more = view(target, c), slot(c) if other is None else view(other, c)
+        if other is None:
+            more = view(own_made, c) if k in made_here else slot(c)
+        else:
+            more = view(other, c)
+        into = view(target, c)
 
         def tile(t, _):
             here = pl.ds(pl.multiple_of(t * 16, 16), 16)
@@ -1020,34 +1096,45 @@
 
         lax.fori_loop(0, rows // 16, tile, 0)
 
-    def pass_in(c):
+    def pass_in(c, source):
         @pl.when(middle)
         def _():
-            push(from_out, from_in, c, sent_in, got_in, inward).start()
+            push(source, from_in, c, sent_in, got_in, inward).start()
 
         @pl.when(jnp.logical_not(middle))
         def _():
-            push(from_out, from_out, c, sent_in, got_out, inward).start()
+            push(source, from_out, c, sent_in, got_out, inward).start()
 
     def gather_in(c):
         @pl.when(has_out)
         def _():
-            load(c).wait()
+            if c in loaded:
+                load(c).wait()
             push(from_out, from_out, c, sent_in, got_out, inward).wait_recv()
             add(from_out, None, c)
-            pass_in(c)
-            if c + depth - 1 < total:
+            pass_in(c, from_out)
+            if c + depth - 1 in loaded:
                 load(c + depth - 1).start()
 
     @pl.when(at_end)
     def _():
-        for c in range(total):
+        for c in loaded:
             if c == 0 or chunks[c][0] != chunks[c - 1][0]:
                 wholes[chunks[c][0]].wait()
-            pass_in(c)
-
-    work = beside(*side_in, *side_out, *side_scratch)
-    next(work)
+            pass_in(c, from_out)
+
+    def advance():
+        k = next(work)
+        if k is not None:
+
+            @pl.when(at_end)
+            def _():
+                for c in range(total):
+                    if chunks[c][0] == k:
+                        pass_in(c, own_made)
+
+    work = beside(*side_in, *side_out, *side_scratch, *[own_made[k] for k in made_here])
+    advance()
 
     def deliveries(c):
         k, i, start, rows = chunks[c]
@@ -1085,7 +1172,7 @@
     lag = 1
     for c in range(total + lag):
         for _ in range(turns.count(c)):
-            next(work)
+            advance()
         if c < total:
             gather_in(c)
         if c >= lag:
@@ -1107,7 +1194,7 @@
             push(from_in, from_in, c, sent_out, got_in, outward).wait_send()
 
 
-def replica_sum(arrays, kinds, identity, beside, turns, inputs, results, side_scratch):
+def replica_sum(arrays, kinds, made_here, identity, beside, turns, inputs, results, side_scratch):
     cuts, outs = [], []
     tall = broad = 0
     for item, kind in zip(arrays, kinds):
@@ -1126,22 +1213,23 @@
     dma = pltpu.SemaphoreType.DMA
     return pl.pallas_call(
         functools.partial(
-            line_kernel, lax.axis_size("replica"), tuple(kinds), tuple(cuts), beside, turns,
+            line_kernel, lax.axis_size("replica"), tuple(kinds), tuple(cuts), tuple(made_here), beside, turns,
             (len(inputs), len(results), len(side_scratch)),
         ),
         out_shape=tuple(outs) + tuple(jax.ShapeDtypeStruct(shape, kind) for shape, kind, _ in results),
-        in_specs=[ANY] * len(arrays) + [spec for _, spec in inputs],
+        in_specs=[ANY] * (len(arrays) - len(made_here)) + [spec for _, spec in inputs],
         out_specs=[ANY] * len(outs) + [spec for _, _, spec in results],
         scratch_shapes=list(side_scratch)
         + buffers * 2
+        + [buffers[k] for k in made_here]
         + [pltpu.VMEM((4, tall, broad), bf16), dma((len(arrays),)), dma((4,))]
         + [dma((count,))] * 4
         + [dma((count, 2))] * 2,
         compiler_params=pltpu.CompilerParams(
-            collective_id=identity, has_side_effects=True, vmem_limit_bytes=61 * 2**20
+            collective_id=identity, has_side_effects=True, vmem_limit_bytes=62 * 2**20
         ),
         cost_estimate=pl.CostEstimate(flops=10**6, bytes_accessed=200 * 2**20, transcendentals=0),
-    )(*arrays, *[item for item, _ in inputs])
+    )(*[item for k, item in enumerate(arrays) if k not in made_here], *[item for item, _ in inputs])
 
 
 def finish_pair_kernel(gain_ref, a_ref, b_ref, wa_ref, wb_ref, outa_ref, outb_ref, grad_ref):
@@ -1165,7 +1253,7 @@
         out_shape=(out, out, jax.ShapeDtypeStruct((rows, 1), f32)),
         in_specs=[thin, wide, wide, wide, wide],
         out_specs=[wide, wide, thin],
-        compiler_params=pltpu.CompilerParams(vmem_limit_bytes=61 * 2**20),
+        compiler_params=pltpu.CompilerParams(vmem_limit_bytes=62 * 2**20),
         cost_estimate=pl.CostEstimate(flops=6 * rows * columns, bytes_accessed=20 * rows * columns, transcendentals=0),
     )(gain, a, b, wa, wb)
 
@@ -1215,7 +1303,7 @@
             tall(down_sum),
         ],
         out_specs=[wide, wide, thin, tall(out_sum), tall(down_sum)],
-        compiler_params=pltpu.CompilerParams(vmem_limit_bytes=61 * 2**20),
+        compiler_params=pltpu.CompilerParams(vmem_limit_bytes=62 * 2**20),
         cost_estimate=pl.CostEstimate(flops=10**7, bytes_accessed=40 * 2**20, transcendentals=0),
     )(gain, mix, wa, wb, out_sum, down_sum)
 
@@ -1248,17 +1336,18 @@
     gain, mlp_gain = low(norm_gain)[:, None], low(mlp_norm_gain)[:, None]
     own_labels = jnp.broadcast_to(segments[0].astype(bf16)[:, None], (rows, 128))
     width = branch_weight.shape[1] // members
-    conv_f = low(conv_weight)
     decay_f = low(decay_param)
-    bias = jnp.stack([low(conv_bias), low(recur_gate_bias), low(input_gate_bias), jax.nn.softplus(-decay_f)])
+    small = (
+        conv_weight, conv_bias[None], recur_gate_bias[None], input_gate_bias[None], jax.nn.softplus(-decay_f)[None],
+    )
     (
-        unit_all, labels, out_low, product, *mixed, mix_w, output_w, unit_two, middle, pair_w,
+        unit_all, labels, out_low, product, *mixed, mix_w, output_w, unit_two, middle, pair_w, down_w,
     ) = front(
-        sequences, x, own_labels, cot, low(jnp.stack([norm_gain, mlp_norm_gain], 1)), conv_f, bias,
+        sequences, x, own_labels, cot, low(jnp.stack([norm_gain, mlp_norm_gain], 1)), small,
         recur_gate_weight, input_gate_weight, branch_weight, input_weight, gate_weight, up_weight, output_weight,
+        down_weight,
     )
     pair_w = pair_w.reshape(depth, -1)
-    down_w = down_weight.astype(bf16)
     whole = ((total, depth), bf16)
     hidden, partial, down_partial, pair_partial = mlp(unit_two, out_low, pair_w, down_w)
     down_partial = down_partial[None]
@@ -1268,27 +1357,24 @@
     vm, dma = pltpu.VMEM, pltpu.SemaphoreType.DMA
     length = total // sequences
     back = replica_sum(
-        [down_partial, pair_partial], ["row", "pair"], 3,
+        [down_partial, pair_partial], ["row", "pair"], (), 3,
         functools.partial(turn_steps, sequences, length),
         (6, 9, 12) + tuple(range(14, 14 + 2 * sequences + 2)),
-        [(partial, ANY)] + [(item, VM) for item in (middle, cot, labels, conv_f, bias, recur_gate_weight, input_gate_weight)]
+        [(partial, ANY)] + [(item, VM) for item in (middle, cot, labels, *small, recur_gate_weight, input_gate_weight)]
         + [(item, ANY) for item in kept],
         [whole + (ANY,), ((rows, depth), f32, ANY), whole + (ANY,), narrow + (ANY,), narrow + (ANY,)]
-        + [(conv_f.shape, f32, VM), ((4, width), f32, VM), (recur_gate_weight.shape, f32, VM), (input_gate_weight.shape, f32, VM)],
+        + [(conv_weight.shape, f32, VM), ((4, width), f32, VM), (recur_gate_weight.shape, f32, VM), (input_gate_weight.shape, f32, VM)],
         plane_scratch(rows, depth, 1, 1)
         + [vm(item.shape, item.dtype) for item in kept]
         + [vm(*whole), vm(*whole), vm((rows, depth), f32), vm(*narrow), vm(*narrow), vm(mixed[-1].shape, f32)]
         + [vm((8 + length, width), f32), vm((8 + length, 128), f32)]
         + [vm((width, width), f32)] * 4
+        + [vm((8, width), f32)] * 2
         + [dma((10,)), dma((5,))],
     )
     down_sum, gate_sum, up_sum, mid_low, middle_grad, partial, branch_low, conv_low = back[:8]
     conv_weight_grad, sums, recur_weight_grad, inject_weight_grad = back[8:]
     gate_grad, up_grad, mlp_gain_grad = finish_pair(mlp_gain, gate_sum, up_sum, gate_weight, up_weight)
-    output_partial = mm_tn(product, mid_low).astype(bf16)[None]
-    mix_low = jnp.concatenate([branch_low, conv_low], 1)
-    mix_low = jnp.pad(mix_low, ((0, 0), (0, -2 * width % 128)))
-    mix_partial = mm_tn(unit_all, mix_low).astype(bf16).reshape(members, -1, mix_low.shape[1])
     size = recur_gate_weight.shape[1]
     gates = jnp.concatenate([recur_weight_grad, inject_weight_grad], 2).reshape(width, 2 * size)
     lanes = -(-max(width, 2 * size) // 128) * 128
@@ -1300,12 +1386,18 @@
         ],
         0,
     ).astype(bf16)[None]
-    again = plane_scratch(rows, depth, 1, 1)
-    output_sum, mix_sum, packed, tokens_grad, block_out = replica_sum(
-        [output_partial, mix_partial, packed], ["row", "side", "row"], 4, end_steps, (1, 2, 3, 4, 6, 7, 14),
-        [(partial, ANY), (middle_grad, VM), (x, VM), (middle, VM), (hidden, ANY), (down_w, ANY)],
+    both = -(-2 * width // 128) * 128
+    mix_shape = jax.ShapeDtypeStruct((members, depth // members, both), bf16)
+    output_shape = jax.ShapeDtypeStruct((1,) + output_w.shape, bf16)
+    again = plane_scratch(rows, depth, 0, 1)
+    packed, output_sum, mix_sum, tokens_grad, block_out = replica_sum(
+        [packed, output_shape, mix_shape], ["row", "row", "side"], (1, 2), 4, functools.partial(end_steps, 1, 2),
+        (0, 1, 2, 3, 4, 7, 8, 9, 10, 11, 12, 19),
+        [(partial, ANY), (middle_grad, VM), (x, VM), (middle, VM)]
+        + [(item, ANY) for item in (hidden, down_w, product, mid_low, unit_all, branch_low, conv_low)],
         [((rows, depth), bf16, VM), ((rows, depth), bf16, VM)],
-        again + again[:2] + [vm(*whole), vm(*whole), vm(hidden.shape, bf16), vm(down_w.shape, bf16), dma((3,))],
+        again + again[3:] + again[:2] + [vm(*whole), vm(hidden.shape, bf16), vm(down_w.shape, bf16)]
+        + [vm(*narrow), vm(*whole), vm(*narrow), vm(*narrow), vm((total, both), bf16), dma((8,))],
     )
     packed = packed.astype(f32)
     branch_grad, input_grad, gain_grad, output_grad, down_grad = finish_rest(

time: 604 us -> 599 us (level)
  matrix products: 10 us -> 0 us
  Pallas kernels: 561 us -> 570 us
  other arithmetic: 16.4 us -> 8.09 us
    dot_general x2 -> x0, matrix products: 10 us -> none  [mm_tn(): lax.dot_general(left, right, (((0,), (0,)), ((), ())), preferred_element_...]
where the time goes in v11:
time: 599 us; the launch traced here: 590 us
  Pallas kernels  570 us (95%)
  local copies, waits for them, and re-layouts  10.6 us (2%)
  other arithmetic  8.09 us (1%)
    pallas_call x2, Pallas kernels, replica_sum(): pl.pallas_call(functools.partial(line_kernel, lax.axis_size('replica'), t...  351 us
    pallas_call x1, Pallas kernels, front(): pl.pallas_call(functools.partial(front_kernel, n, sequences, length), out...  158 us
    pallas_call x1, Pallas kernels, mlp(): pl.pallas_call(mlp_kernel, out_shape=tuple((jax.ShapeDtypeStruct(*item) f...  37.3 us
    pallas_call x1, Pallas kernels, finish_pair(): pl.pallas_call(finish_pair_kernel, grid=(rows // cut,), out_shape=(out, o...  13.5 us

profile of v11, /device:TPU:0, one launch (start us, length us, event | category | flops | bytes accessed | tf_op | source)
XLA Modules:
  0.0 590.1 jit_solution(15070848890308447056)
XLA Ops:
  0.7 0.7 convert.31
  1.3 0.7 convert.32
  2.0 0.8 copy.42.gains_ref
  2.8 0.7 compare_select_fusion
  3.5 0.6 broadcast_in_dim.38.rate_ref.refs_10_
  4.1 1.2 broadcast_in_dim.35.raw_a.refs_7_
  5.4 1.2 broadcast_in_dim.36.raw_b.refs_8_
  6.6 1.2 broadcast_in_dim.37.raw_c.refs_9_
  7.8 0.7 convert_bitcast_fusion
  8.5 0.7 broadcast_in_dim.34.label_ref
  9.2 158.3 %shard_map.305 = (bf16[1024,2048]{1,0:T(8,128)(2,1)}, bf16[1024,128]{1,0:T(8,128)(2,1)}, bf16[1024,2048]{1,0:T(8,128)(2,1)}, bf16[1024,320]{1,0:T(8,128)(2,1)}, ...) custom-call(bf16[128,2048]{1,0:T(8,128)(2,1)} %bitcast.20, ...), custom_call_target="tpu_custom_call" | custom-call | flops 1000000 | bytes 209715200 | tf_op jit(solution)/shard_map/pallas_call | solution.py:670
  167.5 37.3 %shard_map.306 = (bf16[1024,768]{1,0:T(8,128)(2,1)}, bf16[1024,2048]{1,0:T(8,128)(2,1)}, bf16[768,2048]{1,0:T(8,128)(2,1)}, bf16[2048,1536]{1,0:T(8,128)(2,1)}) custom-call(bf16[1024,2048]{1,0:T(8,128)(2,1)} %get-tuple-element.63.two_hbm, bf16[1024,2048]{1,0:T(8,128)(2,1)} %get-tuple-element.64.low_hbm, bf16[2048,1536]{1,0:T(8,128)(2,1)} %bitcast.27, ...), custom_call_target="tpu_custom_call" | custom-call | flops 25769803776 | bytes 37748736 | tf_op jit(solution)/shard_map/pallas_call | solution.py:977
  204.8 228.6 %shard_map.307 = (bf16[768,2048]{1,0:T(8,128)(2,1)}, bf16[256,6144]{1,0:T(8,128)(2,1)}, bf16[256,6144]{1,0:T(8,128)(2,1)}, bf16[1024,2048]{1,0:T(8,128)(2,1)}, f...) custom-call(bf16[1,768,2048]{2,1,0:T(8,128)(2,1)} %bitcast.17, ...), custom_call_target="tpu_custom_call" | custom-call | flops 1000000 | bytes 209715200 | tf_op jit(solution)/shard_map/pallas_call | solution.py:1214
  433.4 0.8 copy.44.gain_ref
  434.2 0.0 copy-start.4
  434.2 0.0 copy-start.3
  434.2 0.0 copy-start.7
  434.2 0.0 copy-start.6
  434.2 13.5 %shard_map.310 = (f32[256,6144]{1,0:T(8,128)}, f32[256,6144]{1,0:T(8,128)}, f32[256,1]{1,0:T(8,128)}) custom-call(f32[256,1]{1,0:T(8,128)} %copy.44.gain_ref, bf16[256,6144]{1,0:T(8,128)(2,1)} %get-tuple-element.103.a_ref, bf16[256,6144]{1,0:T(8,128)(2,1)} %get-tuple-element.104.b_ref, f32[256,6144]{1,0:T(8,128)} %wa_ref.3, f32[256,6144]{1,0:T(8,128)} %wb_ref.3), custom_call_target="tpu_custom_call" | custom-call | flops 9437184 | bytes 31457280 | tf_op jit(solution)/shard_map/pallas_call | solution.py:1250
  447.7 1.6 reduce.5
  449.3 0.0 copy-done.4
  449.3 0.0 copy-done.3
  449.4 0.1 pad_maximum_fusion.1
  449.5 0.0 copy-done.7
  449.5 0.0 copy-done.6
  449.6 0.7 pad_maximum_fusion.refs_0_
  450.3 122.6 %shard_map.308 = (bf16[336,384]{1,0:T(8,128)(2,1)}, bf16[320,2048]{1,0:T(8,128)(2,1)}, bf16[8,256,640]{2,1,0:T(8,128)(2,1)}, bf16[128,2048]{1,0:T(8,128)(2,1)}, bf16[128,2048]{1,0:T(8,128)(2,1)}) custom-call(bf16[1,336,384]{2,1,0:T(8,128)(2,1)} %pad_maximum_fusion.refs_0_, bf16[1024,2048]{1,0:T(8,128)(2,1)} %get-tuple-element.85.refs_1_, ...), custom_call_target="tpu_custom_call" | custom-call | flops 1000000 | bytes 209715200 | tf_op jit(solution)/shard_map/pallas_call | solution.py:1214
  572.9 0.8 copy.43.gain_ref
  573.7 0.0 copy-start
  573.7 0.0 copy-start.5
  573.7 0.0 copy-start.2
  573.7 10.0 %shard_map.309 = (f32[256,2560]{1,0:T(8,128)}, f32[256,2560]{1,0:T(8,128)}, f32[256,1]{1,0:T(8,128)}, f32[320,2048]{1,0:T(8,128)}, f32[768,2048]{1,0:T(8,128)}) custom-call(f32[256,1]{1,0:T(8,128)} %copy.43.gain_ref, bf16[8,256,640]{2,1,0:T(8,128)(2,1)} %get-tuple-element.95.mix_ref, f32[256,2560]{1,0:T(8,128)} %wa_ref.2, f32[256,2560]{1,0:T(8,128)} %wb_ref.2, ...), custom_call_target="tpu_custom_call" | custom-call | flops 10000000 | bytes 41943040 | tf_op jit(solution)/shard_map/pallas_call | solution.py:1287
  583.7 0.0 copy-start.1
  583.7 1.6 reduce
  585.3 0.0 copy-done
  585.3 0.9 fusion.15
  586.3 0.6 fusion.14
  586.9 0.0 copy-done.5
  586.9 0.6 divide_multiply_fusion
  587.5 0.6 slice.28
  588.1 0.0 copy-done.2
  588.1 0.8 copy.47
  588.9 0.0 copy-done.1
  588.9 0.8 copy.48
  (12 shorter events, 0.2 us)
Async XLA Ops:
  434.2 15.1 %copy-start.4 = (f32[2,160,160]{2,1,0:T(8,128)S(1)}, f32[2,160,160]{2,1,0:T(8,128)}, u32[]{:S(2)}) copy-start(f32[2,160,160]{2,1,0:T(8,128)} %get-tuple-element.81) | copy-start | bytes 614404
  434.2 15.1 %copy-start.3 = (f32[2,160,160]{2,1,0:T(8,128)S(1)}, f32[2,160,160]{2,1,0:T(8,128)}, u32[]{:S(2)}) copy-start(f32[2,160,160]{2,1,0:T(8,128)} %get-tuple-element.82) | copy-start | bytes 614404
  434.2 15.3 %copy-start.7 = (f32[4,320]{1,0:T(4,128)S(1)}, f32[4,320]{1,0:T(4,128)}, u32[]{:S(2)}) copy-start(f32[4,320]{1,0:T(4,128)} %get-tuple-element.83) | copy-start | bytes 15364
  434.2 15.3 %copy-start.6 = (f32[4,320]{1,0:T(4,128)S(1)}, f32[4,320]{1,0:T(4,128)}, u32[]{:S(2)}) copy-start(f32[4,320]{1,0:T(4,128)} %get-tuple-element.84) | copy-start | bytes 15364
  573.7 11.7 %copy-start = (bf16[336,384]{1,0:T(8,128)(2,1)S(1)}, bf16[336,384]{1,0:T(8,128)(2,1)}, u32[]{:S(2)}) copy-start(bf16[336,384]{1,0:T(8,128)(2,1)} %get-tuple-element.101) | copy-start | bytes 774148
  573.7 13.2 %copy-start.5 = (f32[320]{0:T(512)S(1)}, f32[320]{0:T(512)}, u32[]{:S(2)}) copy-start(f32[320]{0:T(512)} %param.30) | copy-start | bytes 3844
  573.7 14.4 %copy-start.2 = (bf16[128,2048]{1,0:T(8,128)(2,1)S(1)}, bf16[128,2048]{1,0:T(8,128)(2,1)}, u32[]{:S(2)}) copy-start(bf16[128,2048]{1,0:T(8,128)(2,1)} %get-tuple-element.93) | copy-start | bytes 1572868
  583.7 5.2 copy-start.1

commit v12 on v11

--- a/solution.py
+++ b/solution.py
@@ -106,8 +106,8 @@
 def fill_small(conv, bias, raw_conv, raw_a, raw_b, raw_c, rate):
     conv[0 : raw_conv.shape[0], :] = low(raw_conv[...])
     for row, ref in enumerate((raw_a, raw_b, raw_c)):
-        bias[row : row + 1, :] = low(ref[...])
-    bias[3:4, :] = rate[...]
+        bias[row : row + 1, :] = low(ref[...])[None, :]
+    bias[3:4, :] = rate[...][None, :]
 
 
 def label_masks(label_ref, here, length, width, taps, lines):
@@ -450,7 +450,7 @@
 
         cut_columns(
             tall.at[side],
-            lambda step: gains_ref[pl.ds(pl.multiple_of(z * part + step, 16), 16), 1:2],
+            lambda step: low(gains_ref[pl.ds(pl.multiple_of(z * part + step, 16), 16), 1:2]),
             lambda j: pair_cut.at[j],
             side * ff,
             ff,
@@ -493,7 +493,7 @@
     for side in range(2):
         loads[2 + side].wait()
         cut_columns(
-            wide.at[side], lambda step: gains_ref[pl.ds(step, 16), 0:1], lambda j: mix_cut.at[j, side], 0, width
+            wide.at[side], lambda step: low(gains_ref[pl.ds(step, 16), 0:1]), lambda j: mix_cut.at[j, side], 0, width
         )
     mix_moves = [
         remote(mix_cut.at[place(i)], mix_ref.at[me], mix_sent.at[i], mix_got.at[i], peer(i)) for i in range(1, owners)
@@ -531,8 +531,6 @@
         if k + 2 < cuts:
             down_load(k + 2).start()
 
-    for k in range(2):
-        down_load(k).start()
     pair_own.wait()
     for move in pair_moves:
         move.wait_recv()
@@ -544,10 +542,6 @@
     for wait in waits:
         wait()
     mix_own.wait()
-    for k in range(cuts):
-        down_cast(k)
-    for k in range(cuts - 2, cuts):
-        down_save(k).wait()
     for move in mix_moves:
         move.wait_recv()
     save(unit_ref, unit_out)
@@ -594,6 +588,8 @@
         partial[here, :] = dot_nn(product, ow_ref[...]).astype(bf16)
         return 0
 
+    for k in range(2):
+        down_load(k).start()
     lax.fori_loop(0, sequences, two, 0)
     scatter = scatter_steps(rows, partial, near, far, acc, scatter_sems)
     next(scatter)
@@ -603,6 +599,10 @@
     ):
         save(source, target)
     next(line)
+    for k in range(cuts):
+        down_cast(k)
+    for k in range(cuts - 2, cuts):
+        down_save(k).wait()
     next(low_gather)
     waits = next(low_gather) + next(scatter)
 
@@ -903,7 +903,7 @@
     total, depth = two.shape
     ff = down_w.shape[0]
     tile = 256 if ff % 256 == 0 else 128
-    height = 256
+    height = 512
     steps = total // height
 
     def rows_of(hbm, ref, r, which):
@@ -955,6 +955,8 @@
     saves.append(pltpu.make_async_copy(down_grad, down_out, save_sem.at[2]))
     saves[-1].start()
 
+    height = 256
+
     def column_step(d, _):
         here = pl.ds(pl.multiple_of(d * height, height), height)
         pair_grad[here, :] = dot_tn(two[:, here], pair_low[...]).astype(bf16)
@@ -982,7 +984,7 @@
         scratch_shapes=[vm(item.shape, bf16) for item in (unit_two, out_low, pair_w, down_w)]
         + [vm((total, ff), bf16), vm((total, 2 * ff), bf16)]
         + [vm(*item) for item in kept[1:]]
-        + [dma((3, total // 256)), dma((3,)), dma((depth // 256,))],
+        + [dma((3, total // 512)), dma((3,)), dma((depth // 256,))],
         compiler_params=pltpu.CompilerParams(vmem_limit_bytes=60 * 2**20),
         cost_estimate=pl.CostEstimate(
             flops=2 * total * depth * ff * 8, bytes_accessed=36 * 2**20, transcendentals=total * ff
@@ -1233,17 +1235,18 @@
 
 
 def finish_pair_kernel(gain_ref, a_ref, b_ref, wa_ref, wb_ref, outa_ref, outb_ref, grad_ref):
-    grad = jnp.zeros(gain_ref.shape, f32)
+    gain = low(gain_ref[:, 1:2])
+    grad = jnp.zeros(gain.shape, f32)
     for sum_ref, weight_ref, out_ref in ((a_ref, wa_ref, outa_ref), (b_ref, wb_ref, outb_ref)):
         total = sum_ref[...].astype(f32)
-        out_ref[...] = total * gain_ref[...]
+        out_ref[...] = total * gain
         grad = grad + jnp.sum(total * low(weight_ref[...]), axis=1, keepdims=True)
     grad_ref[...] = grad
 
 
 def finish_pair(gain, a, b, wa, wb):
     rows, columns = wa.shape
-    cut = min(rows, 32)
+    cut = min(rows, 64)
     wide = pl.BlockSpec((cut, columns), lambda i: (i, 0))
     thin = pl.BlockSpec((cut, 1), lambda i: (i, 0))
     out = jax.ShapeDtypeStruct((rows, columns), f32)
@@ -1251,7 +1254,7 @@
         finish_pair_kernel,
         grid=(rows // cut,),
         out_shape=(out, out, jax.ShapeDtypeStruct((rows, 1), f32)),
-        in_specs=[thin, wide, wide, wide, wide],
+        in_specs=[pl.BlockSpec((cut, 2), lambda i: (i, 0)), wide, wide, wide, wide],
         out_specs=[wide, wide, thin],
         compiler_params=pltpu.CompilerParams(vmem_limit_bytes=62 * 2**20),
         cost_estimate=pl.CostEstimate(flops=6 * rows * columns, bytes_accessed=20 * rows * columns, transcendentals=0),
@@ -1261,12 +1264,13 @@
 def finish_rest_kernel(gain_ref, mix_ref, wa_ref, wb_ref, out_sum_ref, down_sum_ref, outa_ref, outb_ref, grad_ref, out_ref, down_ref):
     owners = mix_ref.shape[0]
     width = wa_ref.shape[1] // owners
-    grad = jnp.zeros(gain_ref.shape, f32)
+    gain = low(gain_ref[:, 0:1])
+    grad = jnp.zeros(gain.shape, f32)
     for part, (weight_ref, target_ref) in enumerate(((wa_ref, outa_ref), (wb_ref, outb_ref))):
         total = jnp.concatenate(
             [mix_ref[j, :, part * width : (part + 1) * width].astype(f32) for j in range(owners)], axis=1
         )
-        target_ref[...] = total * gain_ref[...]
+        target_ref[...] = total * gain
         grad = grad + jnp.sum(total * low(weight_ref[...]), axis=1, keepdims=True)
     grad_ref[...] = grad
     out_ref[...] = out_sum_ref[...].astype(f32)
@@ -1283,7 +1287,7 @@
         return pl.BlockSpec((item.shape[0] // steps, item.shape[1]), lambda i: (i, 0))
 
     owners, _, both = mix.shape
-    wide, thin = tall(wa), tall(gain)
+    wide, thin = tall(wa), pl.BlockSpec((rows // steps, 1), lambda i: (i, 0))
     return pl.pallas_call(
         finish_rest_kernel,
         grid=(steps,),
@@ -1295,7 +1299,7 @@
             jax.ShapeDtypeStruct(down_sum.shape, f32),
         ),
         in_specs=[
-            thin,
+            tall(gain),
             pl.BlockSpec((owners, rows // steps, both), lambda i: (0, i, 0)),
             wide,
             wide,
@@ -1333,17 +1337,17 @@
     members = lax.axis_size(GROUP)
     sequences = lax.axis_size("shard")
     total = members * rows
-    gain, mlp_gain = low(norm_gain)[:, None], low(mlp_norm_gain)[:, None]
+    gains = jnp.stack([norm_gain, mlp_norm_gain], 1)
     own_labels = jnp.broadcast_to(segments[0].astype(bf16)[:, None], (rows, 128))
     width = branch_weight.shape[1] // members
     decay_f = low(decay_param)
     small = (
-        conv_weight, conv_bias[None], recur_gate_bias[None], input_gate_bias[None], jax.nn.softplus(-decay_f)[None],
+        conv_weight, conv_bias, recur_gate_bias, input_gate_bias, jax.nn.softplus(-decay_f),
     )
     (
         unit_all, labels, out_low, product, *mixed, mix_w, output_w, unit_two, middle, pair_w, down_w,
     ) = front(
-        sequences, x, own_labels, cot, low(jnp.stack([norm_gain, mlp_norm_gain], 1)), small,
+        sequences, x, own_labels, cot, gains, small,
         recur_gate_weight, input_gate_weight, branch_weight, input_weight, gate_weight, up_weight, output_weight,
         down_weight,
     )
@@ -1374,7 +1378,7 @@
     )
     down_sum, gate_sum, up_sum, mid_low, middle_grad, partial, branch_low, conv_low = back[:8]
     conv_weight_grad, sums, recur_weight_grad, inject_weight_grad = back[8:]
-    gate_grad, up_grad, mlp_gain_grad = finish_pair(mlp_gain, gate_sum, up_sum, gate_weight, up_weight)
+    gate_grad, up_grad, mlp_gain_grad = finish_pair(gains, gate_sum, up_sum, gate_weight, up_weight)
     size = recur_gate_weight.shape[1]
     gates = jnp.concatenate([recur_weight_grad, inject_weight_grad], 2).reshape(width, 2 * size)
     lanes = -(-max(width, 2 * size) // 128) * 128
@@ -1401,7 +1405,7 @@
     )
     packed = packed.astype(f32)
     branch_grad, input_grad, gain_grad, output_grad, down_grad = finish_rest(
-        gain, mix_sum, branch_weight, input_weight, output_sum, down_sum
+        gains, mix_sum, branch_weight, input_weight, output_sum, down_sum
     )
     recur_weight_grad = packed[:width, :size].reshape(-1, size, size)
     inject_weight_grad = packed[:width, size : 2 * size].reshape(-1, size, size)

time: 599 us -> 586 us (0.978)
  Pallas kernels: 570 us -> 562 us
where the time goes in v12:
time: 586 us; the launch traced here: 581 us
  Pallas kernels  562 us (96%)
  other arithmetic  12.2 us (2%)
  local copies, waits for them, and re-layouts  6.29 us (1%)
    pallas_call x2, Pallas kernels, replica_sum(): pl.pallas_call(functools.partial(line_kernel, lax.axis_size('replica'), t...  349 us
    pallas_call x1, Pallas kernels, front(): pl.pallas_call(functools.partial(front_kernel, n, sequences, length), out...  153 us
    pallas_call x1, Pallas kernels, mlp(): pl.pallas_call(mlp_kernel, out_shape=tuple((jax.ShapeDtypeStruct(*item) f...  37.6 us

profile of v12, /device:TPU:0, one launch (start us, length us, event | category | flops | bytes accessed | tf_op | source)
XLA Modules:
  0.0 581.4 jit_solution(6814490550840216224)
XLA Ops:
  0.7 0.7 convert_bitcast_fusion
  1.3 1.3 compare_select_fusion.rate_ref.refs_10_
  2.6 0.7 pad_maximum_fusion.2
  3.3 0.7 broadcast_in_dim.16.label_ref
  4.0 0.8 copy.37.gains_ref.gain_ref
  4.8 153.4 %shard_map.305 = (bf16[1024,2048]{1,0:T(8,128)(2,1)}, bf16[1024,128]{1,0:T(8,128)(2,1)}, bf16[1024,2048]{1,0:T(8,128)(2,1)}, bf16[1024,320]{1,0:T(8,128)(2,1)}, ...) custom-call(bf16[128,2048]{1,0:T(8,128)(2,1)} %bitcast.22, ...), custom_call_target="tpu_custom_call" | custom-call | flops 1000000 | bytes 209715200 | tf_op jit(solution)/shard_map/pallas_call | solution.py:670
  158.2 37.6 %shard_map.306 = (bf16[1024,768]{1,0:T(8,128)(2,1)}, bf16[1024,2048]{1,0:T(8,128)(2,1)}, bf16[768,2048]{1,0:T(8,128)(2,1)}, bf16[2048,1536]{1,0:T(8,128)(2,1)}) custom-call(bf16[1024,2048]{1,0:T(8,128)(2,1)} %get-tuple-element.63.two_hbm, bf16[1024,2048]{1,0:T(8,128)(2,1)} %get-tuple-element.64.low_hbm, bf16[2048,1536]{1,0:T(8,128)(2,1)} %bitcast.31, ...), custom_call_target="tpu_custom_call" | custom-call | flops 25769803776 | bytes 37748736 | tf_op jit(solution)/shard_map/pallas_call | solution.py:979
  195.8 227.1 %shard_map.307 = (bf16[768,2048]{1,0:T(8,128)(2,1)}, bf16[256,6144]{1,0:T(8,128)(2,1)}, bf16[256,6144]{1,0:T(8,128)(2,1)}, bf16[1024,2048]{1,0:T(8,128)(2,1)}, f...) custom-call(bf16[1,768,2048]{2,1,0:T(8,128)(2,1)} %bitcast.19, ...), custom_call_target="tpu_custom_call" | custom-call | flops 1000000 | bytes 209715200 | tf_op jit(solution)/shard_map/pallas_call | solution.py:1216
  422.9 1.0 convert.21
  423.9 0.7 convert.23
  424.6 0.7 convert.24
  425.3 1.0 convert.22
  426.3 0.1 pad_maximum_fusion.1
  426.4 0.7 pad_maximum_fusion.refs_0_
  427.1 0.0 copy-start.2
  427.1 122.2 %shard_map.308 = (bf16[336,384]{1,0:T(8,128)(2,1)}, bf16[320,2048]{1,0:T(8,128)(2,1)}, bf16[8,256,640]{2,1,0:T(8,128)(2,1)}, bf16[128,2048]{1,0:T(8,128)(2,1)}, bf16[128,2048]{1,0:T(8,128)(2,1)}) custom-call(bf16[1,336,384]{2,1,0:T(8,128)(2,1)} %pad_maximum_fusion.refs_0_, bf16[1024,2048]{1,0:T(8,128)(2,1)} %get-tuple-element.85.refs_1_, ...), custom_call_target="tpu_custom_call" | custom-call | flops 1000000 | bytes 209715200 | tf_op jit(solution)/shard_map/pallas_call | solution.py:1216
  549.4 1.3 slice.28
  550.7 1.0 convert_element_type.35
  551.7 0.6 fusion.14
  552.3 0.0 copy-done.2
  552.3 0.6 divide_multiply_fusion
  552.9 1.9 fusion.15
  554.8 9.9 %shard_map.309 = (f32[256,2560]{1,0:T(8,128)}, f32[256,2560]{1,0:T(8,128)}, f32[256,1]{1,0:T(8,128)}, f32[320,2048]{1,0:T(8,128)}, f32[768,2048]{1,0:T(8,128)}) custom-call(f32[256,2]{1,0:T(8,128)} %copy.37.gains_ref.gain_ref, bf16[8,256,640]{2,1,0:T(8,128)(2,1)} %get-tuple-element.95.mix_ref, f32[256,2560]{1,0:T(8,128)} %wa_ref.2, f32[256,2560]{1,0:T(8,128)} %wb_ref.2, ...), custom_call_target="tpu_custom_call" | custom-call | flops 10000000 | bytes 41943040 | tf_op jit(solution)/shard_map/pallas_call | solution.py:1291
  564.6 1.6 reduce
  566.2 0.0 copy-start.1
  566.2 0.0 copy-start
  566.2 11.5 %shard_map.310 = (f32[256,6144]{1,0:T(8,128)}, f32[256,6144]{1,0:T(8,128)}, f32[256,1]{1,0:T(8,128)}) custom-call(f32[256,2]{1,0:T(8,128)} %copy.37.gains_ref.gain_ref, bf16[256,6144]{1,0:T(8,128)(2,1)} %get-tuple-element.103.a_ref, bf16[256,6144]{1,0:T(8,128)(2,1)} %get-tuple-element.104.b_ref, f32[256,6144]{1,0:T(8,128)} %wa_ref.3, f32[256,6144]{1,0:T(8,128)} %wb_ref.3), custom_call_target="tpu_custom_call" | custom-call | flops 9437184 | bytes 31457280 | tf_op jit(solution)/shard_map/pallas_call | solution.py:1253
  577.8 1.6 reduce.5
  579.3 0.0 copy-done.1
  579.3 0.8 copy.42
  580.1 0.0 copy-done
  580.1 0.8 copy.43
  (2 shorter events, 0.0 us)
Async XLA Ops:
  427.1 125.1 %copy-start.2 = (f32[320]{0:T(512)S(1)}, f32[320]{0:T(512)}, u32[]{:S(2)}) copy-start(f32[320]{0:T(512)} %param.30) | copy-start | bytes 3844
  566.2 13.1 %copy-start.1 = (bf16[128,2048]{1,0:T(8,128)(2,1)S(1)}, bf16[128,2048]{1,0:T(8,128)(2,1)}, u32[]{:S(2)}) copy-start(bf16[128,2048]{1,0:T(8,128)(2,1)} %get-tuple-element.93) | copy-start | bytes 1572868
  566.2 13.9 %copy-start = (bf16[128,2048]{1,0:T(8,128)(2,1)S(1)}, bf16[128,2048]{1,0:T(8,128)(2,1)}, u32[]{:S(2)}) copy-start(bf16[128,2048]{1,0:T(8,128)(2,1)} %get-tuple-element.94) | copy-start | bytes 1572868

commit v13 on v12

--- a/solution.py
+++ b/solution.py
@@ -685,13 +685,13 @@
     partial_hbm, middle_ref, cot_ref, label_ref, raw_conv, raw_a, raw_b, raw_c, rate_ref, rw_ref, iw_ref, *rest,
 ):
     kept_hbm, rest = rest[:9], rest[9:]
-    low_out, grad_out, partial_out, branch_low_out, conv_low_out, dconv_ref, sums_ref, drw_ref, diw_ref = rest[:9]
-    scatter_sems, gather_sems = rest[9 + 3 : 9 + 7], rest[9 + 7 : 9 + 11]
-    near, far, acc = rest[9:12]
-    rest = rest[20:]
+    low_out, grad_out, partial_out, branch_low_out, conv_low_out, packed_ref = rest[:6]
+    scatter_sems, gather_sems = rest[6 + 3 : 6 + 7], rest[6 + 7 : 6 + 11]
+    near, far, acc = rest[6:9]
+    rest = rest[17:]
     kept, rest = rest[:9], rest[9:]
     ow_ref, w_ref, pre_ref, conv_in_ref, values_ref, recur_ref, inject_ref, decay_ref, states_ref = kept
-    partial, low_ref, grad_ref, branch_low_ref, conv_low_ref, adj, pad, lines, rbig, ibig, dr, di, conv_ref, bias_ref, load_sem, save_sem = rest
+    partial, low_ref, grad_ref, branch_low_ref, conv_low_ref, adj, pad, lines, rbig, ibig, dr, di, conv_ref, bias_ref, dconv_ref, sums_ref, load_sem, save_sem = rest
     rows = middle_ref.shape[0]
     offsets, at, block = plane()
     first = pltpu.make_async_copy(partial_hbm, partial, load_sem.at[9])
@@ -800,11 +800,12 @@
     for s in range(sequences):
         two(s)
         yield
-    size = drw_ref.shape[1]
-    for h in range(drw_ref.shape[0]):
+    size = rw_ref.shape[1]
+    packed_ref[...] = jnp.zeros_like(packed_ref)
+    for h in range(rw_ref.shape[0]):
         cut = slice(h * size, (h + 1) * size)
-        drw_ref[h] = dr[cut, cut]
-        diw_ref[h] = di[cut, cut]
+        packed_ref[0, cut, 0 : 2 * size] = jnp.concatenate([dr[cut, cut], di[cut, cut]], axis=1).astype(bf16)
+    packed_ref[0, width : width + 16, 0:width] = jnp.concatenate([dconv_ref[...], sums_ref[...]], axis=0).astype(bf16)
     ends = [(partial, partial_out), (branch_low_ref, branch_low_out), (conv_low_ref, conv_low_out)]
     for k, pair in enumerate(ends):
         saves.append(pltpu.make_async_copy(*pair, save_sem.at[2 + k]))
@@ -817,12 +818,12 @@
 def end_steps(
     outputs_at, mixes_at,
     partial_hbm, grad_ref, x_ref, middle_ref, hidden_hbm, down_hbm, product_hbm, mid_hbm, unit_hbm, branch_hbm, conv_hbm,
-    tokens_ref, block_ref, *rest,
+    gate_sum, up_sum, gate_hbm, up_hbm, tokens_ref, block_ref, gain_ref, *rest,
 ):
     near, far, acc = rest[:3]
     scatter_sems, more_sems = rest[3:7], rest[7:11]
-    near_two, far_two, partial, hidden, down, product, tokens_wide, branch_low, conv_low, mix_low, load_sem = rest[11:22]
-    output_made, mix_made = rest[22:]
+    near_two, far_two, partial, hidden, down, product, tokens_wide, branch_low, conv_low, mix_low, sums, weights = rest[11:23]
+    load_sem, gain_sem, output_made, mix_made = rest[23:]
     rows = x_ref.shape[0]
     depth = down.shape[1]
 
@@ -841,6 +842,20 @@
     for d in range(0, depth, 512):
         output_made[0, :, d : d + 512] = dot_tn(product[...], tokens_wide[:, d : d + 512]).astype(bf16)
     again = load(7, unit_hbm, tokens_wide)
+
+    def gain_loads(r):
+        here = pl.ds(r * 16, 16)
+        slot = r % 2
+        return [
+            pltpu.make_async_copy(source.at[here, :], target.at[slot, side], gain_sem.at[slot, 2 * group + side])
+            for group, (target, sources) in enumerate(((sums, (gate_sum, up_sum)), (weights, (gate_hbm, up_hbm))))
+            for side, source in enumerate(sources)
+        ]
+
+    gain_steps = gain_ref.shape[0] // 16
+    for r in range(2):
+        for copy in gain_loads(r):
+            copy.start()
     yield outputs_at
     loads[0].wait()
     scatter = scatter_steps(rows, partial, near, far, acc, scatter_sems)
@@ -892,6 +907,20 @@
 
     by_tiles(rows, out)
     yield None
+    for r in range(gain_steps):
+        slot = r % 2
+        for copy in gain_loads(r):
+            copy.wait()
+        both = jnp.zeros((16, 1), f32)
+        for side in range(2):
+            both = both + jnp.sum(
+                sums[slot, side].astype(f32) * low(weights[slot, side]), axis=1, keepdims=True
+            )
+        gain_ref[r * 16 : (r + 1) * 16, :] = both
+        if r + 2 < gain_steps:
+            for copy in gain_loads(r + 2):
+                copy.start()
+        yield None
     for wait in waits:
         wait()
 
@@ -1234,31 +1263,26 @@
     )(*[item for k, item in enumerate(arrays) if k not in made_here], *[item for item, _ in inputs])
 
 
-def finish_pair_kernel(gain_ref, a_ref, b_ref, wa_ref, wb_ref, outa_ref, outb_ref, grad_ref):
+def finish_pair_kernel(gain_ref, a_ref, b_ref, outa_ref, outb_ref):
     gain = low(gain_ref[:, 1:2])
-    grad = jnp.zeros(gain.shape, f32)
-    for sum_ref, weight_ref, out_ref in ((a_ref, wa_ref, outa_ref), (b_ref, wb_ref, outb_ref)):
-        total = sum_ref[...].astype(f32)
-        out_ref[...] = total * gain
-        grad = grad + jnp.sum(total * low(weight_ref[...]), axis=1, keepdims=True)
-    grad_ref[...] = grad
-
-
-def finish_pair(gain, a, b, wa, wb):
-    rows, columns = wa.shape
+    outa_ref[...] = a_ref[...].astype(f32) * gain
+    outb_ref[...] = b_ref[...].astype(f32) * gain
+
+
+def finish_pair(gain, a, b):
+    rows, columns = a.shape
     cut = min(rows, 64)
     wide = pl.BlockSpec((cut, columns), lambda i: (i, 0))
-    thin = pl.BlockSpec((cut, 1), lambda i: (i, 0))
     out = jax.ShapeDtypeStruct((rows, columns), f32)
     return pl.pallas_call(
         finish_pair_kernel,
         grid=(rows // cut,),
-        out_shape=(out, out, jax.ShapeDtypeStruct((rows, 1), f32)),
-        in_specs=[pl.BlockSpec((cut, 2), lambda i: (i, 0)), wide, wide, wide, wide],
-        out_specs=[wide, wide, thin],
+        out_shape=(out, out),
+        in_specs=[pl.BlockSpec((cut, 2), lambda i: (i, 0)), wide, wide],
+        out_specs=[wide, wide],
         compiler_params=pltpu.CompilerParams(vmem_limit_bytes=62 * 2**20),
-        cost_estimate=pl.CostEstimate(flops=6 * rows * columns, bytes_accessed=20 * rows * columns, transcendentals=0),
-    )(gain, a, b, wa, wb)
+        cost_estimate=pl.CostEstimate(flops=2 * rows * columns, bytes_accessed=12 * rows * columns, transcendentals=0),
+    )(gain, a, b)
 
 
 def finish_rest_kernel(gain_ref, mix_ref, wa_ref, wb_ref, out_sum_ref, down_sum_ref, outa_ref, outb_ref, grad_ref, out_ref, down_ref):
@@ -1360,6 +1384,8 @@
     narrow = ((total, width), bf16)
     vm, dma = pltpu.VMEM, pltpu.SemaphoreType.DMA
     length = total // sequences
+    size = recur_gate_weight.shape[1]
+    lanes = -(-max(width, 2 * size) // 128) * 128
     back = replica_sum(
         [down_partial, pair_partial], ["row", "pair"], (), 3,
         functools.partial(turn_steps, sequences, length),
@@ -1367,50 +1393,41 @@
         [(partial, ANY)] + [(item, VM) for item in (middle, cot, labels, *small, recur_gate_weight, input_gate_weight)]
         + [(item, ANY) for item in kept],
         [whole + (ANY,), ((rows, depth), f32, ANY), whole + (ANY,), narrow + (ANY,), narrow + (ANY,)]
-        + [(conv_weight.shape, f32, VM), ((4, width), f32, VM), (recur_gate_weight.shape, f32, VM), (input_gate_weight.shape, f32, VM)],
+        + [((1, width + 16, lanes), bf16, VM)],
         plane_scratch(rows, depth, 1, 1)
         + [vm(item.shape, item.dtype) for item in kept]
         + [vm(*whole), vm(*whole), vm((rows, depth), f32), vm(*narrow), vm(*narrow), vm(mixed[-1].shape, f32)]
         + [vm((8 + length, width), f32), vm((8 + length, 128), f32)]
         + [vm((width, width), f32)] * 4
         + [vm((8, width), f32)] * 2
+        + [vm((8, width), f32), vm((8, width), f32)]
         + [dma((10,)), dma((5,))],
     )
     down_sum, gate_sum, up_sum, mid_low, middle_grad, partial, branch_low, conv_low = back[:8]
-    conv_weight_grad, sums, recur_weight_grad, inject_weight_grad = back[8:]
-    gate_grad, up_grad, mlp_gain_grad = finish_pair(gains, gate_sum, up_sum, gate_weight, up_weight)
-    size = recur_gate_weight.shape[1]
-    gates = jnp.concatenate([recur_weight_grad, inject_weight_grad], 2).reshape(width, 2 * size)
-    lanes = -(-max(width, 2 * size) // 128) * 128
-    lines = jnp.concatenate([conv_weight_grad, sums], 0)
-    packed = jnp.concatenate(
-        [
-            jnp.pad(gates, ((0, 0), (0, lanes - 2 * size))),
-            jnp.pad(lines, ((0, 16 - lines.shape[0]), (0, lanes - width))),
-        ],
-        0,
-    ).astype(bf16)[None]
+    packed = back[8]
     both = -(-2 * width // 128) * 128
     mix_shape = jax.ShapeDtypeStruct((members, depth // members, both), bf16)
     output_shape = jax.ShapeDtypeStruct((1,) + output_w.shape, bf16)
     again = plane_scratch(rows, depth, 0, 1)
-    packed, output_sum, mix_sum, tokens_grad, block_out = replica_sum(
+    packed, output_sum, mix_sum, tokens_grad, block_out, mlp_gain_grad = replica_sum(
         [packed, output_shape, mix_shape], ["row", "row", "side"], (1, 2), 4, functools.partial(end_steps, 1, 2),
-        (0, 1, 2, 3, 4, 7, 8, 9, 10, 11, 12, 19),
+        (0, 1, 2, 3, 4, 7, 8, 9, 10, 11, 12, 19) + tuple(19 + i // 2 for i in range(gate_weight.shape[0] // 16)),
         [(partial, ANY), (middle_grad, VM), (x, VM), (middle, VM)]
-        + [(item, ANY) for item in (hidden, down_w, product, mid_low, unit_all, branch_low, conv_low)],
-        [((rows, depth), bf16, VM), ((rows, depth), bf16, VM)],
+        + [(item, ANY) for item in (hidden, down_w, product, mid_low, unit_all, branch_low, conv_low, gate_sum, up_sum, gate_weight, up_weight)],
+        [((rows, depth), bf16, VM), ((rows, depth), bf16, VM), ((gate_weight.shape[0], 1), f32, VM)],
         again + again[3:] + again[:2] + [vm(*whole), vm(hidden.shape, bf16), vm(down_w.shape, bf16)]
-        + [vm(*narrow), vm(*whole), vm(*narrow), vm(*narrow), vm((total, both), bf16), dma((8,))],
+        + [vm(*narrow), vm(*whole), vm(*narrow), vm(*narrow), vm((total, both), bf16)]
+        + [vm((2, 2, 16, gate_weight.shape[1]), bf16), vm((2, 2, 16, gate_weight.shape[1]), f32), dma((8,)), dma((2, 4))],
     )
     packed = packed.astype(f32)
+    gate_grad, up_grad = finish_pair(gains, gate_sum, up_sum)
     branch_grad, input_grad, gain_grad, output_grad, down_grad = finish_rest(
         gains, mix_sum, branch_weight, input_weight, output_sum, down_sum
     )
     recur_weight_grad = packed[:width, :size].reshape(-1, size, size)
     inject_weight_grad = packed[:width, size : 2 * size].reshape(-1, size, size)
     conv_weight_grad = packed[width : width + conv_weight.shape[0], :width]
-    conv_bias_grad, recur_bias_grad, inject_bias_grad, rate_grad = [packed[width + conv_weight.shape[0] + i, :width] for i in range(4)]
+    conv_bias_grad, recur_bias_grad, inject_bias_grad, rate_grad = [packed[width + 8 + i, :width] for i in range(4)]
     decay_param_grad = rate_grad * decay_scale * jax.nn.sigmoid(-decay_f)
     return (
         block_out[None],

time: 586 us -> 579 us (0.988)
  no operation moved by 1% of the time
where the time goes in v13:
time: 579 us; the launch traced here: 574 us
  Pallas kernels  558 us (96%)
  other arithmetic  7.99 us (1%)
  local copies, waits for them, and re-layouts  6.26 us (1%)
    pallas_call x2, Pallas kernels, replica_sum(): pl.pallas_call(functools.partial(line_kernel, lax.axis_size('replica'), t...  349 us
    pallas_call x1, Pallas kernels, front(): pl.pallas_call(functools.partial(front_kernel, n, sequences, length), out...  153 us
    pallas_call x1, Pallas kernels, mlp(): pl.pallas_call(mlp_kernel, out_shape=tuple((jax.ShapeDtypeStruct(*item) f...  37.6 us

profile of v13, /device:TPU:0, one launch (start us, length us, event | category | flops | bytes accessed | tf_op | source)
XLA Modules:
  0.0 573.7 jit_solution(7962205085095958149)
XLA Ops:
  0.7 0.7 convert_bitcast_fusion
  1.3 1.3 compare_select_fusion.rate_ref.refs_10_
  2.6 0.7 pad_maximum_fusion
  3.3 0.7 broadcast_in_dim.15.label_ref
  4.0 0.8 copy.37.gains_ref.gain_ref
  4.8 153.4 %shard_map.305 = (bf16[1024,2048]{1,0:T(8,128)(2,1)}, bf16[1024,128]{1,0:T(8,128)(2,1)}, bf16[1024,2048]{1,0:T(8,128)(2,1)}, bf16[1024,320]{1,0:T(8,128)(2,1)}, ...) custom-call(bf16[128,2048]{1,0:T(8,128)(2,1)} %bitcast.17, ...), custom_call_target="tpu_custom_call" | custom-call | flops 1000000 | bytes 209715200 | tf_op jit(solution)/shard_map/pallas_call | solution.py:670
  158.2 37.6 %shard_map.306 = (bf16[1024,768]{1,0:T(8,128)(2,1)}, bf16[1024,2048]{1,0:T(8,128)(2,1)}, bf16[768,2048]{1,0:T(8,128)(2,1)}, bf16[2048,1536]{1,0:T(8,128)(2,1)}) custom-call(bf16[1024,2048]{1,0:T(8,128)(2,1)} %get-tuple-element.60.two_hbm, bf16[1024,2048]{1,0:T(8,128)(2,1)} %get-tuple-element.61.low_hbm, bf16[2048,1536]{1,0:T(8,128)(2,1)} %bitcast.25, ...), custom_call_target="tpu_custom_call" | custom-call | flops 25769803776 | bytes 37748736 | tf_op jit(solution)/shard_map/pallas_call | solution.py:1008
  195.8 226.9 %shard_map.307 = (bf16[768,2048]{1,0:T(8,128)(2,1)}, bf16[256,6144]{1,0:T(8,128)(2,1)}, bf16[256,6144]{1,0:T(8,128)(2,1)}, bf16[1024,2048]{1,0:T(8,128)(2,1)}, f...) custom-call(bf16[1,768,2048]{2,1,0:T(8,128)(2,1)} %bitcast.14, ...), custom_call_target="tpu_custom_call" | custom-call | flops 1000000 | bytes 209715200 | tf_op jit(solution)/shard_map/pallas_call | solution.py:1245
  422.7 0.0 copy-start.2
  422.8 122.4 %shard_map.308 = (bf16[336,384]{1,0:T(8,128)(2,1)}, bf16[320,2048]{1,0:T(8,128)(2,1)}, bf16[8,256,640]{2,1,0:T(8,128)(2,1)}, bf16[128,2048]{1,0:T(8,128)(2,1)}, ...) custom-call(bf16[1,336,384]{2,1,0:T(8,128)(2,1)} %get-tuple-element.78.refs_0_, ...), custom_call_target="tpu_custom_call" | custom-call | flops 1000000 | bytes 209715200 | tf_op jit(solution)/shard_map/pallas_call | solution.py:1245
  545.1 1.6 reduce.5
  546.7 1.3 slice.28
  548.0 1.0 convert_element_type.23
  549.0 0.6 fusion.7
  549.6 0.0 copy-done.2
  549.6 0.6 divide_multiply_fusion
  550.2 1.9 fusion.8
  552.1 8.0 %shard_map.310 = (f32[256,6144]{1,0:T(8,128)}, f32[256,6144]{1,0:T(8,128)}) custom-call(f32[256,2]{1,0:T(8,128)} %copy.37.gains_ref.gain_ref, bf16[256,6144]{1,0:T(8,128)(2,1)} %get-tuple-element.87.refs_12_.a_ref, bf16[256,6144]{1,0:T(8,128)(2,1)} %get-tuple-element.88.refs_13_.b_ref), custom_call_target="tpu_custom_call" | custom-call | flops 3145728 | bytes 18874368 | tf_op jit(solution)/shard_map/pallas_call | solution.py:1277
  560.1 0.0 copy-start.1
  560.1 0.0 copy-start
  560.1 10.0 %shard_map.309 = (f32[256,2560]{1,0:T(8,128)}, f32[256,2560]{1,0:T(8,128)}, f32[256,1]{1,0:T(8,128)}, f32[320,2048]{1,0:T(8,128)}, f32[768,2048]{1,0:T(8,128)}) custom-call(f32[256,2]{1,0:T(8,128)} %copy.37.gains_ref.gain_ref, bf16[8,256,640]{2,1,0:T(8,128)(2,1)} %get-tuple-element.91.mix_ref, f32[256,2560]{1,0:T(8,128)} %wa_ref.1, f32[256,2560]{1,0:T(8,128)} %wb_ref.1, ...), custom_call_target="tpu_custom_call" | custom-call | flops 10000000 | bytes 41943040 | tf_op jit(solution)/shard_map/pallas_call | solution.py:1315
  570.1 1.6 reduce
  571.6 0.0 copy-done.1
  571.6 0.8 copy.42
  572.4 0.0 copy-done
  572.4 0.8 copy.43
Async XLA Ops:
  422.7 126.9 %copy-start.2 = (f32[320]{0:T(512)S(1)}, f32[320]{0:T(512)}, u32[]{:S(2)}) copy-start(f32[320]{0:T(512)} %param.30) | copy-start | bytes 3844
  560.1 11.6 %copy-start.1 = (bf16[128,2048]{1,0:T(8,128)(2,1)S(1)}, bf16[128,2048]{1,0:T(8,128)(2,1)}, u32[]{:S(2)}) copy-start(bf16[128,2048]{1,0:T(8,128)(2,1)} %get-tuple-element.89) | copy-start | bytes 1572868
  560.1 12.3 %copy-start = (bf16[128,2048]{1,0:T(8,128)(2,1)S(1)}, bf16[128,2048]{1,0:T(8,128)(2,1)}, u32[]{:S(2)}) copy-start(bf16[128,2048]{1,0:T(8,128)(2,1)} %get-tuple-element.90) | copy-start | bytes 1572868

commit v14 on v13

--- a/solution.py
+++ b/solution.py
@@ -857,10 +857,6 @@
         for copy in gain_loads(r):
             copy.start()
     yield outputs_at
-    loads[0].wait()
-    scatter = scatter_steps(rows, partial, near, far, acc, scatter_sems)
-    next(scatter)
-    yield None
     loads[1].wait()
     loads[2].wait()
     width = branch_low.shape[1]
@@ -877,6 +873,24 @@
         for j in range(part * owners // 4, (part + 1) * owners // 4):
             mix_made[j] = dot_tn(tokens_wide[:, j * own : (j + 1) * own], mix_low[...]).astype(bf16)
         yield mixes_at if part == 3 else None
+    loads[0].wait()
+    scatter = scatter_steps(rows, partial, near, far, acc, scatter_sems)
+    next(scatter)
+    yield None
+    for r in range(gain_steps):
+        slot = r % 2
+        for copy in gain_loads(r):
+            copy.wait()
+        both = jnp.zeros((16, 1), f32)
+        for side in range(2):
+            both = both + jnp.sum(
+                sums[slot, side].astype(f32) * low(weights[slot, side]), axis=1, keepdims=True
+            )
+        gain_ref[r * 16 : (r + 1) * 16, :] = both
+        if r + 2 < gain_steps:
+            for copy in gain_loads(r + 2):
+                copy.start()
+        yield None
     waits = next(scatter)
 
     def norm(here, i):
@@ -907,20 +921,6 @@
 
     by_tiles(rows, out)
     yield None
-    for r in range(gain_steps):
-        slot = r % 2
-        for copy in gain_loads(r):
-            copy.wait()
-        both = jnp.zeros((16, 1), f32)
-        for side in range(2):
-            both = both + jnp.sum(
-                sums[slot, side].astype(f32) * low(weights[slot, side]), axis=1, keepdims=True
-            )
-        gain_ref[r * 16 : (r + 1) * 16, :] = both
-        if r + 2 < gain_steps:
-            for copy in gain_loads(r + 2):
-                copy.start()
-        yield None
     for wait in waits:
         wait()
 
@@ -1028,6 +1028,10 @@
     return count
 
 
+def chunk_count(height, columns):
+    return pieces(height, max(16, (105 * 1024) // columns // 16 * 16))
+
+
 def line_kernel(n, kinds, cuts, made_here, beside, turns, extra, *refs):
     ins = len(cuts)
     made = ins + kinds.count("pair")
@@ -1230,7 +1234,7 @@
     tall = broad = 0
     for item, kind in zip(arrays, kinds):
         lead, height, columns = item.shape
-        count = pieces(height, max(16, (105 * 1024) // columns // 16 * 16))
+        count = chunk_count(height, columns)
         cuts.append((lead, count, height // count))
         tall, broad = max(tall, height // count), max(broad, columns)
         if kind == "pair":
@@ -1408,10 +1412,12 @@
     both = -(-2 * width // 128) * 128
     mix_shape = jax.ShapeDtypeStruct((members, depth // members, both), bf16)
     output_shape = jax.ShapeDtypeStruct((1,) + output_w.shape, bf16)
+    ahead = sum(chunk_count(*item.shape[1:]) for item in (packed, output_shape))
+    made_by = tuple(min(2 * k, ahead) for k in (1, 2, 3, 4))
     again = plane_scratch(rows, depth, 0, 1)
     packed, output_sum, mix_sum, tokens_grad, block_out, mlp_gain_grad = replica_sum(
         [packed, output_shape, mix_shape], ["row", "row", "side"], (1, 2), 4, functools.partial(end_steps, 1, 2),
-        (0, 1, 2, 3, 4, 7, 8, 9, 10, 11, 12, 19) + tuple(19 + i // 2 for i in range(gate_weight.shape[0] // 16)),
+        made_by + (10, 19, 20, 21, 22, 23, 24, 30) + tuple(11 + i // 2 for i in range(gate_weight.shape[0] // 16)),
         [(partial, ANY), (middle_grad, VM), (x, VM), (middle, VM)]
         + [(item, ANY) for item in (hidden, down_w, product, mid_low, unit_all, branch_low, conv_low, gate_sum, up_sum, gate_weight, up_weight)],
         [((rows, depth), bf16, VM), ((rows, depth), bf16, VM), ((gate_weight.shape[0], 1), f32, VM)],

time: 579 us -> 593 us (1.024)
  Pallas kernels: 558 us -> 573 us
    pallas_call x2, Pallas kernels: 349 us -> 364 us  [replica_sum(): pl.pallas_call(functools.partial(line_kernel, lax.axis_size('replica'), t...]
where the time goes in v14:
time: 593 us; the launch traced here: 588 us
  Pallas kernels  573 us (97%)
  other arithmetic  7.99 us (1%)
  local copies, waits for them, and re-layouts  6.26 us (1%)
    pallas_call x2, Pallas kernels, replica_sum(): pl.pallas_call(functools.partial(line_kernel, lax.axis_size('replica'), t...  364 us
    pallas_call x1, Pallas kernels, front(): pl.pallas_call(functools.partial(front_kernel, n, sequences, length), out...  153 us
    pallas_call x1, Pallas kernels, mlp(): pl.pallas_call(mlp_kernel, out_shape=tuple((jax.ShapeDtypeStruct(*item) f...  37.6 us

profile of v14, /device:TPU:0, one launch (start us, length us, event | category | flops | bytes accessed | tf_op | source)
XLA Modules:
  0.0 588.2 jit_solution(12761282936916210719)
XLA Ops:
  0.7 0.7 convert_bitcast_fusion
  1.3 1.3 compare_select_fusion.rate_ref.refs_10_
  2.6 0.7 pad_maximum_fusion
  3.3 0.7 broadcast_in_dim.15.label_ref
  4.0 0.8 copy.37.gains_ref.gain_ref
  4.8 153.4 %shard_map.305 = (bf16[1024,2048]{1,0:T(8,128)(2,1)}, bf16[1024,128]{1,0:T(8,128)(2,1)}, bf16[1024,2048]{1,0:T(8,128)(2,1)}, bf16[1024,320]{1,0:T(8,128)(2,1)}, ...) custom-call(bf16[128,2048]{1,0:T(8,128)(2,1)} %bitcast.17, ...), custom_call_target="tpu_custom_call" | custom-call | flops 1000000 | bytes 209715200 | tf_op jit(solution)/shard_map/pallas_call | solution.py:670
  158.2 37.6 %shard_map.306 = (bf16[1024,768]{1,0:T(8,128)(2,1)}, bf16[1024,2048]{1,0:T(8,128)(2,1)}, bf16[768,2048]{1,0:T(8,128)(2,1)}, bf16[2048,1536]{1,0:T(8,128)(2,1)}) custom-call(bf16[1024,2048]{1,0:T(8,128)(2,1)} %get-tuple-element.60.two_hbm, bf16[1024,2048]{1,0:T(8,128)(2,1)} %get-tuple-element.61.low_hbm, bf16[2048,1536]{1,0:T(8,128)(2,1)} %bitcast.25, ...), custom_call_target="tpu_custom_call" | custom-call | flops 25769803776 | bytes 37748736 | tf_op jit(solution)/shard_map/pallas_call | solution.py:1008
  195.8 226.9 %shard_map.307 = (bf16[768,2048]{1,0:T(8,128)(2,1)}, bf16[256,6144]{1,0:T(8,128)(2,1)}, bf16[256,6144]{1,0:T(8,128)(2,1)}, bf16[1024,2048]{1,0:T(8,128)(2,1)}, f...) custom-call(bf16[1,768,2048]{2,1,0:T(8,128)(2,1)} %bitcast.14, ...), custom_call_target="tpu_custom_call" | custom-call | flops 1000000 | bytes 209715200 | tf_op jit(solution)/shard_map/pallas_call | solution.py:1249
  422.7 0.0 copy-start.2
  422.8 136.9 %shard_map.308 = (bf16[336,384]{1,0:T(8,128)(2,1)}, bf16[320,2048]{1,0:T(8,128)(2,1)}, bf16[8,256,640]{2,1,0:T(8,128)(2,1)}, bf16[128,2048]{1,0:T(8,128)(2,1)}, ...) custom-call(bf16[1,336,384]{2,1,0:T(8,128)(2,1)} %get-tuple-element.78.refs_0_, ...), custom_call_target="tpu_custom_call" | custom-call | flops 1000000 | bytes 209715200 | tf_op jit(solution)/shard_map/pallas_call | solution.py:1249
  559.6 1.6 reduce.5
  561.2 1.3 slice.28
  562.5 1.0 convert_element_type.23
  563.5 0.6 fusion.7
  564.1 0.0 copy-done.2
  564.1 0.6 divide_multiply_fusion
  564.7 1.9 fusion.8
  566.6 8.0 %shard_map.310 = (f32[256,6144]{1,0:T(8,128)}, f32[256,6144]{1,0:T(8,128)}) custom-call(f32[256,2]{1,0:T(8,128)} %copy.37.gains_ref.gain_ref, bf16[256,6144]{1,0:T(8,128)(2,1)} %get-tuple-element.87.refs_12_.a_ref, bf16[256,6144]{1,0:T(8,128)(2,1)} %get-tuple-element.88.refs_13_.b_ref), custom_call_target="tpu_custom_call" | custom-call | flops 3145728 | bytes 18874368 | tf_op jit(solution)/shard_map/pallas_call | solution.py:1281
  574.6 0.0 copy-start.1
  574.6 0.0 copy-start
  574.6 10.0 %shard_map.309 = (f32[256,2560]{1,0:T(8,128)}, f32[256,2560]{1,0:T(8,128)}, f32[256,1]{1,0:T(8,128)}, f32[320,2048]{1,0:T(8,128)}, f32[768,2048]{1,0:T(8,128)}) custom-call(f32[256,2]{1,0:T(8,128)} %copy.37.gains_ref.gain_ref, bf16[8,256,640]{2,1,0:T(8,128)(2,1)} %get-tuple-element.91.mix_ref, f32[256,2560]{1,0:T(8,128)} %wa_ref.1, f32[256,2560]{1,0:T(8,128)} %wb_ref.1, ...), custom_call_target="tpu_custom_call" | custom-call | flops 10000000 | bytes 41943040 | tf_op jit(solution)/shard_map/pallas_call | solution.py:1319
  584.6 1.6 reduce
  586.1 0.0 copy-done.1
  586.2 0.8 copy.42
  586.9 0.0 copy-done
  586.9 0.8 copy.43
Async XLA Ops:
  422.7 141.4 %copy-start.2 = (f32[320]{0:T(512)S(1)}, f32[320]{0:T(512)}, u32[]{:S(2)}) copy-start(f32[320]{0:T(512)} %param.30) | copy-start | bytes 3844
  574.6 11.6 %copy-start.1 = (bf16[128,2048]{1,0:T(8,128)(2,1)S(1)}, bf16[128,2048]{1,0:T(8,128)(2,1)}, u32[]{:S(2)}) copy-start(bf16[128,2048]{1,0:T(8,128)(2,1)} %get-tuple-element.89) | copy-start | bytes 1572868
  574.6 12.3 %copy-start = (bf16[128,2048]{1,0:T(8,128)(2,1)S(1)}, bf16[128,2048]{1,0:T(8,128)(2,1)}, u32[]{:S(2)}) copy-start(bf16[128,2048]{1,0:T(8,128)(2,1)} %get-tuple-element.90) | copy-start | bytes 1572868

commit v15 on v14

--- a/solution.py
+++ b/solution.py
@@ -1413,11 +1413,11 @@
     mix_shape = jax.ShapeDtypeStruct((members, depth // members, both), bf16)
     output_shape = jax.ShapeDtypeStruct((1,) + output_w.shape, bf16)
     ahead = sum(chunk_count(*item.shape[1:]) for item in (packed, output_shape))
-    made_by = tuple(min(2 * k, ahead) for k in (1, 2, 3, 4))
+    made_by = tuple(min(k, ahead) for k in (0, 0, 1, 2))
     again = plane_scratch(rows, depth, 0, 1)
     packed, output_sum, mix_sum, tokens_grad, block_out, mlp_gain_grad = replica_sum(
         [packed, output_shape, mix_shape], ["row", "row", "side"], (1, 2), 4, functools.partial(end_steps, 1, 2),
-        made_by + (10, 19, 20, 21, 22, 23, 24, 30) + tuple(11 + i // 2 for i in range(gate_weight.shape[0] // 16)),
+        made_by + (4, 10, 11, 12, 13, 14, 15, 22) + tuple(5 + i // 4 for i in range(gate_weight.shape[0] // 16)),
         [(partial, ANY), (middle_grad, VM), (x, VM), (middle, VM)]
         + [(item, ANY) for item in (hidden, down_w, product, mid_low, unit_all, branch_low, conv_low, gate_sum, up_sum, gate_weight, up_weight)],
         [((rows, depth), bf16, VM), ((rows, depth), bf16, VM), ((gate_weight.shape[0], 1), f32, VM)],

time: 593 us -> 585 us (0.987)
  Pallas kernels: 573 us -> 565 us
    pallas_call x2, Pallas kernels: 364 us -> 356 us  [replica_sum(): pl.pallas_call(functools.partial(line_kernel, lax.axis_size('replica'), t...]
where the time goes in v15:
time: 585 us; the launch traced here: 581 us
  Pallas kernels  565 us (97%)
  other arithmetic  7.99 us (1%)
  local copies, waits for them, and re-layouts  6.26 us (1%)
    pallas_call x2, Pallas kernels, replica_sum(): pl.pallas_call(functools.partial(line_kernel, lax.axis_size('replica'), t...  356 us
    pallas_call x1, Pallas kernels, front(): pl.pallas_call(functools.partial(front_kernel, n, sequences, length), out...  153 us
    pallas_call x1, Pallas kernels, mlp(): pl.pallas_call(mlp_kernel, out_shape=tuple((jax.ShapeDtypeStruct(*item) f...  37.6 us

profile of v15, /device:TPU:0, one launch (start us, length us, event | category | flops | bytes accessed | tf_op | source)
XLA Modules:
  0.0 580.7 jit_solution(9715636773305052470)
XLA Ops:
  0.7 0.7 convert_bitcast_fusion
  1.3 1.3 compare_select_fusion.rate_ref.refs_10_
  2.6 0.7 pad_maximum_fusion
  3.3 0.7 broadcast_in_dim.15.label_ref
  4.0 0.8 copy.37.gains_ref.gain_ref
  4.8 153.4 %shard_map.305 = (bf16[1024,2048]{1,0:T(8,128)(2,1)}, bf16[1024,128]{1,0:T(8,128)(2,1)}, bf16[1024,2048]{1,0:T(8,128)(2,1)}, bf16[1024,320]{1,0:T(8,128)(2,1)}, ...) custom-call(bf16[128,2048]{1,0:T(8,128)(2,1)} %bitcast.17, ...), custom_call_target="tpu_custom_call" | custom-call | flops 1000000 | bytes 209715200 | tf_op jit(solution)/shard_map/pallas_call | solution.py:670
  158.2 37.6 %shard_map.306 = (bf16[1024,768]{1,0:T(8,128)(2,1)}, bf16[1024,2048]{1,0:T(8,128)(2,1)}, bf16[768,2048]{1,0:T(8,128)(2,1)}, bf16[2048,1536]{1,0:T(8,128)(2,1)}) custom-call(bf16[1024,2048]{1,0:T(8,128)(2,1)} %get-tuple-element.60.two_hbm, bf16[1024,2048]{1,0:T(8,128)(2,1)} %get-tuple-element.61.low_hbm, bf16[2048,1536]{1,0:T(8,128)(2,1)} %bitcast.25, ...), custom_call_target="tpu_custom_call" | custom-call | flops 25769803776 | bytes 37748736 | tf_op jit(solution)/shard_map/pallas_call | solution.py:1008
  195.8 226.9 %shard_map.307 = (bf16[768,2048]{1,0:T(8,128)(2,1)}, bf16[256,6144]{1,0:T(8,128)(2,1)}, bf16[256,6144]{1,0:T(8,128)(2,1)}, bf16[1024,2048]{1,0:T(8,128)(2,1)}, f...) custom-call(bf16[1,768,2048]{2,1,0:T(8,128)(2,1)} %bitcast.14, ...), custom_call_target="tpu_custom_call" | custom-call | flops 1000000 | bytes 209715200 | tf_op jit(solution)/shard_map/pallas_call | solution.py:1249
  422.7 0.0 copy-start.2
  422.8 129.3 %shard_map.308 = (bf16[336,384]{1,0:T(8,128)(2,1)}, bf16[320,2048]{1,0:T(8,128)(2,1)}, bf16[8,256,640]{2,1,0:T(8,128)(2,1)}, bf16[128,2048]{1,0:T(8,128)(2,1)}, ...) custom-call(bf16[1,336,384]{2,1,0:T(8,128)(2,1)} %get-tuple-element.78.refs_0_, ...), custom_call_target="tpu_custom_call" | custom-call | flops 1000000 | bytes 209715200 | tf_op jit(solution)/shard_map/pallas_call | solution.py:1249
  552.1 1.6 reduce.5
  553.7 1.3 slice.28
  555.0 1.0 convert_element_type.23
  556.0 0.6 fusion.7
  556.6 0.0 copy-done.2
  556.6 0.6 divide_multiply_fusion
  557.2 1.9 fusion.8
  559.1 8.0 %shard_map.310 = (f32[256,6144]{1,0:T(8,128)}, f32[256,6144]{1,0:T(8,128)}) custom-call(f32[256,2]{1,0:T(8,128)} %copy.37.gains_ref.gain_ref, bf16[256,6144]{1,0:T(8,128)(2,1)} %get-tuple-element.87.refs_12_.a_ref, bf16[256,6144]{1,0:T(8,128)(2,1)} %get-tuple-element.88.refs_13_.b_ref), custom_call_target="tpu_custom_call" | custom-call | flops 3145728 | bytes 18874368 | tf_op jit(solution)/shard_map/pallas_call | solution.py:1281
  567.1 0.0 copy-start.1
  567.1 0.0 copy-start
  567.1 10.0 %shard_map.309 = (f32[256,2560]{1,0:T(8,128)}, f32[256,2560]{1,0:T(8,128)}, f32[256,1]{1,0:T(8,128)}, f32[320,2048]{1,0:T(8,128)}, f32[768,2048]{1,0:T(8,128)}) custom-call(f32[256,2]{1,0:T(8,128)} %copy.37.gains_ref.gain_ref, bf16[8,256,640]{2,1,0:T(8,128)(2,1)} %get-tuple-element.91.mix_ref, f32[256,2560]{1,0:T(8,128)} %wa_ref.1, f32[256,2560]{1,0:T(8,128)} %wb_ref.1, ...), custom_call_target="tpu_custom_call" | custom-call | flops 10000000 | bytes 41943040 | tf_op jit(solution)/shard_map/pallas_call | solution.py:1319
  577.0 1.6 reduce
  578.6 0.0 copy-done.1
  578.6 0.8 copy.42
  579.4 0.0 copy-done
  579.4 0.8 copy.43
Async XLA Ops:
  422.7 133.8 %copy-start.2 = (f32[320]{0:T(512)S(1)}, f32[320]{0:T(512)}, u32[]{:S(2)}) copy-start(f32[320]{0:T(512)} %param.30) | copy-start | bytes 3844
  567.1 11.6 %copy-start.1 = (bf16[128,2048]{1,0:T(8,128)(2,1)S(1)}, bf16[128,2048]{1,0:T(8,128)(2,1)}, u32[]{:S(2)}) copy-start(bf16[128,2048]{1,0:T(8,128)(2,1)} %get-tuple-element.89) | copy-start | bytes 1572868
  567.1 12.3 %copy-start = (bf16[128,2048]{1,0:T(8,128)(2,1)S(1)}, bf16[128,2048]{1,0:T(8,128)(2,1)}, u32[]{:S(2)}) copy-start(bf16[128,2048]{1,0:T(8,128)(2,1)} %get-tuple-element.90) | copy-start | bytes 1572868
